TPU v7x, 32 devices: a whole 2x2x4 slice. The times are simulated.
32 devices in a mesh: gx: 4 (over y, x), gy: 8 (over z, core).
Axes of the slice: x: 2, y: 2, z: 4, core: 2. Of those that a mesh axis runs over, the one named last changes fastest.
Arguments:
- fluid_state: float32 [4, 32, 64, 512], P(None, None, 'gy', 'gx'), may hold values from -6 to 6
- particle_pos: float32 [3, 262144], P(None, ('gx', 'gy')), may hold values from -6 to 6
- particle_motion: float32 [6, 262144], P(None, ('gx', 'gy')), may hold values from -6 to 6
- particle_radius: float32 [262144], P(('gx', 'gy')), may hold values from 0.5 to 1
- particle_temp: float32 [262144], P(('gx', 'gy')), may hold values from -6 to 6
- particle_cell: int32 [262144], P(('gx', 'gy')), may hold values from 0 to 32767
- particle_box: int32 [262144, 1], P(('gx', 'gy')), may hold values from 0 to 31; in each aligned block of 8192 rows (0 to 8191, 8192 to 16383, ...) at most 512 rows name the same one
- box_owner: int32 [32], replicated, may hold values from 0 to 31, each once
- contact_mask: int32 [4096, 128, 128], P(('gx', 'gy')), may hold values 0 or 1
Outputs:
- fluid_next: float32 [4, 32, 64, 512], P(None, None, 'gy', 'gx')
- void_fraction: float32 [32, 64, 512], P(None, 'gy', 'gx')
- particle_next: float32 [7, 262144], P(None, ('gx', 'gy'))
Inputs may be any that keep to these rules, and one draw needn't show every extreme that they name: `particle_box`: among the 8192 rows of one device no box is named by more than 512 rows, a bound that some block reaches. `box_owner`: A permutation of the devices.
All inputs are finite; a program needn't handle non-finite values. No bound on the sum of `contact_mask` on one device may be relied on, other than what follows from the above.
Results may differ from a plain program's by a relative error of at most 0.0003.
Values sent between devices are 32-bit elements; how exact they have to be, the bound alone decides.
No kernel may reach another device: no remote copies, remote signals or barrier semaphores. Data moves between devices by JAX's collectives and lax.ppermute only.
A program may use at most 64 MiB of HBM per device.

v0:
```python
import jax
import jax.numpy as jnp
from jax import lax
from jax.sharding import PartitionSpec as P

BLOCK = 128


TIME_STEP = 0.1
STIFFNESS = 0.5
DAMPING_RATE = 0.2
ROTATION_DRAG = 0.1
DRAG_COEFF = 4.0
CONDUCTION = 0.3
HEAT_TRANSFER = 4.0
GRAVITY = 0.3
COUPLING = 4.0
CENTRE_WEIGHT = 0.25
SIDE_WEIGHT = 0.125


def padded_2(value, sides, width):
    for axis, dim in sides:
        size, length = (lax.axis_size(axis), value.shape[dim])
        up = [(i, (i + 1) % size) for i in range(size - 1)]
        down = [(j, i) for i, j in up]
        last = lax.slice_in_dim(value, length - width, length, axis=dim)
        first = lax.slice_in_dim(value, 0, width, axis=dim)
        before = lax.ppermute(last, axis, up)
        after = lax.ppermute(first, axis, down)
        value = jnp.concatenate([before, value, after], axis=dim)
    return value


def stencil(padded):
    interior = padded[:, :, 1:-1, 1:-1]
    z_padded = jnp.pad(interior, ((0, 0), (1, 1), (0, 0), (0, 0)))
    beside_all = z_padded[:, 2:] + z_padded[:, :-2]
    beside_all = beside_all + padded[:, :, 2:, 1:-1] + padded[:, :, :-2, 1:-1]
    beside_all = beside_all + padded[:, :, 1:-1, 2:] + padded[:, :, 1:-1, :-2]
    return CENTRE_WEIGHT * interior + SIDE_WEIGHT * beside_all


def one_hot(indices, count, dtype):
    return (indices[:, None] == jnp.arange(count, dtype=jnp.int32)[None, :]).astype(dtype)


def contact(arrived, mask_blocks):
    position = arrived[0:3]
    velocity = arrived[3:6]
    angular = arrived[6:9]
    fluid_vel = arrived[9:12]
    radius = arrived[12]
    solid_temp = arrived[13]
    gas_temp = arrived[14]
    occupied = (radius > 0.0).astype(jnp.float32)
    pair_mask = mask_blocks.astype(jnp.float32) * occupied[:, :, None] * occupied[:, None, :]
    distance = jnp.zeros(pair_mask.shape, jnp.float32)
    for component in range(3):
        offset = position[component][:, :, None] - position[component][:, None, :]
        distance = distance + offset * offset
    reach_sq = (radius[:, :, None] + radius[:, None, :]) ** 2 + 1.0
    weight = pair_mask * jnp.exp(-distance / reach_sq)
    weight_sum = jnp.sum(weight, axis=2)
    stacked = jnp.concatenate([position, velocity, angular, solid_temp[None]], axis=0)
    mixed = jnp.einsum("bij,cbj->cbi", weight, stacked, precision=lax.Precision.HIGHEST)
    spring = position * weight_sum - mixed[0:3]
    damping = velocity * weight_sum - mixed[3:6]
    drag_force = DRAG_COEFF / (radius * radius + 0.25) * (fluid_vel - velocity)
    upward = jnp.array([0.0, 0.0, 1.0], jnp.float32)[:, None, None]
    velocity_next = (
        velocity
        + TIME_STEP * (STIFFNESS * spring - DAMPING_RATE * damping + drag_force)
        - TIME_STEP * GRAVITY * upward
    )
    angular_next = angular - TIME_STEP * ROTATION_DRAG * (angular * weight_sum + mixed[6:9])
    temp_next = solid_temp + TIME_STEP * (
        CONDUCTION * (mixed[9] - solid_temp * weight_sum) + HEAT_TRANSFER * (gas_temp - solid_temp)
    )
    return jnp.concatenate([velocity_next, angular_next, drag_force, temp_next[None]], axis=0)


def shards(
    fluid_state,
    particle_pos,
    particle_motion,
    particle_radius,
    particle_temp,
    particle_cell,
    particle_box,
    box_owner,
    contact_mask,
):
    devices = lax.axis_size(("gx", "gy"))
    particles = particle_pos.shape[1]
    peer_slots = 2 * particles // devices
    grid_layers = fluid_state.shape[1]
    grid_rows = fluid_state.shape[2]
    grid_cols = fluid_state.shape[3]
    plane_rows = grid_layers * grid_rows
    block_rows = min(particles, 1024)
    num_blocks = particles // block_rows
    highest = lax.Precision.HIGHEST
    padded = padded_2(fluid_state, (("gx", 3), ("gy", 2)), 1)
    filtered = stencil(padded).reshape(4, plane_rows, grid_cols)
    cell_high = (particle_cell // grid_cols).reshape(num_blocks, block_rows)
    cell_low = (particle_cell % grid_cols).reshape(num_blocks, block_rows)

    def look_up(pieces):
        high_ids, low_ids = pieces
        partial_rows = jnp.einsum(
            "khl,pl->kph", filtered, one_hot(low_ids, grid_cols, jnp.float32), precision=highest
        )
        return jnp.sum(partial_rows * one_hot(high_ids, plane_rows, jnp.float32)[None], axis=2)

    at_particle = lax.map(look_up, (cell_high, cell_low)).transpose(1, 0, 2).reshape(4, particles)
    box_ids = particle_box[:, 0]
    device_ids = jnp.arange(devices, dtype=jnp.int32)
    box_match = box_ids[:, None] == device_ids[None, :]
    owner_dev = jnp.sum(jnp.where(box_match, box_owner[None, :], 0), axis=1)
    owner_hot = one_hot(owner_dev, devices, jnp.bfloat16).reshape(num_blocks, block_rows, devices)
    positions = jnp.arange(block_rows, dtype=jnp.int32)
    lower = (positions[:, None] > positions[None, :]).astype(jnp.bfloat16)
    within = jnp.einsum("ij,bjo->bio", lower, owner_hot, preferred_element_type=jnp.float32)
    block_counts = jnp.sum(owner_hot.astype(jnp.float32), axis=1)
    before = jnp.cumsum(block_counts, axis=0) - block_counts
    slot_rank = jnp.sum(
        (within + before[:, None, :]) * owner_hot.astype(jnp.float32), axis=2
    ).astype(jnp.int32)
    owner_blocks = owner_dev.reshape(num_blocks, block_rows)
    payload = jnp.concatenate(
        [
            particle_pos,
            particle_motion,
            at_particle[0:3],
            particle_radius[None],
            particle_temp[None],
            at_particle[3:4],
        ],
        axis=0,
    )
    payload_blocks = payload.reshape(15, num_blocks, block_rows).transpose(1, 0, 2)

    def place(total, pieces):
        values, owners, ranks = pieces
        weighted = values[:, :, None] * one_hot(owners, devices, jnp.float32)[None]
        added = jnp.einsum(
            "cpo,pr->cor", weighted, one_hot(ranks, peer_slots, jnp.float32), precision=highest
        )
        return (total + added, None)

    outgoing, _ = lax.scan(
        place,
        jnp.zeros((15, devices, peer_slots), jnp.float32),
        (payload_blocks, owner_blocks, slot_rank),
    )
    arrived = lax.all_to_all(outgoing, ("gx", "gy"), split_axis=1, concat_axis=1, tiled=True)
    arrived = arrived.reshape(15, devices * peer_slots // BLOCK, BLOCK)
    result = contact(arrived, contact_mask).reshape(10, devices, peer_slots)
    returned = lax.all_to_all(result, ("gx", "gy"), split_axis=1, concat_axis=1, tiled=True)

    def fetch(pieces):
        owners, ranks = pieces
        partial_rows = jnp.einsum(
            "cor,pr->cpo", returned, one_hot(ranks, peer_slots, jnp.float32), precision=highest
        )
        return jnp.sum(partial_rows * one_hot(owners, devices, jnp.float32)[None], axis=2)

    back = lax.map(fetch, (owner_blocks, slot_rank)).transpose(1, 0, 2).reshape(10, particles)
    particle_next = jnp.concatenate([back[0:6], back[9:10]], axis=0)
    volume = particle_radius**3
    deposit_terms = jnp.concatenate(
        [volume[None], -volume[None] * back[6:9], (volume * (back[9] - at_particle[3]))[None]],
        axis=0,
    )
    term_blocks = deposit_terms.reshape(5, num_blocks, block_rows).transpose(1, 0, 2)

    def deposit(total, pieces):
        values, high_ids, low_ids = pieces
        weighted = values[:, :, None] * one_hot(high_ids, plane_rows, jnp.float32)[None]
        added = jnp.einsum(
            "kph,pl->khl", weighted, one_hot(low_ids, grid_cols, jnp.float32), precision=highest
        )
        return (total + added, None)

    deposits, _ = lax.scan(
        deposit,
        jnp.zeros((5, plane_rows, grid_cols), jnp.float32),
        (term_blocks, cell_high, cell_low),
    )
    deposits = deposits.reshape(5, grid_layers, grid_rows, grid_cols)
    deposit_pad = padded_2(deposits, (("gx", 3), ("gy", 2)), 1)
    spread = stencil(deposit_pad)
    crowding = 1.0 + COUPLING * spread[0]
    void_fraction = 1.0 / crowding
    fluid_next = jnp.concatenate(
        [
            fluid_state[0:3] + TIME_STEP * COUPLING * spread[1:4] * crowding,
            fluid_state[3:4] + TIME_STEP * COUPLING * spread[4:5] * crowding,
        ],
        axis=0,
    )
    return (fluid_next, void_fraction, particle_next)


def solution(mesh):
    in_specs = (
        P(None, None, "gy", "gx"),
        P(None, ("gx", "gy")),
        P(None, ("gx", "gy")),
        P(("gx", "gy")),
        P(("gx", "gy")),
        P(("gx", "gy")),
        P(("gx", "gy"), None),
        P(),
        P(("gx", "gy"), None, None),
    )
    out_specs = (P(None, None, "gy", "gx"), P(None, "gy", "gx"), P(None, ("gx", "gy")))
    return jax.shard_map(shards, mesh=mesh, in_specs=in_specs, out_specs=out_specs, check_vma=False)
```

profile of v0, /device:TPU:10, one launch (start us, length us, event | category | flops | bytes accessed | tf_op | source)
XLA Modules:
  0.0 237.2 jit_solution(15134538567253300725)
XLA Ops:
  2.1 3.4 %collective-permute-start = (f32[4,32,8,1]{3,2,1,0:T(8,128)S(1)}, f32[4,32,8,1]{3,2,1,0:T(8,128)S(1)}, u32[]{:S(2)}, u32[]{:S(2)}) collective-permute-start(f32[4,32,8,1]{3,2,1,0:T(8,128)S(1)} %get-tuple-element.252), channel_id=1, source_target_pairs={{0,8},{8,16},{16,24},{1,9},{9,17},{17,25},{2,10},{10,18},{18,26},{... | collective-permute-start | bytes 12296 | tf_op jit(solution)/shard_map/ppermute | solution.py:29
  5.5 2.5 %collective-permute-start.1 = (f32[4,32,8,1]{3,2,1,0:T(8,128)S(1)}, f32[4,32,8,1]{3,2,1,0:T(8,128)S(1)}, u32[]{:S(2)}, u32[]{:S(2)}) collective-permute-start(f32[4,32,8,1]{3,2,1,0:T(8,128)S(1)} %get-tuple-element.251), channel_id=1, source_target_pairs={{8,0},{16,8},{24,16},{9,1},{17,9},{25,17},{10,2},{18,10},{26,18},{... | collective-permute-start | bytes 12296 | tf_op jit(solution)/shard_map/ppermute | solution.py:30
  10.1 7.8 %collective-permute-done = f32[4,32,8,1]{3,2,1,0:T(8,128)S(1)} collective-permute-done((f32[4,32,8,1]{3,2,1,0:T(8,128)S(1)}, f32[4,32,8,1]{3,2,1,0:T(8,128)S(1)}, u32[]{:S(2)}, u32[]{:S(2)}) %collective-permute-start) | collective-permute-done | bytes 4128 | tf_op jit(solution)/shard_map/ppermute | solution.py:29
  17.8 12.0 %collective-permute-done.1 = f32[4,32,8,1]{3,2,1,0:T(8,128)S(1)} collective-permute-done((f32[4,32,8,1]{3,2,1,0:T(8,128)S(1)}, f32[4,32,8,1]{3,2,1,0:T(8,128)S(1)}, u32[]{:S(2)}, u32[]{:S(2)}) %collective-permute-start.1) | collective-permute-done | bytes 4128 | tf_op jit(solution)/shard_map/ppermute | solution.py:30
  33.9 2.4 %collective-permute-start.3 = (f32[4,32,1,130]{3,1,2,0:T(8,128)S(1)}, f32[4,32,1,130]{3,1,2,0:T(8,128)S(1)}, u32[]{:S(2)}, u32[]{:S(2)}) collective-permute-start(f32[4,32,1,130]{3,1,2,0:T(8,128)S(1)} %copy.115), channel_id=1, source_target_pairs={{0,1},{1,2},{2,3},{3,4},{4,5},{5,6},{6,7},{8,9},{9,10},{10,11},{11... | collective-permute-start | bytes 199688 | tf_op jit(solution)/shard_map/ppermute | solution.py:29
  37.4 2.8 %collective-permute-done.3 = f32[4,32,1,130]{3,1,2,0:T(8,128)S(1)} collective-permute-done((f32[4,32,1,130]{3,1,2,0:T(8,128)S(1)}, f32[4,32,1,130]{3,1,2,0:T(8,128)S(1)}, u32[]{:S(2)}, u32[]{:S(2)}) %collective-permute-start.3) | collective-permute-done | bytes 66592 | tf_op jit(solution)/shard_map/ppermute | solution.py:29
  41.4 18.9 %while.42 = (s32[]{:T(128)}, f32[8,4,1024]{2,1,0:T(4,128)S(1)}, s32[8,1024]{1,0:T(8,128)S(1)}, f32[4,256,128]{2,1,0:T(8,128)S(1)}, s32[8,1024]{1,0:T(8,128)S(1)}, /*index=5*/s32[]{:T(128)}) while((s32[]{:T(128)}, f32[8,4,1024]{2,1,0:T(4,128)S(1)}, s32[8,1024]{1,0:T(8,128)S(1)}, f32[4,256,128]{2,1,0:T(8,128)S(1)}, s32[8,1024]{1,0:T(8,128)S(1)}, ...), condition=%wide.region_6.7_spmd, body=%wide.region_4.6_spmd.sunk | while | flops 1613361152 | bytes 2695245 | solution.py:116
  43.9 2.2 multiply_reduce_fusion.2
  46.3 2.2 multiply_reduce_fusion.2
  48.7 2.2 multiply_reduce_fusion.2
  55.7 2.2 multiply_reduce_fusion.2
  61.1 18.0 %while.44 = (s32[]{:T(128)}, f32[15,32,512]{2,1,0:T(8,128)S(1)}, f32[8,15,1024]{2,1,0:T(8,128)S(1)}, s32[8,1024]{1,0:T(8,128)S(1)}, s32[8,1024]{1,0:T(8,128)S(1)}, /*index=5*/s32[]{:T(128)}, s32[]{:T(128)}) while((s32[]{:T(128)}, f32[15,32,512]{2,1,0:T(8,128)S(1)}, f32[8,15,1024]{2,1,0:T(8,128)S(1)}, s32[8,1024]{1,0:T(8,128)S(1)}, ...), condition=%wide.region_8.9_spmd.clone, body=%wide.region_7.8_spmd.clone.sunk | while | flops 3021471744 | bytes 2437215 | solution.py:152
  79.7 29.6 %all_to_all.10 = f32[15,32,512]{2,0,1:T(8,128)S(1)} all-to-all(f32[15,32,512]{2,0,1:T(8,128)S(1)} %copy.117), channel_id=1, replica_groups=mesh['gx'=4,'gy'=8] {'gx','gy'}, dimensions={1} | all-to-all | bytes 1966080 | tf_op jit(solution)/shard_map/all_to_all | solution.py:157
  110.2 16.1 %fusion.101 = (f32[128,128]{1,0:T(8,128)S(1)}, f32[128,128,128]{2,1,0:T(8,128)S(1)}) fusion(f32[128,128]{1,0:T(8,128)S(1)} %bitcast.148, f32[128,128]{1,0:T(8,128)S(1)} %bitcast.151, f32[128,128]{1,0:T(8,128)S(1)} %bitcast.152, f32[128,128]{1,0:T(8,128)S(1)} %bitcast.153, f32[128,128]{1,0:T(8,128)S(1)} %compare_convert_fusion, s32[128,128,128]{2,1,0:T(8,128)} %param.26), kind=kLoop, calls=%fused_computation.160 | loop fusion | flops 37732352 | bytes 17170432 | tf_op jit(solution)/shard_map/reduce_sum | solution.py:64
  126.3 13.3 %fusion.54 = f32[128,10,128]{2,1,0:T(8,128)S(1)} fusion(f32[128,128,128]{2,1,0:T(8,128)S(1)} %get-tuple-element.218, f32[1,128,128]{2,0,1:T(1,128)S(1)} %bitcast.154, f32[3,128,128]{2,0,1:T(4,128)S(1)} %bitcast.143, f32[3,128,128]{2,0,1:T(4,128)S(1)} %bitcast.145, f32[3,128,128]{2,0,1:T(4,128)S(1)} %bitcast.144), kind=kOutput, calls=%fused_computation.55 | convolution fusion | flops 252149760 | bytes 9699328 | tf_op jit(solution)/shard_map/bij,cbj->cbi/dot_general | solution.py:66
  141.6 5.6 %all-to-all-start.1 = ((f32[10,32,512]{2,0,1:T(8,128)}), f32[10,32,512]{2,0,1:T(8,128)S(1)}, u32[]{:S(2)}, u32[]{:S(2)}) async-start(f32[10,32,512]{2,0,1:T(8,128)} %copy.127), calls=%async_computation.1 | async-start | bytes 2097152 | tf_op jit(solution)/shard_map/all_to_all | solution.py:160
  147.2 24.8 %all-to-all-done.1 = f32[10,32,512]{2,0,1:T(8,128)S(1)} async-done(((f32[10,32,512]{2,0,1:T(8,128)}), f32[10,32,512]{2,0,1:T(8,128)S(1)}, u32[]{:S(2)}, u32[]{:S(2)}) %all-to-all-start.1) | async-done | bytes 655392 | tf_op jit(solution)/shard_map/all_to_all | solution.py:160
  172.4 12.5 %while.43 = (s32[]{:T(128)}, f32[8,10,1024]{2,1,0:T(8,128)S(1)}, s32[8,1024]{1,0:T(8,128)S(1)}, f32[10,32,512]{2,1,0:T(8,128)S(1)}, s32[8,1024]{1,0:T(8,128)S(1)}, /*index=5*/s32[]{:T(128)}) while((s32[]{:T(128)}, f32[8,10,1024]{2,1,0:T(8,128)S(1)}, s32[8,1024]{1,0:T(8,128)S(1)}, f32[10,32,512]{2,1,0:T(8,128)S(1)}, ...), condition=%wide.region_12.13_spmd, body=%wide.region_10.12_spmd.sunk | while | flops 2014500864 | bytes 1114189 | solution.py:169
  186.8 26.1 %while.45 = (s32[]{:T(128)}, f32[5,256,128]{2,1,0:T(8,128)S(1)}, f32[8,5,1024]{2,1,0:T(8,128)S(1)}, s32[8,1024]{1,0:T(8,128)S(1)}, s32[8,1024]{1,0:T(8,128)S(1)}, /*index=5*/s32[]{:T(128)}, s32[]{:T(128)}) while((s32[]{:T(128)}, f32[5,256,128]{2,1,0:T(8,128)S(1)}, f32[8,5,1024]{2,1,0:T(8,128)S(1)}, s32[8,1024]{1,0:T(8,128)S(1)}, ...), condition=%wide.region_14.15_spmd.clone, body=%wide.region_13.14_spmd.clone.sunk | while | flops 2015559680 | bytes 3493983 | solution.py:186
  187.0 3.1 %fusion.138 = f32[5,256,128]{2,1,0:T(8,128)S(1)} fusion(f32[1024,256]{0,1:T(8,128)S(1)} %fusion.137, f32[5,1024]{1,0:T(8,128)S(1)} %dynamic-slice_bitcast_fusion.5, f32[5,256,128]{2,1,0:T(8,128)S(1)} %get-tuple-element.463, pred[]{:T(512)S(6)} %compare.12, s32[1024]{0:T(1024)S(1)} %bitcast.176), kind=kOutput, calls=%fused_computation.37.clone.1 | convolution fusion | flops 2015035392 | bytes 2383873 | tf_op jit(solution)/shard_map/while/body/eval_jaxpr/kph,pl->khl/dot_general | solution.py:181
  190.3 3.1 %fusion.138 = f32[5,256,128]{2,1,0:T(8,128)S(1)} fusion(f32[1024,256]{0,1:T(8,128)S(1)} %fusion.137, f32[5,1024]{1,0:T(8,128)S(1)} %dynamic-slice_bitcast_fusion.5, f32[5,256,128]{2,1,0:T(8,128)S(1)} %get-tuple-element.463, pred[]{:T(512)S(6)} %compare.12, s32[1024]{0:T(1024)S(1)} %bitcast.176), kind=kOutput, calls=%fused_computation.37.clone.1 | convolution fusion | flops 2015035392 | bytes 2383873 | tf_op jit(solution)/shard_map/while/body/eval_jaxpr/kph,pl->khl/dot_general | solution.py:181
  193.5 3.1 %fusion.138 = f32[5,256,128]{2,1,0:T(8,128)S(1)} fusion(f32[1024,256]{0,1:T(8,128)S(1)} %fusion.137, f32[5,1024]{1,0:T(8,128)S(1)} %dynamic-slice_bitcast_fusion.5, f32[5,256,128]{2,1,0:T(8,128)S(1)} %get-tuple-element.463, pred[]{:T(512)S(6)} %compare.12, s32[1024]{0:T(1024)S(1)} %bitcast.176), kind=kOutput, calls=%fused_computation.37.clone.1 | convolution fusion | flops 2015035392 | bytes 2383873 | tf_op jit(solution)/shard_map/while/body/eval_jaxpr/kph,pl->khl/dot_general | solution.py:181
  196.8 3.1 %fusion.138 = f32[5,256,128]{2,1,0:T(8,128)S(1)} fusion(f32[1024,256]{0,1:T(8,128)S(1)} %fusion.137, f32[5,1024]{1,0:T(8,128)S(1)} %dynamic-slice_bitcast_fusion.5, f32[5,256,128]{2,1,0:T(8,128)S(1)} %get-tuple-element.463, pred[]{:T(512)S(6)} %compare.12, s32[1024]{0:T(1024)S(1)} %bitcast.176), kind=kOutput, calls=%fused_computation.37.clone.1 | convolution fusion | flops 2015035392 | bytes 2383873 | tf_op jit(solution)/shard_map/while/body/eval_jaxpr/kph,pl->khl/dot_general | solution.py:181
  200.1 3.1 %fusion.138 = f32[5,256,128]{2,1,0:T(8,128)S(1)} fusion(f32[1024,256]{0,1:T(8,128)S(1)} %fusion.137, f32[5,1024]{1,0:T(8,128)S(1)} %dynamic-slice_bitcast_fusion.5, f32[5,256,128]{2,1,0:T(8,128)S(1)} %get-tuple-element.463, pred[]{:T(512)S(6)} %compare.12, s32[1024]{0:T(1024)S(1)} %bitcast.176), kind=kOutput, calls=%fused_computation.37.clone.1 | convolution fusion | flops 2015035392 | bytes 2383873 | tf_op jit(solution)/shard_map/while/body/eval_jaxpr/kph,pl->khl/dot_general | solution.py:181
  203.3 3.1 %fusion.138 = f32[5,256,128]{2,1,0:T(8,128)S(1)} fusion(f32[1024,256]{0,1:T(8,128)S(1)} %fusion.137, f32[5,1024]{1,0:T(8,128)S(1)} %dynamic-slice_bitcast_fusion.5, f32[5,256,128]{2,1,0:T(8,128)S(1)} %get-tuple-element.463, pred[]{:T(512)S(6)} %compare.12, s32[1024]{0:T(1024)S(1)} %bitcast.176), kind=kOutput, calls=%fused_computation.37.clone.1 | convolution fusion | flops 2015035392 | bytes 2383873 | tf_op jit(solution)/shard_map/while/body/eval_jaxpr/kph,pl->khl/dot_general | solution.py:181
  206.6 3.1 %fusion.138 = f32[5,256,128]{2,1,0:T(8,128)S(1)} fusion(f32[1024,256]{0,1:T(8,128)S(1)} %fusion.137, f32[5,1024]{1,0:T(8,128)S(1)} %dynamic-slice_bitcast_fusion.5, f32[5,256,128]{2,1,0:T(8,128)S(1)} %get-tuple-element.463, pred[]{:T(512)S(6)} %compare.12, s32[1024]{0:T(1024)S(1)} %bitcast.176), kind=kOutput, calls=%fused_computation.37.clone.1 | convolution fusion | flops 2015035392 | bytes 2383873 | tf_op jit(solution)/shard_map/while/body/eval_jaxpr/kph,pl->khl/dot_general | solution.py:181
  209.9 3.1 %fusion.138 = f32[5,256,128]{2,1,0:T(8,128)S(1)} fusion(f32[1024,256]{0,1:T(8,128)S(1)} %fusion.137, f32[5,1024]{1,0:T(8,128)S(1)} %dynamic-slice_bitcast_fusion.5, f32[5,256,128]{2,1,0:T(8,128)S(1)} %get-tuple-element.463, pred[]{:T(512)S(6)} %compare.12, s32[1024]{0:T(1024)S(1)} %bitcast.176), kind=kOutput, calls=%fused_computation.37.clone.1 | convolution fusion | flops 2015035392 | bytes 2383873 | tf_op jit(solution)/shard_map/while/body/eval_jaxpr/kph,pl->khl/dot_general | solution.py:181
  213.5 3.4 %collective-permute-start.4 = (f32[5,32,8,1]{1,2,3,0:T(8,128)S(1)}, f32[5,32,8,1]{1,2,3,0:T(8,128)S(1)}, u32[]{:S(2)}, u32[]{:S(2)}) collective-permute-start(f32[5,32,8,1]{1,2,3,0:T(8,128)S(1)} %copy.129), channel_id=1, source_target_pairs={{0,8},{8,16},{16,24},{1,9},{9,17},{17,25},{2,10},{10,18},{18,26},{... | collective-permute-start | bytes 15368 | tf_op jit(solution)/shard_map/ppermute | solution.py:29
  217.2 2.4 %collective-permute-start.5 = (f32[5,32,8,1]{1,2,3,0:T(8,128)S(1)}, f32[5,32,8,1]{1,2,3,0:T(8,128)S(1)}, u32[]{:S(2)}, u32[]{:S(2)}) collective-permute-start(f32[5,32,8,1]{1,2,3,0:T(8,128)S(1)} %copy.130), channel_id=1, source_target_pairs={{8,0},{16,8},{24,16},{9,1},{17,9},{25,17},{10,2},{18,10},{26,18},{... | collective-permute-start | bytes 15368 | tf_op jit(solution)/shard_map/ppermute | solution.py:30
  220.1 3.7 %collective-permute-done.5 = f32[5,32,8,1]{1,2,3,0:T(8,128)S(1)} collective-permute-done((f32[5,32,8,1]{1,2,3,0:T(8,128)S(1)}, f32[5,32,8,1]{1,2,3,0:T(8,128)S(1)}, u32[]{:S(2)}, u32[]{:S(2)}) %collective-permute-start.5) | collective-permute-done | bytes 5152 | tf_op jit(solution)/shard_map/ppermute | solution.py:30
  225.2 2.5 %collective-permute-start.6 = (f32[5,32,1,130]{3,2,1,0:T(1,128)S(1)}, f32[5,32,1,130]{3,2,1,0:T(1,128)S(1)}, u32[]{:S(2)}, u32[]{:S(2)}) collective-permute-start(f32[5,32,1,130]{3,2,1,0:T(1,128)S(1)} %get-tuple-element.227), channel_id=1, source_target_pairs={{1,0},{2,1},{3,2},{4,3},{5,4},{6,5},{7,6},{9,8},{10,9},{11,10},{12... | collective-permute-start | bytes 249608 | tf_op jit(solution)/shard_map/ppermute | solution.py:30
  230.6 3.8 %collective-permute-done.7 = f32[5,32,1,130]{3,2,1,0:T(1,128)S(1)} collective-permute-done((f32[5,32,1,130]{3,2,1,0:T(1,128)S(1)}, f32[5,32,1,130]{3,2,1,0:T(1,128)S(1)}, u32[]{:S(2)}, u32[]{:S(2)}) %collective-permute-start.7) | collective-permute-done | bytes 83232 | tf_op jit(solution)/shard_map/ppermute | solution.py:29
  (197 shorter events, 65.0 us)
Async XLA Ops:
  0.6 39.7 %copy-start = (f32[4,32,8,128]{3,2,1,0:T(8,128)S(1)}, f32[4,32,8,128]{3,2,1,0:T(8,128)}, u32[]{:S(2)}) copy-start(f32[4,32,8,128]{3,2,1,0:T(8,128)} %param.18) | copy-start | bytes 1572868
  2.1 15.7 %collective-permute-start = (f32[4,32,8,1]{3,2,1,0:T(8,128)S(1)}, f32[4,32,8,1]{3,2,1,0:T(8,128)S(1)}, u32[]{:S(2)}, u32[]{:S(2)}) collective-permute-start(f32[4,32,8,1]{3,2,1,0:T(8,128)S(1)} %get-tuple-element.252), channel_id=1, source_target_pairs={{0,8},{8,16},{16,24},{1,9},{9,17},{17,25},{2,10},{10,18},{18,26},{... | collective-permute-start | bytes 12296 | tf_op jit(solution)/shard_map/ppermute | solution.py:29
  5.5 24.3 %collective-permute-start.1 = (f32[4,32,8,1]{3,2,1,0:T(8,128)S(1)}, f32[4,32,8,1]{3,2,1,0:T(8,128)S(1)}, u32[]{:S(2)}, u32[]{:S(2)}) collective-permute-start(f32[4,32,8,1]{3,2,1,0:T(8,128)S(1)} %get-tuple-element.251), channel_id=1, source_target_pairs={{8,0},{16,8},{24,16},{9,1},{17,9},{25,17},{10,2},{18,10},{26,18},{... | collective-permute-start | bytes 12296 | tf_op jit(solution)/shard_map/ppermute | solution.py:30
  32.0 5.3 %collective-permute-start.2 = (f32[4,32,1,130]{3,1,2,0:T(8,128)S(1)}, f32[4,32,1,130]{3,1,2,0:T(8,128)S(1)}, u32[]{:S(2)}, u32[]{:S(2)}) collective-permute-start(f32[4,32,1,130]{3,1,2,0:T(8,128)S(1)} %copy.113), channel_id=1, source_target_pairs={{1,0},{2,1},{3,2},{4,3},{5,4},{6,5},{7,6},{9,8},{10,9},{11,10},{12... | collective-permute-start | bytes 199688 | tf_op jit(solution)/shard_map/ppermute | solution.py:30
  33.9 6.3 %collective-permute-start.3 = (f32[4,32,1,130]{3,1,2,0:T(8,128)S(1)}, f32[4,32,1,130]{3,1,2,0:T(8,128)S(1)}, u32[]{:S(2)}, u32[]{:S(2)}) collective-permute-start(f32[4,32,1,130]{3,1,2,0:T(8,128)S(1)} %copy.115), channel_id=1, source_target_pairs={{0,1},{1,2},{2,3},{3,4},{4,5},{5,6},{6,7},{8,9},{9,10},{10,11},{11... | collective-permute-start | bytes 199688 | tf_op jit(solution)/shard_map/ppermute | solution.py:29
  41.4 19.0 %copy-start.2 = (f32[6,8192]{1,0:T(8,128)S(1)}, f32[6,8192]{1,0:T(8,128)}, u32[]{:S(2)}) copy-start(f32[6,8192]{1,0:T(8,128)} %param.20) | copy-start | bytes 589828
  41.4 19.0 %copy-start.3 = (f32[3,8192]{1,0:T(4,128)S(1)}, f32[3,8192]{1,0:T(4,128)}, u32[]{:S(2)}) copy-start(f32[3,8192]{1,0:T(4,128)} %param.19) | copy-start | bytes 294916
  41.4 19.0 %copy-start.4 = (f32[8192]{0:T(1024)S(1)}, f32[8192]{0:T(1024)}, u32[]{:S(2)}) copy-start(f32[8192]{0:T(1024)} %param.21) | copy-start | bytes 98308
  41.4 19.0 %copy-start.5 = (f32[8192]{0:T(1024)S(1)}, f32[8192]{0:T(1024)}, u32[]{:S(2)}) copy-start(f32[8192]{0:T(1024)} %param.22) | copy-start | bytes 98308
  60.3 0.8 copy-start.1
  126.3 13.6 %copy-start.6 = (f32[3]{0:T(128)S(1)}, f32[3]{0:T(128)}, u32[]{:S(2)}) copy-start(f32[3]{0:T(128)} %constant.118) | copy-start | bytes 40
  141.6 30.5 %all-to-all-start.1 = ((f32[10,32,512]{2,0,1:T(8,128)}), f32[10,32,512]{2,0,1:T(8,128)S(1)}, u32[]{:S(2)}, u32[]{:S(2)}) async-start(f32[10,32,512]{2,0,1:T(8,128)} %copy.127), calls=%async_computation.1 | async-start | bytes 2097152 | tf_op jit(solution)/shard_map/all_to_all | solution.py:160
  213.5 6.2 %collective-permute-start.4 = (f32[5,32,8,1]{1,2,3,0:T(8,128)S(1)}, f32[5,32,8,1]{1,2,3,0:T(8,128)S(1)}, u32[]{:S(2)}, u32[]{:S(2)}) collective-permute-start(f32[5,32,8,1]{1,2,3,0:T(8,128)S(1)} %copy.129), channel_id=1, source_target_pairs={{0,8},{8,16},{16,24},{1,9},{9,17},{17,25},{2,10},{10,18},{18,26},{... | collective-permute-start | bytes 15368 | tf_op jit(solution)/shard_map/ppermute | solution.py:29
  217.2 6.6 %collective-permute-start.5 = (f32[5,32,8,1]{1,2,3,0:T(8,128)S(1)}, f32[5,32,8,1]{1,2,3,0:T(8,128)S(1)}, u32[]{:S(2)}, u32[]{:S(2)}) collective-permute-start(f32[5,32,8,1]{1,2,3,0:T(8,128)S(1)} %copy.130), channel_id=1, source_target_pairs={{8,0},{16,8},{24,16},{9,1},{17,9},{25,17},{10,2},{18,10},{26,18},{... | collective-permute-start | bytes 15368 | tf_op jit(solution)/shard_map/ppermute | solution.py:30
  225.2 5.4 %collective-permute-start.6 = (f32[5,32,1,130]{3,2,1,0:T(1,128)S(1)}, f32[5,32,1,130]{3,2,1,0:T(1,128)S(1)}, u32[]{:S(2)}, u32[]{:S(2)}) collective-permute-start(f32[5,32,1,130]{3,2,1,0:T(1,128)S(1)} %get-tuple-element.227), channel_id=1, source_target_pairs={{1,0},{2,1},{3,2},{4,3},{5,4},{6,5},{7,6},{9,8},{10,9},{11,10},{12... | collective-permute-start | bytes 249608 | tf_op jit(solution)/shard_map/ppermute | solution.py:30
  227.8 6.6 %collective-permute-start.7 = (f32[5,32,1,130]{3,2,1,0:T(1,128)S(1)}, f32[5,32,1,130]{3,2,1,0:T(1,128)S(1)}, u32[]{:S(2)}, u32[]{:S(2)}) collective-permute-start(f32[5,32,1,130]{3,2,1,0:T(1,128)S(1)} %get-tuple-element.228), channel_id=1, source_target_pairs={{0,1},{1,2},{2,3},{3,4},{4,5},{5,6},{6,7},{8,9},{9,10},{10,11},{11... | collective-permute-start | bytes 249608 | tf_op jit(solution)/shard_map/ppermute | solution.py:29
where the time goes:
time: 238 us; the launch traced here: 237 us
  matrix products  85.2 us (36%)
  waiting for transfers between devices  55.1 us (23%)
  other arithmetic  30.6 us (13%)
  blocking collectives  29.6 us (12%)
  starting transfers between devices  26.1 us (11%)
  local copies, waits for them, and re-layouts  7.9 us (3%)
    all_to_all x1, blocking collectives, shards(): lax.all_to_all(outgoing, ('gx', 'gy'), split_axis=1, concat_axis=1, tiled...  29.6 us
    all_to_all x1, waiting for transfers between devices, shards(): lax.all_to_all(result, ('gx', 'gy'), split_axis=1, concat_axis=1, tiled=T...  24.8 us
    dot_general x8, matrix products, deposit(): jnp.einsum('kph,pl->khl', weighted, one_hot(low_ids, grid_cols, jnp.float...  24.6 us
    dot_general x8, matrix products, look_up(): jnp.einsum('khl,pl->kph', filtered, one_hot(low_ids, grid_cols, jnp.float...  17.4 us
    dot_general x8, matrix products, place(): jnp.einsum('cpo,pr->cor', weighted, one_hot(ranks, peer_slots, jnp.float3...  17.3 us
    reduce_sum x1, other arithmetic, contact(): weight_sum = jnp.sum(weight, axis=2)  16.1 us
    ppermute x4, waiting for transfers between devices, padded_2(): after = lax.ppermute(first, axis, down)  15.9 us
    ppermute x4, waiting for transfers between devices, padded_2(): before = lax.ppermute(last, axis, up)  14.4 us
  transfers between devices with their start and end apart: 9, of which 7 were waited for; matrix products, arithmetic and copies ran while one was open for 2% of the time, Pallas kernels for 0%

commit v1 on v0

v1 whole, which is shorter than its diff:
```python
import functools

import jax
import jax.numpy as jnp
from jax import lax
from jax.experimental import pallas as pl
from jax.experimental.pallas import tpu as pltpu
from jax.sharding import PartitionSpec as P

BLOCK = 128
TIME_STEP = 0.1
STIFFNESS = 0.5
DAMPING_RATE = 0.2
ROTATION_DRAG = 0.1
DRAG_COEFF = 4.0
CONDUCTION = 0.3
HEAT_TRANSFER = 4.0
GRAVITY = 0.3
COUPLING = 4.0
CENTRE_WEIGHT = 0.25
SIDE_WEIGHT = 0.125

F32 = jnp.float32
BF16 = jnp.bfloat16
VMEM = pltpu.VMEM
NT = (((1,), (1,)), ((), ()))
NN = (((1,), (0,)), ((), ()))


def split(value):
    high = value.astype(BF16)
    return high, (value - high.astype(F32)).astype(BF16)


def hot(count, row):
    places = lax.broadcasted_iota(jnp.int32, (count, row.shape[1]), 0)
    return jnp.where(places == row, 1.0, 0.0).astype(BF16)


def rank_hot(ranks, slots):
    places = lax.broadcasted_iota(jnp.int32, (slots, ranks.shape[1]), 0)
    return jnp.where(places == ranks, 1.0, 0.0).astype(BF16)


def place_kernel(
    owner_ref, box_ref, pos_ref, motion_ref, radius_ref, temp_ref,
    out_ref, rank_ref, box_of, first_acc, second_acc, *, chunk
):
    devices, rows, _ = out_ref.shape
    layers = rows // 12
    slots = layers * BLOCK
    particles = box_ref.shape[1]

    def invert(b, _):
        box_of[owner_ref[b]] = b
        return 0

    lax.fori_loop(0, devices, invert, 0)
    first_acc[...] = jnp.zeros_like(first_acc)
    second_acc[...] = jnp.zeros_like(second_acc)
    sub = 256
    above = (
        lax.broadcasted_iota(jnp.int32, (sub, sub), 0) < lax.broadcasted_iota(jnp.int32, (sub, sub), 1)
    )
    above = jnp.where(above, 1.0, 0.0).astype(BF16)

    def step(k, carry):
        base = pl.multiple_of(k * chunk, chunk)
        here = pl.ds(base, chunk)
        boxes = box_ref[:, here]
        pieces = []
        for s in range(chunk // sub):
            mine = boxes[:, s * sub : (s + 1) * sub]
            chosen = lax.broadcasted_iota(jnp.int32, (devices, sub), 0) == mine
            ones = jnp.where(chosen, 1.0, 0.0)
            earlier = lax.dot_general(ones.astype(BF16), above, NN, preferred_element_type=F32) + carry
            pieces.append(jnp.sum(jnp.where(chosen, earlier, 0.0), axis=0, keepdims=True))
            carry = carry + jnp.sum(ones, axis=1, keepdims=True)
        ranks = jnp.concatenate(pieces, axis=1).astype(jnp.int32)
        rank_ref[:, here] = ranks
        hot_rank = rank_hot(ranks, slots)
        pos = pos_ref[:, here]
        motion = motion_ref[:, here]
        push = TIME_STEP * STIFFNESS * pos - TIME_STEP * DAMPING_RATE * motion[0:3]
        spin = -TIME_STEP * ROTATION_DRAG * motion[3:6]
        heat = -TIME_STEP * CONDUCTION * temp_ref[:, here]
        first = jnp.concatenate([push, spin, heat, jnp.ones((1, chunk), F32)], axis=0)
        second = jnp.concatenate([pos, radius_ref[:, here]], axis=0)
        first = jnp.concatenate(split(first), axis=0)
        second = jnp.concatenate(split(second), axis=0)
        box16 = jnp.broadcast_to(boxes, (16, chunk)).astype(F32).astype(BF16)
        first_parts = []
        second_parts = []
        for o in range(devices):
            mine = box16 == box_of[o].astype(F32).astype(BF16)
            first_parts.append(jnp.where(mine, first, jnp.zeros_like(first)))
            second_parts.append(jnp.where(mine[0:8], second, jnp.zeros_like(second)))
        first_acc[...] += lax.dot_general(
            jnp.concatenate(first_parts, axis=0), hot_rank, NT, preferred_element_type=F32
        )
        second_acc[...] += lax.dot_general(
            jnp.concatenate(second_parts, axis=0), hot_rank, NT, preferred_element_type=F32
        )
        return carry

    lax.fori_loop(0, particles // chunk, step, jnp.zeros((devices, 1), F32))

    def finish(o, _):
        first = first_acc[pl.ds(pl.multiple_of(16 * o, 16), 8), :] + first_acc[pl.ds(pl.multiple_of(16 * o + 8, 8), 8), :]
        second = second_acc[pl.ds(pl.multiple_of(8 * o, 8), 8), :]
        second = second[0:4] + second[4:8]
        for q in range(layers):
            lanes = slice(q * BLOCK, (q + 1) * BLOCK)
            out_ref[o, 8 * q : 8 * q + 8, :] = first[:, lanes]
            out_ref[o, 8 * layers + 4 * q : 8 * layers + 4 * q + 4, :] = second[:, lanes]
        return 0

    lax.fori_loop(0, devices, finish, 0)


def place(box_owner, boxes, pos, motion, radius, temp, slots):
    devices = box_owner.shape[0]
    particles = pos.shape[1]
    layers = slots // BLOCK
    vmem = pl.BlockSpec(memory_space=VMEM)
    return pl.pallas_call(
        functools.partial(place_kernel, chunk=1024),
        out_shape=(
            jax.ShapeDtypeStruct((devices, 12 * layers, BLOCK), F32),
            jax.ShapeDtypeStruct((1, particles), jnp.int32),
        ),
        in_specs=[pl.BlockSpec(memory_space=pltpu.SMEM)] + [vmem] * 5,
        out_specs=(vmem, vmem),
        scratch_shapes=[
            pltpu.SMEM((devices,), jnp.int32),
            VMEM((16 * devices, slots), F32),
            VMEM((8 * devices, slots), F32),
        ],
        compiler_params=pltpu.CompilerParams(vmem_limit_bytes=40 << 20),
        cost_estimate=pl.CostEstimate(
            flops=2 * 24 * devices * slots * particles, bytes_accessed=1 << 20, transcendentals=0
        ),
        name="place_slots",
    )(box_owner, boxes, pos, motion, radius, temp)


def contact_kernel(slot_ref, mask_ref, out_ref):
    homes, rows, _ = slot_ref.shape
    layers = rows // 12
    sign = lax.broadcasted_iota(jnp.int32, (8, 1), 0)
    sign = jnp.where((sign >= 3) & (sign < 6), 1.0, -1.0)
    for s in range(homes):
        for q in range(layers):
            mixed = slot_ref[s, 8 * q : 8 * q + 8, :]
            near = slot_ref[s, 8 * layers + 4 * q : 8 * layers + 4 * q + 4, :]
            near_i = jnp.transpose(jnp.concatenate([near, near], axis=0))
            distance = None
            for axis in range(3):
                offset = near_i[:, axis : axis + 1] - near[axis : axis + 1, :]
                distance = offset * offset if distance is None else distance + offset * offset
            reach = near_i[:, 3:4] + near[3:4, :]
            reach = reach * reach + 1.0
            inverse = pl.reciprocal(reach, approx=True)
            inverse = inverse * (2.0 - reach * inverse)
            weight = mask_ref[s * layers + q].astype(F32) * jnp.exp(-distance * inverse)
            weight_high, weight_low = split(weight)
            mixed_high, mixed_low = split(mixed)
            both = jnp.concatenate([mixed_high, mixed_low], axis=0)
            sums = lax.dot_general(both, weight_high, NT, preferred_element_type=F32)
            more = lax.dot_general(both, weight_low, NT, preferred_element_type=F32)
            sums = sums + more
            sums = sums[0:8] + sums[8:16]
            out_ref[s, 8 * q : 8 * q + 8, :] = mixed * sums[7:8] + sign * sums


def contact(arrived, mask):
    devices, rows, _ = arrived.shape
    layers = rows // 12
    blocks = mask.shape[0]
    step = 2 if layers > 1 else 8
    return pl.pallas_call(
        contact_kernel,
        grid=(devices // step,),
        out_shape=jax.ShapeDtypeStruct((devices, 8 * layers, BLOCK), F32),
        in_specs=[
            pl.BlockSpec((step, rows, BLOCK), lambda h: (h, 0, 0)),
            pl.BlockSpec((step * layers, BLOCK, BLOCK), lambda h: (h, 0, 0)),
        ],
        out_specs=pl.BlockSpec((step, 8 * layers, BLOCK), lambda h: (h, 0, 0)),
        compiler_params=pltpu.CompilerParams(vmem_limit_bytes=40 << 20),
        cost_estimate=pl.CostEstimate(
            flops=64 * blocks * BLOCK * BLOCK, bytes_accessed=blocks * BLOCK * BLOCK * 4, transcendentals=0
        ),
        name="contact_blocks",
    )(arrived, mask)


def smoothed(centre, y_first, y_last, x_first, x_last):
    layers, rows, cols = centre.shape
    zero = jnp.zeros((1, rows, cols), F32)
    up = jnp.concatenate([centre[1:], zero], axis=0)
    down = jnp.concatenate([zero, centre[:-1]], axis=0)
    row = lax.broadcasted_iota(jnp.int32, (1, rows, cols), 1)
    col = lax.broadcasted_iota(jnp.int32, (1, rows, cols), 2)
    back = jnp.where(row == 0, y_first, pltpu.roll(centre, 1, 1))
    front = jnp.where(row == rows - 1, y_last, pltpu.roll(centre, rows - 1, 1))
    left = jnp.where(col == 0, x_first, pltpu.roll(centre, 1, 2))
    right = jnp.where(col == cols - 1, x_last, pltpu.roll(centre, cols - 1, 2))
    return CENTRE_WEIGHT * centre + SIDE_WEIGHT * ((up + down) + (back + front) + (left + right))


def columns(edge, layers, rows):
    count = edge.shape[0]
    if count < 8:
        edge = jnp.concatenate([edge] * (8 // count), axis=0)
    turned = jnp.transpose(edge)
    parts = [turned[:, a : a + 1] for a in range(count)]
    return jnp.concatenate(parts, axis=0).reshape(layers, rows, 1)


def smooth_field(field_ref, y0_ref, y1_ref, x0_ref, x1_ref, k):
    _, layers, rows, cols = field_ref.shape
    per = layers * rows // BLOCK
    x0 = columns(x0_ref[k * per : (k + 1) * per, :], layers, rows)
    x1 = columns(x1_ref[k * per : (k + 1) * per, :], layers, rows)
    y0 = y0_ref[k].reshape(layers, 1, cols)
    y1 = y1_ref[k].reshape(layers, 1, cols)
    return smoothed(field_ref[k], y0, y1, x0, x1)


def write_edges(field, k, y0_ref, y1_ref, x0_ref, x1_ref):
    layers, rows, cols = field.shape
    y0_ref[k] = field[:, 0, :]
    y1_ref[k] = field[:, rows - 1, :]
    flat = field.reshape(layers * rows, cols)
    for a in range(layers * rows // BLOCK):
        turned = jnp.transpose(flat[a * BLOCK : (a + 1) * BLOCK, :])
        at = k * (layers * rows // BLOCK) + a
        x0_ref[at : at + 1, :] = turned[0:1, :]
        x1_ref[at : at + 1, :] = turned[cols - 1 : cols, :]


def paired_rows(pairs, layers, rows, scratch):
    half = pairs.shape[0]
    cols = pairs.shape[1] // 2
    scratch[pl.ds(0, half, stride=2), :] = pairs[:, :cols]
    scratch[pl.ds(1, half, stride=2), :] = pairs[:, cols:]
    return scratch[...].reshape(layers, rows, cols)


def fluid_kernel(
    fluid_ref, y0_ref, y1_ref, x0_ref, x1_ref, cell_ref, motion_ref, radius_ref, temp_ref,
    base_ref, dep_ref, dy0_ref, dy1_ref, dx0_ref, dx1_ref,
    table, rows_scratch, acc, *, chunk
):
    fields, layers, rows, cols = fluid_ref.shape
    half = layers * rows // 2
    wide = 2 * cols
    particles = cell_ref.shape[1]
    for k in range(fields):
        rows_scratch[...] = smooth_field(fluid_ref, y0_ref, y1_ref, x0_ref, x1_ref, k).reshape(layers * rows, cols)
        here = slice(k * half, (k + 1) * half)
        for part in range(2):
            high, low = split(rows_scratch[pl.ds(part, half, stride=2), :])
            table[0, here, part * cols : (part + 1) * cols] = high
            table[1, here, part * cols : (part + 1) * cols] = low
    acc[...] = jnp.zeros_like(acc)

    def step(i, _):
        here = pl.ds(pl.multiple_of(i * chunk, chunk), chunk)
        cells = cell_ref[:, here]
        hot_low = hot(wide, cells % wide)
        place_high = cells // wide
        hot_high = hot(half, place_high)
        found = lax.dot_general(table[0], hot_low, NN, preferred_element_type=F32)
        found = found + lax.dot_general(table[1], hot_low, NN, preferred_element_type=F32)
        mine = lax.broadcasted_iota(jnp.int32, (half, chunk), 0) == place_high
        seen = [
            jnp.sum(jnp.where(mine, found[k * half : (k + 1) * half], 0.0), axis=0, keepdims=True)
            for k in range(fields)
        ]
        motion = motion_ref[:, here]
        radius = radius_ref[:, here]
        temp = temp_ref[:, here]
        fluid_vel = jnp.concatenate(seen[0:3], axis=0)
        drag = DRAG_COEFF / (radius * radius + 0.25) * (fluid_vel - motion[0:3])
        upward = lax.broadcasted_iota(jnp.int32, (3, 1), 0) == 2
        moved = motion[0:3] + TIME_STEP * drag - jnp.where(upward, TIME_STEP * GRAVITY, 0.0)
        warmed = temp + TIME_STEP * HEAT_TRANSFER * (seen[3] - temp)
        base_ref[:, here] = jnp.concatenate([moved, motion[3:6], warmed, seen[3]], axis=0)
        volume = radius * radius * radius
        terms = jnp.concatenate([volume, -volume * drag], axis=0)
        high, low = split(terms)
        parts = []
        for piece in (high, low):
            parts.append(jnp.concatenate([hot_high * piece[k : k + 1] for k in range(4)], axis=0))
        total = lax.dot_general(parts[0], hot_low, NT, preferred_element_type=F32)
        acc[...] += total + lax.dot_general(parts[1], hot_low, NT, preferred_element_type=F32)
        return 0

    lax.fori_loop(0, particles // chunk, step, 0)
    for k in range(fields):
        field = paired_rows(acc[k * half : (k + 1) * half, :], layers, rows, rows_scratch)
        dep_ref[k] = field
        write_edges(field, k, dy0_ref, dy1_ref, dx0_ref, dx1_ref)


def edge_shapes(fields, layers, rows, cols):
    y_edge = jax.ShapeDtypeStruct((fields, layers, cols), F32)
    x_edge = jax.ShapeDtypeStruct((fields * layers * rows // BLOCK, BLOCK), F32)
    return (y_edge, y_edge, x_edge, x_edge)


def see_and_deposit(fluid, halo, cells, motion, radius, temp):
    fields, layers, rows, cols = fluid.shape
    particles = cells.shape[1]
    vmem = pl.BlockSpec(memory_space=VMEM)
    return pl.pallas_call(
        functools.partial(fluid_kernel, chunk=512),
        out_shape=(
            jax.ShapeDtypeStruct((8, particles), F32),
            jax.ShapeDtypeStruct(fluid.shape, F32),
        ) + edge_shapes(fields, layers, rows, cols),
        in_specs=[vmem] * 9,
        out_specs=(vmem,) * 6,
        scratch_shapes=[
            VMEM((2, fields * layers * rows // 2, 2 * cols), BF16),
            VMEM((layers * rows, cols), F32),
            VMEM((fields * layers * rows // 2, 2 * cols), F32),
        ],
        compiler_params=pltpu.CompilerParams(vmem_limit_bytes=40 << 20),
        cost_estimate=pl.CostEstimate(
            flops=16 * fields * layers * rows * cols * particles, bytes_accessed=2 << 20, transcendentals=0
        ),
        name="see_and_deposit",
    )(fluid, *halo, cells, motion, radius, temp)


def fetch_kernel(
    owner_ref, back_ref, box_ref, rank_ref, cell_ref, radius_ref, base_ref,
    next_ref, dep_ref, dy0_ref, dy1_ref, dx0_ref, dx1_ref,
    box_of, table, acc, rows_scratch, *, chunk, rows
):
    devices, tall, _ = back_ref.shape
    layers = tall // 8
    slots = layers * BLOCK
    particles = box_ref.shape[1]
    half, wide = acc.shape

    def invert(b, _):
        box_of[owner_ref[b]] = b
        return 0

    lax.fori_loop(0, devices, invert, 0)
    for o in range(0, devices, 2):
        for q in range(layers):
            pair = jnp.concatenate(
                [back_ref[o, 8 * q : 8 * q + 8, :], back_ref[o + 1, 8 * q : 8 * q + 8, :]], axis=0
            )
            high, low = split(pair)
            table[0, 8 * o : 8 * o + 16, q * BLOCK : (q + 1) * BLOCK] = high
            table[1, 8 * o : 8 * o + 16, q * BLOCK : (q + 1) * BLOCK] = low
    acc[...] = jnp.zeros_like(acc)

    def step(i, _):
        here = pl.ds(pl.multiple_of(i * chunk, chunk), chunk)
        hot_rank = rank_hot(rank_ref[:, here], slots)
        found = lax.dot_general(table[0], hot_rank, NN, preferred_element_type=F32)
        found = found + lax.dot_general(table[1], hot_rank, NN, preferred_element_type=F32)
        boxes = jnp.broadcast_to(box_ref[:, here], (8, chunk))
        gained = jnp.zeros((8, chunk), F32)
        for o in range(devices):
            gained = jnp.where(boxes == box_of[o], found[8 * o : 8 * o + 8], gained)
        base = base_ref[:, here]
        total = base[0:7] + gained[0:7]
        next_ref[:, here] = total
        radius = radius_ref[:, here]
        term = radius * radius * radius * (total[6:7] - base[7:8])
        high, low = split(term)
        cells = cell_ref[:, here]
        hot_low = hot(wide, cells % wide)
        hot_high = hot(half, cells // wide)
        added = lax.dot_general(hot_high * high, hot_low, NT, preferred_element_type=F32)
        acc[...] += added + lax.dot_general(hot_high * low, hot_low, NT, preferred_element_type=F32)
        return 0

    lax.fori_loop(0, particles // chunk, step, 0)
    field = paired_rows(acc[...], 2 * half // rows, rows, rows_scratch)
    dep_ref[0] = field
    write_edges(field, 0, dy0_ref, dy1_ref, dx0_ref, dx1_ref)


def fetch(box_owner, back, boxes, ranks, cells, radius, base, grid):
    devices, tall, _ = back.shape
    layers, rows, cols = grid
    particles = boxes.shape[1]
    slots = tall // 8 * BLOCK
    half = layers * rows // 2
    vmem = pl.BlockSpec(memory_space=VMEM)
    return pl.pallas_call(
        functools.partial(fetch_kernel, chunk=1024, rows=rows),
        out_shape=(
            jax.ShapeDtypeStruct((7, particles), F32),
            jax.ShapeDtypeStruct((1,) + grid, F32),
        ) + edge_shapes(1, layers, rows, cols),
        in_specs=[pl.BlockSpec(memory_space=pltpu.SMEM)] + [vmem] * 6,
        out_specs=(vmem,) * 6,
        scratch_shapes=[
            pltpu.SMEM((devices,), jnp.int32),
            VMEM((2, 8 * devices, slots), BF16),
            VMEM((half, 2 * cols), F32),
            VMEM((layers * rows, cols), F32),
        ],
        compiler_params=pltpu.CompilerParams(vmem_limit_bytes=40 << 20),
        cost_estimate=pl.CostEstimate(
            flops=32 * devices * slots * particles, bytes_accessed=2 << 20, transcendentals=0
        ),
        name="fetch_and_deposit",
    )(box_owner, back, boxes, ranks, cells, radius, base)


def spread_kernel(
    dep_ref, y0_ref, y1_ref, x0_ref, x1_ref, fluid_ref, next_ref, void_ref, crowd_ref
):
    crowding = 1.0 + COUPLING * smooth_field(dep_ref, y0_ref, y1_ref, x0_ref, x1_ref, 0)
    crowd_ref[...] = crowding
    void_ref[...] = 1.0 / crowding
    for k in range(3):
        spread = smooth_field(dep_ref, y0_ref, y1_ref, x0_ref, x1_ref, k + 1)
        next_ref[k] = fluid_ref[k] + TIME_STEP * COUPLING * spread * crowding


def spread_velocity(dep, halo, fluid):
    vmem = pl.BlockSpec(memory_space=VMEM)
    grid = jax.ShapeDtypeStruct(fluid.shape[1:], F32)
    return pl.pallas_call(
        spread_kernel,
        out_shape=(jax.ShapeDtypeStruct(fluid.shape, F32), grid, grid),
        in_specs=[vmem] * 6,
        out_specs=(vmem,) * 3,
        compiler_params=pltpu.CompilerParams(vmem_limit_bytes=40 << 20),
        cost_estimate=pl.CostEstimate(flops=16 * fluid.size, bytes_accessed=2 << 20, transcendentals=0),
        name="spread_velocity",
    )(dep, *halo, fluid)


def heat_kernel(next_in, dep_ref, y0_ref, y1_ref, x0_ref, x1_ref, fluid_ref, crowd_ref, next_ref):
    spread = smooth_field(dep_ref, y0_ref, y1_ref, x0_ref, x1_ref, 0)
    next_ref[0] = fluid_ref[0] + TIME_STEP * COUPLING * spread * crowd_ref[...]


def spread_heat(fluid_next, dep, halo, fluid, crowding):
    layers, rows, cols = crowding.shape
    whole = [pl.BlockSpec(a.shape, functools.partial(lambda n, i: (0,) * n, a.ndim)) for a in (dep,) + tuple(halo)]
    last = pl.BlockSpec((1, layers, rows, cols), lambda i: (3, 0, 0, 0))
    return pl.pallas_call(
        heat_kernel,
        grid=(1,),
        out_shape=jax.ShapeDtypeStruct(fluid_next.shape, F32),
        in_specs=[pl.BlockSpec(memory_space=pl.ANY)] + whole + [last, pl.BlockSpec((layers, rows, cols), lambda i: (0, 0, 0))],
        out_specs=last,
        input_output_aliases={0: 0},
        compiler_params=pltpu.CompilerParams(vmem_limit_bytes=40 << 20),
        cost_estimate=pl.CostEstimate(flops=16 * crowding.size, bytes_accessed=1 << 20, transcendentals=0),
        name="spread_heat",
    )(fluid_next, dep, *halo, fluid, crowding)


def halo_of(y_first, y_last, x_first, x_last):
    def moved(value, axis, step):
        size = lax.axis_size(axis)
        pairs = [(i, i + step) for i in range(size) if 0 <= i + step < size]
        return lax.ppermute(value, axis, pairs)

    return (
        moved(y_last, "gy", 1),
        moved(y_first, "gy", -1),
        moved(x_last, "gx", 1),
        moved(x_first, "gx", -1),
    )


def shards(
    fluid_state, particle_pos, particle_motion, particle_radius, particle_temp,
    particle_cell, particle_box, box_owner, contact_mask,
):
    devices = lax.axis_size(("gx", "gy"))
    particles = particle_pos.shape[1]
    slots = 2 * particles // devices
    fields, layers, rows, cols = fluid_state.shape
    boxes = particle_box.reshape(1, particles)
    radius = particle_radius.reshape(1, particles)
    temp = particle_temp.reshape(1, particles)
    cells = particle_cell.reshape(1, particles)

    outgoing, ranks = place(box_owner, boxes, particle_pos, particle_motion, radius, temp, slots)
    arrived = lax.all_to_all(outgoing, ("gx", "gy"), split_axis=0, concat_axis=0, tiled=True)
    result = contact(arrived, contact_mask)
    back = lax.all_to_all(result, ("gx", "gy"), split_axis=0, concat_axis=0, tiled=True)

    fluid_halo = halo_of(
        fluid_state[:, :, 0, :],
        fluid_state[:, :, rows - 1, :],
        fluid_state[:, :, :, 0].reshape(-1, BLOCK),
        fluid_state[:, :, :, cols - 1].reshape(-1, BLOCK),
    )
    seen = see_and_deposit(fluid_state, fluid_halo, cells, particle_motion, radius, temp)
    base, deposits = seen[0:2]
    fluid_next, void_fraction, crowding = spread_velocity(deposits, halo_of(*seen[2:6]), fluid_state)

    fetched = fetch(box_owner, back, boxes, ranks, cells, radius, base, (layers, rows, cols))
    particle_next, heat = fetched[0:2]
    fluid_next = spread_heat(fluid_next, heat, halo_of(*fetched[2:6]), fluid_state, crowding)
    return (fluid_next, void_fraction, particle_next)


def solution(mesh):
    in_specs = (
        P(None, None, "gy", "gx"),
        P(None, ("gx", "gy")),
        P(None, ("gx", "gy")),
        P(("gx", "gy")),
        P(("gx", "gy")),
        P(("gx", "gy")),
        P(("gx", "gy"), None),
        P(),
        P(("gx", "gy"), None, None),
    )
    out_specs = (P(None, None, "gy", "gx"), P(None, "gy", "gx"), P(None, ("gx", "gy")))
    return jax.shard_map(shards, mesh=mesh, in_specs=in_specs, out_specs=out_specs, check_vma=False)
```

time: 238 us -> 138 us (0.58)
  matrix products: 85.2 us -> 0 us
  Pallas kernels: 0 us -> 66.2 us
  waiting for transfers between devices: 55.1 us -> 15.8 us
  other arithmetic: 30.6 us -> 0 us
  blocking collectives: 29.6 us -> 0 us
  starting transfers between devices: 26.1 us -> 44.9 us
    dot_general x34 -> x0, matrix products: 85.2 us -> none  [the longest x8 24.6 us: deposit(): jnp.einsum('kph,pl->khl', weighted, one_hot(low_ids, grid_cols, jnp.float...]
    pallas_call x0 -> x6, Pallas kernels: none -> 66.2 us  [the longest x1 19.1 us: see_and_deposit(): pl.pallas_call(functools.partial(fluid_kernel, chunk=512), out_shape=(jax...]
    all_to_all x1 -> x0, blocking collectives: 29.6 us -> none  [shards(): lax.all_to_all(outgoing, ('gx', 'gy'), split_axis=1, concat_axis=1, tiled...]
    ppermute x8 -> x12, waiting for transfers between devices: 30.3 us -> 8.67 us  [moved(): return lax.ppermute(value, axis, pairs)]
    all_to_all x1 -> x2, waiting for transfers between devices: 24.8 us -> 7.1 us  [the longest x1 7.1 us: shards(): lax.all_to_all(outgoing, ('gx', 'gy'), split_axis=0, concat_axis=0, tiled...]
    reduce_sum x3 -> x0, other arithmetic: 17.3 us -> none  [the longest x1 16.1 us: contact(): weight_sum = jnp.sum(weight, axis=2)]
    ppermute x8 -> x12, starting transfers between devices: 20.5 us -> 33.6 us  [moved(): return lax.ppermute(value, axis, pairs)]
    unnamed x15 -> x28, local copies, waits for them, and re-layouts: 0.05 us -> 8.19 us
  transfers between devices with their start and end apart: 9 -> 14, of which waited for: 7 -> 4; matrix products, arithmetic and copies ran while one was open for 2% -> 1% of each run, Pallas kernels for 0% -> 39%
where the time goes in v1:
time: 138 us; the launch traced here: 137 us
  Pallas kernels  66.2 us (48%)
  starting transfers between devices  44.9 us (33%)
  waiting for transfers between devices  15.8 us (11%)
  local copies, waits for them, and re-layouts  8.95 us (6%)
    ppermute x12, starting transfers between devices, moved(): return lax.ppermute(value, axis, pairs)  33.6 us
    pallas_call x1, Pallas kernels, see_and_deposit(): pl.pallas_call(functools.partial(fluid_kernel, chunk=512), out_shape=(jax...  19.1 us
    pallas_call x1, Pallas kernels, contact(): pl.pallas_call(contact_kernel, grid=(devices // step,), out_shape=jax.Sha...  17.6 us
    pallas_call x1, Pallas kernels, fetch(): pl.pallas_call(functools.partial(fetch_kernel, chunk=1024, rows=rows), ou...  14.7 us
    pallas_call x1, Pallas kernels, place(): pl.pallas_call(functools.partial(place_kernel, chunk=1024), out_shape=(ja...  12 us
    ppermute x12, waiting for transfers between devices, moved(): return lax.ppermute(value, axis, pairs)  8.67 us
    unnamed x28, local copies, waits for them, and re-layouts  8.19 us
    all_to_all x1, waiting for transfers between devices, shards(): lax.all_to_all(outgoing, ('gx', 'gy'), split_axis=0, concat_axis=0, tiled...  7.1 us
  transfers between devices with their start and end apart: 14, of which 4 were waited for; matrix products, arithmetic and copies ran while one was open for 1% of the time, Pallas kernels for 39%

profile of v1, /device:TPU:10, one launch (start us, length us, event | category | flops | bytes accessed | tf_op | source)
XLA Modules:
  0.0 136.7 jit_solution(8172014173222048259)
XLA Ops:
  0.6 0.9 copy-done.2
  1.6 0.9 copy-done.4
  2.5 0.8 copy-done.5
  3.2 0.8 copy-done.8
  4.0 0.8 copy-done.10
  4.8 0.7 copy-done.12
  5.4 12.0 %place_slots.1 = (f32[32,48,128]{2,1,0:T(8,128)}, s32[1,8192]{1,0:T(1,128)S(1)}) custom-call(s32[32]{0:T(128)S(1)} %copy-done.12, s32[1,8192]{1,0:T(1,128)S(1)} %bitcast.17, f32[3,8192]{1,0:T(4,128)S(1)} %copy-done.4, f32[6,8192]{1,0:T(8,128)S(1)} %copy-done.2, f32[1,8192]{1,0:T(1,128)S(1)} %bitcast.14, f32[1,8192]{1,0:T(1,128)S(1)} %bitcast.10), custom_call_target="tpu_custom_call" | custom-call | flops 6442450944 | bytes 1048576 | tf_op jit(solution)/shard_map/place_slots/pallas_call | solution.py:126
  17.5 6.0 %all-to-all-start = ((f32[32,48,128]{2,1,0:T(8,128)}), f32[32,48,128]{2,1,0:T(8,128)S(1)}, u32[]{:S(2)}, u32[]{:S(2)}) async-start(f32[32,48,128]{2,1,0:T(8,128)} %get-tuple-element.26), calls=%async_computation | async-start | bytes 1572864 | tf_op jit(solution)/shard_map/all_to_all | solution.py:497
  23.6 2.1 %collective-permute-start = (f32[4,32,128]{2,1,0:T(8,128)S(1)}, f32[4,32,128]{2,1,0:T(8,128)S(1)}, u32[]{:S(2)}, u32[]{:S(2)}) collective-permute-start(f32[4,32,128]{2,1,0:T(8,128)S(1)} %bitcast.20), channel_id=1, source_target_pairs={{0,1},{1,2},{2,3},{3,4},{4,5},{5,6},{6,7},{8,9},{9,10},{10,11},{11... | collective-permute-start | bytes 196616 | tf_op jit(solution)/shard_map/ppermute | solution.py:473
  25.6 3.5 %collective-permute-start.1 = (f32[4,32,128]{2,1,0:T(8,128)S(1)}, f32[4,32,128]{2,1,0:T(8,128)S(1)}, u32[]{:S(2)}, u32[]{:S(2)}) collective-permute-start(f32[4,32,128]{2,1,0:T(8,128)S(1)} %bitcast.19), channel_id=1, source_target_pairs={{1,0},{2,1},{3,2},{4,3},{5,4},{6,5},{7,6},{9,8},{10,9},{11,10},{12... | collective-permute-start | bytes 196616 | tf_op jit(solution)/shard_map/ppermute | solution.py:473
  29.2 0.5 slice_reduce_fusion
  29.8 3.4 %collective-permute-start.2 = (f32[8,128]{1,0:T(8,128)S(1)}, f32[8,128]{1,0:T(8,128)S(1)}, u32[]{:S(2)}, u32[]{:S(2)}) collective-permute-start(f32[8,128]{1,0:T(8,128)S(1)} %reshape_squeeze.6), channel_id=1, source_target_pairs={{0,8},{8,16},{16,24},{1,9},{9,17},{17,25},{2,10},{10,18},{18,26},{... | collective-permute-start | bytes 12296 | tf_op jit(solution)/shard_map/ppermute | solution.py:473
  33.2 2.5 %collective-permute-start.3 = (f32[8,128]{1,0:T(8,128)S(1)}, f32[8,128]{1,0:T(8,128)S(1)}, u32[]{:S(2)}, u32[]{:S(2)}) collective-permute-start(f32[8,128]{1,0:T(8,128)S(1)} %reshape_squeeze.7), channel_id=1, source_target_pairs={{8,0},{16,8},{24,16},{9,1},{17,9},{25,17},{10,2},{18,10},{26,18},{... | collective-permute-start | bytes 12296 | tf_op jit(solution)/shard_map/ppermute | solution.py:473
  35.7 7.1 %all-to-all-done.slot_ref = f32[32,48,128]{2,1,0:T(8,128)S(1)} async-done(((f32[32,48,128]{2,1,0:T(8,128)}), f32[32,48,128]{2,1,0:T(8,128)S(1)}, u32[]{:S(2)}, u32[]{:S(2)}) %all-to-all-start) | async-done | bytes 786464 | tf_op jit(solution)/shard_map/all_to_all | solution.py:497
  42.8 3.4 %copy-done.1 = s32[128,128,128]{2,1,0:T(8,128)S(1)} copy-done((s32[128,128,128]{2,1,0:T(8,128)S(1)}, s32[128,128,128]{2,1,0:T(8,128)}, u32[]{:S(2)}) %copy-start.1) | copy-done | bytes 8388632
  46.2 17.6 %contact_blocks.1 = f32[32,32,128]{2,1,0:T(8,128)} custom-call(f32[32,48,128]{2,1,0:T(8,128)S(1)} %all-to-all-done.slot_ref, s32[128,128,128]{2,1,0:T(8,128)S(1)} %copy-done.1), custom_call_target="tpu_custom_call" | custom-call | flops 134217728 | bytes 8388608 | tf_op jit(solution)/shard_map/contact_blocks/pallas_call | solution.py:181
  63.8 5.2 %all-to-all-start.1 = ((f32[32,32,128]{2,1,0:T(8,128)}), f32[32,32,128]{2,1,0:T(8,128)S(1)}, u32[]{:S(2)}, u32[]{:S(2)}) async-start(f32[32,32,128]{2,1,0:T(8,128)} %contact_blocks.1), calls=%async_computation.1 | async-start | bytes 1048576 | tf_op jit(solution)/shard_map/all_to_all | solution.py:499
  69.1 19.1 %see_and_deposit.1 = (f32[8,8192]{1,0:T(8,128)S(1)}, f32[4,32,8,128]{3,2,1,0:T(8,128)S(1)}, f32[4,32,128]{2,1,0:T(8,128)S(1)}, f32[4,32,128]{2,1,0:T(8,128)S(1)}...) custom-call(f32[4,32,8,128]{3,2,1,0:T(8,128)S(1)} %copy-done, f32[4,32,128]{2,1,0:T(8,128)S(1)} %collective-permute-done.y0_ref, ...), custom_call_target="tpu_custom_call" | custom-call | flops 17179869184 | bytes 2097152 | tf_op jit(solution)/shard_map/see_and_deposit/pallas_call | solution.py:318
  88.2 2.1 %collective-permute-start.4 = (f32[4,32,128]{2,1,0:T(8,128)S(1)}, f32[4,32,128]{2,1,0:T(8,128)S(1)}, u32[]{:S(2)}, u32[]{:S(2)}) collective-permute-start(f32[4,32,128]{2,1,0:T(8,128)S(1)} %get-tuple-element.21), channel_id=1, source_target_pairs={{0,1},{1,2},{2,3},{3,4},{4,5},{5,6},{6,7},{8,9},{9,10},{10,11},{11... | collective-permute-start | bytes 196616 | tf_op jit(solution)/shard_map/ppermute | solution.py:473
  90.3 3.5 %collective-permute-start.5 = (f32[4,32,128]{2,1,0:T(8,128)S(1)}, f32[4,32,128]{2,1,0:T(8,128)S(1)}, u32[]{:S(2)}, u32[]{:S(2)}) collective-permute-start(f32[4,32,128]{2,1,0:T(8,128)S(1)} %get-tuple-element.22), channel_id=1, source_target_pairs={{1,0},{2,1},{3,2},{4,3},{5,4},{6,5},{7,6},{9,8},{10,9},{11,10},{12... | collective-permute-start | bytes 196616 | tf_op jit(solution)/shard_map/ppermute | solution.py:473
  93.8 14.7 %fetch_and_deposit.1 = (f32[7,8192]{1,0:T(8,128)}, f32[1,32,8,128]{3,2,1,0:T(8,128)S(1)}, f32[1,32,128]{2,1,0:T(8,128)S(1)}, f32[1,32,128]{2,1,0:T(8,128)S(1)}, ...) custom-call(s32[32]{0:T(128)S(1)} %copy-done.13, f32[32,32,128]{2,1,0:T(8,128)S(1)} %all-to-all-done.1.back_ref, ...), custom_call_target="tpu_custom_call" | custom-call | flops 4294967296 | bytes 2097152 | tf_op jit(solution)/shard_map/fetch_and_deposit/pallas_call | solution.py:400
  108.5 1.9 %collective-permute-start.8 = (f32[1,32,128]{2,1,0:T(8,128)S(1)}, f32[1,32,128]{2,1,0:T(8,128)S(1)}, u32[]{:S(2)}, u32[]{:S(2)}) collective-permute-start(f32[1,32,128]{2,1,0:T(8,128)S(1)} %get-tuple-element.30), channel_id=1, source_target_pairs={{0,1},{1,2},{2,3},{3,4},{4,5},{5,6},{6,7},{8,9},{9,10},{10,11},{11... | collective-permute-start | bytes 49160 | tf_op jit(solution)/shard_map/ppermute | solution.py:473
  110.4 3.6 %collective-permute-start.9 = (f32[1,32,128]{2,1,0:T(8,128)S(1)}, f32[1,32,128]{2,1,0:T(8,128)S(1)}, u32[]{:S(2)}, u32[]{:S(2)}) collective-permute-start(f32[1,32,128]{2,1,0:T(8,128)S(1)} %get-tuple-element.31), channel_id=1, source_target_pairs={{1,0},{2,1},{3,2},{4,3},{5,4},{6,5},{7,6},{9,8},{10,9},{11,10},{12... | collective-permute-start | bytes 49160 | tf_op jit(solution)/shard_map/ppermute | solution.py:473
  114.0 3.4 %collective-permute-start.6 = (f32[8,128]{1,0:T(8,128)S(1)}, f32[8,128]{1,0:T(8,128)S(1)}, u32[]{:S(2)}, u32[]{:S(2)}) collective-permute-start(f32[8,128]{1,0:T(8,128)S(1)} %get-tuple-element.23), channel_id=1, source_target_pairs={{0,8},{8,16},{16,24},{1,9},{9,17},{17,25},{2,10},{10,18},{18,26},{... | collective-permute-start | bytes 12296 | tf_op jit(solution)/shard_map/ppermute | solution.py:473
  117.4 2.1 %collective-permute-done.6.x0_ref = f32[8,128]{1,0:T(8,128)S(1)} collective-permute-done((f32[8,128]{1,0:T(8,128)S(1)}, f32[8,128]{1,0:T(8,128)S(1)}, u32[]{:S(2)}, u32[]{:S(2)}) %collective-permute-start.6) | collective-permute-done | bytes 4128 | tf_op jit(solution)/shard_map/ppermute | solution.py:473
  119.5 1.9 %collective-permute-start.7 = (f32[8,128]{1,0:T(8,128)S(1)}, f32[8,128]{1,0:T(8,128)S(1)}, u32[]{:S(2)}, u32[]{:S(2)}) collective-permute-start(f32[8,128]{1,0:T(8,128)S(1)} %get-tuple-element.24), channel_id=1, source_target_pairs={{8,0},{16,8},{24,16},{9,1},{17,9},{25,17},{10,2},{18,10},{26,18},{... | collective-permute-start | bytes 12296 | tf_op jit(solution)/shard_map/ppermute | solution.py:473
  121.5 4.5 %collective-permute-done.7.x1_ref = f32[8,128]{1,0:T(8,128)S(1)} collective-permute-done((f32[8,128]{1,0:T(8,128)S(1)}, f32[8,128]{1,0:T(8,128)S(1)}, u32[]{:S(2)}, u32[]{:S(2)}) %collective-permute-start.7) | collective-permute-done | bytes 4128 | tf_op jit(solution)/shard_map/ppermute | solution.py:473
  125.9 3.4 %collective-permute-start.10 = (f32[2,128]{1,0:T(2,128)S(1)}, f32[2,128]{1,0:T(2,128)S(1)}, u32[]{:S(2)}, u32[]{:S(2)}) collective-permute-start(f32[2,128]{1,0:T(2,128)S(1)} %get-tuple-element.32), channel_id=1, source_target_pairs={{0,8},{8,16},{16,24},{1,9},{9,17},{17,25},{2,10},{10,18},{18,26},{... | collective-permute-start | bytes 3080 | tf_op jit(solution)/shard_map/ppermute | solution.py:473
  129.3 2.4 %collective-permute-start.11 = (f32[2,128]{1,0:T(2,128)S(1)}, f32[2,128]{1,0:T(2,128)S(1)}, u32[]{:S(2)}, u32[]{:S(2)}) collective-permute-start(f32[2,128]{1,0:T(2,128)S(1)} %get-tuple-element.33), channel_id=1, source_target_pairs={{8,0},{16,8},{24,16},{9,1},{17,9},{25,17},{10,2},{18,10},{26,18},{... | collective-permute-start | bytes 3080 | tf_op jit(solution)/shard_map/ppermute | solution.py:473
  131.8 1.8 %spread_velocity.1 = (f32[4,32,8,128]{3,2,1,0:T(8,128)}, f32[32,8,128]{2,1,0:T(8,128)}, f32[32,8,128]{2,1,0:T(8,128)S(1)}) custom-call(f32[4,32,8,128]{3,2,1,0:T(8,128)S(1)} %get-tuple-element.20.dep_ref, f32[4,32,128]{2,1,0:T(8,128)S(1)} %collective-permute-done.4.y0_ref, f32[4,32,128]{2,1,0:T(8,128)S(1)} %collective-permute-done.5.y1_ref, ...), custom_call_target="tpu_custom_call" | custom-call | flops 2097152 | bytes 2097152 | tf_op jit(solution)/shard_map/spread_velocity/pallas_call | solution.py:436
  133.6 2.1 %collective-permute-done.11.x1_ref = f32[2,128]{1,0:T(2,128)S(1)} collective-permute-done((f32[2,128]{1,0:T(2,128)S(1)}, f32[2,128]{1,0:T(2,128)S(1)}, u32[]{:S(2)}, u32[]{:S(2)}) %collective-permute-start.11) | collective-permute-done | bytes 1056 | tf_op jit(solution)/shard_map/ppermute | solution.py:473
  135.7 1.0 spread_heat.1
  (34 shorter events, 0.3 us)
Async XLA Ops:
  0.6 1.0 copy-start.2
  1.6 0.9 copy-start.4
  2.5 0.8 copy-start.5
  3.2 0.8 copy-start.8
  4.0 0.8 copy-start.10
  4.8 0.7 copy-start.12
  5.4 18.1 %copy-start = (f32[4,32,8,128]{3,2,1,0:T(8,128)S(1)}, f32[4,32,8,128]{3,2,1,0:T(8,128)}, u32[]{:S(2)}) copy-start(f32[4,32,8,128]{3,2,1,0:T(8,128)} %fluid_ref.5) | copy-start | bytes 1572868
  17.4 51.6 %copy-start.3 = (f32[6,8192]{1,0:T(8,128)S(1)}, f32[6,8192]{1,0:T(8,128)}, u32[]{:S(2)}) copy-start(f32[6,8192]{1,0:T(8,128)} %motion_ref.3) | copy-start | bytes 589828
  17.4 51.6 %copy-start.6 = (f32[8192]{0:T(1024)S(1)}, f32[8192]{0:T(1024)}, u32[]{:S(2)}) copy-start(f32[8192]{0:T(1024)} %param.13) | copy-start | bytes 98308
  17.4 51.6 %copy-start.7 = (s32[8192]{0:T(1024)S(1)}, s32[8192]{0:T(1024)}, u32[]{:S(2)}) copy-start(s32[8192]{0:T(1024)} %param.14) | copy-start | bytes 98308
  17.4 51.7 %copy-start.9 = (f32[8192]{0:T(1024)S(1)}, f32[8192]{0:T(1024)}, u32[]{:S(2)}) copy-start(f32[8192]{0:T(1024)} %param.12) | copy-start | bytes 98308
  17.5 25.3 %all-to-all-start = ((f32[32,48,128]{2,1,0:T(8,128)}), f32[32,48,128]{2,1,0:T(8,128)S(1)}, u32[]{:S(2)}, u32[]{:S(2)}) async-start(f32[32,48,128]{2,1,0:T(8,128)} %get-tuple-element.26), calls=%async_computation | async-start | bytes 1572864 | tf_op jit(solution)/shard_map/all_to_all | solution.py:497
  23.6 45.5 %collective-permute-start = (f32[4,32,128]{2,1,0:T(8,128)S(1)}, f32[4,32,128]{2,1,0:T(8,128)S(1)}, u32[]{:S(2)}, u32[]{:S(2)}) collective-permute-start(f32[4,32,128]{2,1,0:T(8,128)S(1)} %bitcast.20), channel_id=1, source_target_pairs={{0,1},{1,2},{2,3},{3,4},{4,5},{5,6},{6,7},{8,9},{9,10},{10,11},{11... | collective-permute-start | bytes 196616 | tf_op jit(solution)/shard_map/ppermute | solution.py:473
  25.6 43.4 %collective-permute-start.1 = (f32[4,32,128]{2,1,0:T(8,128)S(1)}, f32[4,32,128]{2,1,0:T(8,128)S(1)}, u32[]{:S(2)}, u32[]{:S(2)}) collective-permute-start(f32[4,32,128]{2,1,0:T(8,128)S(1)} %bitcast.19), channel_id=1, source_target_pairs={{1,0},{2,1},{3,2},{4,3},{5,4},{6,5},{7,6},{9,8},{10,9},{11,10},{12... | collective-permute-start | bytes 196616 | tf_op jit(solution)/shard_map/ppermute | solution.py:473
  29.8 39.3 %collective-permute-start.2 = (f32[8,128]{1,0:T(8,128)S(1)}, f32[8,128]{1,0:T(8,128)S(1)}, u32[]{:S(2)}, u32[]{:S(2)}) collective-permute-start(f32[8,128]{1,0:T(8,128)S(1)} %reshape_squeeze.6), channel_id=1, source_target_pairs={{0,8},{8,16},{16,24},{1,9},{9,17},{17,25},{2,10},{10,18},{18,26},{... | collective-permute-start | bytes 12296 | tf_op jit(solution)/shard_map/ppermute | solution.py:473
  33.2 35.8 %collective-permute-start.3 = (f32[8,128]{1,0:T(8,128)S(1)}, f32[8,128]{1,0:T(8,128)S(1)}, u32[]{:S(2)}, u32[]{:S(2)}) collective-permute-start(f32[8,128]{1,0:T(8,128)S(1)} %reshape_squeeze.7), channel_id=1, source_target_pairs={{8,0},{16,8},{24,16},{9,1},{17,9},{25,17},{10,2},{18,10},{26,18},{... | collective-permute-start | bytes 12296 | tf_op jit(solution)/shard_map/ppermute | solution.py:473
  42.8 3.4 %copy-start.1 = (s32[128,128,128]{2,1,0:T(8,128)S(1)}, s32[128,128,128]{2,1,0:T(8,128)}, u32[]{:S(2)}) copy-start(s32[128,128,128]{2,1,0:T(8,128)} %mask_ref.1) | copy-start | bytes 25165828
  63.8 29.9 %all-to-all-start.1 = ((f32[32,32,128]{2,1,0:T(8,128)}), f32[32,32,128]{2,1,0:T(8,128)S(1)}, u32[]{:S(2)}, u32[]{:S(2)}) async-start(f32[32,32,128]{2,1,0:T(8,128)} %contact_blocks.1), calls=%async_computation.1 | async-start | bytes 1048576 | tf_op jit(solution)/shard_map/all_to_all | solution.py:499
  69.1 24.7 %copy-start.11 = (s32[8192,1]{0,1:T(1,128)S(1)}, s32[8192,1]{0,1:T(1,128)}, u32[]{:S(2)}) copy-start(s32[8192,1]{0,1:T(1,128)} %param.15) | copy-start | bytes 98308
  69.1 24.7 %copy-start.13 = (s32[32]{0:T(128)S(1)}, s32[32]{0:T(128)}, u32[]{:S(2)}) copy-start(s32[32]{0:T(128)} %owner_ref.3) | copy-start | bytes 388
  88.2 41.1 %collective-permute-start.4 = (f32[4,32,128]{2,1,0:T(8,128)S(1)}, f32[4,32,128]{2,1,0:T(8,128)S(1)}, u32[]{:S(2)}, u32[]{:S(2)}) collective-permute-start(f32[4,32,128]{2,1,0:T(8,128)S(1)} %get-tuple-element.21), channel_id=1, source_target_pairs={{0,1},{1,2},{2,3},{3,4},{4,5},{5,6},{6,7},{8,9},{9,10},{10,11},{11... | collective-permute-start | bytes 196616 | tf_op jit(solution)/shard_map/ppermute | solution.py:473
  90.3 41.5 %collective-permute-start.5 = (f32[4,32,128]{2,1,0:T(8,128)S(1)}, f32[4,32,128]{2,1,0:T(8,128)S(1)}, u32[]{:S(2)}, u32[]{:S(2)}) collective-permute-start(f32[4,32,128]{2,1,0:T(8,128)S(1)} %get-tuple-element.22), channel_id=1, source_target_pairs={{1,0},{2,1},{3,2},{4,3},{5,4},{6,5},{7,6},{9,8},{10,9},{11,10},{12... | collective-permute-start | bytes 196616 | tf_op jit(solution)/shard_map/ppermute | solution.py:473
  108.5 27.2 %collective-permute-start.8 = (f32[1,32,128]{2,1,0:T(8,128)S(1)}, f32[1,32,128]{2,1,0:T(8,128)S(1)}, u32[]{:S(2)}, u32[]{:S(2)}) collective-permute-start(f32[1,32,128]{2,1,0:T(8,128)S(1)} %get-tuple-element.30), channel_id=1, source_target_pairs={{0,1},{1,2},{2,3},{3,4},{4,5},{5,6},{6,7},{8,9},{9,10},{10,11},{11... | collective-permute-start | bytes 49160 | tf_op jit(solution)/shard_map/ppermute | solution.py:473
  110.4 25.3 %collective-permute-start.9 = (f32[1,32,128]{2,1,0:T(8,128)S(1)}, f32[1,32,128]{2,1,0:T(8,128)S(1)}, u32[]{:S(2)}, u32[]{:S(2)}) collective-permute-start(f32[1,32,128]{2,1,0:T(8,128)S(1)} %get-tuple-element.31), channel_id=1, source_target_pairs={{1,0},{2,1},{3,2},{4,3},{5,4},{6,5},{7,6},{9,8},{10,9},{11,10},{12... | collective-permute-start | bytes 49160 | tf_op jit(solution)/shard_map/ppermute | solution.py:473
  114.0 5.5 %collective-permute-start.6 = (f32[8,128]{1,0:T(8,128)S(1)}, f32[8,128]{1,0:T(8,128)S(1)}, u32[]{:S(2)}, u32[]{:S(2)}) collective-permute-start(f32[8,128]{1,0:T(8,128)S(1)} %get-tuple-element.23), channel_id=1, source_target_pairs={{0,8},{8,16},{16,24},{1,9},{9,17},{17,25},{2,10},{10,18},{18,26},{... | collective-permute-start | bytes 12296 | tf_op jit(solution)/shard_map/ppermute | solution.py:473
  119.5 6.4 %collective-permute-start.7 = (f32[8,128]{1,0:T(8,128)S(1)}, f32[8,128]{1,0:T(8,128)S(1)}, u32[]{:S(2)}, u32[]{:S(2)}) collective-permute-start(f32[8,128]{1,0:T(8,128)S(1)} %get-tuple-element.24), channel_id=1, source_target_pairs={{8,0},{16,8},{24,16},{9,1},{17,9},{25,17},{10,2},{18,10},{26,18},{... | collective-permute-start | bytes 12296 | tf_op jit(solution)/shard_map/ppermute | solution.py:473
  125.9 7.7 %collective-permute-start.10 = (f32[2,128]{1,0:T(2,128)S(1)}, f32[2,128]{1,0:T(2,128)S(1)}, u32[]{:S(2)}, u32[]{:S(2)}) collective-permute-start(f32[2,128]{1,0:T(2,128)S(1)} %get-tuple-element.32), channel_id=1, source_target_pairs={{0,8},{8,16},{16,24},{1,9},{9,17},{17,25},{2,10},{10,18},{18,26},{... | collective-permute-start | bytes 3080 | tf_op jit(solution)/shard_map/ppermute | solution.py:473
  129.3 6.4 %collective-permute-start.11 = (f32[2,128]{1,0:T(2,128)S(1)}, f32[2,128]{1,0:T(2,128)S(1)}, u32[]{:S(2)}, u32[]{:S(2)}) collective-permute-start(f32[2,128]{1,0:T(2,128)S(1)} %get-tuple-element.33), channel_id=1, source_target_pairs={{8,0},{16,8},{24,16},{9,1},{17,9},{25,17},{10,2},{18,10},{26,18},{... | collective-permute-start | bytes 3080 | tf_op jit(solution)/shard_map/ppermute | solution.py:473

commit v2 on v1

v2 whole, which is shorter than its diff:
```python
import functools

import jax
import jax.numpy as jnp
from jax import lax
from jax.experimental import pallas as pl
from jax.experimental.pallas import tpu as pltpu
from jax.sharding import PartitionSpec as P

BLOCK = 128
TIME_STEP = 0.1
STIFFNESS = 0.5
DAMPING_RATE = 0.2
ROTATION_DRAG = 0.1
DRAG_COEFF = 4.0
CONDUCTION = 0.3
HEAT_TRANSFER = 4.0
GRAVITY = 0.3
COUPLING = 4.0
CENTRE_WEIGHT = 0.25
SIDE_WEIGHT = 0.125

F32 = jnp.float32
BF16 = jnp.bfloat16
VMEM = pltpu.VMEM
NT = (((1,), (1,)), ((), ()))
NN = (((1,), (0,)), ((), ()))


def split(value):
    high = value.astype(BF16)
    return high, (value - high.astype(F32)).astype(BF16)


def hot(count, row):
    places = lax.broadcasted_iota(jnp.int32, (count, row.shape[1]), 0)
    return jnp.where(places == row, 1.0, 0.0).astype(BF16)


def invert(owner_ref, box_of):
    def step(b, _):
        box_of[owner_ref[b]] = b
        return 0

    lax.fori_loop(0, owner_ref.shape[0], step, 0)


WINDOW = 256
CHUNK = 1024


def place_kernel(
    owner_ref, box_ref, pos_ref, motion_ref, radius_ref, temp_ref,
    out_ref, slot_ref, spot_ref, tile_ref,
    box_of, tile_of, acc, done
):
    devices, rows, _ = out_ref.shape
    layers = rows // 12
    slots = layers * BLOCK
    particles = box_ref.shape[1]
    sub = 256
    invert(owner_ref, box_of)
    acc[...] = jnp.zeros_like(acc)

    box_row = lax.broadcasted_iota(jnp.int32, (devices, 1), 0)
    owner_column = jnp.zeros((devices, 1), F32)
    for b in range(devices):
        owner_column = jnp.where(box_row == b, owner_ref[b].astype(F32), owner_column)
    above = (
        lax.broadcasted_iota(jnp.int32, (sub, sub), 0) < lax.broadcasted_iota(jnp.int32, (sub, sub), 1)
    )
    above = jnp.where(above, 1.0, 0.0).astype(BF16)
    lane = lax.broadcasted_iota(jnp.int32, (devices, BLOCK), 1)
    tiles = jnp.zeros((devices, BLOCK), F32)
    spans = jnp.zeros((8, BLOCK), F32)
    carry = jnp.zeros((devices, 1), F32)
    per_chunk = CHUNK // sub
    for c in range(particles // CHUNK):
        chosen = []
        for s in range(per_chunk):
            at = c * CHUNK + s * sub
            chosen.append(
                lax.broadcasted_iota(jnp.int32, (devices, sub), 0) == box_ref[:, at : at + sub]
            )
        ones = [jnp.where(mine, 1.0, 0.0) for mine in chosen]
        earlier = lax.dot_general(
            jnp.concatenate(ones, axis=0).astype(BF16), above, NN, preferred_element_type=F32
        )
        tile = jnp.minimum(jnp.floor(carry * (1.0 / BLOCK)), layers - 1.0)
        tiles = jnp.where(lane == c, tile, tiles)
        highest = jnp.zeros((1, 1), F32)
        for s in range(per_chunk):
            at = c * CHUNK + s * sub
            rank = earlier[s * devices : (s + 1) * devices] + carry
            spot = jnp.where(chosen[s], rank - BLOCK * tile, 0.0)
            spot = jnp.sum(spot, axis=0, keepdims=True)
            slot = jnp.where(chosen[s], rank + slots * owner_column, 0.0)
            slot = jnp.sum(slot, axis=0, keepdims=True)
            spot_ref[:, at : at + sub] = spot.astype(jnp.int32)
            slot_ref[:, at : at + sub] = slot.astype(jnp.int32)
            highest = jnp.maximum(highest, jnp.max(spot, axis=1, keepdims=True))
            carry = carry + jnp.sum(ones[s], axis=1, keepdims=True)
        windows = jnp.floor(highest * (1.0 / WINDOW)) + 1.0
        spans = jnp.where(lane[0:8] == c, windows, spans)
    tile_ref[0:devices, :] = tiles.astype(jnp.int32)
    tile_ref[devices : devices + 8, :] = spans.astype(jnp.int32)
    copy = pltpu.make_async_copy(tile_ref, tile_of, done)
    copy.start()
    copy.wait()

    def step(c, _):
        here = pl.ds(pl.multiple_of(c * CHUNK, CHUNK), CHUNK)
        boxes = box_ref[:, here]
        pos = pos_ref[:, here]
        motion = motion_ref[:, here]
        push = TIME_STEP * STIFFNESS * pos - TIME_STEP * DAMPING_RATE * motion[0:3]
        spin = -TIME_STEP * ROTATION_DRAG * motion[3:6]
        heat = -TIME_STEP * CONDUCTION * temp_ref[:, here]
        first = jnp.concatenate([push, spin, heat, jnp.ones((1, CHUNK), F32)], axis=0)
        second = jnp.concatenate([pos, radius_ref[:, here]], axis=0)
        first = jnp.concatenate(split(first), axis=0)
        second = jnp.concatenate(split(second), axis=0)
        box16 = jnp.broadcast_to(boxes, (16, CHUNK)).astype(F32).astype(BF16)
        first_parts = []
        second_parts = []
        for o in range(devices):
            mine = box16 == box_of[o].astype(F32).astype(BF16)
            first_parts.append(jnp.where(mine, first, jnp.zeros_like(first)))
            second_parts.append(jnp.where(mine[0:8], second, jnp.zeros_like(second)))
        parts = jnp.concatenate(first_parts + second_parts, axis=0)

        def window(w, _):
            hot_spot = hot(WINDOW, spot_ref[:, here] - WINDOW * w)
            placed = lax.dot_general(parts, hot_spot, NT, preferred_element_type=F32)
            for o in range(devices):
                tile = tile_of[box_of[o], c] + 2 * w
                one = placed[16 * o : 16 * o + 8] + placed[16 * o + 8 : 16 * o + 16]
                two = placed[16 * devices + 8 * o : 16 * devices + 8 * o + 8]
                two = two + pltpu.roll(two, 4, 0)
                acc[o, tile, 0:8, :] += one[:, :BLOCK]
                acc[o, tile + 1, 0:8, :] += one[:, BLOCK:]
                acc[o, tile, 8:16, :] += two[:, :BLOCK]
                acc[o, tile + 1, 8:16, :] += two[:, BLOCK:]
            return 0

        return lax.fori_loop(0, tile_of[devices, c], window, 0)

    lax.fori_loop(0, particles // CHUNK, step, 0)

    def finish(o, _):
        for q in range(layers):
            out_ref[o, 8 * q : 8 * q + 8, :] = acc[o, q, 0:8, :]
            out_ref[o, 8 * layers + 4 * q : 8 * layers + 4 * q + 4, :] = acc[o, q, 8:12, :]
        return 0

    lax.fori_loop(0, devices, finish, 0)


def place(box_owner, boxes, pos, motion, radius, temp, slots):
    devices = box_owner.shape[0]
    particles = pos.shape[1]
    layers = slots // BLOCK
    vmem = pl.BlockSpec(memory_space=VMEM)
    row = jax.ShapeDtypeStruct((1, particles), jnp.int32)
    table = (devices + 8, BLOCK)
    return pl.pallas_call(
        place_kernel,
        out_shape=(
            jax.ShapeDtypeStruct((devices, 12 * layers, BLOCK), F32), row, row,
            jax.ShapeDtypeStruct(table, jnp.int32),
        ),
        in_specs=[pl.BlockSpec(memory_space=pltpu.SMEM)] + [vmem] * 5,
        out_specs=(vmem,) * 4,
        scratch_shapes=[
            pltpu.SMEM((devices,), jnp.int32),
            pltpu.SMEM(table, jnp.int32),
            VMEM((devices, layers + 3, 16, BLOCK), F32),
            pltpu.SemaphoreType.DMA,
        ],
        compiler_params=pltpu.CompilerParams(vmem_limit_bytes=60 << 20),
        cost_estimate=pl.CostEstimate(
            flops=2 * 24 * devices * WINDOW * particles, bytes_accessed=1 << 20, transcendentals=0
        ),
        name="place_slots",
    )(box_owner, boxes, pos, motion, radius, temp)


def pair_terms(near):
    twice = jnp.concatenate([near, near], axis=0)
    high = twice.astype(BF16).astype(F32)
    low = (twice - high).astype(BF16).astype(F32)
    row = lax.broadcasted_iota(jnp.int32, (8, 1), 0)
    kept = high + low
    squares = kept * kept
    norm = -(squares[0:1] + squares[1:2] + squares[2:3])
    total = jnp.where(row < 3, norm, squares[3:4] + 0.5)
    one = total.astype(BF16).astype(F32)
    rest = total - one
    two = rest.astype(BF16).astype(F32)
    three = (rest - two).astype(BF16).astype(F32)
    third = jnp.where((row == 0) | (row == 3), one, jnp.where((row == 1) | (row == 4), two, three))
    third = jnp.where(row < 6, third, 0.0)
    crossed = 2.0 * jnp.where(row < 4, high, low)
    is_radius = (row == 3) | (row == 7)
    cross_d = jnp.where(is_radius, 0.0, crossed)
    cross_r = jnp.where(is_radius, crossed, 0.0)
    ones = jnp.ones_like(third)
    left = jnp.concatenate([high, low, third, jnp.where(row < 6, ones, 0.0)], axis=0)
    ones_d = jnp.where(row < 3, ones, 0.0)
    ones_r = jnp.where((row >= 3) & (row < 6), ones, 0.0)
    for_d = jnp.concatenate([cross_d, cross_d, ones_d, jnp.where(row < 3, third, 0.0)], axis=0)
    for_r = jnp.concatenate([cross_r, cross_r, ones_r, jnp.where((row >= 3) & (row < 6), third, 0.0)], axis=0)
    right = jnp.concatenate([for_d, for_r], axis=1)
    return left.astype(BF16), right.astype(BF16)


def contact_kernel(slot_ref, mask_ref, out_ref, heat_ref):
    homes, rows, _ = slot_ref.shape
    layers = rows // 12
    sign = lax.broadcasted_iota(jnp.int32, (8, 1), 0)
    sign = jnp.where((sign >= 3) & (sign < 6), 1.0, -1.0)
    for s in range(homes):
        for q in range(layers):
            mixed = slot_ref[s, 8 * q : 8 * q + 8, :]
            near = slot_ref[s, 8 * layers + 4 * q : 8 * layers + 4 * q + 4, :]
            left, right = pair_terms(near)
            pair = lax.dot_general(left, right, (((0,), (0,)), ((), ())), preferred_element_type=F32)
            reach = pair[:, BLOCK:]
            inverse = pl.reciprocal(reach, approx=True)
            inverse = inverse * (2.0 - reach * inverse)
            weight = mask_ref[s * layers + q].astype(F32) * jnp.exp(pair[:, :BLOCK] * inverse)
            weight_high, weight_low = split(weight)
            mixed_high, mixed_low = split(mixed)
            both = jnp.concatenate([mixed_high, mixed_low], axis=0)
            sums = lax.dot_general(both, weight_high, NT, preferred_element_type=F32)
            sums = sums + lax.dot_general(both, weight_low, NT, preferred_element_type=F32)
            sums = sums[0:8] + sums[8:16]
            result = mixed * sums[7:8] + sign * sums
            out_ref[s, 6 * q : 6 * q + 6, :] = result[0:6]
            heat_ref[s, q : q + 1, :] = result[6:7]


def contact(arrived, mask):
    devices, rows, _ = arrived.shape
    layers = rows // 12
    blocks = mask.shape[0]
    step = 2 if layers > 1 else 8
    return pl.pallas_call(
        contact_kernel,
        grid=(devices // step,),
        out_shape=(
            jax.ShapeDtypeStruct((devices, 6 * layers, BLOCK), F32),
            jax.ShapeDtypeStruct((devices, layers, BLOCK), F32),
        ),
        in_specs=[
            pl.BlockSpec((step, rows, BLOCK), lambda h: (h, 0, 0)),
            pl.BlockSpec((step * layers, BLOCK, BLOCK), lambda h: (h, 0, 0)),
        ],
        out_specs=(
            pl.BlockSpec((step, 6 * layers, BLOCK), lambda h: (h, 0, 0)),
            pl.BlockSpec((step, layers, BLOCK), lambda h: (h, 0, 0)),
        ),
        compiler_params=pltpu.CompilerParams(vmem_limit_bytes=60 << 20),
        cost_estimate=pl.CostEstimate(
            flops=64 * blocks * BLOCK * BLOCK, bytes_accessed=blocks * BLOCK * BLOCK * 4, transcendentals=0
        ),
        name="contact_blocks",
    )(arrived, mask)


def smoothed(centre, y_first, y_last, x_first, x_last):
    layers, rows, cols = centre.shape
    zero = jnp.zeros((1, rows, cols), F32)
    up = jnp.concatenate([centre[1:], zero], axis=0)
    down = jnp.concatenate([zero, centre[:-1]], axis=0)
    row = lax.broadcasted_iota(jnp.int32, (1, rows, cols), 1)
    col = lax.broadcasted_iota(jnp.int32, (1, rows, cols), 2)
    back = jnp.where(row == 0, y_first, pltpu.roll(centre, 1, 1))
    front = jnp.where(row == rows - 1, y_last, pltpu.roll(centre, rows - 1, 1))
    left = jnp.where(col == 0, x_first, pltpu.roll(centre, 1, 2))
    right = jnp.where(col == cols - 1, x_last, pltpu.roll(centre, cols - 1, 2))
    return CENTRE_WEIGHT * centre + SIDE_WEIGHT * ((up + down) + (back + front) + (left + right))


def columns(edge, layers, rows):
    count = edge.shape[0]
    if count < 8:
        edge = jnp.concatenate([edge] * (8 // count), axis=0)
    turned = jnp.transpose(edge)
    parts = [turned[:, a : a + 1] for a in range(count)]
    return jnp.concatenate(parts, axis=0).reshape(layers, rows, 1)


def smooth_field(field_ref, y0_ref, y1_ref, x0_ref, x1_ref, k, edge=None):
    at = k if edge is None else edge
    _, layers, rows, cols = field_ref.shape
    per = layers * rows // BLOCK
    x0 = columns(x0_ref[at * per : (at + 1) * per, :], layers, rows)
    x1 = columns(x1_ref[at * per : (at + 1) * per, :], layers, rows)
    y0 = y0_ref[at].reshape(layers, 1, cols)
    y1 = y1_ref[at].reshape(layers, 1, cols)
    return smoothed(field_ref[k], y0, y1, x0, x1)


def write_edges(field, k, y0_ref, y1_ref, x0_ref, x1_ref):
    layers, rows, cols = field.shape
    y0_ref[k] = field[:, 0, :]
    y1_ref[k] = field[:, rows - 1, :]
    flat = field.reshape(layers * rows, cols)
    for a in range(layers * rows // BLOCK):
        turned = jnp.transpose(flat[a * BLOCK : (a + 1) * BLOCK, :])
        at = k * (layers * rows // BLOCK) + a
        x0_ref[at : at + 1, :] = turned[0:1, :]
        x1_ref[at : at + 1, :] = turned[cols - 1 : cols, :]


def paired_rows(pairs, layers, rows, scratch):
    half = pairs.shape[0]
    cols = pairs.shape[1] // 2
    scratch[pl.ds(0, half, stride=2), :] = pairs[:, :cols]
    scratch[pl.ds(1, half, stride=2), :] = pairs[:, cols:]
    return scratch[...].reshape(layers, rows, cols)


def gathered(tables, rows, lanes):
    group = rows // 8
    found = [None] * len(tables)
    for g in range(len(tables[0])):
        mine = group == g
        for k, table in enumerate(tables):
            value = jnp.take_along_axis(table[g], lanes, axis=1, mode="promise_in_bounds")
            found[k] = value if g == 0 else jnp.where(mine, value, found[k])
    mine = lax.broadcasted_iota(jnp.int32, (8, BLOCK), 0) == rows % 8
    return [jnp.sum(jnp.where(mine, value, 0.0), axis=0, keepdims=True) for value in found]


def fluid_kernel(
    fluid_ref, y0_ref, y1_ref, x0_ref, x1_ref, cell_ref, motion_ref, radius_ref, temp_ref,
    base_ref, dep_ref, dy0_ref, dy1_ref, dx0_ref, dx1_ref,
    table, rows_scratch, acc, *, chunk
):
    fields, layers, rows, cols = fluid_ref.shape
    half = layers * rows // 2
    wide = 2 * cols
    particles = cell_ref.shape[1]
    for k in range(fields):
        table[k] = smooth_field(fluid_ref, y0_ref, y1_ref, x0_ref, x1_ref, k)
    acc[...] = jnp.zeros_like(acc)

    def step(i, _):
        here = pl.ds(pl.multiple_of(i * chunk, chunk), chunk)
        cells = cell_ref[:, here]
        hot_low = hot(wide, cells % wide)
        hot_high = hot(half, cells // wide)
        seen = [[] for _ in range(fields)]
        for s in range(chunk // BLOCK):
            wanted = jnp.broadcast_to(cells[:, s * BLOCK : (s + 1) * BLOCK], (8, BLOCK))
            values = gathered(
                [[table[k, z] for z in range(layers)] for k in range(fields)], wanted // cols, wanted % cols
            )
            for k in range(fields):
                seen[k].append(values[k])
        seen = [jnp.concatenate(parts, axis=1) for parts in seen]
        motion = motion_ref[:, here]
        radius = radius_ref[:, here]
        temp = temp_ref[:, here]
        fluid_vel = jnp.concatenate(seen[0:3], axis=0)
        drag = DRAG_COEFF / (radius * radius + 0.25) * (fluid_vel - motion[0:3])
        upward = lax.broadcasted_iota(jnp.int32, (3, 1), 0) == 2
        moved = motion[0:3] + TIME_STEP * drag - jnp.where(upward, TIME_STEP * GRAVITY, 0.0)
        warmed = temp + TIME_STEP * HEAT_TRANSFER * (seen[3] - temp)
        base_ref[:, here] = jnp.concatenate([moved, motion[3:6], warmed, seen[3]], axis=0)
        volume = radius * radius * radius
        terms = jnp.concatenate([volume, -volume * drag], axis=0)
        high, low = split(terms)
        parts = []
        for piece in (high, low):
            parts.append(jnp.concatenate([hot_high * piece[k : k + 1] for k in range(4)], axis=0))
        total = lax.dot_general(parts[0], hot_low, NT, preferred_element_type=F32)
        acc[...] += total + lax.dot_general(parts[1], hot_low, NT, preferred_element_type=F32)
        return 0

    lax.fori_loop(0, particles // chunk, step, 0)
    for k in range(fields):
        field = paired_rows(acc[k * half : (k + 1) * half, :], layers, rows, rows_scratch)
        dep_ref[k] = field
        write_edges(field, k, dy0_ref, dy1_ref, dx0_ref, dx1_ref)


def edge_shapes(fields, layers, rows, cols):
    y_edge = jax.ShapeDtypeStruct((fields, layers, cols), F32)
    x_edge = jax.ShapeDtypeStruct((fields * layers * rows // BLOCK, BLOCK), F32)
    return (y_edge, y_edge, x_edge, x_edge)


def see_and_deposit(fluid, halo, cells, motion, radius, temp):
    fields, layers, rows, cols = fluid.shape
    particles = cells.shape[1]
    vmem = pl.BlockSpec(memory_space=VMEM)
    return pl.pallas_call(
        functools.partial(fluid_kernel, chunk=512),
        out_shape=(
            jax.ShapeDtypeStruct((8, particles), F32),
            jax.ShapeDtypeStruct(fluid.shape, F32),
        ) + edge_shapes(fields, layers, rows, cols),
        in_specs=[vmem] * 9,
        out_specs=(vmem,) * 6,
        scratch_shapes=[
            VMEM(fluid.shape, F32),
            VMEM((layers * rows, cols), F32),
            VMEM((fields * layers * rows // 2, 2 * cols), F32),
        ],
        compiler_params=pltpu.CompilerParams(vmem_limit_bytes=40 << 20),
        cost_estimate=pl.CostEstimate(
            flops=16 * fields * layers * rows * cols * particles, bytes_accessed=2 << 20, transcendentals=0
        ),
        name="see_and_deposit",
    )(fluid, *halo, cells, motion, radius, temp)


def heat_kernel(
    back_ref, slot_ref, cell_ref, radius_ref, base_ref, ey0_ref, ey1_ref, ex0_ref, ex1_ref,
    next_ref, dep_ref, dy0_ref, dy1_ref, dx0_ref, dx1_ref,
    table, acc, rows_scratch, *, chunk, rows
):
    devices, layers, _ = back_ref.shape
    particles = slot_ref.shape[1]
    half, wide = acc.shape
    for o in range(devices):
        table[o * layers : (o + 1) * layers, :] = back_ref[o]
    acc[...] = jnp.zeros_like(acc)

    def step(i, _):
        here = pl.ds(pl.multiple_of(i * chunk, chunk), chunk)
        slots = slot_ref[:, here]
        gained = []
        for s in range(chunk // BLOCK):
            wanted = jnp.broadcast_to(slots[:, s * BLOCK : (s + 1) * BLOCK], (8, BLOCK))
            tiles = [table[8 * g : 8 * g + 8, :] for g in range(devices * layers // 8)]
            gained.append(gathered([tiles], wanted // BLOCK, wanted % BLOCK)[0])
        base = base_ref[6:8, here]
        total = base[0:1] + jnp.concatenate(gained, axis=1)
        next_ref[:, here] = total
        radius = radius_ref[:, here]
        high, low = split(radius * radius * radius * (total - base[1:2]))
        cells = cell_ref[:, here]
        hot_low = hot(wide, cells % wide)
        hot_high = hot(half, cells // wide)
        added = lax.dot_general(hot_high * high, hot_low, NT, preferred_element_type=F32)
        acc[...] += added + lax.dot_general(hot_high * low, hot_low, NT, preferred_element_type=F32)
        return 0

    lax.fori_loop(0, particles // chunk, step, 0)
    field = paired_rows(acc[...], 2 * half // rows, rows, rows_scratch)
    dep_ref[0] = field
    for edge, out in ((ey0_ref, dy0_ref), (ey1_ref, dy1_ref), (ex0_ref, dx0_ref), (ex1_ref, dx1_ref)):
        out[0 : edge.shape[0]] = edge[...]
    write_edges(field, ey0_ref.shape[0], dy0_ref, dy1_ref, dx0_ref, dx1_ref)


def heat_deposit(back, slot_of, cells, radius, base, edges, grid):
    devices = back.shape[0]
    layers, rows, cols = grid
    particles = cells.shape[1]
    half = layers * rows // 2
    fields = edges[0].shape[0] + 1
    vmem = pl.BlockSpec(memory_space=VMEM)
    return pl.pallas_call(
        functools.partial(heat_kernel, chunk=1024, rows=rows),
        out_shape=(
            jax.ShapeDtypeStruct((1, particles), F32),
            jax.ShapeDtypeStruct((1,) + grid, F32),
        ) + edge_shapes(fields, layers, rows, cols),
        in_specs=[vmem] * 9,
        out_specs=(vmem,) * 6,
        scratch_shapes=[
            VMEM((devices * back.shape[1], BLOCK), F32),
            VMEM((half, 2 * cols), F32),
            VMEM((layers * rows, cols), F32),
        ],
        compiler_params=pltpu.CompilerParams(vmem_limit_bytes=40 << 20),
        cost_estimate=pl.CostEstimate(
            flops=4 * half * 2 * cols * particles, bytes_accessed=1 << 20, transcendentals=0
        ),
        name="heat_deposit",
    )(back, slot_of, cells, radius, base, *edges)


def fetch_kernel(
    owner_ref, tile_ref, back_ref, box_ref, spot_ref, base_ref, warm_ref, next_ref, box_of, table, wanted
):
    devices, tall, _ = back_ref.shape
    layers = tall // 6
    particles = box_ref.shape[1]
    invert(owner_ref, box_of)
    blank = jnp.zeros((2, BLOCK), F32)
    for o in range(devices):
        for q in range(layers):
            piece = jnp.concatenate([back_ref[o, 6 * q : 6 * q + 6, :], blank], axis=0)
            high, low = split(piece)
            table[o, q] = jnp.concatenate([high, low], axis=0)
        for q in range(layers, layers + 3):
            table[o, q] = jnp.zeros((16, BLOCK), BF16)

    def step(c, _):
        here = pl.ds(pl.multiple_of(c * CHUNK, CHUNK), CHUNK)
        boxes = jnp.broadcast_to(box_ref[:, here], (8, CHUNK))

        def window(w, total):
            for o in range(devices):
                tile = tile_ref[box_of[o], c] + 2 * w
                wanted[16 * o : 16 * o + 16, 0:BLOCK] = table[o, tile]
                wanted[16 * o : 16 * o + 16, BLOCK:] = table[o, tile + 1]
            hot_spot = hot(WINDOW, spot_ref[:, here] - WINDOW * w)
            found = lax.dot_general(wanted[...], hot_spot, NN, preferred_element_type=F32)
            gained = jnp.zeros((8, CHUNK), F32)
            for o in range(devices):
                value = found[16 * o : 16 * o + 8] + found[16 * o + 8 : 16 * o + 16]
                gained = jnp.where(boxes == box_of[o], value, gained)
            return total + gained

        gained = lax.fori_loop(0, tile_ref[devices, c], window, jnp.zeros((8, CHUNK), F32))
        next_ref[:, here] = jnp.concatenate(
            [base_ref[0:6, here] + gained[0:6], warm_ref[:, here]], axis=0
        )
        return 0

    lax.fori_loop(0, particles // CHUNK, step, 0)


def fetch(box_owner, tiles, back, boxes, spots, base, warm):
    devices, tall, _ = back.shape
    particles = boxes.shape[1]
    layers = tall // 6
    vmem = pl.BlockSpec(memory_space=VMEM)
    smem = pl.BlockSpec(memory_space=pltpu.SMEM)
    return pl.pallas_call(
        fetch_kernel,
        out_shape=jax.ShapeDtypeStruct((7, particles), F32),
        in_specs=[smem, smem] + [vmem] * 5,
        out_specs=vmem,
        scratch_shapes=[
            pltpu.SMEM((devices,), jnp.int32),
            VMEM((devices, layers + 3, 16, BLOCK), BF16),
            VMEM((16 * devices, WINDOW), BF16),
        ],
        compiler_params=pltpu.CompilerParams(vmem_limit_bytes=40 << 20),
        cost_estimate=pl.CostEstimate(
            flops=32 * devices * WINDOW * particles, bytes_accessed=1 << 20, transcendentals=0
        ),
        name="fetch_slots",
    )(box_owner, tiles, back, boxes, spots, base, warm)


def spread_kernel(dep_ref, heat_ref, y0_ref, y1_ref, x0_ref, x1_ref, fluid_ref, next_ref, void_ref):
    halo = (y0_ref, y1_ref, x0_ref, x1_ref)
    crowding = 1.0 + COUPLING * smooth_field(dep_ref, *halo, 0)
    void_ref[...] = 1.0 / crowding
    for k in range(3):
        next_ref[k] = fluid_ref[k] + TIME_STEP * COUPLING * smooth_field(dep_ref, *halo, k + 1) * crowding
    warmth = smooth_field(heat_ref, *halo, 0, 4)
    next_ref[3] = fluid_ref[3] + TIME_STEP * COUPLING * warmth * crowding


def spread(dep, heat, halo, fluid):
    vmem = pl.BlockSpec(memory_space=VMEM)
    return pl.pallas_call(
        spread_kernel,
        out_shape=(jax.ShapeDtypeStruct(fluid.shape, F32), jax.ShapeDtypeStruct(fluid.shape[1:], F32)),
        in_specs=[vmem] * 7,
        out_specs=(vmem,) * 2,
        compiler_params=pltpu.CompilerParams(vmem_limit_bytes=40 << 20),
        cost_estimate=pl.CostEstimate(flops=20 * fluid.size, bytes_accessed=2 << 20, transcendentals=0),
        name="spread_fields",
    )(dep, heat, *halo, fluid)


def halo_of(y_first, y_last, x_first, x_last):
    def moved(value, axis, step):
        size = lax.axis_size(axis)
        pairs = [(i, i + step) for i in range(size) if 0 <= i + step < size]
        return lax.ppermute(value, axis, pairs)

    return (
        moved(y_last, "gy", 1),
        moved(y_first, "gy", -1),
        moved(x_last, "gx", 1),
        moved(x_first, "gx", -1),
    )


def shards(
    fluid_state, particle_pos, particle_motion, particle_radius, particle_temp,
    particle_cell, particle_box, box_owner, contact_mask,
):
    devices = lax.axis_size(("gx", "gy"))
    particles = particle_pos.shape[1]
    slots = 2 * particles // devices
    fields, layers, rows, cols = fluid_state.shape
    boxes = particle_box.reshape(1, particles)
    radius = particle_radius.reshape(1, particles)
    temp = particle_temp.reshape(1, particles)
    cells = particle_cell.reshape(1, particles)

    outgoing, slot_of, spots, tiles = place(
        box_owner, boxes, particle_pos, particle_motion, radius, temp, slots
    )
    arrived = lax.all_to_all(outgoing, ("gx", "gy"), split_axis=0, concat_axis=0, tiled=True)

    fluid_halo = halo_of(
        fluid_state[:, :, 0, :],
        fluid_state[:, :, rows - 1, :],
        fluid_state[:, :, :, 0].reshape(-1, BLOCK),
        fluid_state[:, :, :, cols - 1].reshape(-1, BLOCK),
    )
    seen = see_and_deposit(fluid_state, fluid_halo, cells, particle_motion, radius, temp)
    arrived, base, deposits, *edges = lax.optimization_barrier((arrived,) + tuple(seen))

    result, heat = contact(arrived, contact_mask)
    heat_back = lax.all_to_all(heat, ("gx", "gy"), split_axis=0, concat_axis=0, tiled=True)
    back = lax.all_to_all(result, ("gx", "gy"), split_axis=0, concat_axis=0, tiled=True)

    warm, heat_field, *edges = heat_deposit(
        heat_back, slot_of, cells, radius, base, edges, (layers, rows, cols)
    )
    fluid_next, void_fraction = spread(deposits, heat_field, halo_of(*edges), fluid_state)
    back, void_fraction = lax.optimization_barrier((back, void_fraction))
    particle_next = fetch(box_owner, tiles, back, boxes, spots, base, warm)
    return (fluid_next, void_fraction, particle_next)


def solution(mesh):
    in_specs = (
        P(None, None, "gy", "gx"),
        P(None, ("gx", "gy")),
        P(None, ("gx", "gy")),
        P(("gx", "gy")),
        P(("gx", "gy")),
        P(("gx", "gy")),
        P(("gx", "gy"), None),
        P(),
        P(("gx", "gy"), None, None),
    )
    out_specs = (P(None, None, "gy", "gx"), P(None, "gy", "gx"), P(None, ("gx", "gy")))
    return jax.shard_map(shards, mesh=mesh, in_specs=in_specs, out_specs=out_specs, check_vma=False)
```

time: 138 us -> 120 us (0.87)
  starting transfers between devices: 44.9 us -> 33.5 us
  blocking collectives: 0 us -> 10.5 us
  waiting for transfers between devices: 15.8 us -> 6.88 us
  local copies, waits for them, and re-layouts: 8.95 us -> 4.18 us
  Pallas kernels: 66.2 us -> 63 us
    ppermute x12 -> x8, starting transfers between devices: 33.6 us -> 22.8 us  [moved(): return lax.ppermute(value, axis, pairs)]
    all_to_all x0 -> x1, blocking collectives: none -> 10.5 us  [shards(): lax.all_to_all(heat, ('gx', 'gy'), split_axis=0, concat_axis=0, tiled=True)]
    unnamed x28 -> x22, local copies, waits for them, and re-layouts: 8.19 us -> 0.94 us
    ppermute x12 -> x8, waiting for transfers between devices: 8.67 us -> 4 us  [moved(): return lax.ppermute(value, axis, pairs)]
    all_to_all x1, waiting for transfers between devices: 7.1 us -> 2.88 us  [shards(): lax.all_to_all(outgoing, ('gx', 'gy'), split_axis=0, concat_axis=0, tiled...]
    pallas_call x1, Pallas kernels: 19.1 us -> 16.3 us  [see_and_deposit(): pl.pallas_call(functools.partial(fluid_kernel, chunk=512), out_shape=(jax...]
  transfers between devices with their start and end apart: 14 -> 10, of which waited for: 4 -> 2; matrix products, arithmetic and copies ran while one was open for 1% -> 2% of each run, Pallas kernels for 39% -> 31%
where the time goes in v2:
time: 120 us; the launch traced here: 119 us
  Pallas kernels  63 us (52%)
  starting transfers between devices  33.5 us (28%)
  blocking collectives  10.5 us (9%)
  waiting for transfers between devices  6.88 us (6%)
  local copies, waits for them, and re-layouts  4.18 us (3%)
    ppermute x8, starting transfers between devices, moved(): return lax.ppermute(value, axis, pairs)  22.8 us
    pallas_call x1, Pallas kernels, contact(): pl.pallas_call(contact_kernel, grid=(devices // step,), out_shape=(jax.Sh...  20.1 us
    pallas_call x1, Pallas kernels, see_and_deposit(): pl.pallas_call(functools.partial(fluid_kernel, chunk=512), out_shape=(jax...  16.3 us
    pallas_call x1, Pallas kernels, place(): pl.pallas_call(place_kernel, out_shape=(jax.ShapeDtypeStruct((devices, 12...  11.7 us
    all_to_all x1, blocking collectives, shards(): lax.all_to_all(heat, ('gx', 'gy'), split_axis=0, concat_axis=0, tiled=True)  10.5 us
    pallas_call x1, Pallas kernels, heat_deposit(): pl.pallas_call(functools.partial(heat_kernel, chunk=1024, rows=rows), out...  7.18 us
    all_to_all x1, starting transfers between devices, shards(): lax.all_to_all(outgoing, ('gx', 'gy'), split_axis=0, concat_axis=0, tiled...  6.02 us
    pallas_call x1, Pallas kernels, fetch(): pl.pallas_call(fetch_kernel, out_shape=jax.ShapeDtypeStruct((7, particles...  5.76 us
  transfers between devices with their start and end apart: 10, of which 2 were waited for; matrix products, arithmetic and copies ran while one was open for 2% of the time, Pallas kernels for 31%

profile of v2, /device:TPU:10, one launch (start us, length us, event | category | flops | bytes accessed | tf_op | source)
XLA Modules:
  0.0 119.0 jit_solution(7029435354468146917)
XLA Ops:
  0.6 0.0 copy-start
  0.6 0.0 copy-start.1
  0.7 0.0 copy-start.4
  0.7 0.0 copy-start.2
  0.7 1.4 %fusion = (f32[4,32,1,128]{3,2,1,0:T(1,128)S(1)}, f32[4,32,1,128]{3,2,1,0:T(1,128)S(1)}) fusion(f32[4,32,8,128]{3,2,1,0:T(8,128)} %fluid_ref.3), kind=kLoop, calls=%fused_computation.2 | loop fusion | bytes 262144 | tf_op jit(solution)/shard_map/slice | solution.py:611
  2.0 1.9 %collective-permute-start = (f32[4,32,128]{2,1,0:T(8,128)S(1)}, f32[4,32,128]{2,1,0:T(8,128)S(1)}, u32[]{:S(2)}, u32[]{:S(2)}) collective-permute-start(f32[4,32,128]{2,1,0:T(8,128)S(1)} %bitcast.20), channel_id=1, source_target_pairs={{0,1},{1,2},{2,3},{3,4},{4,5},{5,6},{6,7},{8,9},{9,10},{10,11},{11... | collective-permute-start | bytes 196616 | tf_op jit(solution)/shard_map/ppermute | solution.py:582
  4.0 3.6 %collective-permute-start.1 = (f32[4,32,128]{2,1,0:T(8,128)S(1)}, f32[4,32,128]{2,1,0:T(8,128)S(1)}, u32[]{:S(2)}, u32[]{:S(2)}) collective-permute-start(f32[4,32,128]{2,1,0:T(8,128)S(1)} %bitcast.19), channel_id=1, source_target_pairs={{1,0},{2,1},{3,2},{4,3},{5,4},{6,5},{7,6},{9,8},{10,9},{11,10},{12... | collective-permute-start | bytes 196616 | tf_op jit(solution)/shard_map/ppermute | solution.py:582
  7.6 1.7 %slice_reduce_fusion = (f32[4,32,8]{2,1,0:T(8,128)S(1)}, f32[4,32,8]{2,1,0:T(8,128)S(1)}) fusion(f32[4,32,8,128]{3,2,1,0:T(8,128)} %fluid_ref.3), kind=kLoop, calls=%fused_computation | loop fusion | bytes 16384 | tf_op jit(solution)/shard_map/slice | solution.py:613
  9.3 0.1 reshape_squeeze.6
  9.4 3.4 %collective-permute-start.2 = (f32[8,128]{1,0:T(8,128)S(1)}, f32[8,128]{1,0:T(8,128)S(1)}, u32[]{:S(2)}, u32[]{:S(2)}) collective-permute-start(f32[8,128]{1,0:T(8,128)S(1)} %reshape_squeeze.6), channel_id=1, source_target_pairs={{0,8},{8,16},{16,24},{1,9},{9,17},{17,25},{2,10},{10,18},{18,26},{... | collective-permute-start | bytes 12296 | tf_op jit(solution)/shard_map/ppermute | solution.py:582
  12.8 0.1 reshape_squeeze.7
  12.9 2.4 %collective-permute-start.3 = (f32[8,128]{1,0:T(8,128)S(1)}, f32[8,128]{1,0:T(8,128)S(1)}, u32[]{:S(2)}, u32[]{:S(2)}) collective-permute-start(f32[8,128]{1,0:T(8,128)S(1)} %reshape_squeeze.7), channel_id=1, source_target_pairs={{8,0},{16,8},{24,16},{9,1},{17,9},{25,17},{10,2},{18,10},{26,18},{... | collective-permute-start | bytes 12296 | tf_op jit(solution)/shard_map/ppermute | solution.py:582
  15.4 11.7 %place_slots.1 = (f32[32,48,128]{2,1,0:T(8,128)}, s32[1,8192]{1,0:T(1,128)}, s32[1,8192]{1,0:T(1,128)}, s32[40,128]{1,0:T(8,128)}) custom-call(s32[32]{0:T(128)} %owner_ref.3, s32[1,8192]{1,0:T(1,128)} %bitcast.17, f32[3,8192]{1,0:T(4,128)} %pos_ref.1, f32[6,8192]{1,0:T(8,128)} %motion_ref.3, f32[1,8192]{1,0:T(1,128)} %bitcast.14, f32[1,8192]{1,0:T(1,128)} %bitcast.10), custom_call_target="tpu_custom_call" | custom-call | flops 3221225472 | bytes 1048576 | tf_op jit(solution)/shard_map/place_slots/pallas_call | solution.py:166
  27.1 6.0 %all-to-all-start = ((f32[32,48,128]{2,1,0:T(8,128)}), f32[32,48,128]{2,1,0:T(8,128)S(1)}, u32[]{:S(2)}, u32[]{:S(2)}) async-start(f32[32,48,128]{2,1,0:T(8,128)} %get-tuple-element.32), calls=%async_computation | async-start | bytes 1572864 | tf_op jit(solution)/shard_map/all_to_all | solution.py:608
  33.1 0.0 collective-permute-done.y0_ref
  33.2 16.3 %see_and_deposit.1 = (f32[8,8192]{1,0:T(8,128)S(1)}, f32[4,32,8,128]{3,2,1,0:T(8,128)S(1)}, f32[4,32,128]{2,1,0:T(8,128)S(1)}, f32[4,32,128]{2,1,0:T(8,128)S(1)}...) custom-call(f32[4,32,8,128]{3,2,1,0:T(8,128)S(1)} %copy-done, f32[4,32,128]{2,1,0:T(8,128)S(1)} %collective-permute-done.y0_ref, ...), custom_call_target="tpu_custom_call" | custom-call | flops 17179869184 | bytes 2097152 | tf_op jit(solution)/shard_map/see_and_deposit/pallas_call | solution.py:400
  49.5 0.0 copy-start.7
  49.5 0.0 copy-start.5
  49.5 0.0 copy-start.6
  49.6 2.9 %all-to-all-done.slot_ref = f32[32,48,128]{2,1,0:T(8,128)S(1)} async-done(((f32[32,48,128]{2,1,0:T(8,128)}), f32[32,48,128]{2,1,0:T(8,128)S(1)}, u32[]{:S(2)}, u32[]{:S(2)}) %all-to-all-start) | async-done | bytes 786464 | tf_op jit(solution)/shard_map/all_to_all | solution.py:608
  52.4 0.9 copy-done.10
  53.3 20.1 %contact_blocks.1 = (f32[32,24,128]{2,1,0:T(8,128)}, f32[32,4,128]{2,1,0:T(4,128)}) custom-call(f32[32,48,128]{2,1,0:T(8,128)} %copy-done.10, s32[128,128,128]{2,1,0:T(8,128)} %mask_ref.1), custom_call_target="tpu_custom_call" | custom-call | flops 134217728 | bytes 8388608 | tf_op jit(solution)/shard_map/contact_blocks/pallas_call | solution.py:248
  73.4 10.5 %all_to_all.15.back_ref = f32[32,4,128]{2,1,0:T(4,128)S(1)} all-to-all(f32[32,4,128]{2,1,0:T(4,128)} %get-tuple-element.41), channel_id=1, replica_groups=mesh['gx'=4,'gy'=8] {'gx','gy'}, dimensions={0} | all-to-all | bytes 131072 | tf_op jit(solution)/shard_map/all_to_all | solution.py:620
  83.9 4.7 %all-to-all-start.2 = ((f32[32,24,128]{2,1,0:T(8,128)}), f32[32,24,128]{2,1,0:T(8,128)S(1)}, u32[]{:S(2)}, u32[]{:S(2)}) async-start(f32[32,24,128]{2,1,0:T(8,128)} %get-tuple-element.54), calls=%async_computation.2 | async-start | bytes 786432 | tf_op jit(solution)/shard_map/all_to_all | solution.py:621
  88.6 7.2 %heat_deposit.1 = (f32[1,8192]{1,0:T(1,128)S(1)}, f32[1,32,8,128]{3,2,1,0:T(8,128)S(1)}, f32[5,32,128]{2,1,0:T(8,128)S(1)}, f32[5,32,128]{2,1,0:T(8,128)S(1)}, f...) custom-call(f32[32,4,128]{2,1,0:T(4,128)S(1)} %all_to_all.15.back_ref, s32[1,8192]{1,0:T(1,128)S(1)} %copy-done.7, ...), custom_call_target="tpu_custom_call" | custom-call | flops 1073741824 | bytes 1048576 | tf_op jit(solution)/shard_map/heat_deposit/pallas_call | solution.py:468
  95.8 2.1 %collective-permute-start.4 = (f32[5,32,128]{2,1,0:T(8,128)S(1)}, f32[5,32,128]{2,1,0:T(8,128)S(1)}, u32[]{:S(2)}, u32[]{:S(2)}) collective-permute-start(f32[5,32,128]{2,1,0:T(8,128)S(1)} %get-tuple-element.49), channel_id=1, source_target_pairs={{0,1},{1,2},{2,3},{3,4},{4,5},{5,6},{6,7},{8,9},{9,10},{10,11},{11... | collective-permute-start | bytes 245768 | tf_op jit(solution)/shard_map/ppermute | solution.py:582
  97.8 3.5 %collective-permute-start.5 = (f32[5,32,128]{2,1,0:T(8,128)S(1)}, f32[5,32,128]{2,1,0:T(8,128)S(1)}, u32[]{:S(2)}, u32[]{:S(2)}) collective-permute-start(f32[5,32,128]{2,1,0:T(8,128)S(1)} %get-tuple-element.50), channel_id=1, source_target_pairs={{1,0},{2,1},{3,2},{4,3},{5,4},{6,5},{7,6},{9,8},{10,9},{11,10},{12... | collective-permute-start | bytes 245768 | tf_op jit(solution)/shard_map/ppermute | solution.py:582
  101.3 3.4 %collective-permute-start.6 = (f32[10,128]{1,0:T(8,128)S(1)}, f32[10,128]{1,0:T(8,128)S(1)}, u32[]{:S(2)}, u32[]{:S(2)}) collective-permute-start(f32[10,128]{1,0:T(8,128)S(1)} %get-tuple-element.51), channel_id=1, source_target_pairs={{0,8},{8,16},{16,24},{1,9},{9,17},{17,25},{2,10},{10,18},{18,26},{... | collective-permute-start | bytes 15368 | tf_op jit(solution)/shard_map/ppermute | solution.py:582
  104.7 2.4 %collective-permute-start.7 = (f32[10,128]{1,0:T(8,128)S(1)}, f32[10,128]{1,0:T(8,128)S(1)}, u32[]{:S(2)}, u32[]{:S(2)}) collective-permute-start(f32[10,128]{1,0:T(8,128)S(1)} %get-tuple-element.52), channel_id=1, source_target_pairs={{8,0},{16,8},{24,16},{9,1},{17,9},{25,17},{10,2},{18,10},{26,18},{... | collective-permute-start | bytes 15368 | tf_op jit(solution)/shard_map/ppermute | solution.py:582
  107.2 4.0 %collective-permute-done.7.x1_ref = f32[10,128]{1,0:T(8,128)S(1)} collective-permute-done((f32[10,128]{1,0:T(8,128)S(1)}, f32[10,128]{1,0:T(8,128)S(1)}, u32[]{:S(2)}, u32[]{:S(2)}) %collective-permute-start.7) | collective-permute-done | bytes 5152 | tf_op jit(solution)/shard_map/ppermute | solution.py:582
  111.2 2.0 %spread_fields.1 = (f32[4,32,8,128]{3,2,1,0:T(8,128)}, f32[32,8,128]{2,1,0:T(8,128)}) custom-call(f32[4,32,8,128]{3,2,1,0:T(8,128)S(1)} %get-tuple-element.39.dep_ref, f32[1,32,8,128]{3,2,1,0:T(8,128)S(1)} %get-tuple-element.48.heat_ref, f32[5,32,128]{2,1,0:T(8,128)S(1)} %collective-permute-done.4.y0_ref, f32[5,32,128]{2,1,0:T(8,128)S(1)} %collective-permute-done.5.y1_ref, ...), custom_call_target="tpu_custom_call" | custom-call | flops 2621440 | bytes 2097152 | tf_op jit(solution)/shard_map/spread_fields/pallas_call | solution.py:567
  113.2 5.8 %fetch_slots.1 = f32[7,8192]{1,0:T(8,128)} custom-call(s32[32]{0:T(128)S(1)} %copy-done.6, s32[40,128]{1,0:T(8,128)S(1)} %copy-done.9, f32[32,24,128]{2,1,0:T(8,128)S(1)} %all-to-all-done.2.back_ref, s32[1,8192]{1,0:T(1,128)S(1)} %bitcast.18, s32[1,8192]{1,0:T(1,128)S(1)} %copy-done.8, f32[8,8192]{1,0:T(8,128)S(1)} %get-tuple-element.43.base_ref, ...), custom_call_target="tpu_custom_call" | custom-call | flops 2147483648 | bytes 1048576 | tf_op jit(solution)/shard_map/fetch_slots/pallas_call | solution.py:537
  (21 shorter events, 0.0 us)
Async XLA Ops:
  0.6 32.5 %copy-start = (f32[4,32,8,128]{3,2,1,0:T(8,128)S(1)}, f32[4,32,8,128]{3,2,1,0:T(8,128)}, u32[]{:S(2)}) copy-start(f32[4,32,8,128]{3,2,1,0:T(8,128)} %fluid_ref.3) | copy-start | bytes 1572868
  0.6 32.5 %copy-start.1 = (f32[6,8192]{1,0:T(8,128)S(1)}, f32[6,8192]{1,0:T(8,128)}, u32[]{:S(2)}) copy-start(f32[6,8192]{1,0:T(8,128)} %motion_ref.3) | copy-start | bytes 589828
  0.7 32.5 %copy-start.4 = (f32[8192]{0:T(1024)S(1)}, f32[8192]{0:T(1024)}, u32[]{:S(2)}) copy-start(f32[8192]{0:T(1024)} %param.12) | copy-start | bytes 98308
  0.7 32.5 %copy-start.2 = (f32[8192]{0:T(1024)S(1)}, f32[8192]{0:T(1024)}, u32[]{:S(2)}) copy-start(f32[8192]{0:T(1024)} %param.13) | copy-start | bytes 98308
  0.7 32.5 %copy-start.3 = (s32[8192]{0:T(1024)S(1)}, s32[8192]{0:T(1024)}, u32[]{:S(2)}) copy-start(s32[8192]{0:T(1024)} %param.14) | copy-start | bytes 98308
  2.0 31.1 %collective-permute-start = (f32[4,32,128]{2,1,0:T(8,128)S(1)}, f32[4,32,128]{2,1,0:T(8,128)S(1)}, u32[]{:S(2)}, u32[]{:S(2)}) collective-permute-start(f32[4,32,128]{2,1,0:T(8,128)S(1)} %bitcast.20), channel_id=1, source_target_pairs={{0,1},{1,2},{2,3},{3,4},{4,5},{5,6},{6,7},{8,9},{9,10},{10,11},{11... | collective-permute-start | bytes 196616 | tf_op jit(solution)/shard_map/ppermute | solution.py:582
  4.0 29.2 %collective-permute-start.1 = (f32[4,32,128]{2,1,0:T(8,128)S(1)}, f32[4,32,128]{2,1,0:T(8,128)S(1)}, u32[]{:S(2)}, u32[]{:S(2)}) collective-permute-start(f32[4,32,128]{2,1,0:T(8,128)S(1)} %bitcast.19), channel_id=1, source_target_pairs={{1,0},{2,1},{3,2},{4,3},{5,4},{6,5},{7,6},{9,8},{10,9},{11,10},{12... | collective-permute-start | bytes 196616 | tf_op jit(solution)/shard_map/ppermute | solution.py:582
  9.4 23.7 %collective-permute-start.2 = (f32[8,128]{1,0:T(8,128)S(1)}, f32[8,128]{1,0:T(8,128)S(1)}, u32[]{:S(2)}, u32[]{:S(2)}) collective-permute-start(f32[8,128]{1,0:T(8,128)S(1)} %reshape_squeeze.6), channel_id=1, source_target_pairs={{0,8},{8,16},{16,24},{1,9},{9,17},{17,25},{2,10},{10,18},{18,26},{... | collective-permute-start | bytes 12296 | tf_op jit(solution)/shard_map/ppermute | solution.py:582
  12.9 20.2 %collective-permute-start.3 = (f32[8,128]{1,0:T(8,128)S(1)}, f32[8,128]{1,0:T(8,128)S(1)}, u32[]{:S(2)}, u32[]{:S(2)}) collective-permute-start(f32[8,128]{1,0:T(8,128)S(1)} %reshape_squeeze.7), channel_id=1, source_target_pairs={{8,0},{16,8},{24,16},{9,1},{17,9},{25,17},{10,2},{18,10},{26,18},{... | collective-permute-start | bytes 12296 | tf_op jit(solution)/shard_map/ppermute | solution.py:582
  27.1 25.4 %all-to-all-start = ((f32[32,48,128]{2,1,0:T(8,128)}), f32[32,48,128]{2,1,0:T(8,128)S(1)}, u32[]{:S(2)}, u32[]{:S(2)}) async-start(f32[32,48,128]{2,1,0:T(8,128)} %get-tuple-element.32), calls=%async_computation | async-start | bytes 1572864 | tf_op jit(solution)/shard_map/all_to_all | solution.py:608
  49.5 39.1 %copy-start.7 = (s32[1,8192]{1,0:T(1,128)S(1)}, s32[1,8192]{1,0:T(1,128)}, u32[]{:S(2)}) copy-start(s32[1,8192]{1,0:T(1,128)} %get-tuple-element.42.slot_ref) | copy-start | bytes 98308
  49.5 63.7 %copy-start.5 = (s32[8192,1]{0,1:T(1,128)S(1)}, s32[8192,1]{0,1:T(1,128)}, u32[]{:S(2)}) copy-start(s32[8192,1]{0,1:T(1,128)} %param.15) | copy-start | bytes 98308
  49.5 63.7 %copy-start.6 = (s32[32]{0:T(128)S(1)}, s32[32]{0:T(128)}, u32[]{:S(2)}) copy-start(s32[32]{0:T(128)} %owner_ref.3) | copy-start | bytes 388
  49.5 63.7 %copy-start.8 = (s32[1,8192]{1,0:T(1,128)S(1)}, s32[1,8192]{1,0:T(1,128)}, u32[]{:S(2)}) copy-start(s32[1,8192]{1,0:T(1,128)} %get-tuple-element.59.spot_ref) | copy-start | bytes 98308
  49.6 63.7 %copy-start.9 = (s32[40,128]{1,0:T(8,128)S(1)}, s32[40,128]{1,0:T(8,128)}, u32[]{:S(2)}) copy-start(s32[40,128]{1,0:T(8,128)} %get-tuple-element.57.tile_ref) | copy-start | bytes 61444
  52.4 0.9 copy-start.10
  83.9 29.3 %all-to-all-start.2 = ((f32[32,24,128]{2,1,0:T(8,128)}), f32[32,24,128]{2,1,0:T(8,128)S(1)}, u32[]{:S(2)}, u32[]{:S(2)}) async-start(f32[32,24,128]{2,1,0:T(8,128)} %get-tuple-element.54), calls=%async_computation.2 | async-start | bytes 786432 | tf_op jit(solution)/shard_map/all_to_all | solution.py:621
  95.8 15.4 %collective-permute-start.4 = (f32[5,32,128]{2,1,0:T(8,128)S(1)}, f32[5,32,128]{2,1,0:T(8,128)S(1)}, u32[]{:S(2)}, u32[]{:S(2)}) collective-permute-start(f32[5,32,128]{2,1,0:T(8,128)S(1)} %get-tuple-element.49), channel_id=1, source_target_pairs={{0,1},{1,2},{2,3},{3,4},{4,5},{5,6},{6,7},{8,9},{9,10},{10,11},{11... | collective-permute-start | bytes 245768 | tf_op jit(solution)/shard_map/ppermute | solution.py:582
  97.8 13.4 %collective-permute-start.5 = (f32[5,32,128]{2,1,0:T(8,128)S(1)}, f32[5,32,128]{2,1,0:T(8,128)S(1)}, u32[]{:S(2)}, u32[]{:S(2)}) collective-permute-start(f32[5,32,128]{2,1,0:T(8,128)S(1)} %get-tuple-element.50), channel_id=1, source_target_pairs={{1,0},{2,1},{3,2},{4,3},{5,4},{6,5},{7,6},{9,8},{10,9},{11,10},{12... | collective-permute-start | bytes 245768 | tf_op jit(solution)/shard_map/ppermute | solution.py:582
  101.3 5.9 %collective-permute-start.6 = (f32[10,128]{1,0:T(8,128)S(1)}, f32[10,128]{1,0:T(8,128)S(1)}, u32[]{:S(2)}, u32[]{:S(2)}) collective-permute-start(f32[10,128]{1,0:T(8,128)S(1)} %get-tuple-element.51), channel_id=1, source_target_pairs={{0,8},{8,16},{16,24},{1,9},{9,17},{17,25},{2,10},{10,18},{18,26},{... | collective-permute-start | bytes 15368 | tf_op jit(solution)/shard_map/ppermute | solution.py:582
  104.7 6.4 %collective-permute-start.7 = (f32[10,128]{1,0:T(8,128)S(1)}, f32[10,128]{1,0:T(8,128)S(1)}, u32[]{:S(2)}, u32[]{:S(2)}) collective-permute-start(f32[10,128]{1,0:T(8,128)S(1)} %get-tuple-element.52), channel_id=1, source_target_pairs={{8,0},{16,8},{24,16},{9,1},{17,9},{25,17},{10,2},{18,10},{26,18},{... | collective-permute-start | bytes 15368 | tf_op jit(solution)/shard_map/ppermute | solution.py:582

commit v3 on v2

--- a/solution.py
+++ b/solution.py
@@ -23,7 +23,6 @@
 F32 = jnp.float32
 BF16 = jnp.bfloat16
 VMEM = pltpu.VMEM
-NT = (((1,), (1,)), ((), ()))
 NN = (((1,), (0,)), ((), ()))
 
 
@@ -35,6 +34,16 @@
 def hot(count, row):
     places = lax.broadcasted_iota(jnp.int32, (count, row.shape[1]), 0)
     return jnp.where(places == row, 1.0, 0.0).astype(BF16)
+
+
+def hot_columns(count, row):
+    n = row.shape[1] // BLOCK
+    tiles = [row[:, a * BLOCK : (a + 1) * BLOCK] for a in range(n)]
+    turned = jnp.transpose(jnp.concatenate(tiles * (8 // n), axis=0).astype(F32))
+    places = lax.broadcasted_iota(jnp.int32, (BLOCK, count), 1).astype(F32)
+    return jnp.concatenate(
+        [jnp.where(places == turned[:, a : a + 1], 1.0, 0.0).astype(BF16) for a in range(n)], axis=0
+    )
 
 
 def invert(owner_ref, box_of):
@@ -54,8 +63,7 @@
     out_ref, slot_ref, spot_ref, tile_ref,
     box_of, tile_of, acc, done
 ):
-    devices, rows, _ = out_ref.shape
-    layers = rows // 12
+    devices, _, layers, _ = out_ref.shape
     slots = layers * BLOCK
     particles = box_ref.shape[1]
     sub = 256
@@ -116,7 +124,7 @@
         push = TIME_STEP * STIFFNESS * pos - TIME_STEP * DAMPING_RATE * motion[0:3]
         spin = -TIME_STEP * ROTATION_DRAG * motion[3:6]
         heat = -TIME_STEP * CONDUCTION * temp_ref[:, here]
-        first = jnp.concatenate([push, spin, heat, jnp.ones((1, CHUNK), F32)], axis=0)
+        first = jnp.concatenate([push, spin, heat, jnp.zeros((1, CHUNK), F32)], axis=0)
         second = jnp.concatenate([pos, radius_ref[:, here]], axis=0)
         first = jnp.concatenate(split(first), axis=0)
         second = jnp.concatenate(split(second), axis=0)
@@ -130,8 +138,8 @@
         parts = jnp.concatenate(first_parts + second_parts, axis=0)
 
         def window(w, _):
-            hot_spot = hot(WINDOW, spot_ref[:, here] - WINDOW * w)
-            placed = lax.dot_general(parts, hot_spot, NT, preferred_element_type=F32)
+            hot_spot = hot_columns(WINDOW, spot_ref[:, here] - WINDOW * w)
+            placed = lax.dot_general(parts, hot_spot, NN, preferred_element_type=F32)
             for o in range(devices):
                 tile = tile_of[box_of[o], c] + 2 * w
                 one = placed[16 * o : 16 * o + 8] + placed[16 * o + 8 : 16 * o + 16]
@@ -149,8 +157,8 @@
 
     def finish(o, _):
         for q in range(layers):
-            out_ref[o, 8 * q : 8 * q + 8, :] = acc[o, q, 0:8, :]
-            out_ref[o, 8 * layers + 4 * q : 8 * layers + 4 * q + 4, :] = acc[o, q, 8:12, :]
+            out_ref[o, 0:7, q, :] = acc[o, q, 0:7, :]
+            out_ref[o, 7:11, q, :] = acc[o, q, 8:12, :]
         return 0
 
     lax.fori_loop(0, devices, finish, 0)
@@ -166,7 +174,7 @@
     return pl.pallas_call(
         place_kernel,
         out_shape=(
-            jax.ShapeDtypeStruct((devices, 12 * layers, BLOCK), F32), row, row,
+            jax.ShapeDtypeStruct((devices, 11, layers, BLOCK), F32), row, row,
             jax.ShapeDtypeStruct(table, jnp.int32),
         ),
         in_specs=[pl.BlockSpec(memory_space=pltpu.SMEM)] + [vmem] * 5,
@@ -211,55 +219,76 @@
     for_d = jnp.concatenate([cross_d, cross_d, ones_d, jnp.where(row < 3, third, 0.0)], axis=0)
     for_r = jnp.concatenate([cross_r, cross_r, ones_r, jnp.where((row >= 3) & (row < 6), third, 0.0)], axis=0)
     right = jnp.concatenate([for_d, for_r], axis=1)
-    return left.astype(BF16), right.astype(BF16)
-
-
-def contact_kernel(slot_ref, mask_ref, out_ref, heat_ref):
-    homes, rows, _ = slot_ref.shape
-    layers = rows // 12
-    sign = lax.broadcasted_iota(jnp.int32, (8, 1), 0)
-    sign = jnp.where((sign >= 3) & (sign < 6), 1.0, -1.0)
-    for s in range(homes):
-        for q in range(layers):
-            mixed = slot_ref[s, 8 * q : 8 * q + 8, :]
-            near = slot_ref[s, 8 * layers + 4 * q : 8 * layers + 4 * q + 4, :]
+    return left, right.astype(BF16)
+
+
+def contact_kernel(slot_ref, mask_ref, out_ref):
+    homes, _, layers, _ = slot_ref.shape
+    blocks = [(s, q) for s in range(homes) for q in range(layers)]
+    row = lax.broadcasted_iota(jnp.int32, (8, 1), 0)
+    sign = jnp.where((row >= 3) & (row < 6), 1.0, -1.0)
+    mixed = []
+    stacked = []
+    pairs = []
+    for first in range(0, len(blocks), 4):
+        lefts = []
+        rights = []
+        for g, (s, q) in enumerate(blocks[first : first + 4]):
+            near = slot_ref[s, 7:11, q, :]
+            occupied = jnp.where(near[3:4] > 0.0, 1.0, 0.0)
+            mine = jnp.concatenate([slot_ref[s, 0:7, q, :], occupied], axis=0)
+            mixed.append(mine)
+            high = mine.astype(BF16).astype(F32)
+            stacked += [high, mine - high]
             left, right = pair_terms(near)
-            pair = lax.dot_general(left, right, (((0,), (0,)), ((), ())), preferred_element_type=F32)
-            reach = pair[:, BLOCK:]
-            inverse = pl.reciprocal(reach, approx=True)
-            inverse = inverse * (2.0 - reach * inverse)
-            weight = mask_ref[s * layers + q].astype(F32) * jnp.exp(pair[:, :BLOCK] * inverse)
-            weight_high, weight_low = split(weight)
-            mixed_high, mixed_low = split(mixed)
-            both = jnp.concatenate([mixed_high, mixed_low], axis=0)
-            sums = lax.dot_general(both, weight_high, NT, preferred_element_type=F32)
-            sums = sums + lax.dot_general(both, weight_low, NT, preferred_element_type=F32)
-            sums = sums[0:8] + sums[8:16]
-            result = mixed * sums[7:8] + sign * sums
-            out_ref[s, 6 * q : 6 * q + 6, :] = result[0:6]
-            heat_ref[s, q : q + 1, :] = result[6:7]
+            lefts.append(left)
+            spots = [jnp.zeros_like(right)] * 4
+            spots[g] = right
+            rights.append(jnp.concatenate(spots, axis=0))
+        turned = jnp.transpose(jnp.concatenate(lefts, axis=0)).astype(BF16)
+        pairs.append(
+            lax.dot_general(turned, jnp.concatenate(rights, axis=1), NN, preferred_element_type=F32)
+        )
+    columns = jnp.transpose(jnp.concatenate(stacked, axis=0)).astype(BF16)
+    lane = lax.broadcasted_iota(jnp.int32, (BLOCK, BLOCK), 1) // 16
+    highs = []
+    lows = []
+    right = []
+    for b in range(len(blocks)):
+        at = 2 * BLOCK * (b % 4)
+        pair = pairs[b // 4]
+        reach = pair[:, at + BLOCK : at + 2 * BLOCK]
+        inverse = pl.reciprocal(reach, approx=True)
+        inverse = inverse * (2.0 - reach * inverse)
+        weight = mask_ref[b].astype(F32) * jnp.exp(pair[:, at : at + BLOCK] * inverse)
+        high, low = split(weight)
+        highs.append(high)
+        lows.append(low)
+        right.append(jnp.where(lane == b, columns, jnp.zeros_like(columns)))
+    sums = lax.dot_general(
+        jnp.concatenate(highs + lows, axis=1), jnp.concatenate(right + right, axis=0), NN,
+        preferred_element_type=F32,
+    )
+    sums = jnp.transpose(sums)
+    for b, (s, q) in enumerate(blocks):
+        total = sums[16 * b : 16 * b + 8] + sums[16 * b + 8 : 16 * b + 16]
+        result = mixed[b] * total[7:8] + sign * total
+        out_ref[s, :, q, :] = result[0:7]
 
 
 def contact(arrived, mask):
-    devices, rows, _ = arrived.shape
-    layers = rows // 12
+    devices, values, layers, _ = arrived.shape
     blocks = mask.shape[0]
-    step = 2 if layers > 1 else 8
+    step = 8 // layers
     return pl.pallas_call(
         contact_kernel,
         grid=(devices // step,),
-        out_shape=(
-            jax.ShapeDtypeStruct((devices, 6 * layers, BLOCK), F32),
-            jax.ShapeDtypeStruct((devices, layers, BLOCK), F32),
-        ),
+        out_shape=jax.ShapeDtypeStruct((devices, 7, layers, BLOCK), F32),
         in_specs=[
-            pl.BlockSpec((step, rows, BLOCK), lambda h: (h, 0, 0)),
+            pl.BlockSpec((step, values, layers, BLOCK), lambda h: (h, 0, 0, 0)),
             pl.BlockSpec((step * layers, BLOCK, BLOCK), lambda h: (h, 0, 0)),
         ],
-        out_specs=(
-            pl.BlockSpec((step, 6 * layers, BLOCK), lambda h: (h, 0, 0)),
-            pl.BlockSpec((step, layers, BLOCK), lambda h: (h, 0, 0)),
-        ),
+        out_specs=pl.BlockSpec((step, 7, layers, BLOCK), lambda h: (h, 0, 0, 0)),
         compiler_params=pltpu.CompilerParams(vmem_limit_bytes=60 << 20),
         cost_estimate=pl.CostEstimate(
             flops=64 * blocks * BLOCK * BLOCK, bytes_accessed=blocks * BLOCK * BLOCK * 4, transcendentals=0
@@ -350,7 +379,7 @@
     def step(i, _):
         here = pl.ds(pl.multiple_of(i * chunk, chunk), chunk)
         cells = cell_ref[:, here]
-        hot_low = hot(wide, cells % wide)
+        hot_low = hot_columns(wide, cells % wide)
         hot_high = hot(half, cells // wide)
         seen = [[] for _ in range(fields)]
         for s in range(chunk // BLOCK):
@@ -376,8 +405,8 @@
         parts = []
         for piece in (high, low):
             parts.append(jnp.concatenate([hot_high * piece[k : k + 1] for k in range(4)], axis=0))
-        total = lax.dot_general(parts[0], hot_low, NT, preferred_element_type=F32)
-        acc[...] += total + lax.dot_general(parts[1], hot_low, NT, preferred_element_type=F32)
+        total = lax.dot_general(parts[0], hot_low, NN, preferred_element_type=F32)
+        acc[...] += total + lax.dot_general(parts[1], hot_low, NN, preferred_element_type=F32)
         return 0
 
     lax.fori_loop(0, particles // chunk, step, 0)
@@ -423,11 +452,11 @@
     next_ref, dep_ref, dy0_ref, dy1_ref, dx0_ref, dx1_ref,
     table, acc, rows_scratch, *, chunk, rows
 ):
-    devices, layers, _ = back_ref.shape
+    devices, _, layers, _ = back_ref.shape
     particles = slot_ref.shape[1]
     half, wide = acc.shape
     for o in range(devices):
-        table[o * layers : (o + 1) * layers, :] = back_ref[o]
+        table[o * layers : (o + 1) * layers, :] = back_ref[o, 6]
     acc[...] = jnp.zeros_like(acc)
 
     def step(i, _):
@@ -444,10 +473,10 @@
         radius = radius_ref[:, here]
         high, low = split(radius * radius * radius * (total - base[1:2]))
         cells = cell_ref[:, here]
-        hot_low = hot(wide, cells % wide)
+        hot_low = hot_columns(wide, cells % wide)
         hot_high = hot(half, cells // wide)
-        added = lax.dot_general(hot_high * high, hot_low, NT, preferred_element_type=F32)
-        acc[...] += added + lax.dot_general(hot_high * low, hot_low, NT, preferred_element_type=F32)
+        added = lax.dot_general(hot_high * high, hot_low, NN, preferred_element_type=F32)
+        acc[...] += added + lax.dot_general(hot_high * low, hot_low, NN, preferred_element_type=F32)
         return 0
 
     lax.fori_loop(0, particles // chunk, step, 0)
@@ -474,7 +503,7 @@
         in_specs=[vmem] * 9,
         out_specs=(vmem,) * 6,
         scratch_shapes=[
-            VMEM((devices * back.shape[1], BLOCK), F32),
+            VMEM((devices * back.shape[2], BLOCK), F32),
             VMEM((half, 2 * cols), F32),
             VMEM((layers * rows, cols), F32),
         ],
@@ -489,14 +518,13 @@
 def fetch_kernel(
     owner_ref, tile_ref, back_ref, box_ref, spot_ref, base_ref, warm_ref, next_ref, box_of, table, wanted
 ):
-    devices, tall, _ = back_ref.shape
-    layers = tall // 6
+    devices, _, layers, _ = back_ref.shape
     particles = box_ref.shape[1]
     invert(owner_ref, box_of)
     blank = jnp.zeros((2, BLOCK), F32)
     for o in range(devices):
         for q in range(layers):
-            piece = jnp.concatenate([back_ref[o, 6 * q : 6 * q + 6, :], blank], axis=0)
+            piece = jnp.concatenate([back_ref[o, 0:6, q, :], blank], axis=0)
             high, low = split(piece)
             table[o, q] = jnp.concatenate([high, low], axis=0)
         for q in range(layers, layers + 3):
@@ -529,9 +557,8 @@
 
 
 def fetch(box_owner, tiles, back, boxes, spots, base, warm):
-    devices, tall, _ = back.shape
+    devices, _, layers, _ = back.shape
     particles = boxes.shape[1]
-    layers = tall // 6
     vmem = pl.BlockSpec(memory_space=VMEM)
     smem = pl.BlockSpec(memory_space=pltpu.SMEM)
     return pl.pallas_call(
@@ -607,25 +634,24 @@
     )
     arrived = lax.all_to_all(outgoing, ("gx", "gy"), split_axis=0, concat_axis=0, tiled=True)
 
+    spots, fluid = lax.optimization_barrier((spots, fluid_state))
     fluid_halo = halo_of(
-        fluid_state[:, :, 0, :],
-        fluid_state[:, :, rows - 1, :],
-        fluid_state[:, :, :, 0].reshape(-1, BLOCK),
-        fluid_state[:, :, :, cols - 1].reshape(-1, BLOCK),
+        fluid[:, :, 0, :],
+        fluid[:, :, rows - 1, :],
+        fluid[:, :, :, 0].reshape(-1, BLOCK),
+        fluid[:, :, :, cols - 1].reshape(-1, BLOCK),
     )
     seen = see_and_deposit(fluid_state, fluid_halo, cells, particle_motion, radius, temp)
     arrived, base, deposits, *edges = lax.optimization_barrier((arrived,) + tuple(seen))
 
-    result, heat = contact(arrived, contact_mask)
-    heat_back = lax.all_to_all(heat, ("gx", "gy"), split_axis=0, concat_axis=0, tiled=True)
+    result = contact(arrived, contact_mask)
     back = lax.all_to_all(result, ("gx", "gy"), split_axis=0, concat_axis=0, tiled=True)
-
     warm, heat_field, *edges = heat_deposit(
-        heat_back, slot_of, cells, radius, base, edges, (layers, rows, cols)
-    )
-    fluid_next, void_fraction = spread(deposits, heat_field, halo_of(*edges), fluid_state)
-    back, void_fraction = lax.optimization_barrier((back, void_fraction))
+        back, slot_of, cells, radius, base, edges, (layers, rows, cols)
+    )
+    halo = halo_of(*edges)
     particle_next = fetch(box_owner, tiles, back, boxes, spots, base, warm)
+    fluid_next, void_fraction = spread(deposits, heat_field, halo, fluid_state)
     return (fluid_next, void_fraction, particle_next)
 
 

time: 120 us -> 113 us (0.942)
  blocking collectives: 10.5 us -> 18.4 us
  waiting for transfers between devices: 6.88 us -> 0.02 us
  starting transfers between devices: 33.5 us -> 27.6 us
  local copies, waits for them, and re-layouts: 4.18 us -> 1.71 us
    all_to_all x1, blocking collectives: 10.5 us -> 18.4 us  [shards(): lax.all_to_all(result, ('gx', 'gy'), split_axis=0, concat_axis=0, tiled=T...]
    all_to_all x1 -> x0, starting transfers between devices: 4.67 us -> none  [shards(): lax.all_to_all(result, ('gx', 'gy'), split_axis=0, concat_axis=0, tiled=T...]
    ppermute x8, waiting for transfers between devices: 4 us -> 0.02 us  [moved(): return lax.ppermute(value, axis, pairs)]
    pallas_call x1, Pallas kernels: 16.3 us -> 19.6 us  [see_and_deposit(): pl.pallas_call(functools.partial(fluid_kernel, chunk=512), out_shape=(jax...]
    all_to_all x1, waiting for transfers between devices: 2.88 us -> 0.01 us  [shards(): lax.all_to_all(outgoing, ('gx', 'gy'), split_axis=0, concat_axis=0, tiled...]
    slice x2 -> x1, local copies, waits for them, and re-layouts: 3.07 us -> 0.5 us  [shards(): fluid[:, :, :, 0].reshape(-1, BLOCK)]
    pallas_call x2, Pallas kernels: 31.8 us -> 29.5 us  [the longest x1 15.7 us: contact(): pl.pallas_call(contact_kernel, grid=(devices // step,), out_shape=jax.Sha...]
    pallas_call x1, Pallas kernels: 7.18 us -> 5.21 us  [heat_deposit(): pl.pallas_call(functools.partial(heat_kernel, chunk=1024, rows=rows), out...]
  transfers between devices with their start and end apart: 10 -> 9, of which waited for: 2 -> 0; matrix products, arithmetic and copies ran while one was open for 2% -> 1% of each run, Pallas kernels for 31% -> 23%
where the time goes in v3:
time: 113 us; the launch traced here: 111 us
  Pallas kernels  62.3 us (55%)
  starting transfers between devices  27.6 us (24%)
  blocking collectives  18.4 us (16%)
  local copies, waits for them, and re-layouts  1.71 us (2%)
    ppermute x8, starting transfers between devices, moved(): return lax.ppermute(value, axis, pairs)  21.6 us
    pallas_call x1, Pallas kernels, see_and_deposit(): pl.pallas_call(functools.partial(fluid_kernel, chunk=512), out_shape=(jax...  19.6 us
    all_to_all x1, blocking collectives, shards(): lax.all_to_all(result, ('gx', 'gy'), split_axis=0, concat_axis=0, tiled=T...  18.4 us
    pallas_call x1, Pallas kernels, contact(): pl.pallas_call(contact_kernel, grid=(devices // step,), out_shape=jax.Sha...  15.7 us
    pallas_call x1, Pallas kernels, place(): pl.pallas_call(place_kernel, out_shape=(jax.ShapeDtypeStruct((devices, 11...  13.8 us
    all_to_all x1, starting transfers between devices, shards(): lax.all_to_all(outgoing, ('gx', 'gy'), split_axis=0, concat_axis=0, tiled...  6.04 us
    pallas_call x1, Pallas kernels, fetch(): pl.pallas_call(fetch_kernel, out_shape=jax.ShapeDtypeStruct((7, particles...  5.94 us
    pallas_call x1, Pallas kernels, heat_deposit(): pl.pallas_call(functools.partial(heat_kernel, chunk=1024, rows=rows), out...  5.21 us
  transfers between devices with their start and end apart: 9, of which 0 were waited for; matrix products, arithmetic and copies ran while one was open for 1% of the time, Pallas kernels for 23%

profile of v3, /device:TPU:10, one launch (start us, length us, event | category | flops | bytes accessed | tf_op | source)
XLA Modules:
  0.0 110.9 jit_solution(3453270316373305119)
XLA Ops:
  0.7 13.8 %place_slots.1 = (f32[32,11,4,128]{3,2,1,0:T(4,128)}, s32[1,8192]{1,0:T(1,128)}, s32[1,8192]{1,0:T(1,128)}, s32[40,128]{1,0:T(8,128)}) custom-call(s32[32]{0:T(128)} %owner_ref.3, s32[1,8192]{1,0:T(1,128)} %bitcast.15, f32[3,8192]{1,0:T(4,128)} %pos_ref.1, f32[6,8192]{1,0:T(8,128)} %motion_ref.3, f32[1,8192]{1,0:T(1,128)} %bitcast.12, f32[1,8192]{1,0:T(1,128)} %bitcast.8), custom_call_target="tpu_custom_call" | custom-call | flops 3221225472 | bytes 1048576 | tf_op jit(solution)/shard_map/place_slots/pallas_call | solution.py:174
  14.5 0.1 copy.14
  14.7 1.9 %collective-permute-start.1 = (f32[4,32,128]{2,1,0:T(8,128)S(1)}, f32[4,32,128]{2,1,0:T(8,128)S(1)}, u32[]{:S(2)}, u32[]{:S(2)}) collective-permute-start(f32[4,32,128]{2,1,0:T(8,128)S(1)} %get-tuple-element.59), channel_id=1, source_target_pairs={{1,0},{2,1},{3,2},{4,3},{5,4},{6,5},{7,6},{9,8},{10,9},{11,10},{12... | collective-permute-start | bytes 196616 | tf_op jit(solution)/shard_map/ppermute | solution.py:609
  16.6 2.4 %collective-permute-start = (f32[4,32,128]{2,1,0:T(8,128)S(1)}, f32[4,32,128]{2,1,0:T(8,128)S(1)}, u32[]{:S(2)}, u32[]{:S(2)}) collective-permute-start(f32[4,32,128]{2,1,0:T(8,128)S(1)} %get-tuple-element.60), channel_id=1, source_target_pairs={{0,1},{1,2},{2,3},{3,4},{4,5},{5,6},{6,7},{8,9},{9,10},{10,11},{11... | collective-permute-start | bytes 196616 | tf_op jit(solution)/shard_map/ppermute | solution.py:609
  19.0 0.5 slice_reduce_fusion
  19.5 0.1 reshape_squeeze.6
  19.6 3.4 %collective-permute-start.2 = (f32[8,128]{1,0:T(8,128)S(1)}, f32[8,128]{1,0:T(8,128)S(1)}, u32[]{:S(2)}, u32[]{:S(2)}) collective-permute-start(f32[8,128]{1,0:T(8,128)S(1)} %reshape_squeeze.6), channel_id=1, source_target_pairs={{0,8},{8,16},{16,24},{1,9},{9,17},{17,25},{2,10},{10,18},{18,26},{... | collective-permute-start | bytes 12296 | tf_op jit(solution)/shard_map/ppermute | solution.py:609
  23.0 0.1 reshape_squeeze.7
  23.1 2.4 %collective-permute-start.3 = (f32[8,128]{1,0:T(8,128)S(1)}, f32[8,128]{1,0:T(8,128)S(1)}, u32[]{:S(2)}, u32[]{:S(2)}) collective-permute-start(f32[8,128]{1,0:T(8,128)S(1)} %reshape_squeeze.7), channel_id=1, source_target_pairs={{8,0},{16,8},{24,16},{9,1},{17,9},{25,17},{10,2},{18,10},{26,18},{... | collective-permute-start | bytes 12296 | tf_op jit(solution)/shard_map/ppermute | solution.py:609
  25.5 6.0 %all-to-all-start = ((f32[32,11,4,128]{3,2,1,0:T(4,128)}), f32[32,11,4,128]{3,2,1,0:T(4,128)S(1)}, u32[]{:S(2)}, u32[]{:S(2)}) async-start(f32[32,11,4,128]{3,2,1,0:T(4,128)} %get-tuple-element.30), calls=%async_computation | async-start | bytes 1441792 | tf_op jit(solution)/shard_map/all_to_all | solution.py:635
  31.6 0.0 collective-permute-done.2.x0_ref
  31.6 0.0 collective-permute-done.3.x1_ref
  31.6 0.0 collective-permute-done.1.y1_ref
  31.6 0.0 collective-permute-done.y0_ref
  31.7 19.6 %see_and_deposit.1 = (f32[8,8192]{1,0:T(8,128)S(1)}, f32[4,32,8,128]{3,2,1,0:T(8,128)S(1)}, f32[4,32,128]{2,1,0:T(8,128)S(1)}, f32[4,32,128]{2,1,0:T(8,128)S(1)}...) custom-call(f32[4,32,8,128]{3,2,1,0:T(8,128)S(1)} %copy-done, f32[4,32,128]{2,1,0:T(8,128)S(1)} %collective-permute-done.y0_ref, ...), custom_call_target="tpu_custom_call" | custom-call | flops 17179869184 | bytes 2097152 | tf_op jit(solution)/shard_map/see_and_deposit/pallas_call | solution.py:429
  51.2 0.0 copy-start.7
  51.3 0.0 copy-start.5
  51.3 0.0 copy-start.6
  51.3 0.0 copy-start.8
  51.3 0.0 all-to-all-done.slot_ref
  51.3 0.9 copy-done.10
  52.2 15.7 %contact_blocks.1 = f32[32,7,4,128]{3,2,1,0:T(4,128)} custom-call(f32[32,11,4,128]{3,2,1,0:T(4,128)} %copy-done.10, s32[128,128,128]{2,1,0:T(8,128)} %mask_ref.1), custom_call_target="tpu_custom_call" | custom-call | flops 134217728 | bytes 8388608 | tf_op jit(solution)/shard_map/contact_blocks/pallas_call | solution.py:283
  67.9 18.4 %all_to_all.10.back_ref = f32[32,7,4,128]{3,2,1,0:T(4,128)S(1)} all-to-all(f32[32,7,4,128]{3,2,1,0:T(4,128)} %contact_blocks.1), channel_id=1, replica_groups=mesh['gx'=4,'gy'=8] {'gx','gy'}, dimensions={0} | all-to-all | bytes 917504 | tf_op jit(solution)/shard_map/all_to_all | solution.py:648
  86.3 5.2 %heat_deposit.1 = (f32[1,8192]{1,0:T(1,128)S(1)}, f32[1,32,8,128]{3,2,1,0:T(8,128)S(1)}, f32[5,32,128]{2,1,0:T(8,128)S(1)}, f32[5,32,128]{2,1,0:T(8,128)S(1)}, f...) custom-call(f32[32,7,4,128]{3,2,1,0:T(4,128)S(1)} %all_to_all.10.back_ref, s32[1,8192]{1,0:T(1,128)S(1)} %copy-done.7, ...), custom_call_target="tpu_custom_call" | custom-call | flops 1073741824 | bytes 1048576 | tf_op jit(solution)/shard_map/heat_deposit/pallas_call | solution.py:497
  91.5 3.4 %collective-permute-start.6 = (f32[10,128]{1,0:T(8,128)S(1)}, f32[10,128]{1,0:T(8,128)S(1)}, u32[]{:S(2)}, u32[]{:S(2)}) collective-permute-start(f32[10,128]{1,0:T(8,128)S(1)} %get-tuple-element.50), channel_id=1, source_target_pairs={{0,8},{8,16},{16,24},{1,9},{9,17},{17,25},{2,10},{10,18},{18,26},{... | collective-permute-start | bytes 15368 | tf_op jit(solution)/shard_map/ppermute | solution.py:609
  94.9 2.4 %collective-permute-start.7 = (f32[10,128]{1,0:T(8,128)S(1)}, f32[10,128]{1,0:T(8,128)S(1)}, u32[]{:S(2)}, u32[]{:S(2)}) collective-permute-start(f32[10,128]{1,0:T(8,128)S(1)} %get-tuple-element.51), channel_id=1, source_target_pairs={{8,0},{16,8},{24,16},{9,1},{17,9},{25,17},{10,2},{18,10},{26,18},{... | collective-permute-start | bytes 15368 | tf_op jit(solution)/shard_map/ppermute | solution.py:609
  97.3 1.9 %collective-permute-start.4 = (f32[5,32,128]{2,1,0:T(8,128)S(1)}, f32[5,32,128]{2,1,0:T(8,128)S(1)}, u32[]{:S(2)}, u32[]{:S(2)}) collective-permute-start(f32[5,32,128]{2,1,0:T(8,128)S(1)} %get-tuple-element.48), channel_id=1, source_target_pairs={{0,1},{1,2},{2,3},{3,4},{4,5},{5,6},{6,7},{8,9},{9,10},{10,11},{11... | collective-permute-start | bytes 245768 | tf_op jit(solution)/shard_map/ppermute | solution.py:609
  99.3 3.6 %collective-permute-start.5 = (f32[5,32,128]{2,1,0:T(8,128)S(1)}, f32[5,32,128]{2,1,0:T(8,128)S(1)}, u32[]{:S(2)}, u32[]{:S(2)}) collective-permute-start(f32[5,32,128]{2,1,0:T(8,128)S(1)} %get-tuple-element.49), channel_id=1, source_target_pairs={{1,0},{2,1},{3,2},{4,3},{5,4},{6,5},{7,6},{9,8},{10,9},{11,10},{12... | collective-permute-start | bytes 245768 | tf_op jit(solution)/shard_map/ppermute | solution.py:609
  102.9 5.9 %fetch_slots.1 = f32[7,8192]{1,0:T(8,128)} custom-call(s32[32]{0:T(128)S(1)} %copy-done.6, s32[40,128]{1,0:T(8,128)S(1)} %copy-done.9, f32[32,7,4,128]{3,2,1,0:T(4,128)S(1)} %all_to_all.10.back_ref, s32[1,8192]{1,0:T(1,128)S(1)} %bitcast.16, s32[1,8192]{1,0:T(1,128)S(1)} %copy-done.8, f32[8,8192]{1,0:T(8,128)S(1)} %get-tuple-element.42.base_ref, ...), custom_call_target="tpu_custom_call" | custom-call | flops 2147483648 | bytes 1048576 | tf_op jit(solution)/shard_map/fetch_slots/pallas_call | solution.py:564
  108.9 0.0 collective-permute-done.6.x0_ref
  108.9 0.0 collective-permute-done.5.y1_ref
  108.9 2.0 %spread_fields.1 = (f32[4,32,8,128]{3,2,1,0:T(8,128)}, f32[32,8,128]{2,1,0:T(8,128)}) custom-call(f32[4,32,8,128]{3,2,1,0:T(8,128)S(1)} %get-tuple-element.39.dep_ref, f32[1,32,8,128]{3,2,1,0:T(8,128)S(1)} %get-tuple-element.47.heat_ref, f32[5,32,128]{2,1,0:T(8,128)S(1)} %collective-permute-done.4.y0_ref, f32[5,32,128]{2,1,0:T(8,128)S(1)} %collective-permute-done.5.y1_ref, ...), custom_call_target="tpu_custom_call" | custom-call | flops 2621440 | bytes 2097152 | tf_op jit(solution)/shard_map/spread_fields/pallas_call | solution.py:594
  (20 shorter events, 0.1 us)
Async XLA Ops:
  0.6 31.0 %copy-start.1 = (f32[6,8192]{1,0:T(8,128)S(1)}, f32[6,8192]{1,0:T(8,128)}, u32[]{:S(2)}) copy-start(f32[6,8192]{1,0:T(8,128)} %motion_ref.3) | copy-start | bytes 589828
  0.6 31.0 %copy-start.2 = (f32[8192]{0:T(1024)S(1)}, f32[8192]{0:T(1024)}, u32[]{:S(2)}) copy-start(f32[8192]{0:T(1024)} %param.13) | copy-start | bytes 98308
  0.7 31.0 %copy-start.4 = (f32[8192]{0:T(1024)S(1)}, f32[8192]{0:T(1024)}, u32[]{:S(2)}) copy-start(f32[8192]{0:T(1024)} %param.12) | copy-start | bytes 98308
  0.7 13.9 %copy-start = (f32[4,32,8,128]{3,2,1,0:T(8,128)S(1)}, f32[4,32,8,128]{3,2,1,0:T(8,128)}, u32[]{:S(2)}) copy-start(f32[4,32,8,128]{3,2,1,0:T(8,128)} %fluid_ref.3) | copy-start | bytes 1572868
  0.7 31.0 %copy-start.3 = (s32[8192]{0:T(1024)S(1)}, s32[8192]{0:T(1024)}, u32[]{:S(2)}) copy-start(s32[8192]{0:T(1024)} %param.14) | copy-start | bytes 98308
  14.7 16.9 %collective-permute-start.1 = (f32[4,32,128]{2,1,0:T(8,128)S(1)}, f32[4,32,128]{2,1,0:T(8,128)S(1)}, u32[]{:S(2)}, u32[]{:S(2)}) collective-permute-start(f32[4,32,128]{2,1,0:T(8,128)S(1)} %get-tuple-element.59), channel_id=1, source_target_pairs={{1,0},{2,1},{3,2},{4,3},{5,4},{6,5},{7,6},{9,8},{10,9},{11,10},{12... | collective-permute-start | bytes 196616 | tf_op jit(solution)/shard_map/ppermute | solution.py:609
  16.6 15.0 %collective-permute-start = (f32[4,32,128]{2,1,0:T(8,128)S(1)}, f32[4,32,128]{2,1,0:T(8,128)S(1)}, u32[]{:S(2)}, u32[]{:S(2)}) collective-permute-start(f32[4,32,128]{2,1,0:T(8,128)S(1)} %get-tuple-element.60), channel_id=1, source_target_pairs={{0,1},{1,2},{2,3},{3,4},{4,5},{5,6},{6,7},{8,9},{9,10},{10,11},{11... | collective-permute-start | bytes 196616 | tf_op jit(solution)/shard_map/ppermute | solution.py:609
  19.6 12.0 %collective-permute-start.2 = (f32[8,128]{1,0:T(8,128)S(1)}, f32[8,128]{1,0:T(8,128)S(1)}, u32[]{:S(2)}, u32[]{:S(2)}) collective-permute-start(f32[8,128]{1,0:T(8,128)S(1)} %reshape_squeeze.6), channel_id=1, source_target_pairs={{0,8},{8,16},{16,24},{1,9},{9,17},{17,25},{2,10},{10,18},{18,26},{... | collective-permute-start | bytes 12296 | tf_op jit(solution)/shard_map/ppermute | solution.py:609
  23.1 8.5 %collective-permute-start.3 = (f32[8,128]{1,0:T(8,128)S(1)}, f32[8,128]{1,0:T(8,128)S(1)}, u32[]{:S(2)}, u32[]{:S(2)}) collective-permute-start(f32[8,128]{1,0:T(8,128)S(1)} %reshape_squeeze.7), channel_id=1, source_target_pairs={{8,0},{16,8},{24,16},{9,1},{17,9},{25,17},{10,2},{18,10},{26,18},{... | collective-permute-start | bytes 12296 | tf_op jit(solution)/shard_map/ppermute | solution.py:609
  25.5 25.8 %all-to-all-start = ((f32[32,11,4,128]{3,2,1,0:T(4,128)}), f32[32,11,4,128]{3,2,1,0:T(4,128)S(1)}, u32[]{:S(2)}, u32[]{:S(2)}) async-start(f32[32,11,4,128]{3,2,1,0:T(4,128)} %get-tuple-element.30), calls=%async_computation | async-start | bytes 1441792 | tf_op jit(solution)/shard_map/all_to_all | solution.py:635
  51.2 35.0 %copy-start.7 = (s32[1,8192]{1,0:T(1,128)S(1)}, s32[1,8192]{1,0:T(1,128)}, u32[]{:S(2)}) copy-start(s32[1,8192]{1,0:T(1,128)} %get-tuple-element.41.slot_ref) | copy-start | bytes 98308
  51.3 51.7 %copy-start.5 = (s32[8192,1]{0,1:T(1,128)S(1)}, s32[8192,1]{0,1:T(1,128)}, u32[]{:S(2)}) copy-start(s32[8192,1]{0,1:T(1,128)} %param.15) | copy-start | bytes 98308
  51.3 51.7 %copy-start.6 = (s32[32]{0:T(128)S(1)}, s32[32]{0:T(128)}, u32[]{:S(2)}) copy-start(s32[32]{0:T(128)} %owner_ref.3) | copy-start | bytes 388
  51.3 51.7 %copy-start.8 = (s32[1,8192]{1,0:T(1,128)S(1)}, s32[1,8192]{1,0:T(1,128)}, u32[]{:S(2)}) copy-start(s32[1,8192]{1,0:T(1,128)} %get-tuple-element.55.spot_ref) | copy-start | bytes 98308
  51.3 51.7 %copy-start.9 = (s32[40,128]{1,0:T(8,128)S(1)}, s32[40,128]{1,0:T(8,128)}, u32[]{:S(2)}) copy-start(s32[40,128]{1,0:T(8,128)} %get-tuple-element.54.tile_ref) | copy-start | bytes 61444
  51.3 0.9 copy-start.10
  91.5 17.4 %collective-permute-start.6 = (f32[10,128]{1,0:T(8,128)S(1)}, f32[10,128]{1,0:T(8,128)S(1)}, u32[]{:S(2)}, u32[]{:S(2)}) collective-permute-start(f32[10,128]{1,0:T(8,128)S(1)} %get-tuple-element.50), channel_id=1, source_target_pairs={{0,8},{8,16},{16,24},{1,9},{9,17},{17,25},{2,10},{10,18},{18,26},{... | collective-permute-start | bytes 15368 | tf_op jit(solution)/shard_map/ppermute | solution.py:609
  94.9 14.0 %collective-permute-start.7 = (f32[10,128]{1,0:T(8,128)S(1)}, f32[10,128]{1,0:T(8,128)S(1)}, u32[]{:S(2)}, u32[]{:S(2)}) collective-permute-start(f32[10,128]{1,0:T(8,128)S(1)} %get-tuple-element.51), channel_id=1, source_target_pairs={{8,0},{16,8},{24,16},{9,1},{17,9},{25,17},{10,2},{18,10},{26,18},{... | collective-permute-start | bytes 15368 | tf_op jit(solution)/shard_map/ppermute | solution.py:609
  97.3 11.6 %collective-permute-start.4 = (f32[5,32,128]{2,1,0:T(8,128)S(1)}, f32[5,32,128]{2,1,0:T(8,128)S(1)}, u32[]{:S(2)}, u32[]{:S(2)}) collective-permute-start(f32[5,32,128]{2,1,0:T(8,128)S(1)} %get-tuple-element.48), channel_id=1, source_target_pairs={{0,1},{1,2},{2,3},{3,4},{4,5},{5,6},{6,7},{8,9},{9,10},{10,11},{11... | collective-permute-start | bytes 245768 | tf_op jit(solution)/shard_map/ppermute | solution.py:609
  99.3 9.6 %collective-permute-start.5 = (f32[5,32,128]{2,1,0:T(8,128)S(1)}, f32[5,32,128]{2,1,0:T(8,128)S(1)}, u32[]{:S(2)}, u32[]{:S(2)}) collective-permute-start(f32[5,32,128]{2,1,0:T(8,128)S(1)} %get-tuple-element.49), channel_id=1, source_target_pairs={{1,0},{2,1},{3,2},{4,3},{5,4},{6,5},{7,6},{9,8},{10,9},{11,10},{12... | collective-permute-start | bytes 245768 | tf_op jit(solution)/shard_map/ppermute | solution.py:609

commit v4 on v2

--- a/solution.py
+++ b/solution.py
@@ -23,8 +23,8 @@
 F32 = jnp.float32
 BF16 = jnp.bfloat16
 VMEM = pltpu.VMEM
+NN = (((1,), (0,)), ((), ()))
 NT = (((1,), (1,)), ((), ()))
-NN = (((1,), (0,)), ((), ()))
 
 
 def split(value):
@@ -35,6 +35,16 @@
 def hot(count, row):
     places = lax.broadcasted_iota(jnp.int32, (count, row.shape[1]), 0)
     return jnp.where(places == row, 1.0, 0.0).astype(BF16)
+
+
+def hot_columns(count, row):
+    n = row.shape[1] // BLOCK
+    tiles = [row[:, a * BLOCK : (a + 1) * BLOCK] for a in range(n)]
+    turned = jnp.transpose(jnp.concatenate(tiles * (8 // n), axis=0).astype(F32))
+    places = lax.broadcasted_iota(jnp.int32, (BLOCK, count), 1).astype(F32)
+    return jnp.concatenate(
+        [jnp.where(places == turned[:, a : a + 1], 1.0, 0.0).astype(BF16) for a in range(n)], axis=0
+    )
 
 
 def invert(owner_ref, box_of):
@@ -119,14 +129,17 @@
         first = jnp.concatenate([push, spin, heat, jnp.ones((1, CHUNK), F32)], axis=0)
         second = jnp.concatenate([pos, radius_ref[:, here]], axis=0)
         first = jnp.concatenate(split(first), axis=0)
-        second = jnp.concatenate(split(second), axis=0)
+        second = jnp.concatenate(split(second) * 2, axis=0)
+        lower = lax.broadcasted_iota(jnp.int32, (16, 1), 0) < 8
         box16 = jnp.broadcast_to(boxes, (16, CHUNK)).astype(F32).astype(BF16)
         first_parts = []
         second_parts = []
         for o in range(devices):
             mine = box16 == box_of[o].astype(F32).astype(BF16)
             first_parts.append(jnp.where(mine, first, jnp.zeros_like(first)))
-            second_parts.append(jnp.where(mine[0:8], second, jnp.zeros_like(second)))
+            if o % 2 == 0:
+                either = jnp.where(lower, box_of[o].astype(F32), box_of[o + 1].astype(F32)).astype(BF16)
+                second_parts.append(jnp.where(box16 == either, second, jnp.zeros_like(second)))
         parts = jnp.concatenate(first_parts + second_parts, axis=0)
 
         def window(w, _):
@@ -211,55 +224,93 @@
     for_d = jnp.concatenate([cross_d, cross_d, ones_d, jnp.where(row < 3, third, 0.0)], axis=0)
     for_r = jnp.concatenate([cross_r, cross_r, ones_r, jnp.where((row >= 3) & (row < 6), third, 0.0)], axis=0)
     right = jnp.concatenate([for_d, for_r], axis=1)
-    return left.astype(BF16), right.astype(BF16)
-
-
-def contact_kernel(slot_ref, mask_ref, out_ref, heat_ref):
+    return left, right.astype(BF16)
+
+
+def contact_kernel(slot_ref, mask_ref, out_ref):
     homes, rows, _ = slot_ref.shape
     layers = rows // 12
-    sign = lax.broadcasted_iota(jnp.int32, (8, 1), 0)
-    sign = jnp.where((sign >= 3) & (sign < 6), 1.0, -1.0)
-    for s in range(homes):
-        for q in range(layers):
-            mixed = slot_ref[s, 8 * q : 8 * q + 8, :]
-            near = slot_ref[s, 8 * layers + 4 * q : 8 * layers + 4 * q + 4, :]
-            left, right = pair_terms(near)
-            pair = lax.dot_general(left, right, (((0,), (0,)), ((), ())), preferred_element_type=F32)
-            reach = pair[:, BLOCK:]
+    blocks = [(s, q) for s in range(homes) for q in range(layers)]
+    row = lax.broadcasted_iota(jnp.int32, (8, 1), 0)
+    sign = jnp.where((row >= 3) & (row < 6), 1.0, -1.0)
+    lane = lax.broadcasted_iota(jnp.int32, (BLOCK, BLOCK), 1) // 16
+
+    def pairs_of(group):
+        pairs = []
+        for first in range(0, 8, 4):
+            lefts = []
+            rights = []
+            for g, (s, q) in enumerate(group[first : first + 4]):
+                left, right = pair_terms(slot_ref[s, 8 * layers + 4 * q : 8 * layers + 4 * q + 4, :])
+                lefts.append(left)
+                spots = [jnp.zeros_like(right)] * 4
+                spots[g] = right
+                rights.append(jnp.concatenate(spots, axis=0))
+            turned = jnp.transpose(jnp.concatenate(lefts, axis=0)).astype(BF16)
+            pairs.append(
+                lax.dot_general(turned, jnp.concatenate(rights, axis=1), NN, preferred_element_type=F32)
+            )
+        return pairs
+
+    def sums_of(number, group, pairs):
+        stacked = []
+        for s, q in group:
+            mine = slot_ref[s, 8 * q : 8 * q + 8, :]
+            high = mine.astype(BF16).astype(F32)
+            stacked += [high, mine - high]
+        columns = jnp.transpose(jnp.concatenate(stacked, axis=0)).astype(BF16)
+        highs = []
+        lows = []
+        right = []
+        for b in range(8):
+            at = 2 * BLOCK * (b % 4)
+            pair = pairs[b // 4]
+            reach = pair[:, at + BLOCK : at + 2 * BLOCK]
             inverse = pl.reciprocal(reach, approx=True)
             inverse = inverse * (2.0 - reach * inverse)
-            weight = mask_ref[s * layers + q].astype(F32) * jnp.exp(pair[:, :BLOCK] * inverse)
-            weight_high, weight_low = split(weight)
-            mixed_high, mixed_low = split(mixed)
-            both = jnp.concatenate([mixed_high, mixed_low], axis=0)
-            sums = lax.dot_general(both, weight_high, NT, preferred_element_type=F32)
-            sums = sums + lax.dot_general(both, weight_low, NT, preferred_element_type=F32)
-            sums = sums[0:8] + sums[8:16]
-            result = mixed * sums[7:8] + sign * sums
-            out_ref[s, 6 * q : 6 * q + 6, :] = result[0:6]
-            heat_ref[s, q : q + 1, :] = result[6:7]
+            weight = mask_ref[8 * number + b].astype(F32) * jnp.exp(pair[:, at : at + BLOCK] * inverse)
+            high, low = split(weight)
+            highs.append(high)
+            lows.append(low)
+            right.append(jnp.where(lane == b, columns, jnp.zeros_like(columns)))
+        return lax.dot_general(
+            jnp.concatenate(highs + lows, axis=1), jnp.concatenate(right + right, axis=0), NN,
+            preferred_element_type=F32,
+        )
+
+    def finish(group, sums):
+        sums = jnp.transpose(sums)
+        for b, (s, q) in enumerate(group):
+            total = sums[16 * b : 16 * b + 8] + sums[16 * b + 8 : 16 * b + 16]
+            out_ref[s, 8 * q : 8 * q + 8, :] = slot_ref[s, 8 * q : 8 * q + 8, :] * total[7:8] + sign * total
+
+    groups = [blocks[i : i + 8] for i in range(0, len(blocks), 8)]
+    pairs = pairs_of(groups[0])
+    before = None
+    for number, group in enumerate(groups):
+        later = pairs_of(groups[number + 1]) if number + 1 < len(groups) else None
+        sums = sums_of(number, group, pairs)
+        if before is not None:
+            finish(*before)
+        before = (group, sums)
+        pairs = later
+    finish(*before)
 
 
 def contact(arrived, mask):
     devices, rows, _ = arrived.shape
     layers = rows // 12
     blocks = mask.shape[0]
-    step = 2 if layers > 1 else 8
+    step = 32 // layers
     return pl.pallas_call(
         contact_kernel,
         grid=(devices // step,),
-        out_shape=(
-            jax.ShapeDtypeStruct((devices, 6 * layers, BLOCK), F32),
-            jax.ShapeDtypeStruct((devices, layers, BLOCK), F32),
-        ),
+        out_shape=jax.ShapeDtypeStruct((devices, 8 * layers, BLOCK), F32),
         in_specs=[
             pl.BlockSpec((step, rows, BLOCK), lambda h: (h, 0, 0)),
             pl.BlockSpec((step * layers, BLOCK, BLOCK), lambda h: (h, 0, 0)),
         ],
-        out_specs=(
-            pl.BlockSpec((step, 6 * layers, BLOCK), lambda h: (h, 0, 0)),
-            pl.BlockSpec((step, layers, BLOCK), lambda h: (h, 0, 0)),
-        ),
+        out_specs=pl.BlockSpec((step, 8 * layers, BLOCK), lambda h: (h, 0, 0)),
         compiler_params=pltpu.CompilerParams(vmem_limit_bytes=60 << 20),
         cost_estimate=pl.CostEstimate(
             flops=64 * blocks * BLOCK * BLOCK, bytes_accessed=blocks * BLOCK * BLOCK * 4, transcendentals=0
@@ -334,24 +385,18 @@
     return [jnp.sum(jnp.where(mine, value, 0.0), axis=0, keepdims=True) for value in found]
 
 
-def fluid_kernel(
+def look_kernel(
     fluid_ref, y0_ref, y1_ref, x0_ref, x1_ref, cell_ref, motion_ref, radius_ref, temp_ref,
-    base_ref, dep_ref, dy0_ref, dy1_ref, dx0_ref, dx1_ref,
-    table, rows_scratch, acc, *, chunk
+    base_ref, term_ref, table, *, chunk
 ):
     fields, layers, rows, cols = fluid_ref.shape
-    half = layers * rows // 2
-    wide = 2 * cols
     particles = cell_ref.shape[1]
     for k in range(fields):
         table[k] = smooth_field(fluid_ref, y0_ref, y1_ref, x0_ref, x1_ref, k)
-    acc[...] = jnp.zeros_like(acc)
 
     def step(i, _):
         here = pl.ds(pl.multiple_of(i * chunk, chunk), chunk)
         cells = cell_ref[:, here]
-        hot_low = hot(wide, cells % wide)
-        hot_high = hot(half, cells // wide)
         seen = [[] for _ in range(fields)]
         for s in range(chunk // BLOCK):
             wanted = jnp.broadcast_to(cells[:, s * BLOCK : (s + 1) * BLOCK], (8, BLOCK))
@@ -371,13 +416,48 @@
         warmed = temp + TIME_STEP * HEAT_TRANSFER * (seen[3] - temp)
         base_ref[:, here] = jnp.concatenate([moved, motion[3:6], warmed, seen[3]], axis=0)
         volume = radius * radius * radius
-        terms = jnp.concatenate([volume, -volume * drag], axis=0)
-        high, low = split(terms)
-        parts = []
-        for piece in (high, low):
-            parts.append(jnp.concatenate([hot_high * piece[k : k + 1] for k in range(4)], axis=0))
-        total = lax.dot_general(parts[0], hot_low, NT, preferred_element_type=F32)
-        acc[...] += total + lax.dot_general(parts[1], hot_low, NT, preferred_element_type=F32)
+        term_ref[:, here] = jnp.concatenate([volume, -volume * drag], axis=0)
+        return 0
+
+    lax.fori_loop(0, particles // chunk, step, 0)
+
+
+def look_up(fluid, halo, cells, motion, radius, temp):
+    particles = cells.shape[1]
+    vmem = pl.BlockSpec(memory_space=VMEM)
+    return pl.pallas_call(
+        functools.partial(look_kernel, chunk=512),
+        out_shape=(
+            jax.ShapeDtypeStruct((8, particles), F32),
+            jax.ShapeDtypeStruct((4, particles), F32),
+        ),
+        in_specs=[vmem] * 9,
+        out_specs=(vmem,) * 2,
+        scratch_shapes=[VMEM(fluid.shape, F32)],
+        compiler_params=pltpu.CompilerParams(vmem_limit_bytes=40 << 20),
+        cost_estimate=pl.CostEstimate(flops=1 << 33, bytes_accessed=2 << 20, transcendentals=0),
+        name="look_up",
+    )(fluid, *halo, cells, motion, radius, temp)
+
+
+def deposit_kernel(
+    cell_ref, term_ref, dep_ref, dy0_ref, dy1_ref, dx0_ref, dx1_ref, rows_scratch, acc, *, chunk
+):
+    fields, layers, rows, cols = dep_ref.shape
+    half = layers * rows // 2
+    wide = 2 * cols
+    particles = cell_ref.shape[1]
+    acc[...] = jnp.zeros_like(acc)
+
+    def step(i, _):
+        here = pl.ds(pl.multiple_of(i * chunk, chunk), chunk)
+        cells = cell_ref[:, here]
+        hot_low = hot(wide, cells % wide)
+        hot_high = hot(half, cells // wide)
+        high, low = split(term_ref[:, here])
+        parts = [hot_high * piece[k : k + 1] for piece in (high, low) for k in range(fields)]
+        total = lax.dot_general(jnp.concatenate(parts, axis=0), hot_low, NT, preferred_element_type=F32)
+        acc[...] += total[: fields * half] + total[fields * half :]
         return 0
 
     lax.fori_loop(0, particles // chunk, step, 0)
@@ -393,29 +473,26 @@
     return (y_edge, y_edge, x_edge, x_edge)
 
 
-def see_and_deposit(fluid, halo, cells, motion, radius, temp):
-    fields, layers, rows, cols = fluid.shape
+def deposit(cells, terms, grid):
+    layers, rows, cols = grid
+    fields = terms.shape[0]
     particles = cells.shape[1]
     vmem = pl.BlockSpec(memory_space=VMEM)
     return pl.pallas_call(
-        functools.partial(fluid_kernel, chunk=512),
-        out_shape=(
-            jax.ShapeDtypeStruct((8, particles), F32),
-            jax.ShapeDtypeStruct(fluid.shape, F32),
-        ) + edge_shapes(fields, layers, rows, cols),
-        in_specs=[vmem] * 9,
-        out_specs=(vmem,) * 6,
+        functools.partial(deposit_kernel, chunk=1024),
+        out_shape=(jax.ShapeDtypeStruct((fields,) + grid, F32),) + edge_shapes(fields, layers, rows, cols),
+        in_specs=[vmem] * 2,
+        out_specs=(vmem,) * 5,
         scratch_shapes=[
-            VMEM(fluid.shape, F32),
             VMEM((layers * rows, cols), F32),
             VMEM((fields * layers * rows // 2, 2 * cols), F32),
         ],
         compiler_params=pltpu.CompilerParams(vmem_limit_bytes=40 << 20),
         cost_estimate=pl.CostEstimate(
-            flops=16 * fields * layers * rows * cols * particles, bytes_accessed=2 << 20, transcendentals=0
+            flops=4 * fields * layers * rows * cols * particles, bytes_accessed=2 << 20, transcendentals=0
         ),
-        name="see_and_deposit",
-    )(fluid, *halo, cells, motion, radius, temp)
+        name="deposit_fields",
+    )(cells, terms)
 
 
 def heat_kernel(
@@ -423,11 +500,13 @@
     next_ref, dep_ref, dy0_ref, dy1_ref, dx0_ref, dx1_ref,
     table, acc, rows_scratch, *, chunk, rows
 ):
-    devices, layers, _ = back_ref.shape
+    devices, tall, _ = back_ref.shape
+    layers = tall // 8
     particles = slot_ref.shape[1]
     half, wide = acc.shape
     for o in range(devices):
-        table[o * layers : (o + 1) * layers, :] = back_ref[o]
+        for q in range(layers):
+            table[o * layers + q : o * layers + q + 1, :] = back_ref[o, 8 * q + 6 : 8 * q + 7, :]
     acc[...] = jnp.zeros_like(acc)
 
     def step(i, _):
@@ -444,10 +523,10 @@
         radius = radius_ref[:, here]
         high, low = split(radius * radius * radius * (total - base[1:2]))
         cells = cell_ref[:, here]
-        hot_low = hot(wide, cells % wide)
+        hot_low = hot_columns(wide, cells % wide)
         hot_high = hot(half, cells // wide)
-        added = lax.dot_general(hot_high * high, hot_low, NT, preferred_element_type=F32)
-        acc[...] += added + lax.dot_general(hot_high * low, hot_low, NT, preferred_element_type=F32)
+        added = lax.dot_general(hot_high * high, hot_low, NN, preferred_element_type=F32)
+        acc[...] += added + lax.dot_general(hot_high * low, hot_low, NN, preferred_element_type=F32)
         return 0
 
     lax.fori_loop(0, particles // chunk, step, 0)
@@ -474,7 +553,7 @@
         in_specs=[vmem] * 9,
         out_specs=(vmem,) * 6,
         scratch_shapes=[
-            VMEM((devices * back.shape[1], BLOCK), F32),
+            VMEM((devices * back.shape[1] // 8, BLOCK), F32),
             VMEM((half, 2 * cols), F32),
             VMEM((layers * rows, cols), F32),
         ],
@@ -490,14 +569,12 @@
     owner_ref, tile_ref, back_ref, box_ref, spot_ref, base_ref, warm_ref, next_ref, box_of, table, wanted
 ):
     devices, tall, _ = back_ref.shape
-    layers = tall // 6
+    layers = tall // 8
     particles = box_ref.shape[1]
     invert(owner_ref, box_of)
-    blank = jnp.zeros((2, BLOCK), F32)
     for o in range(devices):
         for q in range(layers):
-            piece = jnp.concatenate([back_ref[o, 6 * q : 6 * q + 6, :], blank], axis=0)
-            high, low = split(piece)
+            high, low = split(back_ref[o, 8 * q : 8 * q + 8, :])
             table[o, q] = jnp.concatenate([high, low], axis=0)
         for q in range(layers, layers + 3):
             table[o, q] = jnp.zeros((16, BLOCK), BF16)
@@ -530,8 +607,8 @@
 
 def fetch(box_owner, tiles, back, boxes, spots, base, warm):
     devices, tall, _ = back.shape
+    layers = tall // 8
     particles = boxes.shape[1]
-    layers = tall // 6
     vmem = pl.BlockSpec(memory_space=VMEM)
     smem = pl.BlockSpec(memory_space=pltpu.SMEM)
     return pl.pallas_call(
@@ -607,25 +684,26 @@
     )
     arrived = lax.all_to_all(outgoing, ("gx", "gy"), split_axis=0, concat_axis=0, tiled=True)
 
+    spots, fluid = lax.optimization_barrier((spots, fluid_state))
     fluid_halo = halo_of(
-        fluid_state[:, :, 0, :],
-        fluid_state[:, :, rows - 1, :],
-        fluid_state[:, :, :, 0].reshape(-1, BLOCK),
-        fluid_state[:, :, :, cols - 1].reshape(-1, BLOCK),
+        fluid[:, :, 0, :],
+        fluid[:, :, rows - 1, :],
+        fluid[:, :, :, 0].reshape(-1, BLOCK),
+        fluid[:, :, :, cols - 1].reshape(-1, BLOCK),
     )
-    seen = see_and_deposit(fluid_state, fluid_halo, cells, particle_motion, radius, temp)
-    arrived, base, deposits, *edges = lax.optimization_barrier((arrived,) + tuple(seen))
-
-    result, heat = contact(arrived, contact_mask)
-    heat_back = lax.all_to_all(heat, ("gx", "gy"), split_axis=0, concat_axis=0, tiled=True)
+    base, terms = look_up(fluid_state, fluid_halo, cells, particle_motion, radius, temp)
+    arrived, base, terms = lax.optimization_barrier((arrived, base, terms))
+
+    result = contact(arrived, contact_mask)
+    result, terms = lax.optimization_barrier((result, terms))
+    deposits, *edges = deposit(cells, terms, (layers, rows, cols))
     back = lax.all_to_all(result, ("gx", "gy"), split_axis=0, concat_axis=0, tiled=True)
-
     warm, heat_field, *edges = heat_deposit(
-        heat_back, slot_of, cells, radius, base, edges, (layers, rows, cols)
+        back, slot_of, cells, radius, base, edges, (layers, rows, cols)
     )
-    fluid_next, void_fraction = spread(deposits, heat_field, halo_of(*edges), fluid_state)
-    back, void_fraction = lax.optimization_barrier((back, void_fraction))
+    halo = halo_of(*edges)
     particle_next = fetch(box_owner, tiles, back, boxes, spots, base, warm)
+    fluid_next, void_fraction = spread(deposits, heat_field, halo, fluid_state)
     return (fluid_next, void_fraction, particle_next)
 
 

time: 120 us -> 103 us (0.86)
  Pallas kernels: 63 us -> 51 us
  blocking collectives: 10.5 us -> 0 us
  waiting for transfers between devices: 6.88 us -> 11.5 us
  starting transfers between devices: 33.5 us -> 36.6 us
  local copies, waits for them, and re-layouts: 4.18 us -> 1.71 us
    all_to_all x1 -> x0, blocking collectives: 10.5 us -> none  [shards(): lax.all_to_all(heat, ('gx', 'gy'), split_axis=0, concat_axis=0, tiled=True)]
    pallas_call x2 -> x3, Pallas kernels: 36.4 us -> 26.7 us  [the longest x1 11.3 us: look_up(): pl.pallas_call(functools.partial(look_kernel, chunk=512), out_shape=(jax....]
    all_to_all x1, waiting for transfers between devices: 0.01 us -> 7.55 us  [shards(): lax.all_to_all(result, ('gx', 'gy'), split_axis=0, concat_axis=0, tiled=T...]
    all_to_all x1, starting transfers between devices: 4.67 us -> 9.05 us  [shards(): lax.all_to_all(result, ('gx', 'gy'), split_axis=0, concat_axis=0, tiled=T...]
    all_to_all x1, waiting for transfers between devices: 2.88 us -> 0.01 us  [shards(): lax.all_to_all(outgoing, ('gx', 'gy'), split_axis=0, concat_axis=0, tiled...]
    slice x2 -> x1, local copies, waits for them, and re-layouts: 3.07 us -> 0.5 us  [shards(): fluid[:, :, :, 0].reshape(-1, BLOCK)]
    pallas_call x1, Pallas kernels: 7.18 us -> 5.24 us  [heat_deposit(): pl.pallas_call(functools.partial(heat_kernel, chunk=1024, rows=rows), out...]
    ppermute x8, starting transfers between devices: 22.8 us -> 21.6 us  [moved(): return lax.ppermute(value, axis, pairs)]
  transfers between devices with their start and end apart: 10 -> 10, of which waited for: 2 -> 2; matrix products, arithmetic and copies ran while one was open for 2% -> 1% of each run, Pallas kernels for 31% -> 23%
where the time goes in v4:
time: 103 us; the launch traced here: 102 us
  Pallas kernels  51 us (50%)
  starting transfers between devices  36.6 us (36%)
  waiting for transfers between devices  11.5 us (11%)
  local copies, waits for them, and re-layouts  1.71 us (2%)
    ppermute x8, starting transfers between devices, moved(): return lax.ppermute(value, axis, pairs)  21.6 us
    pallas_call x1, Pallas kernels, place(): pl.pallas_call(place_kernel, out_shape=(jax.ShapeDtypeStruct((devices, 12...  11.3 us
    pallas_call x1, Pallas kernels, look_up(): pl.pallas_call(functools.partial(look_kernel, chunk=512), out_shape=(jax....  11.3 us
    pallas_call x1, Pallas kernels, contact(): pl.pallas_call(contact_kernel, grid=(devices // step,), out_shape=jax.Sha...  9.17 us
    all_to_all x1, starting transfers between devices, shards(): lax.all_to_all(result, ('gx', 'gy'), split_axis=0, concat_axis=0, tiled=T...  9.05 us
    all_to_all x1, waiting for transfers between devices, shards(): lax.all_to_all(result, ('gx', 'gy'), split_axis=0, concat_axis=0, tiled=T...  7.55 us
    pallas_call x1, Pallas kernels, deposit(): pl.pallas_call(functools.partial(deposit_kernel, chunk=1024), out_shape=(...  6.27 us
    all_to_all x1, starting transfers between devices, shards(): lax.all_to_all(outgoing, ('gx', 'gy'), split_axis=0, concat_axis=0, tiled...  6.01 us
  transfers between devices with their start and end apart: 10, of which 2 were waited for; matrix products, arithmetic and copies ran while one was open for 1% of the time, Pallas kernels for 23%

profile of v4, /device:TPU:10, one launch (start us, length us, event | category | flops | bytes accessed | tf_op | source)
XLA Modules:
  0.0 101.8 jit_solution(10764124966816948042)
XLA Ops:
  0.7 11.3 %place_slots.1 = (f32[32,48,128]{2,1,0:T(8,128)}, s32[1,8192]{1,0:T(1,128)}, s32[1,8192]{1,0:T(1,128)}, s32[40,128]{1,0:T(8,128)}) custom-call(s32[32]{0:T(128)} %owner_ref.3, s32[1,8192]{1,0:T(1,128)} %bitcast.16, f32[3,8192]{1,0:T(4,128)} %pos_ref.1, f32[6,8192]{1,0:T(8,128)} %motion_ref.3, f32[1,8192]{1,0:T(1,128)} %bitcast.13, f32[1,8192]{1,0:T(1,128)} %bitcast.8), custom_call_target="tpu_custom_call" | custom-call | flops 3221225472 | bytes 1048576 | tf_op jit(solution)/shard_map/place_slots/pallas_call | solution.py:179
  12.0 6.0 %all-to-all-start = ((f32[32,48,128]{2,1,0:T(8,128)}), f32[32,48,128]{2,1,0:T(8,128)S(1)}, u32[]{:S(2)}, u32[]{:S(2)}) async-start(f32[32,48,128]{2,1,0:T(8,128)} %get-tuple-element.29), calls=%async_computation | async-start | bytes 1572864 | tf_op jit(solution)/shard_map/all_to_all | solution.py:685
  18.1 0.1 copy.14
  18.2 2.2 %collective-permute-start.1 = (f32[4,32,128]{2,1,0:T(8,128)S(1)}, f32[4,32,128]{2,1,0:T(8,128)S(1)}, u32[]{:S(2)}, u32[]{:S(2)}) collective-permute-start(f32[4,32,128]{2,1,0:T(8,128)S(1)} %get-tuple-element.57), channel_id=1, source_target_pairs={{1,0},{2,1},{3,2},{4,3},{5,4},{6,5},{7,6},{9,8},{10,9},{11,10},{12... | collective-permute-start | bytes 196616 | tf_op jit(solution)/shard_map/ppermute | solution.py:659
  20.4 2.1 %collective-permute-start = (f32[4,32,128]{2,1,0:T(8,128)S(1)}, f32[4,32,128]{2,1,0:T(8,128)S(1)}, u32[]{:S(2)}, u32[]{:S(2)}) collective-permute-start(f32[4,32,128]{2,1,0:T(8,128)S(1)} %get-tuple-element.58), channel_id=1, source_target_pairs={{0,1},{1,2},{2,3},{3,4},{4,5},{5,6},{6,7},{8,9},{9,10},{10,11},{11... | collective-permute-start | bytes 196616 | tf_op jit(solution)/shard_map/ppermute | solution.py:659
  22.5 0.5 slice_reduce_fusion
  23.0 0.1 reshape_squeeze.6
  23.1 3.4 %collective-permute-start.2 = (f32[8,128]{1,0:T(8,128)S(1)}, f32[8,128]{1,0:T(8,128)S(1)}, u32[]{:S(2)}, u32[]{:S(2)}) collective-permute-start(f32[8,128]{1,0:T(8,128)S(1)} %reshape_squeeze.6), channel_id=1, source_target_pairs={{0,8},{8,16},{16,24},{1,9},{9,17},{17,25},{2,10},{10,18},{18,26},{... | collective-permute-start | bytes 12296 | tf_op jit(solution)/shard_map/ppermute | solution.py:659
  26.5 0.1 reshape_squeeze.7
  26.6 2.5 %collective-permute-start.3 = (f32[8,128]{1,0:T(8,128)S(1)}, f32[8,128]{1,0:T(8,128)S(1)}, u32[]{:S(2)}, u32[]{:S(2)}) collective-permute-start(f32[8,128]{1,0:T(8,128)S(1)} %reshape_squeeze.7), channel_id=1, source_target_pairs={{8,0},{16,8},{24,16},{9,1},{17,9},{25,17},{10,2},{18,10},{26,18},{... | collective-permute-start | bytes 12296 | tf_op jit(solution)/shard_map/ppermute | solution.py:659
  29.1 0.0 collective-permute-done.2.x0_ref
  29.1 3.9 %collective-permute-done.3.x1_ref = f32[8,128]{1,0:T(8,128)S(1)} collective-permute-done((f32[8,128]{1,0:T(8,128)S(1)}, f32[8,128]{1,0:T(8,128)S(1)}, u32[]{:S(2)}, u32[]{:S(2)}) %collective-permute-start.3) | collective-permute-done | bytes 4128 | tf_op jit(solution)/shard_map/ppermute | solution.py:659
  33.0 0.0 collective-permute-done.1.y1_ref
  33.0 0.0 collective-permute-done.y0_ref
  33.1 11.3 %look_up.1 = (f32[8,8192]{1,0:T(8,128)S(1)}, f32[4,8192]{1,0:T(4,128)S(1)}) custom-call(f32[4,32,8,128]{3,2,1,0:T(8,128)S(1)} %copy-done, f32[4,32,128]{2,1,0:T(8,128)S(1)} %collective-permute-done.y0_ref, f32[4,32,128]{2,1,0:T(8,128)S(1)} %collective-permute-done.1.y1_ref, f32[8,128]{1,0:T(8,128)S(1)} %collective-permute-done.2.x0_ref, ...), custom_call_target="tpu_custom_call" | custom-call | flops 8589934592 | bytes 2097152 | tf_op jit(solution)/shard_map/look_up/pallas_call | solution.py:428
  44.4 0.9 copy-done.10
  45.2 9.2 %contact_blocks.1 = f32[32,32,128]{2,1,0:T(8,128)} custom-call(f32[32,48,128]{2,1,0:T(8,128)} %copy-done.10, s32[128,128,128]{2,1,0:T(8,128)} %mask_ref.1), custom_call_target="tpu_custom_call" | custom-call | flops 134217728 | bytes 8388608 | tf_op jit(solution)/shard_map/contact_blocks/pallas_call | solution.py:305
  54.4 9.0 %all-to-all-start.1 = ((f32[32,32,128]{2,1,0:T(8,128)}), f32[32,32,128]{2,1,0:T(8,128)S(1)}, u32[]{:S(2)}, u32[]{:S(2)}) async-start(f32[32,32,128]{2,1,0:T(8,128)} %contact_blocks.1), calls=%async_computation.1 | async-start | bytes 1048576 | tf_op jit(solution)/shard_map/all_to_all | solution.py:700
  63.5 0.0 copy-start.5
  63.5 0.0 copy-start.6
  63.5 0.0 copy-start.8
  63.5 6.3 %deposit_fields.1 = (f32[4,32,8,128]{3,2,1,0:T(8,128)S(1)}, f32[4,32,128]{2,1,0:T(8,128)S(1)}, f32[4,32,128]{2,1,0:T(8,128)S(1)}, f32[8,128]{1,0:T(8,128)S(1)}, f32[8,128]{1,0:T(8,128)S(1)}) custom-call(s32[1,8192]{1,0:T(1,128)S(1)} %bitcast.11, f32[4,8192]{1,0:T(4,128)S(1)} %get-tuple-element.36.term_ref), custom_call_target="tpu_custom_call" | custom-call | flops 4294967296 | bytes 2097152 | tf_op jit(solution)/shard_map/deposit_fields/pallas_call | solution.py:481
  69.8 7.6 %all-to-all-done.1.back_ref = f32[32,32,128]{2,1,0:T(8,128)S(1)} async-done(((f32[32,32,128]{2,1,0:T(8,128)}), f32[32,32,128]{2,1,0:T(8,128)S(1)}, u32[]{:S(2)}, u32[]{:S(2)}) %all-to-all-start.1) | async-done | bytes 524320 | tf_op jit(solution)/shard_map/all_to_all | solution.py:700
  77.4 5.2 %heat_deposit.1 = (f32[1,8192]{1,0:T(1,128)S(1)}, f32[1,32,8,128]{3,2,1,0:T(8,128)S(1)}, f32[5,32,128]{2,1,0:T(8,128)S(1)}, f32[5,32,128]{2,1,0:T(8,128)S(1)}, f...) custom-call(f32[32,32,128]{2,1,0:T(8,128)S(1)} %all-to-all-done.1.back_ref, s32[1,8192]{1,0:T(1,128)S(1)} %copy-done.7, ...), custom_call_target="tpu_custom_call" | custom-call | flops 1073741824 | bytes 1048576 | tf_op jit(solution)/shard_map/heat_deposit/pallas_call | solution.py:547
  82.6 3.4 %collective-permute-start.6 = (f32[10,128]{1,0:T(8,128)S(1)}, f32[10,128]{1,0:T(8,128)S(1)}, u32[]{:S(2)}, u32[]{:S(2)}) collective-permute-start(f32[10,128]{1,0:T(8,128)S(1)} %get-tuple-element.48), channel_id=1, source_target_pairs={{0,8},{8,16},{16,24},{1,9},{9,17},{17,25},{2,10},{10,18},{18,26},{... | collective-permute-start | bytes 15368 | tf_op jit(solution)/shard_map/ppermute | solution.py:659
  86.0 2.5 %collective-permute-start.7 = (f32[10,128]{1,0:T(8,128)S(1)}, f32[10,128]{1,0:T(8,128)S(1)}, u32[]{:S(2)}, u32[]{:S(2)}) collective-permute-start(f32[10,128]{1,0:T(8,128)S(1)} %get-tuple-element.49), channel_id=1, source_target_pairs={{8,0},{16,8},{24,16},{9,1},{17,9},{25,17},{10,2},{18,10},{26,18},{... | collective-permute-start | bytes 15368 | tf_op jit(solution)/shard_map/ppermute | solution.py:659
  88.5 1.9 %collective-permute-start.4 = (f32[5,32,128]{2,1,0:T(8,128)S(1)}, f32[5,32,128]{2,1,0:T(8,128)S(1)}, u32[]{:S(2)}, u32[]{:S(2)}) collective-permute-start(f32[5,32,128]{2,1,0:T(8,128)S(1)} %get-tuple-element.46), channel_id=1, source_target_pairs={{0,1},{1,2},{2,3},{3,4},{4,5},{5,6},{6,7},{8,9},{9,10},{10,11},{11... | collective-permute-start | bytes 245768 | tf_op jit(solution)/shard_map/ppermute | solution.py:659
  90.4 3.6 %collective-permute-start.5 = (f32[5,32,128]{2,1,0:T(8,128)S(1)}, f32[5,32,128]{2,1,0:T(8,128)S(1)}, u32[]{:S(2)}, u32[]{:S(2)}) collective-permute-start(f32[5,32,128]{2,1,0:T(8,128)S(1)} %get-tuple-element.47), channel_id=1, source_target_pairs={{1,0},{2,1},{3,2},{4,3},{5,4},{6,5},{7,6},{9,8},{10,9},{11,10},{12... | collective-permute-start | bytes 245768 | tf_op jit(solution)/shard_map/ppermute | solution.py:659
  94.1 5.7 %fetch_slots.1 = f32[7,8192]{1,0:T(8,128)} custom-call(s32[32]{0:T(128)S(1)} %copy-done.6, s32[40,128]{1,0:T(8,128)S(1)} %copy-done.9, f32[32,32,128]{2,1,0:T(8,128)S(1)} %all-to-all-done.1.back_ref, s32[1,8192]{1,0:T(1,128)S(1)} %bitcast.17, s32[1,8192]{1,0:T(1,128)S(1)} %copy-done.8, f32[8,8192]{1,0:T(8,128)S(1)} %get-tuple-element.40.base_ref, ...), custom_call_target="tpu_custom_call" | custom-call | flops 2147483648 | bytes 1048576 | tf_op jit(solution)/shard_map/fetch_slots/pallas_call | solution.py:614
  99.8 0.0 collective-permute-done.6.x0_ref
  99.8 0.0 collective-permute-done.5.y1_ref
  99.8 2.0 %spread_fields.1 = (f32[4,32,8,128]{3,2,1,0:T(8,128)}, f32[32,8,128]{2,1,0:T(8,128)}) custom-call(f32[4,32,8,128]{3,2,1,0:T(8,128)S(1)} %get-tuple-element.37.dep_ref, f32[1,32,8,128]{3,2,1,0:T(8,128)S(1)} %get-tuple-element.45.heat_ref, f32[5,32,128]{2,1,0:T(8,128)S(1)} %collective-permute-done.4.y0_ref, f32[5,32,128]{2,1,0:T(8,128)S(1)} %collective-permute-done.5.y1_ref, ...), custom_call_target="tpu_custom_call" | custom-call | flops 2621440 | bytes 2097152 | tf_op jit(solution)/shard_map/spread_fields/pallas_call | solution.py:644
  (22 shorter events, 0.1 us)
Async XLA Ops:
  0.6 32.4 %copy-start.1 = (f32[6,8192]{1,0:T(8,128)S(1)}, f32[6,8192]{1,0:T(8,128)}, u32[]{:S(2)}) copy-start(f32[6,8192]{1,0:T(8,128)} %motion_ref.3) | copy-start | bytes 589828
  0.6 32.4 %copy-start.2 = (f32[8192]{0:T(1024)S(1)}, f32[8192]{0:T(1024)}, u32[]{:S(2)}) copy-start(f32[8192]{0:T(1024)} %param.13) | copy-start | bytes 98308
  0.7 32.4 %copy-start.4 = (f32[8192]{0:T(1024)S(1)}, f32[8192]{0:T(1024)}, u32[]{:S(2)}) copy-start(f32[8192]{0:T(1024)} %param.12) | copy-start | bytes 98308
  0.7 17.4 %copy-start = (f32[4,32,8,128]{3,2,1,0:T(8,128)S(1)}, f32[4,32,8,128]{3,2,1,0:T(8,128)}, u32[]{:S(2)}) copy-start(f32[4,32,8,128]{3,2,1,0:T(8,128)} %fluid_ref.3) | copy-start | bytes 1572868
  0.7 32.4 %copy-start.3 = (s32[8192]{0:T(1024)S(1)}, s32[8192]{0:T(1024)}, u32[]{:S(2)}) copy-start(s32[8192]{0:T(1024)} %param.14) | copy-start | bytes 98308
  12.0 32.3 %all-to-all-start = ((f32[32,48,128]{2,1,0:T(8,128)}), f32[32,48,128]{2,1,0:T(8,128)S(1)}, u32[]{:S(2)}, u32[]{:S(2)}) async-start(f32[32,48,128]{2,1,0:T(8,128)} %get-tuple-element.29), calls=%async_computation | async-start | bytes 1572864 | tf_op jit(solution)/shard_map/all_to_all | solution.py:685
  18.2 14.8 %collective-permute-start.1 = (f32[4,32,128]{2,1,0:T(8,128)S(1)}, f32[4,32,128]{2,1,0:T(8,128)S(1)}, u32[]{:S(2)}, u32[]{:S(2)}) collective-permute-start(f32[4,32,128]{2,1,0:T(8,128)S(1)} %get-tuple-element.57), channel_id=1, source_target_pairs={{1,0},{2,1},{3,2},{4,3},{5,4},{6,5},{7,6},{9,8},{10,9},{11,10},{12... | collective-permute-start | bytes 196616 | tf_op jit(solution)/shard_map/ppermute | solution.py:659
  20.4 12.6 %collective-permute-start = (f32[4,32,128]{2,1,0:T(8,128)S(1)}, f32[4,32,128]{2,1,0:T(8,128)S(1)}, u32[]{:S(2)}, u32[]{:S(2)}) collective-permute-start(f32[4,32,128]{2,1,0:T(8,128)S(1)} %get-tuple-element.58), channel_id=1, source_target_pairs={{0,1},{1,2},{2,3},{3,4},{4,5},{5,6},{6,7},{8,9},{9,10},{10,11},{11... | collective-permute-start | bytes 196616 | tf_op jit(solution)/shard_map/ppermute | solution.py:659
  23.1 5.9 %collective-permute-start.2 = (f32[8,128]{1,0:T(8,128)S(1)}, f32[8,128]{1,0:T(8,128)S(1)}, u32[]{:S(2)}, u32[]{:S(2)}) collective-permute-start(f32[8,128]{1,0:T(8,128)S(1)} %reshape_squeeze.6), channel_id=1, source_target_pairs={{0,8},{8,16},{16,24},{1,9},{9,17},{17,25},{2,10},{10,18},{18,26},{... | collective-permute-start | bytes 12296 | tf_op jit(solution)/shard_map/ppermute | solution.py:659
  26.6 6.4 %collective-permute-start.3 = (f32[8,128]{1,0:T(8,128)S(1)}, f32[8,128]{1,0:T(8,128)S(1)}, u32[]{:S(2)}, u32[]{:S(2)}) collective-permute-start(f32[8,128]{1,0:T(8,128)S(1)} %reshape_squeeze.7), channel_id=1, source_target_pairs={{8,0},{16,8},{24,16},{9,1},{17,9},{25,17},{10,2},{18,10},{26,18},{... | collective-permute-start | bytes 12296 | tf_op jit(solution)/shard_map/ppermute | solution.py:659
  44.4 0.9 copy-start.10
  54.4 22.9 %copy-start.7 = (s32[1,8192]{1,0:T(1,128)S(1)}, s32[1,8192]{1,0:T(1,128)}, u32[]{:S(2)}) copy-start(s32[1,8192]{1,0:T(1,128)} %get-tuple-element.39.slot_ref) | copy-start | bytes 98308
  54.4 22.9 %all-to-all-start.1 = ((f32[32,32,128]{2,1,0:T(8,128)}), f32[32,32,128]{2,1,0:T(8,128)S(1)}, u32[]{:S(2)}, u32[]{:S(2)}) async-start(f32[32,32,128]{2,1,0:T(8,128)} %contact_blocks.1), calls=%async_computation.1 | async-start | bytes 1048576 | tf_op jit(solution)/shard_map/all_to_all | solution.py:700
  63.5 30.6 %copy-start.5 = (s32[8192,1]{0,1:T(1,128)S(1)}, s32[8192,1]{0,1:T(1,128)}, u32[]{:S(2)}) copy-start(s32[8192,1]{0,1:T(1,128)} %param.15) | copy-start | bytes 98308
  63.5 30.6 %copy-start.6 = (s32[32]{0:T(128)S(1)}, s32[32]{0:T(128)}, u32[]{:S(2)}) copy-start(s32[32]{0:T(128)} %owner_ref.3) | copy-start | bytes 388
  63.5 30.6 %copy-start.8 = (s32[1,8192]{1,0:T(1,128)S(1)}, s32[1,8192]{1,0:T(1,128)}, u32[]{:S(2)}) copy-start(s32[1,8192]{1,0:T(1,128)} %get-tuple-element.53.spot_ref) | copy-start | bytes 98308
  63.5 30.6 %copy-start.9 = (s32[40,128]{1,0:T(8,128)S(1)}, s32[40,128]{1,0:T(8,128)}, u32[]{:S(2)}) copy-start(s32[40,128]{1,0:T(8,128)} %get-tuple-element.52.tile_ref) | copy-start | bytes 61444
  82.6 17.2 %collective-permute-start.6 = (f32[10,128]{1,0:T(8,128)S(1)}, f32[10,128]{1,0:T(8,128)S(1)}, u32[]{:S(2)}, u32[]{:S(2)}) collective-permute-start(f32[10,128]{1,0:T(8,128)S(1)} %get-tuple-element.48), channel_id=1, source_target_pairs={{0,8},{8,16},{16,24},{1,9},{9,17},{17,25},{2,10},{10,18},{18,26},{... | collective-permute-start | bytes 15368 | tf_op jit(solution)/shard_map/ppermute | solution.py:659
  86.0 13.8 %collective-permute-start.7 = (f32[10,128]{1,0:T(8,128)S(1)}, f32[10,128]{1,0:T(8,128)S(1)}, u32[]{:S(2)}, u32[]{:S(2)}) collective-permute-start(f32[10,128]{1,0:T(8,128)S(1)} %get-tuple-element.49), channel_id=1, source_target_pairs={{8,0},{16,8},{24,16},{9,1},{17,9},{25,17},{10,2},{18,10},{26,18},{... | collective-permute-start | bytes 15368 | tf_op jit(solution)/shard_map/ppermute | solution.py:659
  88.5 11.4 %collective-permute-start.4 = (f32[5,32,128]{2,1,0:T(8,128)S(1)}, f32[5,32,128]{2,1,0:T(8,128)S(1)}, u32[]{:S(2)}, u32[]{:S(2)}) collective-permute-start(f32[5,32,128]{2,1,0:T(8,128)S(1)} %get-tuple-element.46), channel_id=1, source_target_pairs={{0,1},{1,2},{2,3},{3,4},{4,5},{5,6},{6,7},{8,9},{9,10},{10,11},{11... | collective-permute-start | bytes 245768 | tf_op jit(solution)/shard_map/ppermute | solution.py:659
  90.4 9.5 %collective-permute-start.5 = (f32[5,32,128]{2,1,0:T(8,128)S(1)}, f32[5,32,128]{2,1,0:T(8,128)S(1)}, u32[]{:S(2)}, u32[]{:S(2)}) collective-permute-start(f32[5,32,128]{2,1,0:T(8,128)S(1)} %get-tuple-element.47), channel_id=1, source_target_pairs={{1,0},{2,1},{3,2},{4,3},{5,4},{6,5},{7,6},{9,8},{10,9},{11,10},{12... | collective-permute-start | bytes 245768 | tf_op jit(solution)/shard_map/ppermute | solution.py:659

commit v5 on v4

--- a/solution.py
+++ b/solution.py
@@ -112,8 +112,11 @@
             carry = carry + jnp.sum(ones[s], axis=1, keepdims=True)
         windows = jnp.floor(highest * (1.0 / WINDOW)) + 1.0
         spans = jnp.where(lane[0:8] == c, windows, spans)
-    tile_ref[0:devices, :] = tiles.astype(jnp.int32)
-    tile_ref[devices : devices + 8, :] = spans.astype(jnp.int32)
+    if devices < BLOCK:
+        tiles = jnp.concatenate([tiles, jnp.zeros((BLOCK - devices, BLOCK), F32)], axis=0)
+    count = tile_ref.shape[0] - 8
+    tile_ref[0:count, :] = jnp.transpose(tiles)[0:count].astype(jnp.int32)
+    tile_ref[count : count + 8, :] = spans.astype(jnp.int32)
     copy = pltpu.make_async_copy(tile_ref, tile_of, done)
     copy.start()
     copy.wait()
@@ -146,7 +149,7 @@
             hot_spot = hot(WINDOW, spot_ref[:, here] - WINDOW * w)
             placed = lax.dot_general(parts, hot_spot, NT, preferred_element_type=F32)
             for o in range(devices):
-                tile = tile_of[box_of[o], c] + 2 * w
+                tile = tile_of[c, box_of[o]] + 2 * w
                 one = placed[16 * o : 16 * o + 8] + placed[16 * o + 8 : 16 * o + 16]
                 two = placed[16 * devices + 8 * o : 16 * devices + 8 * o + 8]
                 two = two + pltpu.roll(two, 4, 0)
@@ -156,7 +159,7 @@
                 acc[o, tile + 1, 8:16, :] += two[:, BLOCK:]
             return 0
 
-        return lax.fori_loop(0, tile_of[devices, c], window, 0)
+        return lax.fori_loop(0, tile_of[tile_ref.shape[0] - 8, c], window, 0)
 
     lax.fori_loop(0, particles // CHUNK, step, 0)
 
@@ -175,7 +178,7 @@
     layers = slots // BLOCK
     vmem = pl.BlockSpec(memory_space=VMEM)
     row = jax.ShapeDtypeStruct((1, particles), jnp.int32)
-    table = (devices + 8, BLOCK)
+    table = (-(-particles // (8 * CHUNK)) * 8 + 8, BLOCK)
     return pl.pallas_call(
         place_kernel,
         out_shape=(
@@ -387,25 +390,32 @@
 
 def look_kernel(
     fluid_ref, y0_ref, y1_ref, x0_ref, x1_ref, cell_ref, motion_ref, radius_ref, temp_ref,
-    base_ref, term_ref, table, *, chunk
+    base_ref, term_ref, table, rows_scratch, *, chunk
 ):
     fields, layers, rows, cols = fluid_ref.shape
     particles = cell_ref.shape[1]
+    half = layers * rows // 2
+    wide = 2 * cols
     for k in range(fields):
-        table[k] = smooth_field(fluid_ref, y0_ref, y1_ref, x0_ref, x1_ref, k)
+        rows_scratch[...] = smooth_field(fluid_ref, y0_ref, y1_ref, x0_ref, x1_ref, k).reshape(layers * rows, cols)
+        here = slice(k * half, (k + 1) * half)
+        for part in range(2):
+            high, low = split(rows_scratch[pl.ds(part, half, stride=2), :])
+            table[here, part * cols : (part + 1) * cols] = high
+            table[here, wide + part * cols : wide + (part + 1) * cols] = low
 
     def step(i, _):
         here = pl.ds(pl.multiple_of(i * chunk, chunk), chunk)
         cells = cell_ref[:, here]
-        seen = [[] for _ in range(fields)]
-        for s in range(chunk // BLOCK):
-            wanted = jnp.broadcast_to(cells[:, s * BLOCK : (s + 1) * BLOCK], (8, BLOCK))
-            values = gathered(
-                [[table[k, z] for z in range(layers)] for k in range(fields)], wanted // cols, wanted % cols
-            )
-            for k in range(fields):
-                seen[k].append(values[k])
-        seen = [jnp.concatenate(parts, axis=1) for parts in seen]
+        hot_low = hot(wide, cells % wide)
+        found = lax.dot_general(
+            table[...], jnp.concatenate([hot_low, hot_low], axis=0), NN, preferred_element_type=F32
+        )
+        mine = lax.broadcasted_iota(jnp.int32, (half, chunk), 0) == cells // wide
+        seen = [
+            jnp.sum(jnp.where(mine, found[k * half : (k + 1) * half], 0.0), axis=0, keepdims=True)
+            for k in range(fields)
+        ]
         motion = motion_ref[:, here]
         radius = radius_ref[:, here]
         temp = temp_ref[:, here]
@@ -423,6 +433,7 @@
 
 
 def look_up(fluid, halo, cells, motion, radius, temp):
+    fields, layers, rows, cols = fluid.shape
     particles = cells.shape[1]
     vmem = pl.BlockSpec(memory_space=VMEM)
     return pl.pallas_call(
@@ -433,7 +444,10 @@
         ),
         in_specs=[vmem] * 9,
         out_specs=(vmem,) * 2,
-        scratch_shapes=[VMEM(fluid.shape, F32)],
+        scratch_shapes=[
+            VMEM((fields * layers * rows // 2, 4 * cols), BF16),
+            VMEM((layers * rows, cols), F32),
+        ],
         compiler_params=pltpu.CompilerParams(vmem_limit_bytes=40 << 20),
         cost_estimate=pl.CostEstimate(flops=1 << 33, bytes_accessed=2 << 20, transcendentals=0),
         name="look_up",
@@ -585,7 +599,7 @@
 
         def window(w, total):
             for o in range(devices):
-                tile = tile_ref[box_of[o], c] + 2 * w
+                tile = tile_ref[c, box_of[o]] + 2 * w
                 wanted[16 * o : 16 * o + 16, 0:BLOCK] = table[o, tile]
                 wanted[16 * o : 16 * o + 16, BLOCK:] = table[o, tile + 1]
             hot_spot = hot(WINDOW, spot_ref[:, here] - WINDOW * w)
@@ -596,7 +610,9 @@
                 gained = jnp.where(boxes == box_of[o], value, gained)
             return total + gained
 
-        gained = lax.fori_loop(0, tile_ref[devices, c], window, jnp.zeros((8, CHUNK), F32))
+        gained = lax.fori_loop(
+            0, tile_ref[tile_ref.shape[0] - 8, c], window, jnp.zeros((8, CHUNK), F32)
+        )
         next_ref[:, here] = jnp.concatenate(
             [base_ref[0:6, here] + gained[0:6], warm_ref[:, here]], axis=0
         )
@@ -691,11 +707,9 @@
         fluid[:, :, :, 0].reshape(-1, BLOCK),
         fluid[:, :, :, cols - 1].reshape(-1, BLOCK),
     )
+    result = contact(arrived, contact_mask)
+    result, *fluid_halo = lax.optimization_barrier((result,) + tuple(fluid_halo))
     base, terms = look_up(fluid_state, fluid_halo, cells, particle_motion, radius, temp)
-    arrived, base, terms = lax.optimization_barrier((arrived, base, terms))
-
-    result = contact(arrived, contact_mask)
-    result, terms = lax.optimization_barrier((result, terms))
     deposits, *edges = deposit(cells, terms, (layers, rows, cols))
     back = lax.all_to_all(result, ("gx", "gy"), split_axis=0, concat_axis=0, tiled=True)
     warm, heat_field, *edges = heat_deposit(

time: 103 us -> 93.4 us (0.907)
  starting transfers between devices: 36.6 us -> 32.8 us
  waiting for transfers between devices: 11.5 us -> 8.32 us
  Pallas kernels: 51 us -> 48.1 us
    all_to_all x1, waiting for transfers between devices: 0.01 us -> 8.3 us  [shards(): lax.all_to_all(outgoing, ('gx', 'gy'), split_axis=0, concat_axis=0, tiled...]
    all_to_all x1, waiting for transfers between devices: 7.55 us -> 0.01 us  [shards(): lax.all_to_all(result, ('gx', 'gy'), split_axis=0, concat_axis=0, tiled=T...]
    ppermute x8, waiting for transfers between devices: 3.97 us -> 0.02 us  [moved(): return lax.ppermute(value, axis, pairs)]
    all_to_all x1, starting transfers between devices: 9.05 us -> 5.18 us  [shards(): lax.all_to_all(result, ('gx', 'gy'), split_axis=0, concat_axis=0, tiled=T...]
    pallas_call x1, Pallas kernels: 11.3 us -> 8.76 us  [look_up(): pl.pallas_call(functools.partial(look_kernel, chunk=512), out_shape=(jax....]
  transfers between devices with their start and end apart: 10 -> 10, of which waited for: 2 -> 1; matrix products, arithmetic and copies ran while one was open for 1% -> 1% of each run, Pallas kernels for 23% -> 32%
where the time goes in v5:
time: 93.4 us; the launch traced here: 91.9 us
  Pallas kernels  48.1 us (51%)
  starting transfers between devices  32.8 us (35%)
  waiting for transfers between devices  8.32 us (9%)
  local copies, waits for them, and re-layouts  1.73 us (2%)
  between operations  0.96 us (1%)
    ppermute x8, starting transfers between devices, moved(): return lax.ppermute(value, axis, pairs)  21.6 us
    pallas_call x1, Pallas kernels, place(): pl.pallas_call(place_kernel, out_shape=(jax.ShapeDtypeStruct((devices, 12...  11 us
    pallas_call x1, Pallas kernels, contact(): pl.pallas_call(contact_kernel, grid=(devices // step,), out_shape=jax.Sha...  9.21 us
    pallas_call x1, Pallas kernels, look_up(): pl.pallas_call(functools.partial(look_kernel, chunk=512), out_shape=(jax....  8.76 us
    all_to_all x1, waiting for transfers between devices, shards(): lax.all_to_all(outgoing, ('gx', 'gy'), split_axis=0, concat_axis=0, tiled...  8.3 us
    pallas_call x1, Pallas kernels, deposit(): pl.pallas_call(functools.partial(deposit_kernel, chunk=1024), out_shape=(...  6.27 us
    all_to_all x1, starting transfers between devices, shards(): lax.all_to_all(outgoing, ('gx', 'gy'), split_axis=0, concat_axis=0, tiled...  6.02 us
    pallas_call x1, Pallas kernels, fetch(): pl.pallas_call(fetch_kernel, out_shape=jax.ShapeDtypeStruct((7, particles...  5.56 us
  transfers between devices with their start and end apart: 10, of which 1 were waited for; matrix products, arithmetic and copies ran while one was open for 1% of the time, Pallas kernels for 32%

profile of v5, /device:TPU:10, one launch (start us, length us, event | category | flops | bytes accessed | tf_op | source)
XLA Modules:
  0.0 91.9 jit_solution(815856869939842437)
XLA Ops:
  0.6 11.0 %place_slots.1 = (f32[32,48,128]{2,1,0:T(8,128)}, s32[1,8192]{1,0:T(1,128)}, s32[1,8192]{1,0:T(1,128)}, s32[16,128]{1,0:T(8,128)}) custom-call(s32[32]{0:T(128)} %owner_ref.3, s32[1,8192]{1,0:T(1,128)} %bitcast.16, f32[3,8192]{1,0:T(4,128)} %pos_ref.1, f32[6,8192]{1,0:T(8,128)} %motion_ref.3, f32[1,8192]{1,0:T(1,128)} %bitcast.13, f32[1,8192]{1,0:T(1,128)} %bitcast.8), custom_call_target="tpu_custom_call" | custom-call | flops 3221225472 | bytes 1048576 | tf_op jit(solution)/shard_map/place_slots/pallas_call | solution.py:182
  11.7 0.0 copy-start.1
  11.7 0.0 copy-start.2
  11.7 0.0 copy-start.3
  11.7 0.0 copy-start.4
  11.7 6.0 %all-to-all-start = ((f32[32,48,128]{2,1,0:T(8,128)}), f32[32,48,128]{2,1,0:T(8,128)S(1)}, u32[]{:S(2)}, u32[]{:S(2)}) async-start(f32[32,48,128]{2,1,0:T(8,128)} %get-tuple-element.29), calls=%async_computation | async-start | bytes 1572864 | tf_op jit(solution)/shard_map/all_to_all | solution.py:701
  17.8 0.1 copy.14
  17.9 2.2 %collective-permute-start.1 = (f32[4,32,128]{2,1,0:T(8,128)S(1)}, f32[4,32,128]{2,1,0:T(8,128)S(1)}, u32[]{:S(2)}, u32[]{:S(2)}) collective-permute-start(f32[4,32,128]{2,1,0:T(8,128)S(1)} %get-tuple-element.57), channel_id=1, source_target_pairs={{1,0},{2,1},{3,2},{4,3},{5,4},{6,5},{7,6},{9,8},{10,9},{11,10},{12... | collective-permute-start | bytes 196616 | tf_op jit(solution)/shard_map/ppermute | solution.py:675
  20.1 2.1 %collective-permute-start = (f32[4,32,128]{2,1,0:T(8,128)S(1)}, f32[4,32,128]{2,1,0:T(8,128)S(1)}, u32[]{:S(2)}, u32[]{:S(2)}) collective-permute-start(f32[4,32,128]{2,1,0:T(8,128)S(1)} %get-tuple-element.58), channel_id=1, source_target_pairs={{0,1},{1,2},{2,3},{3,4},{4,5},{5,6},{6,7},{8,9},{9,10},{10,11},{11... | collective-permute-start | bytes 196616 | tf_op jit(solution)/shard_map/ppermute | solution.py:675
  22.3 0.5 slice_reduce_fusion
  22.8 0.1 reshape_squeeze.6
  22.8 3.4 %collective-permute-start.2 = (f32[8,128]{1,0:T(8,128)S(1)}, f32[8,128]{1,0:T(8,128)S(1)}, u32[]{:S(2)}, u32[]{:S(2)}) collective-permute-start(f32[8,128]{1,0:T(8,128)S(1)} %reshape_squeeze.6), channel_id=1, source_target_pairs={{0,8},{8,16},{16,24},{1,9},{9,17},{17,25},{2,10},{10,18},{18,26},{... | collective-permute-start | bytes 12296 | tf_op jit(solution)/shard_map/ppermute | solution.py:675
  26.2 0.1 reshape_squeeze.7
  26.3 2.5 %collective-permute-start.3 = (f32[8,128]{1,0:T(8,128)S(1)}, f32[8,128]{1,0:T(8,128)S(1)}, u32[]{:S(2)}, u32[]{:S(2)}) collective-permute-start(f32[8,128]{1,0:T(8,128)S(1)} %reshape_squeeze.7), channel_id=1, source_target_pairs={{8,0},{16,8},{24,16},{9,1},{17,9},{25,17},{10,2},{18,10},{26,18},{... | collective-permute-start | bytes 12296 | tf_op jit(solution)/shard_map/ppermute | solution.py:675
  28.8 8.3 %all-to-all-done.slot_ref = f32[32,48,128]{2,1,0:T(8,128)S(1)} async-done(((f32[32,48,128]{2,1,0:T(8,128)}), f32[32,48,128]{2,1,0:T(8,128)S(1)}, u32[]{:S(2)}, u32[]{:S(2)}) %all-to-all-start) | async-done | bytes 786464 | tf_op jit(solution)/shard_map/all_to_all | solution.py:701
  37.1 0.9 copy-done.10
  38.0 9.2 %contact_blocks.1 = f32[32,32,128]{2,1,0:T(8,128)} custom-call(f32[32,48,128]{2,1,0:T(8,128)} %copy-done.10, s32[128,128,128]{2,1,0:T(8,128)} %mask_ref.1), custom_call_target="tpu_custom_call" | custom-call | flops 134217728 | bytes 8388608 | tf_op jit(solution)/shard_map/contact_blocks/pallas_call | solution.py:308
  47.2 0.0 collective-permute-done.2.x0_ref
  47.2 5.2 %all-to-all-start.1 = ((f32[32,32,128]{2,1,0:T(8,128)}), f32[32,32,128]{2,1,0:T(8,128)S(1)}, u32[]{:S(2)}, u32[]{:S(2)}) async-start(f32[32,32,128]{2,1,0:T(8,128)} %contact_blocks.1), calls=%async_computation.1 | async-start | bytes 1048576 | tf_op jit(solution)/shard_map/all_to_all | solution.py:714
  52.4 8.8 %look_up.1 = (f32[8,8192]{1,0:T(8,128)S(1)}, f32[4,8192]{1,0:T(4,128)S(1)}) custom-call(f32[4,32,8,128]{3,2,1,0:T(8,128)S(1)} %copy-done, f32[4,32,128]{2,1,0:T(8,128)S(1)} %collective-permute-done.y0_ref, f32[4,32,128]{2,1,0:T(8,128)S(1)} %collective-permute-done.1.y1_ref, f32[8,128]{1,0:T(8,128)S(1)} %collective-permute-done.2.x0_ref, ...), custom_call_target="tpu_custom_call" | custom-call | flops 8589934592 | bytes 2097152 | tf_op jit(solution)/shard_map/look_up/pallas_call | solution.py:439
  61.2 0.0 copy-start.7
  61.2 0.0 copy-start.5
  61.2 0.0 copy-start.6
  61.2 0.0 copy-start.8
  61.3 6.3 %deposit_fields.1 = (f32[4,32,8,128]{3,2,1,0:T(8,128)S(1)}, f32[4,32,128]{2,1,0:T(8,128)S(1)}, f32[4,32,128]{2,1,0:T(8,128)S(1)}, f32[8,128]{1,0:T(8,128)S(1)}, f32[8,128]{1,0:T(8,128)S(1)}) custom-call(s32[1,8192]{1,0:T(1,128)S(1)} %bitcast.11, f32[4,8192]{1,0:T(4,128)S(1)} %get-tuple-element.36.term_ref), custom_call_target="tpu_custom_call" | custom-call | flops 4294967296 | bytes 2097152 | tf_op jit(solution)/shard_map/deposit_fields/pallas_call | solution.py:495
  67.6 5.2 %heat_deposit.1 = (f32[1,8192]{1,0:T(1,128)S(1)}, f32[1,32,8,128]{3,2,1,0:T(8,128)S(1)}, f32[5,32,128]{2,1,0:T(8,128)S(1)}, f32[5,32,128]{2,1,0:T(8,128)S(1)}, f...) custom-call(f32[32,32,128]{2,1,0:T(8,128)S(1)} %all-to-all-done.1.back_ref, s32[1,8192]{1,0:T(1,128)S(1)} %copy-done.7, ...), custom_call_target="tpu_custom_call" | custom-call | flops 1073741824 | bytes 1048576 | tf_op jit(solution)/shard_map/heat_deposit/pallas_call | solution.py:561
  72.8 3.4 %collective-permute-start.6 = (f32[10,128]{1,0:T(8,128)S(1)}, f32[10,128]{1,0:T(8,128)S(1)}, u32[]{:S(2)}, u32[]{:S(2)}) collective-permute-start(f32[10,128]{1,0:T(8,128)S(1)} %get-tuple-element.48), channel_id=1, source_target_pairs={{0,8},{8,16},{16,24},{1,9},{9,17},{17,25},{2,10},{10,18},{18,26},{... | collective-permute-start | bytes 15368 | tf_op jit(solution)/shard_map/ppermute | solution.py:675
  76.2 2.4 %collective-permute-start.7 = (f32[10,128]{1,0:T(8,128)S(1)}, f32[10,128]{1,0:T(8,128)S(1)}, u32[]{:S(2)}, u32[]{:S(2)}) collective-permute-start(f32[10,128]{1,0:T(8,128)S(1)} %get-tuple-element.49), channel_id=1, source_target_pairs={{8,0},{16,8},{24,16},{9,1},{17,9},{25,17},{10,2},{18,10},{26,18},{... | collective-permute-start | bytes 15368 | tf_op jit(solution)/shard_map/ppermute | solution.py:675
  78.7 1.9 %collective-permute-start.4 = (f32[5,32,128]{2,1,0:T(8,128)S(1)}, f32[5,32,128]{2,1,0:T(8,128)S(1)}, u32[]{:S(2)}, u32[]{:S(2)}) collective-permute-start(f32[5,32,128]{2,1,0:T(8,128)S(1)} %get-tuple-element.46), channel_id=1, source_target_pairs={{0,1},{1,2},{2,3},{3,4},{4,5},{5,6},{6,7},{8,9},{9,10},{10,11},{11... | collective-permute-start | bytes 245768 | tf_op jit(solution)/shard_map/ppermute | solution.py:675
  80.6 3.6 %collective-permute-start.5 = (f32[5,32,128]{2,1,0:T(8,128)S(1)}, f32[5,32,128]{2,1,0:T(8,128)S(1)}, u32[]{:S(2)}, u32[]{:S(2)}) collective-permute-start(f32[5,32,128]{2,1,0:T(8,128)S(1)} %get-tuple-element.47), channel_id=1, source_target_pairs={{1,0},{2,1},{3,2},{4,3},{5,4},{6,5},{7,6},{9,8},{10,9},{11,10},{12... | collective-permute-start | bytes 245768 | tf_op jit(solution)/shard_map/ppermute | solution.py:675
  84.3 5.6 %fetch_slots.1 = f32[7,8192]{1,0:T(8,128)} custom-call(s32[32]{0:T(128)S(1)} %copy-done.6, s32[16,128]{1,0:T(8,128)S(1)} %copy-done.9, f32[32,32,128]{2,1,0:T(8,128)S(1)} %all-to-all-done.1.back_ref, s32[1,8192]{1,0:T(1,128)S(1)} %bitcast.17, s32[1,8192]{1,0:T(1,128)S(1)} %copy-done.8, f32[8,8192]{1,0:T(8,128)S(1)} %get-tuple-element.40.base_ref, ...), custom_call_target="tpu_custom_call" | custom-call | flops 2147483648 | bytes 1048576 | tf_op jit(solution)/shard_map/fetch_slots/pallas_call | solution.py:630
  89.9 2.0 %spread_fields.1 = (f32[4,32,8,128]{3,2,1,0:T(8,128)}, f32[32,8,128]{2,1,0:T(8,128)}) custom-call(f32[4,32,8,128]{3,2,1,0:T(8,128)S(1)} %get-tuple-element.37.dep_ref, f32[1,32,8,128]{3,2,1,0:T(8,128)S(1)} %get-tuple-element.45.heat_ref, f32[5,32,128]{2,1,0:T(8,128)S(1)} %collective-permute-done.4.y0_ref, f32[5,32,128]{2,1,0:T(8,128)S(1)} %collective-permute-done.5.y1_ref, ...), custom_call_target="tpu_custom_call" | custom-call | flops 2621440 | bytes 2097152 | tf_op jit(solution)/shard_map/spread_fields/pallas_call | solution.py:660
  (22 shorter events, 0.1 us)
Async XLA Ops:
  0.6 17.1 %copy-start = (f32[4,32,8,128]{3,2,1,0:T(8,128)S(1)}, f32[4,32,8,128]{3,2,1,0:T(8,128)}, u32[]{:S(2)}) copy-start(f32[4,32,8,128]{3,2,1,0:T(8,128)} %fluid_ref.3) | copy-start | bytes 1572868
  11.7 40.7 %copy-start.1 = (f32[6,8192]{1,0:T(8,128)S(1)}, f32[6,8192]{1,0:T(8,128)}, u32[]{:S(2)}) copy-start(f32[6,8192]{1,0:T(8,128)} %motion_ref.3) | copy-start | bytes 589828
  11.7 40.7 %copy-start.2 = (f32[8192]{0:T(1024)S(1)}, f32[8192]{0:T(1024)}, u32[]{:S(2)}) copy-start(f32[8192]{0:T(1024)} %param.13) | copy-start | bytes 98308
  11.7 40.7 %copy-start.3 = (s32[8192]{0:T(1024)S(1)}, s32[8192]{0:T(1024)}, u32[]{:S(2)}) copy-start(s32[8192]{0:T(1024)} %param.14) | copy-start | bytes 98308
  11.7 40.7 %copy-start.4 = (f32[8192]{0:T(1024)S(1)}, f32[8192]{0:T(1024)}, u32[]{:S(2)}) copy-start(f32[8192]{0:T(1024)} %param.12) | copy-start | bytes 98308
  11.7 25.4 %all-to-all-start = ((f32[32,48,128]{2,1,0:T(8,128)}), f32[32,48,128]{2,1,0:T(8,128)S(1)}, u32[]{:S(2)}, u32[]{:S(2)}) async-start(f32[32,48,128]{2,1,0:T(8,128)} %get-tuple-element.29), calls=%async_computation | async-start | bytes 1572864 | tf_op jit(solution)/shard_map/all_to_all | solution.py:701
  17.9 29.3 %collective-permute-start.1 = (f32[4,32,128]{2,1,0:T(8,128)S(1)}, f32[4,32,128]{2,1,0:T(8,128)S(1)}, u32[]{:S(2)}, u32[]{:S(2)}) collective-permute-start(f32[4,32,128]{2,1,0:T(8,128)S(1)} %get-tuple-element.57), channel_id=1, source_target_pairs={{1,0},{2,1},{3,2},{4,3},{5,4},{6,5},{7,6},{9,8},{10,9},{11,10},{12... | collective-permute-start | bytes 196616 | tf_op jit(solution)/shard_map/ppermute | solution.py:675
  20.1 27.1 %collective-permute-start = (f32[4,32,128]{2,1,0:T(8,128)S(1)}, f32[4,32,128]{2,1,0:T(8,128)S(1)}, u32[]{:S(2)}, u32[]{:S(2)}) collective-permute-start(f32[4,32,128]{2,1,0:T(8,128)S(1)} %get-tuple-element.58), channel_id=1, source_target_pairs={{0,1},{1,2},{2,3},{3,4},{4,5},{5,6},{6,7},{8,9},{9,10},{10,11},{11... | collective-permute-start | bytes 196616 | tf_op jit(solution)/shard_map/ppermute | solution.py:675
  22.8 24.3 %collective-permute-start.2 = (f32[8,128]{1,0:T(8,128)S(1)}, f32[8,128]{1,0:T(8,128)S(1)}, u32[]{:S(2)}, u32[]{:S(2)}) collective-permute-start(f32[8,128]{1,0:T(8,128)S(1)} %reshape_squeeze.6), channel_id=1, source_target_pairs={{0,8},{8,16},{16,24},{1,9},{9,17},{17,25},{2,10},{10,18},{18,26},{... | collective-permute-start | bytes 12296 | tf_op jit(solution)/shard_map/ppermute | solution.py:675
  26.3 20.9 %collective-permute-start.3 = (f32[8,128]{1,0:T(8,128)S(1)}, f32[8,128]{1,0:T(8,128)S(1)}, u32[]{:S(2)}, u32[]{:S(2)}) collective-permute-start(f32[8,128]{1,0:T(8,128)S(1)} %reshape_squeeze.7), channel_id=1, source_target_pairs={{8,0},{16,8},{24,16},{9,1},{17,9},{25,17},{10,2},{18,10},{26,18},{... | collective-permute-start | bytes 12296 | tf_op jit(solution)/shard_map/ppermute | solution.py:675
  37.1 0.9 copy-start.10
  47.2 20.3 %all-to-all-start.1 = ((f32[32,32,128]{2,1,0:T(8,128)}), f32[32,32,128]{2,1,0:T(8,128)S(1)}, u32[]{:S(2)}, u32[]{:S(2)}) async-start(f32[32,32,128]{2,1,0:T(8,128)} %contact_blocks.1), calls=%async_computation.1 | async-start | bytes 1048576 | tf_op jit(solution)/shard_map/all_to_all | solution.py:714
  61.2 6.3 %copy-start.7 = (s32[1,8192]{1,0:T(1,128)S(1)}, s32[1,8192]{1,0:T(1,128)}, u32[]{:S(2)}) copy-start(s32[1,8192]{1,0:T(1,128)} %get-tuple-element.39.slot_ref) | copy-start | bytes 98308
  61.2 23.0 %copy-start.5 = (s32[8192,1]{0,1:T(1,128)S(1)}, s32[8192,1]{0,1:T(1,128)}, u32[]{:S(2)}) copy-start(s32[8192,1]{0,1:T(1,128)} %param.15) | copy-start | bytes 98308
  61.2 23.0 %copy-start.6 = (s32[32]{0:T(128)S(1)}, s32[32]{0:T(128)}, u32[]{:S(2)}) copy-start(s32[32]{0:T(128)} %owner_ref.3) | copy-start | bytes 388
  61.2 23.0 %copy-start.8 = (s32[1,8192]{1,0:T(1,128)S(1)}, s32[1,8192]{1,0:T(1,128)}, u32[]{:S(2)}) copy-start(s32[1,8192]{1,0:T(1,128)} %get-tuple-element.53.spot_ref) | copy-start | bytes 98308
  61.3 23.0 %copy-start.9 = (s32[16,128]{1,0:T(8,128)S(1)}, s32[16,128]{1,0:T(8,128)}, u32[]{:S(2)}) copy-start(s32[16,128]{1,0:T(8,128)} %get-tuple-element.52.tile_ref) | copy-start | bytes 24580
  72.8 17.0 %collective-permute-start.6 = (f32[10,128]{1,0:T(8,128)S(1)}, f32[10,128]{1,0:T(8,128)S(1)}, u32[]{:S(2)}, u32[]{:S(2)}) collective-permute-start(f32[10,128]{1,0:T(8,128)S(1)} %get-tuple-element.48), channel_id=1, source_target_pairs={{0,8},{8,16},{16,24},{1,9},{9,17},{17,25},{2,10},{10,18},{18,26},{... | collective-permute-start | bytes 15368 | tf_op jit(solution)/shard_map/ppermute | solution.py:675
  76.2 13.6 %collective-permute-start.7 = (f32[10,128]{1,0:T(8,128)S(1)}, f32[10,128]{1,0:T(8,128)S(1)}, u32[]{:S(2)}, u32[]{:S(2)}) collective-permute-start(f32[10,128]{1,0:T(8,128)S(1)} %get-tuple-element.49), channel_id=1, source_target_pairs={{8,0},{16,8},{24,16},{9,1},{17,9},{25,17},{10,2},{18,10},{26,18},{... | collective-permute-start | bytes 15368 | tf_op jit(solution)/shard_map/ppermute | solution.py:675
  78.7 11.2 %collective-permute-start.4 = (f32[5,32,128]{2,1,0:T(8,128)S(1)}, f32[5,32,128]{2,1,0:T(8,128)S(1)}, u32[]{:S(2)}, u32[]{:S(2)}) collective-permute-start(f32[5,32,128]{2,1,0:T(8,128)S(1)} %get-tuple-element.46), channel_id=1, source_target_pairs={{0,1},{1,2},{2,3},{3,4},{4,5},{5,6},{6,7},{8,9},{9,10},{10,11},{11... | collective-permute-start | bytes 245768 | tf_op jit(solution)/shard_map/ppermute | solution.py:675
  80.6 9.3 %collective-permute-start.5 = (f32[5,32,128]{2,1,0:T(8,128)S(1)}, f32[5,32,128]{2,1,0:T(8,128)S(1)}, u32[]{:S(2)}, u32[]{:S(2)}) collective-permute-start(f32[5,32,128]{2,1,0:T(8,128)S(1)} %get-tuple-element.47), channel_id=1, source_target_pairs={{1,0},{2,1},{3,2},{4,3},{5,4},{6,5},{7,6},{9,8},{10,9},{11,10},{12... | collective-permute-start | bytes 245768 | tf_op jit(solution)/shard_map/ppermute | solution.py:675

commit v6 on v5

--- a/solution.py
+++ b/solution.py
@@ -35,16 +35,6 @@
 def hot(count, row):
     places = lax.broadcasted_iota(jnp.int32, (count, row.shape[1]), 0)
     return jnp.where(places == row, 1.0, 0.0).astype(BF16)
-
-
-def hot_columns(count, row):
-    n = row.shape[1] // BLOCK
-    tiles = [row[:, a * BLOCK : (a + 1) * BLOCK] for a in range(n)]
-    turned = jnp.transpose(jnp.concatenate(tiles * (8 // n), axis=0).astype(F32))
-    places = lax.broadcasted_iota(jnp.int32, (BLOCK, count), 1).astype(F32)
-    return jnp.concatenate(
-        [jnp.where(places == turned[:, a : a + 1], 1.0, 0.0).astype(BF16) for a in range(n)], axis=0
-    )
 
 
 def invert(owner_ref, box_of):
@@ -388,16 +378,13 @@
     return [jnp.sum(jnp.where(mine, value, 0.0), axis=0, keepdims=True) for value in found]
 
 
-def look_kernel(
-    fluid_ref, y0_ref, y1_ref, x0_ref, x1_ref, cell_ref, motion_ref, radius_ref, temp_ref,
-    base_ref, term_ref, table, rows_scratch, *, chunk
-):
+def look_kernel(fluid_ref, cell_ref, seen_ref, table, rows_scratch, *, chunk):
     fields, layers, rows, cols = fluid_ref.shape
     particles = cell_ref.shape[1]
     half = layers * rows // 2
     wide = 2 * cols
     for k in range(fields):
-        rows_scratch[...] = smooth_field(fluid_ref, y0_ref, y1_ref, x0_ref, x1_ref, k).reshape(layers * rows, cols)
+        rows_scratch[...] = smoothed(fluid_ref[k], 0.0, 0.0, 0.0, 0.0).reshape(layers * rows, cols)
         here = slice(k * half, (k + 1) * half)
         for part in range(2):
             high, low = split(rows_scratch[pl.ds(part, half, stride=2), :])
@@ -416,59 +403,88 @@
             jnp.sum(jnp.where(mine, found[k * half : (k + 1) * half], 0.0), axis=0, keepdims=True)
             for k in range(fields)
         ]
-        motion = motion_ref[:, here]
-        radius = radius_ref[:, here]
-        temp = temp_ref[:, here]
-        fluid_vel = jnp.concatenate(seen[0:3], axis=0)
-        drag = DRAG_COEFF / (radius * radius + 0.25) * (fluid_vel - motion[0:3])
-        upward = lax.broadcasted_iota(jnp.int32, (3, 1), 0) == 2
-        moved = motion[0:3] + TIME_STEP * drag - jnp.where(upward, TIME_STEP * GRAVITY, 0.0)
-        warmed = temp + TIME_STEP * HEAT_TRANSFER * (seen[3] - temp)
-        base_ref[:, here] = jnp.concatenate([moved, motion[3:6], warmed, seen[3]], axis=0)
-        volume = radius * radius * radius
-        term_ref[:, here] = jnp.concatenate([volume, -volume * drag], axis=0)
+        seen_ref[:, here] = jnp.concatenate(seen, axis=0)
         return 0
 
     lax.fori_loop(0, particles // chunk, step, 0)
 
 
-def look_up(fluid, halo, cells, motion, radius, temp):
+def look_up(fluid, cells):
     fields, layers, rows, cols = fluid.shape
     particles = cells.shape[1]
     vmem = pl.BlockSpec(memory_space=VMEM)
     return pl.pallas_call(
         functools.partial(look_kernel, chunk=512),
-        out_shape=(
-            jax.ShapeDtypeStruct((8, particles), F32),
-            jax.ShapeDtypeStruct((4, particles), F32),
-        ),
-        in_specs=[vmem] * 9,
-        out_specs=(vmem,) * 2,
+        out_shape=jax.ShapeDtypeStruct((fields, particles), F32),
+        in_specs=[vmem] * 2,
+        out_specs=vmem,
         scratch_shapes=[
             VMEM((fields * layers * rows // 2, 4 * cols), BF16),
             VMEM((layers * rows, cols), F32),
         ],
         compiler_params=pltpu.CompilerParams(vmem_limit_bytes=40 << 20),
-        cost_estimate=pl.CostEstimate(flops=1 << 33, bytes_accessed=2 << 20, transcendentals=0),
+        cost_estimate=pl.CostEstimate(
+            flops=8 * fields * layers * rows * cols * particles // 4, bytes_accessed=1 << 20, transcendentals=0
+        ),
         name="look_up",
-    )(fluid, *halo, cells, motion, radius, temp)
+    )(fluid, cells)
 
 
 def deposit_kernel(
-    cell_ref, term_ref, dep_ref, dy0_ref, dy1_ref, dx0_ref, dx1_ref, rows_scratch, acc, *, chunk
+    y0_ref, y1_ref, x0_ref, x1_ref, cell_ref, seen_ref, motion_ref, radius_ref, temp_ref,
+    base_ref, dep_ref, dy0_ref, dy1_ref, dx0_ref, dx1_ref, x_table, rows_scratch, acc, *, chunk
 ):
     fields, layers, rows, cols = dep_ref.shape
     half = layers * rows // 2
     wide = 2 * cols
     particles = cell_ref.shape[1]
+    per = layers * rows // BLOCK
+    for k in range(fields):
+        x_table[k] = jnp.zeros_like(x_table[k])
+        x_table[k, 0:per, :] = x0_ref[k * per : (k + 1) * per, :]
+        x_table[k, per : 2 * per, :] = x1_ref[k * per : (k + 1) * per, :]
     acc[...] = jnp.zeros_like(acc)
 
     def step(i, _):
         here = pl.ds(pl.multiple_of(i * chunk, chunk), chunk)
         cells = cell_ref[:, here]
+        beside = [[] for _ in range(fields)]
+        for s in range(chunk // BLOCK):
+            cell = jnp.broadcast_to(cells[:, s * BLOCK : (s + 1) * BLOCK], (8, BLOCK))
+            high = cell // cols
+            low = cell % cols
+            y = high % rows
+            from_y = gathered(
+                [
+                    [ref[k, 8 * g : 8 * g + 8, :] for ref in (y0_ref, y1_ref) for g in range(layers // 8)]
+                    for k in range(fields)
+                ],
+                high // rows + jnp.where(y == 0, 0, layers),
+                low,
+            )
+            from_x = gathered(
+                [[x_table[k, 8 * g : 8 * g + 8, :] for g in range(x_table.shape[1] // 8)] for k in range(fields)],
+                high // BLOCK + jnp.where(low == 0, 0, per),
+                high % BLOCK,
+            )
+            on_y = (y[0:1] == 0) | (y[0:1] == rows - 1)
+            on_x = (low[0:1] == 0) | (low[0:1] == cols - 1)
+            for k in range(fields):
+                beside[k].append(jnp.where(on_y, from_y[k], 0.0) + jnp.where(on_x, from_x[k], 0.0))
+        beside = jnp.concatenate([jnp.concatenate(parts, axis=1) for parts in beside], axis=0)
+        seen = seen_ref[:, here] + SIDE_WEIGHT * beside
+        motion = motion_ref[:, here]
+        radius = radius_ref[:, here]
+        temp = temp_ref[:, here]
+        drag = DRAG_COEFF / (radius * radius + 0.25) * (seen[0:3] - motion[0:3])
+        upward = lax.broadcasted_iota(jnp.int32, (3, 1), 0) == 2
+        moved = motion[0:3] + TIME_STEP * drag - jnp.where(upward, TIME_STEP * GRAVITY, 0.0)
+        warmed = temp + TIME_STEP * HEAT_TRANSFER * (seen[3:4] - temp)
+        base_ref[:, here] = jnp.concatenate([moved, motion[3:6], warmed, seen[3:4]], axis=0)
+        volume = radius * radius * radius
+        high, low = split(jnp.concatenate([volume, -volume * drag], axis=0))
         hot_low = hot(wide, cells % wide)
         hot_high = hot(half, cells // wide)
-        high, low = split(term_ref[:, here])
         parts = [hot_high * piece[k : k + 1] for piece in (high, low) for k in range(fields)]
         total = lax.dot_general(jnp.concatenate(parts, axis=0), hot_low, NT, preferred_element_type=F32)
         acc[...] += total[: fields * half] + total[fields * half :]
@@ -487,17 +503,21 @@
     return (y_edge, y_edge, x_edge, x_edge)
 
 
-def deposit(cells, terms, grid):
+def deposit(halo, cells, seen, motion, radius, temp, grid):
     layers, rows, cols = grid
-    fields = terms.shape[0]
-    particles = cells.shape[1]
+    fields, particles = seen.shape
+    tall = -(-2 * layers * rows // (8 * BLOCK)) * 8
     vmem = pl.BlockSpec(memory_space=VMEM)
     return pl.pallas_call(
         functools.partial(deposit_kernel, chunk=1024),
-        out_shape=(jax.ShapeDtypeStruct((fields,) + grid, F32),) + edge_shapes(fields, layers, rows, cols),
-        in_specs=[vmem] * 2,
-        out_specs=(vmem,) * 5,
+        out_shape=(
+            jax.ShapeDtypeStruct((8, particles), F32),
+            jax.ShapeDtypeStruct((fields,) + grid, F32),
+        ) + edge_shapes(fields, layers, rows, cols),
+        in_specs=[vmem] * 9,
+        out_specs=(vmem,) * 6,
         scratch_shapes=[
+            VMEM((fields, tall, BLOCK), F32),
             VMEM((layers * rows, cols), F32),
             VMEM((fields * layers * rows // 2, 2 * cols), F32),
         ],
@@ -506,7 +526,7 @@
             flops=4 * fields * layers * rows * cols * particles, bytes_accessed=2 << 20, transcendentals=0
         ),
         name="deposit_fields",
-    )(cells, terms)
+    )(*halo, cells, seen, motion, radius, temp)
 
 
 def heat_kernel(
@@ -537,10 +557,11 @@
         radius = radius_ref[:, here]
         high, low = split(radius * radius * radius * (total - base[1:2]))
         cells = cell_ref[:, here]
-        hot_low = hot_columns(wide, cells % wide)
+        hot_low = hot(wide, cells % wide)
         hot_high = hot(half, cells // wide)
-        added = lax.dot_general(hot_high * high, hot_low, NN, preferred_element_type=F32)
-        acc[...] += added + lax.dot_general(hot_high * low, hot_low, NN, preferred_element_type=F32)
+        parts = jnp.concatenate([hot_high * high, hot_high * low], axis=0)
+        added = lax.dot_general(parts, hot_low, NT, preferred_element_type=F32)
+        acc[...] += added[:half] + added[half:]
         return 0
 
     lax.fori_loop(0, particles // chunk, step, 0)
@@ -707,10 +728,14 @@
         fluid[:, :, :, 0].reshape(-1, BLOCK),
         fluid[:, :, :, cols - 1].reshape(-1, BLOCK),
     )
+    seen = look_up(fluid, cells)
+    arrived, seen = lax.optimization_barrier((arrived, seen))
     result = contact(arrived, contact_mask)
+
     result, *fluid_halo = lax.optimization_barrier((result,) + tuple(fluid_halo))
-    base, terms = look_up(fluid_state, fluid_halo, cells, particle_motion, radius, temp)
-    deposits, *edges = deposit(cells, terms, (layers, rows, cols))
+    base, deposits, *edges = deposit(
+        fluid_halo, cells, seen, particle_motion, radius, temp, (layers, rows, cols)
+    )
     back = lax.all_to_all(result, ("gx", "gy"), split_axis=0, concat_axis=0, tiled=True)
     warm, heat_field, *edges = heat_deposit(
         back, slot_of, cells, radius, base, edges, (layers, rows, cols)

time: 93.4 us -> 93.5 us (level)
  waiting for transfers between devices: 8.32 us -> 5 us
  Pallas kernels: 48.1 us -> 51 us
    all_to_all x1, waiting for transfers between devices: 8.3 us -> 0.26 us  [shards(): lax.all_to_all(outgoing, ('gx', 'gy'), split_axis=0, concat_axis=0, tiled...]
    all_to_all x1, waiting for transfers between devices: 0.01 us -> 4.72 us  [shards(): lax.all_to_all(result, ('gx', 'gy'), split_axis=0, concat_axis=0, tiled=T...]
    pallas_call x1, Pallas kernels: 6.27 us -> 9.08 us  [deposit(): pl.pallas_call(functools.partial(deposit_kernel, chunk=1024), out_shape=(...]
    pallas_call x1, Pallas kernels: 5.24 us -> 6.2 us  [heat_deposit(): pl.pallas_call(functools.partial(heat_kernel, chunk=1024, rows=rows), out...]
  transfers between devices with their start and end apart: 10 -> 10, of which waited for: 1 -> 2; matrix products, arithmetic and copies ran while one was open for 1% -> 1% of each run, Pallas kernels for 32% -> 35%
where the time goes in v6:
time: 93.5 us; the launch traced here: 91.9 us
  Pallas kernels  51 us (55%)
  starting transfers between devices  33.2 us (36%)
  waiting for transfers between devices  5 us (5%)
  local copies, waits for them, and re-layouts  1.73 us (2%)
  between operations  0.94 us (1%)
    ppermute x8, starting transfers between devices, moved(): return lax.ppermute(value, axis, pairs)  21.6 us
    pallas_call x1, Pallas kernels, place(): pl.pallas_call(place_kernel, out_shape=(jax.ShapeDtypeStruct((devices, 12...  11 us
    pallas_call x1, Pallas kernels, contact(): pl.pallas_call(contact_kernel, grid=(devices // step,), out_shape=jax.Sha...  9.17 us
    pallas_call x1, Pallas kernels, deposit(): pl.pallas_call(functools.partial(deposit_kernel, chunk=1024), out_shape=(...  9.08 us
    pallas_call x1, Pallas kernels, look_up(): pl.pallas_call(functools.partial(look_kernel, chunk=512), out_shape=jax.S...  7.98 us
    pallas_call x1, Pallas kernels, heat_deposit(): pl.pallas_call(functools.partial(heat_kernel, chunk=1024, rows=rows), out...  6.2 us
    all_to_all x1, starting transfers between devices, shards(): lax.all_to_all(outgoing, ('gx', 'gy'), split_axis=0, concat_axis=0, tiled...  6.03 us
    all_to_all x1, starting transfers between devices, shards(): lax.all_to_all(result, ('gx', 'gy'), split_axis=0, concat_axis=0, tiled=T...  5.6 us
  transfers between devices with their start and end apart: 10, of which 2 were waited for; matrix products, arithmetic and copies ran while one was open for 1% of the time, Pallas kernels for 35%

profile of v6, /device:TPU:10, one launch (start us, length us, event | category | flops | bytes accessed | tf_op | source)
XLA Modules:
  0.0 91.9 jit_solution(1405818778855846837)
XLA Ops:
  0.7 11.0 %place_slots.1 = (f32[32,48,128]{2,1,0:T(8,128)}, s32[1,8192]{1,0:T(1,128)}, s32[1,8192]{1,0:T(1,128)}, s32[16,128]{1,0:T(8,128)}) custom-call(s32[32]{0:T(128)} %owner_ref.3, s32[1,8192]{1,0:T(1,128)} %bitcast.16, f32[3,8192]{1,0:T(4,128)} %pos_ref.1, f32[6,8192]{1,0:T(8,128)} %motion_ref.3, f32[1,8192]{1,0:T(1,128)} %bitcast.13, f32[1,8192]{1,0:T(1,128)} %bitcast.8), custom_call_target="tpu_custom_call" | custom-call | flops 3221225472 | bytes 1048576 | tf_op jit(solution)/shard_map/place_slots/pallas_call | solution.py:172
  11.7 6.0 %all-to-all-start = ((f32[32,48,128]{2,1,0:T(8,128)}), f32[32,48,128]{2,1,0:T(8,128)S(1)}, u32[]{:S(2)}, u32[]{:S(2)}) async-start(f32[32,48,128]{2,1,0:T(8,128)} %get-tuple-element.30), calls=%async_computation | async-start | bytes 1572864 | tf_op jit(solution)/shard_map/all_to_all | solution.py:722
  17.7 0.5 slice_reduce_fusion
  18.2 0.1 reshape_squeeze.6
  18.3 3.4 %collective-permute-start.2 = (f32[8,128]{1,0:T(8,128)S(1)}, f32[8,128]{1,0:T(8,128)S(1)}, u32[]{:S(2)}, u32[]{:S(2)}) collective-permute-start(f32[8,128]{1,0:T(8,128)S(1)} %reshape_squeeze.6), channel_id=1, source_target_pairs={{0,8},{8,16},{16,24},{1,9},{9,17},{17,25},{2,10},{10,18},{18,26},{... | collective-permute-start | bytes 12296 | tf_op jit(solution)/shard_map/ppermute | solution.py:696
  21.7 0.1 reshape_squeeze.7
  21.8 2.5 %collective-permute-start.3 = (f32[8,128]{1,0:T(8,128)S(1)}, f32[8,128]{1,0:T(8,128)S(1)}, u32[]{:S(2)}, u32[]{:S(2)}) collective-permute-start(f32[8,128]{1,0:T(8,128)S(1)} %reshape_squeeze.7), channel_id=1, source_target_pairs={{8,0},{16,8},{24,16},{9,1},{17,9},{25,17},{10,2},{18,10},{26,18},{... | collective-permute-start | bytes 12296 | tf_op jit(solution)/shard_map/ppermute | solution.py:696
  24.3 0.1 copy.14
  24.4 1.9 %collective-permute-start.1 = (f32[4,32,128]{2,1,0:T(8,128)S(1)}, f32[4,32,128]{2,1,0:T(8,128)S(1)}, u32[]{:S(2)}, u32[]{:S(2)}) collective-permute-start(f32[4,32,128]{2,1,0:T(8,128)S(1)} %get-tuple-element.59), channel_id=1, source_target_pairs={{1,0},{2,1},{3,2},{4,3},{5,4},{6,5},{7,6},{9,8},{10,9},{11,10},{12... | collective-permute-start | bytes 196616 | tf_op jit(solution)/shard_map/ppermute | solution.py:696
  26.3 2.4 %collective-permute-start = (f32[4,32,128]{2,1,0:T(8,128)S(1)}, f32[4,32,128]{2,1,0:T(8,128)S(1)}, u32[]{:S(2)}, u32[]{:S(2)}) collective-permute-start(f32[4,32,128]{2,1,0:T(8,128)S(1)} %get-tuple-element.60), channel_id=1, source_target_pairs={{0,1},{1,2},{2,3},{3,4},{4,5},{5,6},{6,7},{8,9},{9,10},{10,11},{11... | collective-permute-start | bytes 196616 | tf_op jit(solution)/shard_map/ppermute | solution.py:696
  28.8 0.0 copy-start.1
  28.8 0.0 copy-start.2
  28.8 0.0 copy-start.4
  28.8 8.0 %look_up.1.seen_ref = f32[4,8192]{1,0:T(4,128)S(1)} custom-call(f32[4,32,8,128]{3,2,1,0:T(8,128)S(1)} %copy-done, s32[1,8192]{1,0:T(1,128)S(1)} %bitcast.10), custom_call_target="tpu_custom_call" | custom-call | flops 2147483648 | bytes 1048576 | tf_op jit(solution)/shard_map/look_up/pallas_call | solution.py:416
  36.8 0.3 all-to-all-done.slot_ref
  37.1 0.9 copy-done.10
  37.9 9.2 %contact_blocks.1 = f32[32,32,128]{2,1,0:T(8,128)} custom-call(f32[32,48,128]{2,1,0:T(8,128)} %copy-done.10, s32[128,128,128]{2,1,0:T(8,128)} %mask_ref.1), custom_call_target="tpu_custom_call" | custom-call | flops 134217728 | bytes 8388608 | tf_op jit(solution)/shard_map/contact_blocks/pallas_call | solution.py:298
  47.1 0.0 collective-permute-done.2.x0_ref
  47.1 0.0 collective-permute-done.1.y1_ref
  47.1 5.6 %all-to-all-start.1 = ((f32[32,32,128]{2,1,0:T(8,128)}), f32[32,32,128]{2,1,0:T(8,128)S(1)}, u32[]{:S(2)}, u32[]{:S(2)}) async-start(f32[32,32,128]{2,1,0:T(8,128)} %contact_blocks.1), calls=%async_computation.1 | async-start | bytes 1048576 | tf_op jit(solution)/shard_map/all_to_all | solution.py:739
  52.8 0.0 copy-start.5
  52.8 0.0 copy-start.6
  52.8 0.0 copy-start.8
  52.8 9.1 %deposit_fields.1 = (f32[8,8192]{1,0:T(8,128)S(1)}, f32[4,32,8,128]{3,2,1,0:T(8,128)S(1)}, f32[4,32,128]{2,1,0:T(8,128)S(1)}, f32[4,32,128]{2,1,0:T(8,128)S(1)},...) custom-call(f32[4,32,128]{2,1,0:T(8,128)S(1)} %collective-permute-done.y0_ref, ...), custom_call_target="tpu_custom_call" | custom-call | flops 4294967296 | bytes 2097152 | tf_op jit(solution)/shard_map/deposit_fields/pallas_call | solution.py:511
  61.9 4.7 %all-to-all-done.1.back_ref = f32[32,32,128]{2,1,0:T(8,128)S(1)} async-done(((f32[32,32,128]{2,1,0:T(8,128)}), f32[32,32,128]{2,1,0:T(8,128)S(1)}, u32[]{:S(2)}, u32[]{:S(2)}) %all-to-all-start.1) | async-done | bytes 524320 | tf_op jit(solution)/shard_map/all_to_all | solution.py:739
  66.6 6.2 %heat_deposit.1 = (f32[1,8192]{1,0:T(1,128)S(1)}, f32[1,32,8,128]{3,2,1,0:T(8,128)S(1)}, f32[5,32,128]{2,1,0:T(8,128)S(1)}, f32[5,32,128]{2,1,0:T(8,128)S(1)}, f...) custom-call(f32[32,32,128]{2,1,0:T(8,128)S(1)} %all-to-all-done.1.back_ref, s32[1,8192]{1,0:T(1,128)S(1)} %copy-done.7, ...), custom_call_target="tpu_custom_call" | custom-call | flops 1073741824 | bytes 1048576 | tf_op jit(solution)/shard_map/heat_deposit/pallas_call | solution.py:582
  72.8 3.4 %collective-permute-start.6 = (f32[10,128]{1,0:T(8,128)S(1)}, f32[10,128]{1,0:T(8,128)S(1)}, u32[]{:S(2)}, u32[]{:S(2)}) collective-permute-start(f32[10,128]{1,0:T(8,128)S(1)} %get-tuple-element.50), channel_id=1, source_target_pairs={{0,8},{8,16},{16,24},{1,9},{9,17},{17,25},{2,10},{10,18},{18,26},{... | collective-permute-start | bytes 15368 | tf_op jit(solution)/shard_map/ppermute | solution.py:696
  76.2 2.5 %collective-permute-start.7 = (f32[10,128]{1,0:T(8,128)S(1)}, f32[10,128]{1,0:T(8,128)S(1)}, u32[]{:S(2)}, u32[]{:S(2)}) collective-permute-start(f32[10,128]{1,0:T(8,128)S(1)} %get-tuple-element.51), channel_id=1, source_target_pairs={{8,0},{16,8},{24,16},{9,1},{17,9},{25,17},{10,2},{18,10},{26,18},{... | collective-permute-start | bytes 15368 | tf_op jit(solution)/shard_map/ppermute | solution.py:696
  78.7 1.9 %collective-permute-start.4 = (f32[5,32,128]{2,1,0:T(8,128)S(1)}, f32[5,32,128]{2,1,0:T(8,128)S(1)}, u32[]{:S(2)}, u32[]{:S(2)}) collective-permute-start(f32[5,32,128]{2,1,0:T(8,128)S(1)} %get-tuple-element.48), channel_id=1, source_target_pairs={{0,1},{1,2},{2,3},{3,4},{4,5},{5,6},{6,7},{8,9},{9,10},{10,11},{11... | collective-permute-start | bytes 245768 | tf_op jit(solution)/shard_map/ppermute | solution.py:696
  80.6 3.6 %collective-permute-start.5 = (f32[5,32,128]{2,1,0:T(8,128)S(1)}, f32[5,32,128]{2,1,0:T(8,128)S(1)}, u32[]{:S(2)}, u32[]{:S(2)}) collective-permute-start(f32[5,32,128]{2,1,0:T(8,128)S(1)} %get-tuple-element.49), channel_id=1, source_target_pairs={{1,0},{2,1},{3,2},{4,3},{5,4},{6,5},{7,6},{9,8},{10,9},{11,10},{12... | collective-permute-start | bytes 245768 | tf_op jit(solution)/shard_map/ppermute | solution.py:696
  84.3 5.6 %fetch_slots.1 = f32[7,8192]{1,0:T(8,128)} custom-call(s32[32]{0:T(128)S(1)} %copy-done.6, s32[16,128]{1,0:T(8,128)S(1)} %copy-done.9, f32[32,32,128]{2,1,0:T(8,128)S(1)} %all-to-all-done.1.back_ref, s32[1,8192]{1,0:T(1,128)S(1)} %bitcast.17, s32[1,8192]{1,0:T(1,128)S(1)} %copy-done.8, f32[8,8192]{1,0:T(8,128)S(1)} %get-tuple-element.42.base_ref, ...), custom_call_target="tpu_custom_call" | custom-call | flops 2147483648 | bytes 1048576 | tf_op jit(solution)/shard_map/fetch_slots/pallas_call | solution.py:651
  89.9 2.0 %spread_fields.1 = (f32[4,32,8,128]{3,2,1,0:T(8,128)}, f32[32,8,128]{2,1,0:T(8,128)}) custom-call(f32[4,32,8,128]{3,2,1,0:T(8,128)S(1)} %get-tuple-element.39.dep_ref, f32[1,32,8,128]{3,2,1,0:T(8,128)S(1)} %get-tuple-element.47.heat_ref, f32[5,32,128]{2,1,0:T(8,128)S(1)} %collective-permute-done.4.y0_ref, f32[5,32,128]{2,1,0:T(8,128)S(1)} %collective-permute-done.5.y1_ref, ...), custom_call_target="tpu_custom_call" | custom-call | flops 2621440 | bytes 2097152 | tf_op jit(solution)/shard_map/spread_fields/pallas_call | solution.py:681
  (22 shorter events, 0.1 us)
Async XLA Ops:
  0.6 17.1 %copy-start = (f32[4,32,8,128]{3,2,1,0:T(8,128)S(1)}, f32[4,32,8,128]{3,2,1,0:T(8,128)}, u32[]{:S(2)}) copy-start(f32[4,32,8,128]{3,2,1,0:T(8,128)} %fluid_ref.2) | copy-start | bytes 1572868
  0.6 28.1 %copy-start.3 = (s32[8192]{0:T(1024)S(1)}, s32[8192]{0:T(1024)}, u32[]{:S(2)}) copy-start(s32[8192]{0:T(1024)} %param.14) | copy-start | bytes 98308
  11.7 25.4 %all-to-all-start = ((f32[32,48,128]{2,1,0:T(8,128)}), f32[32,48,128]{2,1,0:T(8,128)S(1)}, u32[]{:S(2)}, u32[]{:S(2)}) async-start(f32[32,48,128]{2,1,0:T(8,128)} %get-tuple-element.30), calls=%async_computation | async-start | bytes 1572864 | tf_op jit(solution)/shard_map/all_to_all | solution.py:722
  18.3 28.8 %collective-permute-start.2 = (f32[8,128]{1,0:T(8,128)S(1)}, f32[8,128]{1,0:T(8,128)S(1)}, u32[]{:S(2)}, u32[]{:S(2)}) collective-permute-start(f32[8,128]{1,0:T(8,128)S(1)} %reshape_squeeze.6), channel_id=1, source_target_pairs={{0,8},{8,16},{16,24},{1,9},{9,17},{17,25},{2,10},{10,18},{18,26},{... | collective-permute-start | bytes 12296 | tf_op jit(solution)/shard_map/ppermute | solution.py:696
  21.8 25.3 %collective-permute-start.3 = (f32[8,128]{1,0:T(8,128)S(1)}, f32[8,128]{1,0:T(8,128)S(1)}, u32[]{:S(2)}, u32[]{:S(2)}) collective-permute-start(f32[8,128]{1,0:T(8,128)S(1)} %reshape_squeeze.7), channel_id=1, source_target_pairs={{8,0},{16,8},{24,16},{9,1},{17,9},{25,17},{10,2},{18,10},{26,18},{... | collective-permute-start | bytes 12296 | tf_op jit(solution)/shard_map/ppermute | solution.py:696
  24.4 22.7 %collective-permute-start.1 = (f32[4,32,128]{2,1,0:T(8,128)S(1)}, f32[4,32,128]{2,1,0:T(8,128)S(1)}, u32[]{:S(2)}, u32[]{:S(2)}) collective-permute-start(f32[4,32,128]{2,1,0:T(8,128)S(1)} %get-tuple-element.59), channel_id=1, source_target_pairs={{1,0},{2,1},{3,2},{4,3},{5,4},{6,5},{7,6},{9,8},{10,9},{11,10},{12... | collective-permute-start | bytes 196616 | tf_op jit(solution)/shard_map/ppermute | solution.py:696
  26.3 20.8 %collective-permute-start = (f32[4,32,128]{2,1,0:T(8,128)S(1)}, f32[4,32,128]{2,1,0:T(8,128)S(1)}, u32[]{:S(2)}, u32[]{:S(2)}) collective-permute-start(f32[4,32,128]{2,1,0:T(8,128)S(1)} %get-tuple-element.60), channel_id=1, source_target_pairs={{0,1},{1,2},{2,3},{3,4},{4,5},{5,6},{6,7},{8,9},{9,10},{10,11},{11... | collective-permute-start | bytes 196616 | tf_op jit(solution)/shard_map/ppermute | solution.py:696
  28.8 24.0 %copy-start.1 = (f32[6,8192]{1,0:T(8,128)S(1)}, f32[6,8192]{1,0:T(8,128)}, u32[]{:S(2)}) copy-start(f32[6,8192]{1,0:T(8,128)} %motion_ref.3) | copy-start | bytes 589828
  28.8 24.0 %copy-start.2 = (f32[8192]{0:T(1024)S(1)}, f32[8192]{0:T(1024)}, u32[]{:S(2)}) copy-start(f32[8192]{0:T(1024)} %param.13) | copy-start | bytes 98308
  28.8 24.0 %copy-start.4 = (f32[8192]{0:T(1024)S(1)}, f32[8192]{0:T(1024)}, u32[]{:S(2)}) copy-start(f32[8192]{0:T(1024)} %param.12) | copy-start | bytes 98308
  37.1 0.9 copy-start.10
  47.1 19.5 %copy-start.7 = (s32[1,8192]{1,0:T(1,128)S(1)}, s32[1,8192]{1,0:T(1,128)}, u32[]{:S(2)}) copy-start(s32[1,8192]{1,0:T(1,128)} %get-tuple-element.41.slot_ref) | copy-start | bytes 98308
  47.1 19.5 %all-to-all-start.1 = ((f32[32,32,128]{2,1,0:T(8,128)}), f32[32,32,128]{2,1,0:T(8,128)S(1)}, u32[]{:S(2)}, u32[]{:S(2)}) async-start(f32[32,32,128]{2,1,0:T(8,128)} %contact_blocks.1), calls=%async_computation.1 | async-start | bytes 1048576 | tf_op jit(solution)/shard_map/all_to_all | solution.py:739
  52.8 31.5 %copy-start.5 = (s32[8192,1]{0,1:T(1,128)S(1)}, s32[8192,1]{0,1:T(1,128)}, u32[]{:S(2)}) copy-start(s32[8192,1]{0,1:T(1,128)} %param.15) | copy-start | bytes 98308
  52.8 31.5 %copy-start.6 = (s32[32]{0:T(128)S(1)}, s32[32]{0:T(128)}, u32[]{:S(2)}) copy-start(s32[32]{0:T(128)} %owner_ref.3) | copy-start | bytes 388
  52.8 31.5 %copy-start.8 = (s32[1,8192]{1,0:T(1,128)S(1)}, s32[1,8192]{1,0:T(1,128)}, u32[]{:S(2)}) copy-start(s32[1,8192]{1,0:T(1,128)} %get-tuple-element.55.spot_ref) | copy-start | bytes 98308
  52.8 31.5 %copy-start.9 = (s32[16,128]{1,0:T(8,128)S(1)}, s32[16,128]{1,0:T(8,128)}, u32[]{:S(2)}) copy-start(s32[16,128]{1,0:T(8,128)} %get-tuple-element.54.tile_ref) | copy-start | bytes 24580
  72.8 17.0 %collective-permute-start.6 = (f32[10,128]{1,0:T(8,128)S(1)}, f32[10,128]{1,0:T(8,128)S(1)}, u32[]{:S(2)}, u32[]{:S(2)}) collective-permute-start(f32[10,128]{1,0:T(8,128)S(1)} %get-tuple-element.50), channel_id=1, source_target_pairs={{0,8},{8,16},{16,24},{1,9},{9,17},{17,25},{2,10},{10,18},{18,26},{... | collective-permute-start | bytes 15368 | tf_op jit(solution)/shard_map/ppermute | solution.py:696
  76.2 13.6 %collective-permute-start.7 = (f32[10,128]{1,0:T(8,128)S(1)}, f32[10,128]{1,0:T(8,128)S(1)}, u32[]{:S(2)}, u32[]{:S(2)}) collective-permute-start(f32[10,128]{1,0:T(8,128)S(1)} %get-tuple-element.51), channel_id=1, source_target_pairs={{8,0},{16,8},{24,16},{9,1},{17,9},{25,17},{10,2},{18,10},{26,18},{... | collective-permute-start | bytes 15368 | tf_op jit(solution)/shard_map/ppermute | solution.py:696
  78.7 11.2 %collective-permute-start.4 = (f32[5,32,128]{2,1,0:T(8,128)S(1)}, f32[5,32,128]{2,1,0:T(8,128)S(1)}, u32[]{:S(2)}, u32[]{:S(2)}) collective-permute-start(f32[5,32,128]{2,1,0:T(8,128)S(1)} %get-tuple-element.48), channel_id=1, source_target_pairs={{0,1},{1,2},{2,3},{3,4},{4,5},{5,6},{6,7},{8,9},{9,10},{10,11},{11... | collective-permute-start | bytes 245768 | tf_op jit(solution)/shard_map/ppermute | solution.py:696
  80.6 9.3 %collective-permute-start.5 = (f32[5,32,128]{2,1,0:T(8,128)S(1)}, f32[5,32,128]{2,1,0:T(8,128)S(1)}, u32[]{:S(2)}, u32[]{:S(2)}) collective-permute-start(f32[5,32,128]{2,1,0:T(8,128)S(1)} %get-tuple-element.49), channel_id=1, source_target_pairs={{1,0},{2,1},{3,2},{4,3},{5,4},{6,5},{7,6},{9,8},{10,9},{11,10},{12... | collective-permute-start | bytes 245768 | tf_op jit(solution)/shard_map/ppermute | solution.py:696

commit v7 on v6

--- a/solution.py
+++ b/solution.py
@@ -37,6 +37,16 @@
     return jnp.where(places == row, 1.0, 0.0).astype(BF16)
 
 
+def hot_columns(count, row):
+    n = row.shape[1] // BLOCK
+    tiles = [row[:, a * BLOCK : (a + 1) * BLOCK] for a in range(n)]
+    turned = jnp.transpose(jnp.concatenate(tiles * (8 // n), axis=0).astype(F32))
+    places = lax.broadcasted_iota(jnp.int32, (BLOCK, count), 1).astype(F32)
+    return jnp.concatenate(
+        [jnp.where(places == turned[:, a : a + 1], 1.0, 0.0).astype(BF16) for a in range(n)], axis=0
+    )
+
+
 def invert(owner_ref, box_of):
     def step(b, _):
         box_of[owner_ref[b]] = b
@@ -72,7 +82,7 @@
     above = jnp.where(above, 1.0, 0.0).astype(BF16)
     lane = lax.broadcasted_iota(jnp.int32, (devices, BLOCK), 1)
     tiles = jnp.zeros((devices, BLOCK), F32)
-    spans = jnp.zeros((8, BLOCK), F32)
+    highest = jnp.zeros((1, sub), F32)
     carry = jnp.zeros((devices, 1), F32)
     per_chunk = CHUNK // sub
     for c in range(particles // CHUNK):
@@ -88,7 +98,6 @@
         )
         tile = jnp.minimum(jnp.floor(carry * (1.0 / BLOCK)), layers - 1.0)
         tiles = jnp.where(lane == c, tile, tiles)
-        highest = jnp.zeros((1, 1), F32)
         for s in range(per_chunk):
             at = c * CHUNK + s * sub
             rank = earlier[s * devices : (s + 1) * devices] + carry
@@ -98,20 +107,19 @@
             slot = jnp.sum(slot, axis=0, keepdims=True)
             spot_ref[:, at : at + sub] = spot.astype(jnp.int32)
             slot_ref[:, at : at + sub] = slot.astype(jnp.int32)
-            highest = jnp.maximum(highest, jnp.max(spot, axis=1, keepdims=True))
+            highest = jnp.maximum(highest, spot)
             carry = carry + jnp.sum(ones[s], axis=1, keepdims=True)
-        windows = jnp.floor(highest * (1.0 / WINDOW)) + 1.0
-        spans = jnp.where(lane[0:8] == c, windows, spans)
     if devices < BLOCK:
         tiles = jnp.concatenate([tiles, jnp.zeros((BLOCK - devices, BLOCK), F32)], axis=0)
     count = tile_ref.shape[0] - 8
     tile_ref[0:count, :] = jnp.transpose(tiles)[0:count].astype(jnp.int32)
-    tile_ref[count : count + 8, :] = spans.astype(jnp.int32)
+    windows = jnp.floor(jnp.max(highest, axis=1, keepdims=True) * (1.0 / WINDOW)) + 1.0
+    tile_ref[count : count + 8, :] = jnp.broadcast_to(windows, (8, BLOCK)).astype(jnp.int32)
     copy = pltpu.make_async_copy(tile_ref, tile_of, done)
     copy.start()
     copy.wait()
 
-    def step(c, _):
+    def step(w, c, _):
         here = pl.ds(pl.multiple_of(c * CHUNK, CHUNK), CHUNK)
         boxes = box_ref[:, here]
         pos = pos_ref[:, here]
@@ -135,23 +143,26 @@
                 second_parts.append(jnp.where(box16 == either, second, jnp.zeros_like(second)))
         parts = jnp.concatenate(first_parts + second_parts, axis=0)
 
-        def window(w, _):
-            hot_spot = hot(WINDOW, spot_ref[:, here] - WINDOW * w)
-            placed = lax.dot_general(parts, hot_spot, NT, preferred_element_type=F32)
-            for o in range(devices):
-                tile = tile_of[c, box_of[o]] + 2 * w
-                one = placed[16 * o : 16 * o + 8] + placed[16 * o + 8 : 16 * o + 16]
-                two = placed[16 * devices + 8 * o : 16 * devices + 8 * o + 8]
-                two = two + pltpu.roll(two, 4, 0)
-                acc[o, tile, 0:8, :] += one[:, :BLOCK]
-                acc[o, tile + 1, 0:8, :] += one[:, BLOCK:]
-                acc[o, tile, 8:16, :] += two[:, :BLOCK]
-                acc[o, tile + 1, 8:16, :] += two[:, BLOCK:]
-            return 0
-
-        return lax.fori_loop(0, tile_of[tile_ref.shape[0] - 8, c], window, 0)
-
-    lax.fori_loop(0, particles // CHUNK, step, 0)
+        hot_spot = hot(WINDOW, spot_ref[:, here] - WINDOW * w)
+        placed = lax.dot_general(parts, hot_spot, NT, preferred_element_type=F32)
+        for o in range(devices):
+            tile = tile_of[c, box_of[o]] + 2 * w
+            one = placed[16 * o : 16 * o + 8] + placed[16 * o + 8 : 16 * o + 16]
+            two = placed[16 * devices + 8 * o : 16 * devices + 8 * o + 8]
+            two = two + pltpu.roll(two, 4, 0)
+            acc[o, tile, 0:8, :] += one[:, :BLOCK]
+            acc[o, tile + 1, 0:8, :] += one[:, BLOCK:]
+            acc[o, tile, 8:16, :] += two[:, :BLOCK]
+            acc[o, tile + 1, 8:16, :] += two[:, BLOCK:]
+        return 0
+
+    chunks = particles // CHUNK
+    lax.fori_loop(0, chunks, functools.partial(step, 0), 0, unroll=2)
+
+    def later(w, _):
+        return lax.fori_loop(0, chunks, functools.partial(step, w), 0)
+
+    lax.fori_loop(1, tile_of[tile_ref.shape[0] - 8, 0], later, 0)
 
     def finish(o, _):
         for q in range(layers):
@@ -304,7 +315,7 @@
             pl.BlockSpec((step * layers, BLOCK, BLOCK), lambda h: (h, 0, 0)),
         ],
         out_specs=pl.BlockSpec((step, 8 * layers, BLOCK), lambda h: (h, 0, 0)),
-        compiler_params=pltpu.CompilerParams(vmem_limit_bytes=60 << 20),
+        compiler_params=pltpu.CompilerParams(vmem_limit_bytes=54 << 20),
         cost_estimate=pl.CostEstimate(
             flops=64 * blocks * BLOCK * BLOCK, bytes_accessed=blocks * BLOCK * BLOCK * 4, transcendentals=0
         ),
@@ -557,10 +568,10 @@
         radius = radius_ref[:, here]
         high, low = split(radius * radius * radius * (total - base[1:2]))
         cells = cell_ref[:, here]
-        hot_low = hot(wide, cells % wide)
+        hot_low = hot_columns(wide, cells % wide)
         hot_high = hot(half, cells // wide)
         parts = jnp.concatenate([hot_high * high, hot_high * low], axis=0)
-        added = lax.dot_general(parts, hot_low, NT, preferred_element_type=F32)
+        added = lax.dot_general(parts, hot_low, NN, preferred_element_type=F32)
         acc[...] += added[:half] + added[half:]
         return 0
 
@@ -601,7 +612,7 @@
 
 
 def fetch_kernel(
-    owner_ref, tile_ref, back_ref, box_ref, spot_ref, base_ref, warm_ref, next_ref, box_of, table, wanted
+    owner_ref, tile_ref, back_ref, box_ref, spot_ref, base_ref, warm_ref, next_ref, box_of, table
 ):
     devices, tall, _ = back_ref.shape
     layers = tall // 8
@@ -614,32 +625,40 @@
         for q in range(layers, layers + 3):
             table[o, q] = jnp.zeros((16, BLOCK), BF16)
 
-    def step(c, _):
+    def gained_of(w, c):
         here = pl.ds(pl.multiple_of(c * CHUNK, CHUNK), CHUNK)
         boxes = jnp.broadcast_to(box_ref[:, here], (8, CHUNK))
-
-        def window(w, total):
-            for o in range(devices):
-                tile = tile_ref[c, box_of[o]] + 2 * w
-                wanted[16 * o : 16 * o + 16, 0:BLOCK] = table[o, tile]
-                wanted[16 * o : 16 * o + 16, BLOCK:] = table[o, tile + 1]
-            hot_spot = hot(WINDOW, spot_ref[:, here] - WINDOW * w)
-            found = lax.dot_general(wanted[...], hot_spot, NN, preferred_element_type=F32)
-            gained = jnp.zeros((8, CHUNK), F32)
-            for o in range(devices):
-                value = found[16 * o : 16 * o + 8] + found[16 * o + 8 : 16 * o + 16]
-                gained = jnp.where(boxes == box_of[o], value, gained)
-            return total + gained
-
-        gained = lax.fori_loop(
-            0, tile_ref[tile_ref.shape[0] - 8, c], window, jnp.zeros((8, CHUNK), F32)
+        tile = [tile_ref[c, box_of[o]] + 2 * w for o in range(devices)]
+        wanted = jnp.concatenate(
+            [jnp.concatenate([table[o, tile[o]], table[o, tile[o] + 1]], axis=1) for o in range(devices)], axis=0
         )
+        hot_spot = hot(WINDOW, spot_ref[:, here] - WINDOW * w)
+        found = lax.dot_general(wanted, hot_spot, NN, preferred_element_type=F32)
+        gained = jnp.zeros((8, CHUNK), F32)
+        for o in range(devices):
+            value = found[16 * o : 16 * o + 8] + found[16 * o + 8 : 16 * o + 16]
+            gained = jnp.where(boxes == box_of[o], value, gained)
+        return here, gained
+
+    def step(c, _):
+        here, gained = gained_of(0, c)
         next_ref[:, here] = jnp.concatenate(
             [base_ref[0:6, here] + gained[0:6], warm_ref[:, here]], axis=0
         )
         return 0
 
-    lax.fori_loop(0, particles // CHUNK, step, 0)
+    chunks = particles // CHUNK
+    lax.fori_loop(0, chunks, step, 0, unroll=2)
+
+    def later(w, _):
+        def again(c, _):
+            here, gained = gained_of(w, c)
+            next_ref[0:6, here] += gained[0:6]
+            return 0
+
+        return lax.fori_loop(0, chunks, again, 0)
+
+    lax.fori_loop(1, tile_ref[tile_ref.shape[0] - 8, 0], later, 0)
 
 
 def fetch(box_owner, tiles, back, boxes, spots, base, warm):
@@ -656,7 +675,6 @@
         scratch_shapes=[
             pltpu.SMEM((devices,), jnp.int32),
             VMEM((devices, layers + 3, 16, BLOCK), BF16),
-            VMEM((16 * devices, WINDOW), BF16),
         ],
         compiler_params=pltpu.CompilerParams(vmem_limit_bytes=40 << 20),
         cost_estimate=pl.CostEstimate(

time: 93.5 us -> 91.1 us (0.974)
  Pallas kernels: 51 us -> 48.7 us
    pallas_call x1, Pallas kernels: 11 us -> 9.53 us  [place(): pl.pallas_call(place_kernel, out_shape=(jax.ShapeDtypeStruct((devices, 12...]
where the time goes in v7:
time: 91.1 us; the launch traced here: 89.5 us
  Pallas kernels  48.7 us (53%)
  starting transfers between devices  33.2 us (36%)
  waiting for transfers between devices  5 us (5%)
  local copies, waits for them, and re-layouts  1.73 us (2%)
  between operations  0.94 us (1%)
    ppermute x8, starting transfers between devices, moved(): return lax.ppermute(value, axis, pairs)  21.6 us
    pallas_call x1, Pallas kernels, place(): pl.pallas_call(place_kernel, out_shape=(jax.ShapeDtypeStruct((devices, 12...  9.53 us
    pallas_call x1, Pallas kernels, contact(): pl.pallas_call(contact_kernel, grid=(devices // step,), out_shape=jax.Sha...  9.17 us
    pallas_call x1, Pallas kernels, deposit(): pl.pallas_call(functools.partial(deposit_kernel, chunk=1024), out_shape=(...  9.08 us
    pallas_call x1, Pallas kernels, look_up(): pl.pallas_call(functools.partial(look_kernel, chunk=512), out_shape=jax.S...  7.98 us
    pallas_call x1, Pallas kernels, heat_deposit(): pl.pallas_call(functools.partial(heat_kernel, chunk=1024, rows=rows), out...  6.07 us
    all_to_all x1, starting transfers between devices, shards(): lax.all_to_all(outgoing, ('gx', 'gy'), split_axis=0, concat_axis=0, tiled...  6.02 us
    all_to_all x1, starting transfers between devices, shards(): lax.all_to_all(result, ('gx', 'gy'), split_axis=0, concat_axis=0, tiled=T...  5.59 us
  transfers between devices with their start and end apart: 10, of which 2 were waited for; matrix products, arithmetic and copies ran while one was open for 1% of the time, Pallas kernels for 35%

profile of v7, /device:TPU:10, one launch (start us, length us, event | category | flops | bytes accessed | tf_op | source)
XLA Modules:
  0.0 89.5 jit_solution(5825654074690098062)
XLA Ops:
  0.7 9.5 %place_slots.1 = (f32[32,48,128]{2,1,0:T(8,128)}, s32[1,8192]{1,0:T(1,128)}, s32[1,8192]{1,0:T(1,128)}, s32[16,128]{1,0:T(8,128)}) custom-call(s32[32]{0:T(128)} %owner_ref.3, s32[1,8192]{1,0:T(1,128)} %bitcast.16, f32[3,8192]{1,0:T(4,128)} %pos_ref.1, f32[6,8192]{1,0:T(8,128)} %motion_ref.3, f32[1,8192]{1,0:T(1,128)} %bitcast.13, f32[1,8192]{1,0:T(1,128)} %bitcast.8), custom_call_target="tpu_custom_call" | custom-call | flops 3221225472 | bytes 1048576 | tf_op jit(solution)/shard_map/place_slots/pallas_call | solution.py:183
  10.2 6.0 %all-to-all-start = ((f32[32,48,128]{2,1,0:T(8,128)}), f32[32,48,128]{2,1,0:T(8,128)S(1)}, u32[]{:S(2)}, u32[]{:S(2)}) async-start(f32[32,48,128]{2,1,0:T(8,128)} %get-tuple-element.30), calls=%async_computation | async-start | bytes 1572864 | tf_op jit(solution)/shard_map/all_to_all | solution.py:740
  16.2 0.5 slice_reduce_fusion
  16.7 0.1 reshape_squeeze.6
  16.8 3.4 %collective-permute-start.2 = (f32[8,128]{1,0:T(8,128)S(1)}, f32[8,128]{1,0:T(8,128)S(1)}, u32[]{:S(2)}, u32[]{:S(2)}) collective-permute-start(f32[8,128]{1,0:T(8,128)S(1)} %reshape_squeeze.6), channel_id=1, source_target_pairs={{0,8},{8,16},{16,24},{1,9},{9,17},{17,25},{2,10},{10,18},{18,26},{... | collective-permute-start | bytes 12296 | tf_op jit(solution)/shard_map/ppermute | solution.py:714
  20.2 0.1 reshape_squeeze.7
  20.3 2.5 %collective-permute-start.3 = (f32[8,128]{1,0:T(8,128)S(1)}, f32[8,128]{1,0:T(8,128)S(1)}, u32[]{:S(2)}, u32[]{:S(2)}) collective-permute-start(f32[8,128]{1,0:T(8,128)S(1)} %reshape_squeeze.7), channel_id=1, source_target_pairs={{8,0},{16,8},{24,16},{9,1},{17,9},{25,17},{10,2},{18,10},{26,18},{... | collective-permute-start | bytes 12296 | tf_op jit(solution)/shard_map/ppermute | solution.py:714
  22.8 0.1 copy.14
  22.9 1.9 %collective-permute-start.1 = (f32[4,32,128]{2,1,0:T(8,128)S(1)}, f32[4,32,128]{2,1,0:T(8,128)S(1)}, u32[]{:S(2)}, u32[]{:S(2)}) collective-permute-start(f32[4,32,128]{2,1,0:T(8,128)S(1)} %get-tuple-element.59), channel_id=1, source_target_pairs={{1,0},{2,1},{3,2},{4,3},{5,4},{6,5},{7,6},{9,8},{10,9},{11,10},{12... | collective-permute-start | bytes 196616 | tf_op jit(solution)/shard_map/ppermute | solution.py:714
  24.8 2.4 %collective-permute-start = (f32[4,32,128]{2,1,0:T(8,128)S(1)}, f32[4,32,128]{2,1,0:T(8,128)S(1)}, u32[]{:S(2)}, u32[]{:S(2)}) collective-permute-start(f32[4,32,128]{2,1,0:T(8,128)S(1)} %get-tuple-element.60), channel_id=1, source_target_pairs={{0,1},{1,2},{2,3},{3,4},{4,5},{5,6},{6,7},{8,9},{9,10},{10,11},{11... | collective-permute-start | bytes 196616 | tf_op jit(solution)/shard_map/ppermute | solution.py:714
  27.2 0.0 copy-start.1
  27.3 0.0 copy-start.2
  27.3 0.0 copy-start.4
  27.3 8.0 %look_up.1.seen_ref = f32[4,8192]{1,0:T(4,128)S(1)} custom-call(f32[4,32,8,128]{3,2,1,0:T(8,128)S(1)} %copy-done, s32[1,8192]{1,0:T(1,128)S(1)} %bitcast.10), custom_call_target="tpu_custom_call" | custom-call | flops 2147483648 | bytes 1048576 | tf_op jit(solution)/shard_map/look_up/pallas_call | solution.py:427
  35.3 0.3 all-to-all-done.slot_ref
  35.5 0.9 copy-done.10
  36.4 9.2 %contact_blocks.1 = f32[32,32,128]{2,1,0:T(8,128)} custom-call(f32[32,48,128]{2,1,0:T(8,128)} %copy-done.10, s32[128,128,128]{2,1,0:T(8,128)} %mask_ref.1), custom_call_target="tpu_custom_call" | custom-call | flops 134217728 | bytes 8388608 | tf_op jit(solution)/shard_map/contact_blocks/pallas_call | solution.py:309
  45.6 0.0 collective-permute-done.2.x0_ref
  45.6 0.0 collective-permute-done.1.y1_ref
  45.6 5.6 %all-to-all-start.1 = ((f32[32,32,128]{2,1,0:T(8,128)}), f32[32,32,128]{2,1,0:T(8,128)S(1)}, u32[]{:S(2)}, u32[]{:S(2)}) async-start(f32[32,32,128]{2,1,0:T(8,128)} %contact_blocks.1), calls=%async_computation.1 | async-start | bytes 1048576 | tf_op jit(solution)/shard_map/all_to_all | solution.py:757
  51.3 0.0 copy-start.5
  51.3 0.0 copy-start.6
  51.3 0.0 copy-start.8
  51.3 9.1 %deposit_fields.1 = (f32[8,8192]{1,0:T(8,128)S(1)}, f32[4,32,8,128]{3,2,1,0:T(8,128)S(1)}, f32[4,32,128]{2,1,0:T(8,128)S(1)}, f32[4,32,128]{2,1,0:T(8,128)S(1)},...) custom-call(f32[4,32,128]{2,1,0:T(8,128)S(1)} %collective-permute-done.y0_ref, ...), custom_call_target="tpu_custom_call" | custom-call | flops 4294967296 | bytes 2097152 | tf_op jit(solution)/shard_map/deposit_fields/pallas_call | solution.py:522
  60.4 4.7 %all-to-all-done.1.back_ref = f32[32,32,128]{2,1,0:T(8,128)S(1)} async-done(((f32[32,32,128]{2,1,0:T(8,128)}), f32[32,32,128]{2,1,0:T(8,128)S(1)}, u32[]{:S(2)}, u32[]{:S(2)}) %all-to-all-start.1) | async-done | bytes 524320 | tf_op jit(solution)/shard_map/all_to_all | solution.py:757
  65.1 6.1 %heat_deposit.1 = (f32[1,8192]{1,0:T(1,128)S(1)}, f32[1,32,8,128]{3,2,1,0:T(8,128)S(1)}, f32[5,32,128]{2,1,0:T(8,128)S(1)}, f32[5,32,128]{2,1,0:T(8,128)S(1)}, f...) custom-call(f32[32,32,128]{2,1,0:T(8,128)S(1)} %all-to-all-done.1.back_ref, s32[1,8192]{1,0:T(1,128)S(1)} %copy-done.7, ...), custom_call_target="tpu_custom_call" | custom-call | flops 1073741824 | bytes 1048576 | tf_op jit(solution)/shard_map/heat_deposit/pallas_call | solution.py:593
  71.2 3.4 %collective-permute-start.6 = (f32[10,128]{1,0:T(8,128)S(1)}, f32[10,128]{1,0:T(8,128)S(1)}, u32[]{:S(2)}, u32[]{:S(2)}) collective-permute-start(f32[10,128]{1,0:T(8,128)S(1)} %get-tuple-element.50), channel_id=1, source_target_pairs={{0,8},{8,16},{16,24},{1,9},{9,17},{17,25},{2,10},{10,18},{18,26},{... | collective-permute-start | bytes 15368 | tf_op jit(solution)/shard_map/ppermute | solution.py:714
  74.6 2.5 %collective-permute-start.7 = (f32[10,128]{1,0:T(8,128)S(1)}, f32[10,128]{1,0:T(8,128)S(1)}, u32[]{:S(2)}, u32[]{:S(2)}) collective-permute-start(f32[10,128]{1,0:T(8,128)S(1)} %get-tuple-element.51), channel_id=1, source_target_pairs={{8,0},{16,8},{24,16},{9,1},{17,9},{25,17},{10,2},{18,10},{26,18},{... | collective-permute-start | bytes 15368 | tf_op jit(solution)/shard_map/ppermute | solution.py:714
  77.0 1.9 %collective-permute-start.4 = (f32[5,32,128]{2,1,0:T(8,128)S(1)}, f32[5,32,128]{2,1,0:T(8,128)S(1)}, u32[]{:S(2)}, u32[]{:S(2)}) collective-permute-start(f32[5,32,128]{2,1,0:T(8,128)S(1)} %get-tuple-element.48), channel_id=1, source_target_pairs={{0,1},{1,2},{2,3},{3,4},{4,5},{5,6},{6,7},{8,9},{9,10},{10,11},{11... | collective-permute-start | bytes 245768 | tf_op jit(solution)/shard_map/ppermute | solution.py:714
  79.0 3.6 %collective-permute-start.5 = (f32[5,32,128]{2,1,0:T(8,128)S(1)}, f32[5,32,128]{2,1,0:T(8,128)S(1)}, u32[]{:S(2)}, u32[]{:S(2)}) collective-permute-start(f32[5,32,128]{2,1,0:T(8,128)S(1)} %get-tuple-element.49), channel_id=1, source_target_pairs={{1,0},{2,1},{3,2},{4,3},{5,4},{6,5},{7,6},{9,8},{10,9},{11,10},{12... | collective-permute-start | bytes 245768 | tf_op jit(solution)/shard_map/ppermute | solution.py:714
  82.7 4.8 %fetch_slots.1 = f32[7,8192]{1,0:T(8,128)} custom-call(s32[32]{0:T(128)S(1)} %copy-done.6, s32[16,128]{1,0:T(8,128)S(1)} %copy-done.9, f32[32,32,128]{2,1,0:T(8,128)S(1)} %all-to-all-done.1.back_ref, s32[1,8192]{1,0:T(1,128)S(1)} %bitcast.17, s32[1,8192]{1,0:T(1,128)S(1)} %copy-done.8, f32[8,8192]{1,0:T(8,128)S(1)} %get-tuple-element.42.base_ref, ...), custom_call_target="tpu_custom_call" | custom-call | flops 2147483648 | bytes 1048576 | tf_op jit(solution)/shard_map/fetch_slots/pallas_call | solution.py:670
  87.5 2.0 %spread_fields.1 = (f32[4,32,8,128]{3,2,1,0:T(8,128)}, f32[32,8,128]{2,1,0:T(8,128)}) custom-call(f32[4,32,8,128]{3,2,1,0:T(8,128)S(1)} %get-tuple-element.39.dep_ref, f32[1,32,8,128]{3,2,1,0:T(8,128)S(1)} %get-tuple-element.47.heat_ref, f32[5,32,128]{2,1,0:T(8,128)S(1)} %collective-permute-done.4.y0_ref, f32[5,32,128]{2,1,0:T(8,128)S(1)} %collective-permute-done.5.y1_ref, ...), custom_call_target="tpu_custom_call" | custom-call | flops 2621440 | bytes 2097152 | tf_op jit(solution)/shard_map/spread_fields/pallas_call | solution.py:699
  (22 shorter events, 0.1 us)
Async XLA Ops:
  0.6 15.6 %copy-start = (f32[4,32,8,128]{3,2,1,0:T(8,128)S(1)}, f32[4,32,8,128]{3,2,1,0:T(8,128)}, u32[]{:S(2)}) copy-start(f32[4,32,8,128]{3,2,1,0:T(8,128)} %fluid_ref.2) | copy-start | bytes 1572868
  0.6 26.6 %copy-start.3 = (s32[8192]{0:T(1024)S(1)}, s32[8192]{0:T(1024)}, u32[]{:S(2)}) copy-start(s32[8192]{0:T(1024)} %param.14) | copy-start | bytes 98308
  10.2 25.4 %all-to-all-start = ((f32[32,48,128]{2,1,0:T(8,128)}), f32[32,48,128]{2,1,0:T(8,128)S(1)}, u32[]{:S(2)}, u32[]{:S(2)}) async-start(f32[32,48,128]{2,1,0:T(8,128)} %get-tuple-element.30), calls=%async_computation | async-start | bytes 1572864 | tf_op jit(solution)/shard_map/all_to_all | solution.py:740
  16.8 28.8 %collective-permute-start.2 = (f32[8,128]{1,0:T(8,128)S(1)}, f32[8,128]{1,0:T(8,128)S(1)}, u32[]{:S(2)}, u32[]{:S(2)}) collective-permute-start(f32[8,128]{1,0:T(8,128)S(1)} %reshape_squeeze.6), channel_id=1, source_target_pairs={{0,8},{8,16},{16,24},{1,9},{9,17},{17,25},{2,10},{10,18},{18,26},{... | collective-permute-start | bytes 12296 | tf_op jit(solution)/shard_map/ppermute | solution.py:714
  20.3 25.3 %collective-permute-start.3 = (f32[8,128]{1,0:T(8,128)S(1)}, f32[8,128]{1,0:T(8,128)S(1)}, u32[]{:S(2)}, u32[]{:S(2)}) collective-permute-start(f32[8,128]{1,0:T(8,128)S(1)} %reshape_squeeze.7), channel_id=1, source_target_pairs={{8,0},{16,8},{24,16},{9,1},{17,9},{25,17},{10,2},{18,10},{26,18},{... | collective-permute-start | bytes 12296 | tf_op jit(solution)/shard_map/ppermute | solution.py:714
  22.9 22.7 %collective-permute-start.1 = (f32[4,32,128]{2,1,0:T(8,128)S(1)}, f32[4,32,128]{2,1,0:T(8,128)S(1)}, u32[]{:S(2)}, u32[]{:S(2)}) collective-permute-start(f32[4,32,128]{2,1,0:T(8,128)S(1)} %get-tuple-element.59), channel_id=1, source_target_pairs={{1,0},{2,1},{3,2},{4,3},{5,4},{6,5},{7,6},{9,8},{10,9},{11,10},{12... | collective-permute-start | bytes 196616 | tf_op jit(solution)/shard_map/ppermute | solution.py:714
  24.8 20.8 %collective-permute-start = (f32[4,32,128]{2,1,0:T(8,128)S(1)}, f32[4,32,128]{2,1,0:T(8,128)S(1)}, u32[]{:S(2)}, u32[]{:S(2)}) collective-permute-start(f32[4,32,128]{2,1,0:T(8,128)S(1)} %get-tuple-element.60), channel_id=1, source_target_pairs={{0,1},{1,2},{2,3},{3,4},{4,5},{5,6},{6,7},{8,9},{9,10},{10,11},{11... | collective-permute-start | bytes 196616 | tf_op jit(solution)/shard_map/ppermute | solution.py:714
  27.2 24.0 %copy-start.1 = (f32[6,8192]{1,0:T(8,128)S(1)}, f32[6,8192]{1,0:T(8,128)}, u32[]{:S(2)}) copy-start(f32[6,8192]{1,0:T(8,128)} %motion_ref.3) | copy-start | bytes 589828
  27.3 24.0 %copy-start.2 = (f32[8192]{0:T(1024)S(1)}, f32[8192]{0:T(1024)}, u32[]{:S(2)}) copy-start(f32[8192]{0:T(1024)} %param.13) | copy-start | bytes 98308
  27.3 24.0 %copy-start.4 = (f32[8192]{0:T(1024)S(1)}, f32[8192]{0:T(1024)}, u32[]{:S(2)}) copy-start(f32[8192]{0:T(1024)} %param.12) | copy-start | bytes 98308
  35.5 0.9 copy-start.10
  45.6 19.5 %copy-start.7 = (s32[1,8192]{1,0:T(1,128)S(1)}, s32[1,8192]{1,0:T(1,128)}, u32[]{:S(2)}) copy-start(s32[1,8192]{1,0:T(1,128)} %get-tuple-element.41.slot_ref) | copy-start | bytes 98308
  45.6 19.5 %all-to-all-start.1 = ((f32[32,32,128]{2,1,0:T(8,128)}), f32[32,32,128]{2,1,0:T(8,128)S(1)}, u32[]{:S(2)}, u32[]{:S(2)}) async-start(f32[32,32,128]{2,1,0:T(8,128)} %contact_blocks.1), calls=%async_computation.1 | async-start | bytes 1048576 | tf_op jit(solution)/shard_map/all_to_all | solution.py:757
  51.3 31.4 %copy-start.5 = (s32[8192,1]{0,1:T(1,128)S(1)}, s32[8192,1]{0,1:T(1,128)}, u32[]{:S(2)}) copy-start(s32[8192,1]{0,1:T(1,128)} %param.15) | copy-start | bytes 98308
  51.3 31.4 %copy-start.6 = (s32[32]{0:T(128)S(1)}, s32[32]{0:T(128)}, u32[]{:S(2)}) copy-start(s32[32]{0:T(128)} %owner_ref.3) | copy-start | bytes 388
  51.3 31.4 %copy-start.8 = (s32[1,8192]{1,0:T(1,128)S(1)}, s32[1,8192]{1,0:T(1,128)}, u32[]{:S(2)}) copy-start(s32[1,8192]{1,0:T(1,128)} %get-tuple-element.55.spot_ref) | copy-start | bytes 98308
  51.3 31.4 %copy-start.9 = (s32[16,128]{1,0:T(8,128)S(1)}, s32[16,128]{1,0:T(8,128)}, u32[]{:S(2)}) copy-start(s32[16,128]{1,0:T(8,128)} %get-tuple-element.54.tile_ref) | copy-start | bytes 24580
  71.2 16.3 %collective-permute-start.6 = (f32[10,128]{1,0:T(8,128)S(1)}, f32[10,128]{1,0:T(8,128)S(1)}, u32[]{:S(2)}, u32[]{:S(2)}) collective-permute-start(f32[10,128]{1,0:T(8,128)S(1)} %get-tuple-element.50), channel_id=1, source_target_pairs={{0,8},{8,16},{16,24},{1,9},{9,17},{17,25},{2,10},{10,18},{18,26},{... | collective-permute-start | bytes 15368 | tf_op jit(solution)/shard_map/ppermute | solution.py:714
  74.6 12.9 %collective-permute-start.7 = (f32[10,128]{1,0:T(8,128)S(1)}, f32[10,128]{1,0:T(8,128)S(1)}, u32[]{:S(2)}, u32[]{:S(2)}) collective-permute-start(f32[10,128]{1,0:T(8,128)S(1)} %get-tuple-element.51), channel_id=1, source_target_pairs={{8,0},{16,8},{24,16},{9,1},{17,9},{25,17},{10,2},{18,10},{26,18},{... | collective-permute-start | bytes 15368 | tf_op jit(solution)/shard_map/ppermute | solution.py:714
  77.0 10.5 %collective-permute-start.4 = (f32[5,32,128]{2,1,0:T(8,128)S(1)}, f32[5,32,128]{2,1,0:T(8,128)S(1)}, u32[]{:S(2)}, u32[]{:S(2)}) collective-permute-start(f32[5,32,128]{2,1,0:T(8,128)S(1)} %get-tuple-element.48), channel_id=1, source_target_pairs={{0,1},{1,2},{2,3},{3,4},{4,5},{5,6},{6,7},{8,9},{9,10},{10,11},{11... | collective-permute-start | bytes 245768 | tf_op jit(solution)/shard_map/ppermute | solution.py:714
  79.0 8.5 %collective-permute-start.5 = (f32[5,32,128]{2,1,0:T(8,128)S(1)}, f32[5,32,128]{2,1,0:T(8,128)S(1)}, u32[]{:S(2)}, u32[]{:S(2)}) collective-permute-start(f32[5,32,128]{2,1,0:T(8,128)S(1)} %get-tuple-element.49), channel_id=1, source_target_pairs={{1,0},{2,1},{3,2},{4,3},{5,4},{6,5},{7,6},{9,8},{10,9},{11,10},{12... | collective-permute-start | bytes 245768 | tf_op jit(solution)/shard_map/ppermute | solution.py:714

commit v8 on v7

--- a/solution.py
+++ b/solution.py
@@ -315,7 +315,7 @@
             pl.BlockSpec((step * layers, BLOCK, BLOCK), lambda h: (h, 0, 0)),
         ],
         out_specs=pl.BlockSpec((step, 8 * layers, BLOCK), lambda h: (h, 0, 0)),
-        compiler_params=pltpu.CompilerParams(vmem_limit_bytes=54 << 20),
+        compiler_params=pltpu.CompilerParams(vmem_limit_bytes=40 << 20),
         cost_estimate=pl.CostEstimate(
             flops=64 * blocks * BLOCK * BLOCK, bytes_accessed=blocks * BLOCK * BLOCK * 4, transcendentals=0
         ),
@@ -346,18 +346,26 @@
     return jnp.concatenate(parts, axis=0).reshape(layers, rows, 1)
 
 
-def smooth_field(field_ref, y0_ref, y1_ref, x0_ref, x1_ref, k, edge=None):
+def smooth_field(field_ref, y0_ref, y1_ref, x_first, x_last, k, edge=None):
     at = k if edge is None else edge
     _, layers, rows, cols = field_ref.shape
     per = layers * rows // BLOCK
-    x0 = columns(x0_ref[at * per : (at + 1) * per, :], layers, rows)
-    x1 = columns(x1_ref[at * per : (at + 1) * per, :], layers, rows)
+    x0 = columns(x_first[at * per : (at + 1) * per, :], layers, rows)
+    x1 = columns(x_last[at * per : (at + 1) * per, :], layers, rows)
     y0 = y0_ref[at].reshape(layers, 1, cols)
     y1 = y1_ref[at].reshape(layers, 1, cols)
     return smoothed(field_ref[k], y0, y1, x0, x1)
 
 
-def write_edges(field, k, y0_ref, y1_ref, x0_ref, x1_ref):
+def x_beside(gathered_ref):
+    at = lax.axis_index("gx")
+    last = gathered_ref.shape[0] - 1
+    before = gathered_ref[jnp.maximum(at - 1, 0), 1]
+    after = gathered_ref[jnp.minimum(at + 1, last), 0]
+    return jnp.where(at > 0, before, 0.0), jnp.where(at < last, after, 0.0)
+
+
+def write_edges(field, k, y0_ref, y1_ref, x_ref):
     layers, rows, cols = field.shape
     y0_ref[k] = field[:, 0, :]
     y1_ref[k] = field[:, rows - 1, :]
@@ -365,8 +373,8 @@
     for a in range(layers * rows // BLOCK):
         turned = jnp.transpose(flat[a * BLOCK : (a + 1) * BLOCK, :])
         at = k * (layers * rows // BLOCK) + a
-        x0_ref[at : at + 1, :] = turned[0:1, :]
-        x1_ref[at : at + 1, :] = turned[cols - 1 : cols, :]
+        x_ref[0, at : at + 1, :] = turned[0:1, :]
+        x_ref[1, at : at + 1, :] = turned[cols - 1 : cols, :]
 
 
 def paired_rows(pairs, layers, rows, scratch):
@@ -417,7 +425,7 @@
         seen_ref[:, here] = jnp.concatenate(seen, axis=0)
         return 0
 
-    lax.fori_loop(0, particles // chunk, step, 0)
+    lax.fori_loop(0, particles // chunk, step, 0, unroll=2)
 
 
 def look_up(fluid, cells):
@@ -442,18 +450,19 @@
 
 
 def deposit_kernel(
-    y0_ref, y1_ref, x0_ref, x1_ref, cell_ref, seen_ref, motion_ref, radius_ref, temp_ref,
-    base_ref, dep_ref, dy0_ref, dy1_ref, dx0_ref, dx1_ref, x_table, rows_scratch, acc, *, chunk
+    y0_ref, y1_ref, x_ref, cell_ref, seen_ref, motion_ref, radius_ref, temp_ref,
+    base_ref, dep_ref, dy0_ref, dy1_ref, dx_ref, x_table, rows_scratch, acc, *, chunk
 ):
     fields, layers, rows, cols = dep_ref.shape
     half = layers * rows // 2
     wide = 2 * cols
     particles = cell_ref.shape[1]
     per = layers * rows // BLOCK
+    x_first, x_last = x_beside(x_ref)
     for k in range(fields):
         x_table[k] = jnp.zeros_like(x_table[k])
-        x_table[k, 0:per, :] = x0_ref[k * per : (k + 1) * per, :]
-        x_table[k, per : 2 * per, :] = x1_ref[k * per : (k + 1) * per, :]
+        x_table[k, 0:per, :] = x_first[k * per : (k + 1) * per]
+        x_table[k, per : 2 * per, :] = x_last[k * per : (k + 1) * per]
     acc[...] = jnp.zeros_like(acc)
 
     def step(i, _):
@@ -505,13 +514,13 @@
     for k in range(fields):
         field = paired_rows(acc[k * half : (k + 1) * half, :], layers, rows, rows_scratch)
         dep_ref[k] = field
-        write_edges(field, k, dy0_ref, dy1_ref, dx0_ref, dx1_ref)
+        write_edges(field, k, dy0_ref, dy1_ref, dx_ref)
 
 
 def edge_shapes(fields, layers, rows, cols):
     y_edge = jax.ShapeDtypeStruct((fields, layers, cols), F32)
-    x_edge = jax.ShapeDtypeStruct((fields * layers * rows // BLOCK, BLOCK), F32)
-    return (y_edge, y_edge, x_edge, x_edge)
+    x_edges = jax.ShapeDtypeStruct((2, fields * layers * rows // BLOCK, BLOCK), F32)
+    return (y_edge, y_edge, x_edges)
 
 
 def deposit(halo, cells, seen, motion, radius, temp, grid):
@@ -525,8 +534,8 @@
             jax.ShapeDtypeStruct((8, particles), F32),
             jax.ShapeDtypeStruct((fields,) + grid, F32),
         ) + edge_shapes(fields, layers, rows, cols),
-        in_specs=[vmem] * 9,
-        out_specs=(vmem,) * 6,
+        in_specs=[vmem] * 8,
+        out_specs=(vmem,) * 5,
         scratch_shapes=[
             VMEM((fields, tall, BLOCK), F32),
             VMEM((layers * rows, cols), F32),
@@ -541,8 +550,8 @@
 
 
 def heat_kernel(
-    back_ref, slot_ref, cell_ref, radius_ref, base_ref, ey0_ref, ey1_ref, ex0_ref, ex1_ref,
-    next_ref, dep_ref, dy0_ref, dy1_ref, dx0_ref, dx1_ref,
+    back_ref, slot_ref, cell_ref, radius_ref, base_ref, ey0_ref, ey1_ref, ex_ref,
+    next_ref, dep_ref, dy0_ref, dy1_ref, dx_ref,
     table, acc, rows_scratch, *, chunk, rows
 ):
     devices, tall, _ = back_ref.shape
@@ -570,17 +579,17 @@
         cells = cell_ref[:, here]
         hot_low = hot_columns(wide, cells % wide)
         hot_high = hot(half, cells // wide)
-        parts = jnp.concatenate([hot_high * high, hot_high * low], axis=0)
-        added = lax.dot_general(parts, hot_low, NN, preferred_element_type=F32)
-        acc[...] += added[:half] + added[half:]
+        added = lax.dot_general(hot_high * high, hot_low, NN, preferred_element_type=F32)
+        acc[...] += added + lax.dot_general(hot_high * low, hot_low, NN, preferred_element_type=F32)
         return 0
 
-    lax.fori_loop(0, particles // chunk, step, 0)
+    lax.fori_loop(0, particles // chunk, step, 0, unroll=2)
     field = paired_rows(acc[...], 2 * half // rows, rows, rows_scratch)
     dep_ref[0] = field
-    for edge, out in ((ey0_ref, dy0_ref), (ey1_ref, dy1_ref), (ex0_ref, dx0_ref), (ex1_ref, dx1_ref)):
+    for edge, out in ((ey0_ref, dy0_ref), (ey1_ref, dy1_ref)):
         out[0 : edge.shape[0]] = edge[...]
-    write_edges(field, ey0_ref.shape[0], dy0_ref, dy1_ref, dx0_ref, dx1_ref)
+    dx_ref[:, 0 : ex_ref.shape[1], :] = ex_ref[...]
+    write_edges(field, ey0_ref.shape[0], dy0_ref, dy1_ref, dx_ref)
 
 
 def heat_deposit(back, slot_of, cells, radius, base, edges, grid):
@@ -596,8 +605,8 @@
             jax.ShapeDtypeStruct((1, particles), F32),
             jax.ShapeDtypeStruct((1,) + grid, F32),
         ) + edge_shapes(fields, layers, rows, cols),
-        in_specs=[vmem] * 9,
-        out_specs=(vmem,) * 6,
+        in_specs=[vmem] * 8,
+        out_specs=(vmem,) * 5,
         scratch_shapes=[
             VMEM((devices * back.shape[1] // 8, BLOCK), F32),
             VMEM((half, 2 * cols), F32),
@@ -684,8 +693,8 @@
     )(box_owner, tiles, back, boxes, spots, base, warm)
 
 
-def spread_kernel(dep_ref, heat_ref, y0_ref, y1_ref, x0_ref, x1_ref, fluid_ref, next_ref, void_ref):
-    halo = (y0_ref, y1_ref, x0_ref, x1_ref)
+def spread_kernel(dep_ref, heat_ref, y0_ref, y1_ref, x_ref, fluid_ref, next_ref, void_ref):
+    halo = (y0_ref, y1_ref) + x_beside(x_ref)
     crowding = 1.0 + COUPLING * smooth_field(dep_ref, *halo, 0)
     void_ref[...] = 1.0 / crowding
     for k in range(3):
@@ -699,7 +708,7 @@
     return pl.pallas_call(
         spread_kernel,
         out_shape=(jax.ShapeDtypeStruct(fluid.shape, F32), jax.ShapeDtypeStruct(fluid.shape[1:], F32)),
-        in_specs=[vmem] * 7,
+        in_specs=[vmem] * 6,
         out_specs=(vmem,) * 2,
         compiler_params=pltpu.CompilerParams(vmem_limit_bytes=40 << 20),
         cost_estimate=pl.CostEstimate(flops=20 * fluid.size, bytes_accessed=2 << 20, transcendentals=0),
@@ -707,7 +716,7 @@
     )(dep, heat, *halo, fluid)
 
 
-def halo_of(y_first, y_last, x_first, x_last):
+def halo_of(y_first, y_last, x_edges):
     def moved(value, axis, step):
         size = lax.axis_size(axis)
         pairs = [(i, i + step) for i in range(size) if 0 <= i + step < size]
@@ -716,8 +725,7 @@
     return (
         moved(y_last, "gy", 1),
         moved(y_first, "gy", -1),
-        moved(x_last, "gx", 1),
-        moved(x_first, "gx", -1),
+        lax.all_gather(x_edges, "gx"),
     )
 
 
@@ -743,8 +751,7 @@
     fluid_halo = halo_of(
         fluid[:, :, 0, :],
         fluid[:, :, rows - 1, :],
-        fluid[:, :, :, 0].reshape(-1, BLOCK),
-        fluid[:, :, :, cols - 1].reshape(-1, BLOCK),
+        jnp.stack([fluid[:, :, :, 0].reshape(-1, BLOCK), fluid[:, :, :, cols - 1].reshape(-1, BLOCK)]),
     )
     seen = look_up(fluid, cells)
     arrived, seen = lax.optimization_barrier((arrived, seen))

time: 91.1 us -> 93 us (1.021)
  blocking collectives: 0 us -> 16 us
  starting transfers between devices: 33.2 us -> 20.9 us
  Pallas kernels: 48.7 us -> 44.6 us
  local copies, waits for them, and re-layouts: 1.73 us -> 4.22 us
    all_gather x0 -> x2, blocking collectives: none -> 16 us  [halo_of(): lax.all_gather(x_edges, 'gx')]
    ppermute x8 -> x4, starting transfers between devices: 21.6 us -> 9.89 us  [moved(): return lax.ppermute(value, axis, pairs)]
    unnamed x22, local copies, waits for them, and re-layouts: 0.94 us -> 3.43 us
    pallas_call x1, Pallas kernels: 9.17 us -> 7.46 us  [contact(): pl.pallas_call(contact_kernel, grid=(devices // step,), out_shape=jax.Sha...]
    pallas_call x1, Pallas kernels: 7.98 us -> 6.65 us  [look_up(): pl.pallas_call(functools.partial(look_kernel, chunk=512), out_shape=jax.S...]
    pallas_call x1, Pallas kernels: 6.07 us -> 5.02 us  [heat_deposit(): pl.pallas_call(functools.partial(heat_kernel, chunk=1024, rows=rows), out...]
  transfers between devices with their start and end apart: 10 -> 6, of which waited for: 2 -> 1; matrix products, arithmetic and copies ran while one was open for 1% -> 1% of each run, Pallas kernels for 35% -> 31%
where the time goes in v8:
time: 93 us; the launch traced here: 91.4 us
  Pallas kernels  44.6 us (48%)
  starting transfers between devices  20.9 us (22%)
  blocking collectives  16 us (17%)
  waiting for transfers between devices  4.76 us (5%)
  local copies, waits for them, and re-layouts  4.22 us (5%)
    all_gather x2, blocking collectives, halo_of(): lax.all_gather(x_edges, 'gx')  16 us
    ppermute x4, starting transfers between devices, moved(): return lax.ppermute(value, axis, pairs)  9.89 us
    pallas_call x1, Pallas kernels, place(): pl.pallas_call(place_kernel, out_shape=(jax.ShapeDtypeStruct((devices, 12...  9.53 us
    pallas_call x1, Pallas kernels, deposit(): pl.pallas_call(functools.partial(deposit_kernel, chunk=1024), out_shape=(...  9.05 us
    pallas_call x1, Pallas kernels, contact(): pl.pallas_call(contact_kernel, grid=(devices // step,), out_shape=jax.Sha...  7.46 us
    pallas_call x1, Pallas kernels, look_up(): pl.pallas_call(functools.partial(look_kernel, chunk=512), out_shape=jax.S...  6.65 us
    all_to_all x1, starting transfers between devices, shards(): lax.all_to_all(outgoing, ('gx', 'gy'), split_axis=0, concat_axis=0, tiled...  6.02 us
    pallas_call x1, Pallas kernels, heat_deposit(): pl.pallas_call(functools.partial(heat_kernel, chunk=1024, rows=rows), out...  5.02 us
  transfers between devices with their start and end apart: 6, of which 1 were waited for; matrix products, arithmetic and copies ran while one was open for 1% of the time, Pallas kernels for 31%

profile of v8, /device:TPU:10, one launch (start us, length us, event | category | flops | bytes accessed | tf_op | source)
XLA Modules:
  0.0 91.4 jit_solution(1500117461932255469)
XLA Ops:
  0.7 9.5 %place_slots.1 = (f32[32,48,128]{2,1,0:T(8,128)}, s32[1,8192]{1,0:T(1,128)}, s32[1,8192]{1,0:T(1,128)}, s32[16,128]{1,0:T(8,128)}) custom-call(s32[32]{0:T(128)} %owner_ref.3, s32[1,8192]{1,0:T(1,128)} %bitcast.20, f32[3,8192]{1,0:T(4,128)} %pos_ref.1, f32[6,8192]{1,0:T(8,128)} %motion_ref.3, f32[1,8192]{1,0:T(1,128)} %bitcast.17, f32[1,8192]{1,0:T(1,128)} %bitcast.12), custom_call_target="tpu_custom_call" | custom-call | flops 3221225472 | bytes 1048576 | tf_op jit(solution)/shard_map/place_slots/pallas_call | solution.py:183
  10.2 6.0 %all-to-all-start = ((f32[32,48,128]{2,1,0:T(8,128)}), f32[32,48,128]{2,1,0:T(8,128)S(1)}, u32[]{:S(2)}, u32[]{:S(2)}) async-start(f32[32,48,128]{2,1,0:T(8,128)} %get-tuple-element.27), calls=%async_computation | async-start | bytes 1572864 | tf_op jit(solution)/shard_map/all_to_all | solution.py:748
  16.2 0.1 copy.16
  16.4 2.2 %collective-permute-start.1 = (f32[4,32,128]{2,1,0:T(8,128)S(1)}, f32[4,32,128]{2,1,0:T(8,128)S(1)}, u32[]{:S(2)}, u32[]{:S(2)}) collective-permute-start(f32[4,32,128]{2,1,0:T(8,128)S(1)} %get-tuple-element.53), channel_id=1, source_target_pairs={{1,0},{2,1},{3,2},{4,3},{5,4},{6,5},{7,6},{9,8},{10,9},{11,10},{12... | collective-permute-start | bytes 196616 | tf_op jit(solution)/shard_map/ppermute | solution.py:723
  18.6 2.1 %collective-permute-start = (f32[4,32,128]{2,1,0:T(8,128)S(1)}, f32[4,32,128]{2,1,0:T(8,128)S(1)}, u32[]{:S(2)}, u32[]{:S(2)}) collective-permute-start(f32[4,32,128]{2,1,0:T(8,128)S(1)} %get-tuple-element.54), channel_id=1, source_target_pairs={{0,1},{1,2},{2,3},{3,4},{4,5},{5,6},{6,7},{8,9},{9,10},{10,11},{11... | collective-permute-start | bytes 196616 | tf_op jit(solution)/shard_map/ppermute | solution.py:723
  20.7 0.5 slice_reduce_fusion.1
  21.2 0.1 stack_reshape_squeeze.6
  21.3 0.1 stack_reshape_squeeze.7
  21.4 0.0 copy-start.2
  21.4 0.0 copy-start.3
  21.4 0.0 copy-start.5
  21.4 6.6 %look_up.1.seen_ref = f32[4,8192]{1,0:T(4,128)S(1)} custom-call(f32[4,32,8,128]{3,2,1,0:T(8,128)S(1)} %copy-done.1, s32[1,8192]{1,0:T(1,128)S(1)} %bitcast.14), custom_call_target="tpu_custom_call" | custom-call | flops 2147483648 | bytes 1048576 | tf_op jit(solution)/shard_map/look_up/pallas_call | solution.py:435
  28.1 8.1 %all-gather = f32[8,8,128]{2,1,0:T(8,128)S(1)} all-gather(f32[2,8,128]{2,1,0:T(8,128)S(1)} %pad_maximum_fusion), channel_id=2, replica_groups=mesh['gx'=4,'gy'=8] {'gx'}, dimensions={0}, use_global_device_ids=true | all-gather | bytes 40960 | tf_op jit(solution)/shard_map/all_gather | solution.py:728
  36.2 0.0 all-to-all-done.slot_ref
  36.2 0.0 copy-start
  36.2 3.4 %copy-done = s32[128,128,128]{2,1,0:T(8,128)S(1)} copy-done((s32[128,128,128]{2,1,0:T(8,128)S(1)}, s32[128,128,128]{2,1,0:T(8,128)}, u32[]{:S(2)}) %copy-start) | copy-done | bytes 8388632
  39.6 7.5 %contact_blocks.1 = f32[32,32,128]{2,1,0:T(8,128)} custom-call(f32[32,48,128]{2,1,0:T(8,128)S(1)} %all-to-all-done.slot_ref, s32[128,128,128]{2,1,0:T(8,128)S(1)} %copy-done), custom_call_target="tpu_custom_call" | custom-call | flops 134217728 | bytes 8388608 | tf_op jit(solution)/shard_map/contact_blocks/pallas_call | solution.py:309
  47.1 0.0 collective-permute-done.1.y1_ref
  47.1 0.0 collective-permute-done.y0_ref
  47.1 5.0 %all-to-all-start.1 = ((f32[32,32,128]{2,1,0:T(8,128)}), f32[32,32,128]{2,1,0:T(8,128)S(1)}, u32[]{:S(2)}, u32[]{:S(2)}) async-start(f32[32,32,128]{2,1,0:T(8,128)} %contact_blocks.1), calls=%async_computation.1 | async-start | bytes 1048576 | tf_op jit(solution)/shard_map/all_to_all | solution.py:764
  52.1 0.0 copy-start.6
  52.1 0.0 copy-start.7
  52.2 0.0 copy-start.9
  52.2 9.0 %deposit_fields.1 = (f32[8,8192]{1,0:T(8,128)S(1)}, f32[4,32,8,128]{3,2,1,0:T(8,128)S(1)}, f32[4,32,128]{2,1,0:T(8,128)S(1)}, f32[4,32,128]{2,1,0:T(8,128)S(1)}, f32[2,8,128]{2,1,0:T(8,128)S(1)}) custom-call(f32[4,32,128]{2,1,0:T(8,128)S(1)} %collective-permute-done.y0_ref, f32[4,32,128]{2,1,0:T(8,128)S(1)} %collective-permute-done.1.y1_ref, ...), custom_call_target="tpu_custom_call" | custom-call | flops 4294967296 | bytes 2097152 | tf_op jit(solution)/shard_map/deposit_fields/pallas_call | solution.py:531
  61.2 4.7 %all-to-all-done.1.back_ref = f32[32,32,128]{2,1,0:T(8,128)S(1)} async-done(((f32[32,32,128]{2,1,0:T(8,128)}), f32[32,32,128]{2,1,0:T(8,128)S(1)}, u32[]{:S(2)}, u32[]{:S(2)}) %all-to-all-start.1) | async-done | bytes 524320 | tf_op jit(solution)/shard_map/all_to_all | solution.py:764
  66.0 5.0 %heat_deposit.1 = (f32[1,8192]{1,0:T(1,128)S(1)}, f32[1,32,8,128]{3,2,1,0:T(8,128)S(1)}, f32[5,32,128]{2,1,0:T(8,128)S(1)}, f32[5,32,128]{2,1,0:T(8,128)S(1)}, f32[2,10,128]{2,1,0:T(8,128)S(1)}) custom-call(f32[32,32,128]{2,1,0:T(8,128)S(1)} %all-to-all-done.1.back_ref, s32[1,8192]{1,0:T(1,128)S(1)} %copy-done.8, s32[1,8192]{1,0:T(1,128)S(1)} %bitcast.16, ...), custom_call_target="tpu_custom_call" | custom-call | flops 1073741824 | bytes 1048576 | tf_op jit(solution)/shard_map/heat_deposit/pallas_call | solution.py:602
  71.0 1.9 %collective-permute-start.2 = (f32[5,32,128]{2,1,0:T(8,128)S(1)}, f32[5,32,128]{2,1,0:T(8,128)S(1)}, u32[]{:S(2)}, u32[]{:S(2)}) collective-permute-start(f32[5,32,128]{2,1,0:T(8,128)S(1)} %get-tuple-element.43), channel_id=1, source_target_pairs={{0,1},{1,2},{2,3},{3,4},{4,5},{5,6},{6,7},{8,9},{9,10},{10,11},{11... | collective-permute-start | bytes 245768 | tf_op jit(solution)/shard_map/ppermute | solution.py:723
  72.9 3.6 %collective-permute-start.3 = (f32[5,32,128]{2,1,0:T(8,128)S(1)}, f32[5,32,128]{2,1,0:T(8,128)S(1)}, u32[]{:S(2)}, u32[]{:S(2)}) collective-permute-start(f32[5,32,128]{2,1,0:T(8,128)S(1)} %get-tuple-element.44), channel_id=1, source_target_pairs={{1,0},{2,1},{3,2},{4,3},{5,4},{6,5},{7,6},{9,8},{10,9},{11,10},{12... | collective-permute-start | bytes 245768 | tf_op jit(solution)/shard_map/ppermute | solution.py:723
  76.6 4.8 %fetch_slots.1 = f32[7,8192]{1,0:T(8,128)} custom-call(s32[32]{0:T(128)S(1)} %copy-done.7, s32[16,128]{1,0:T(8,128)S(1)} %copy-done.10, f32[32,32,128]{2,1,0:T(8,128)S(1)} %all-to-all-done.1.back_ref, s32[1,8192]{1,0:T(1,128)S(1)} %bitcast.21, s32[1,8192]{1,0:T(1,128)S(1)} %copy-done.9, f32[8,8192]{1,0:T(8,128)S(1)} %get-tuple-element.38.base_ref, ...), custom_call_target="tpu_custom_call" | custom-call | flops 2147483648 | bytes 1048576 | tf_op jit(solution)/shard_map/fetch_slots/pallas_call | solution.py:679
  81.5 7.9 %all-gather.1 = f32[8,10,128]{2,1,0:T(8,128)S(1)} all-gather(f32[2,10,128]{2,1,0:T(8,128)S(1)} %get-tuple-element.45), channel_id=3, replica_groups=mesh['gx'=4,'gy'=8] {'gx'}, dimensions={0}, use_global_device_ids=true | all-gather | bytes 51200 | tf_op jit(solution)/shard_map/all_gather | solution.py:728
  89.4 0.0 collective-permute-done.3.y1_ref
  89.4 2.0 %spread_fields.1 = (f32[4,32,8,128]{3,2,1,0:T(8,128)}, f32[32,8,128]{2,1,0:T(8,128)}) custom-call(f32[4,32,8,128]{3,2,1,0:T(8,128)S(1)} %get-tuple-element.35.dep_ref, f32[1,32,8,128]{3,2,1,0:T(8,128)S(1)} %get-tuple-element.42.heat_ref, f32[5,32,128]{2,1,0:T(8,128)S(1)} %collective-permute-done.2.y0_ref, f32[5,32,128]{2,1,0:T(8,128)S(1)} %collective-permute-done.3.y1_ref, ...), custom_call_target="tpu_custom_call" | custom-call | flops 2621440 | bytes 2097152 | tf_op jit(solution)/shard_map/spread_fields/pallas_call | solution.py:708
  (17 shorter events, 0.0 us)
Async XLA Ops:
  0.6 15.6 %copy-start.1 = (f32[4,32,8,128]{3,2,1,0:T(8,128)S(1)}, f32[4,32,8,128]{3,2,1,0:T(8,128)}, u32[]{:S(2)}) copy-start(f32[4,32,8,128]{3,2,1,0:T(8,128)} %fluid_ref.2) | copy-start | bytes 1572868
  0.6 20.7 %copy-start.4 = (s32[8192]{0:T(1024)S(1)}, s32[8192]{0:T(1024)}, u32[]{:S(2)}) copy-start(s32[8192]{0:T(1024)} %param.14) | copy-start | bytes 98308
  10.2 26.0 %all-to-all-start = ((f32[32,48,128]{2,1,0:T(8,128)}), f32[32,48,128]{2,1,0:T(8,128)S(1)}, u32[]{:S(2)}, u32[]{:S(2)}) async-start(f32[32,48,128]{2,1,0:T(8,128)} %get-tuple-element.27), calls=%async_computation | async-start | bytes 1572864 | tf_op jit(solution)/shard_map/all_to_all | solution.py:748
  16.4 30.7 %collective-permute-start.1 = (f32[4,32,128]{2,1,0:T(8,128)S(1)}, f32[4,32,128]{2,1,0:T(8,128)S(1)}, u32[]{:S(2)}, u32[]{:S(2)}) collective-permute-start(f32[4,32,128]{2,1,0:T(8,128)S(1)} %get-tuple-element.53), channel_id=1, source_target_pairs={{1,0},{2,1},{3,2},{4,3},{5,4},{6,5},{7,6},{9,8},{10,9},{11,10},{12... | collective-permute-start | bytes 196616 | tf_op jit(solution)/shard_map/ppermute | solution.py:723
  18.6 28.5 %collective-permute-start = (f32[4,32,128]{2,1,0:T(8,128)S(1)}, f32[4,32,128]{2,1,0:T(8,128)S(1)}, u32[]{:S(2)}, u32[]{:S(2)}) collective-permute-start(f32[4,32,128]{2,1,0:T(8,128)S(1)} %get-tuple-element.54), channel_id=1, source_target_pairs={{0,1},{1,2},{2,3},{3,4},{4,5},{5,6},{6,7},{8,9},{9,10},{10,11},{11... | collective-permute-start | bytes 196616 | tf_op jit(solution)/shard_map/ppermute | solution.py:723
  21.4 30.7 %copy-start.2 = (f32[6,8192]{1,0:T(8,128)S(1)}, f32[6,8192]{1,0:T(8,128)}, u32[]{:S(2)}) copy-start(f32[6,8192]{1,0:T(8,128)} %motion_ref.3) | copy-start | bytes 589828
  21.4 30.7 %copy-start.3 = (f32[8192]{0:T(1024)S(1)}, f32[8192]{0:T(1024)}, u32[]{:S(2)}) copy-start(f32[8192]{0:T(1024)} %param.13) | copy-start | bytes 98308
  21.4 30.7 %copy-start.5 = (f32[8192]{0:T(1024)S(1)}, f32[8192]{0:T(1024)}, u32[]{:S(2)}) copy-start(f32[8192]{0:T(1024)} %param.12) | copy-start | bytes 98308
  36.2 3.4 %copy-start = (s32[128,128,128]{2,1,0:T(8,128)S(1)}, s32[128,128,128]{2,1,0:T(8,128)}, u32[]{:S(2)}) copy-start(s32[128,128,128]{2,1,0:T(8,128)} %mask_ref.1) | copy-start | bytes 25165828
  47.1 18.9 %copy-start.8 = (s32[1,8192]{1,0:T(1,128)S(1)}, s32[1,8192]{1,0:T(1,128)}, u32[]{:S(2)}) copy-start(s32[1,8192]{1,0:T(1,128)} %get-tuple-element.37.slot_ref) | copy-start | bytes 98308
  47.1 18.9 %all-to-all-start.1 = ((f32[32,32,128]{2,1,0:T(8,128)}), f32[32,32,128]{2,1,0:T(8,128)S(1)}, u32[]{:S(2)}, u32[]{:S(2)}) async-start(f32[32,32,128]{2,1,0:T(8,128)} %contact_blocks.1), calls=%async_computation.1 | async-start | bytes 1048576 | tf_op jit(solution)/shard_map/all_to_all | solution.py:764
  52.1 24.5 %copy-start.6 = (s32[8192,1]{0,1:T(1,128)S(1)}, s32[8192,1]{0,1:T(1,128)}, u32[]{:S(2)}) copy-start(s32[8192,1]{0,1:T(1,128)} %param.15) | copy-start | bytes 98308
  52.1 24.5 %copy-start.7 = (s32[32]{0:T(128)S(1)}, s32[32]{0:T(128)}, u32[]{:S(2)}) copy-start(s32[32]{0:T(128)} %owner_ref.3) | copy-start | bytes 388
  52.2 24.5 %copy-start.9 = (s32[1,8192]{1,0:T(1,128)S(1)}, s32[1,8192]{1,0:T(1,128)}, u32[]{:S(2)}) copy-start(s32[1,8192]{1,0:T(1,128)} %get-tuple-element.49.spot_ref) | copy-start | bytes 98308
  52.2 24.5 %copy-start.10 = (s32[16,128]{1,0:T(8,128)S(1)}, s32[16,128]{1,0:T(8,128)}, u32[]{:S(2)}) copy-start(s32[16,128]{1,0:T(8,128)} %get-tuple-element.48.tile_ref) | copy-start | bytes 24580
  71.0 18.4 %collective-permute-start.2 = (f32[5,32,128]{2,1,0:T(8,128)S(1)}, f32[5,32,128]{2,1,0:T(8,128)S(1)}, u32[]{:S(2)}, u32[]{:S(2)}) collective-permute-start(f32[5,32,128]{2,1,0:T(8,128)S(1)} %get-tuple-element.43), channel_id=1, source_target_pairs={{0,1},{1,2},{2,3},{3,4},{4,5},{5,6},{6,7},{8,9},{9,10},{10,11},{11... | collective-permute-start | bytes 245768 | tf_op jit(solution)/shard_map/ppermute | solution.py:723
  72.9 16.4 %collective-permute-start.3 = (f32[5,32,128]{2,1,0:T(8,128)S(1)}, f32[5,32,128]{2,1,0:T(8,128)S(1)}, u32[]{:S(2)}, u32[]{:S(2)}) collective-permute-start(f32[5,32,128]{2,1,0:T(8,128)S(1)} %get-tuple-element.44), channel_id=1, source_target_pairs={{1,0},{2,1},{3,2},{4,3},{5,4},{6,5},{7,6},{9,8},{10,9},{11,10},{12... | collective-permute-start | bytes 245768 | tf_op jit(solution)/shard_map/ppermute | solution.py:723

commit v9 on v7

--- a/solution.py
+++ b/solution.py
@@ -315,7 +315,7 @@
             pl.BlockSpec((step * layers, BLOCK, BLOCK), lambda h: (h, 0, 0)),
         ],
         out_specs=pl.BlockSpec((step, 8 * layers, BLOCK), lambda h: (h, 0, 0)),
-        compiler_params=pltpu.CompilerParams(vmem_limit_bytes=54 << 20),
+        compiler_params=pltpu.CompilerParams(vmem_limit_bytes=32 << 20),
         cost_estimate=pl.CostEstimate(
             flops=64 * blocks * BLOCK * BLOCK, bytes_accessed=blocks * BLOCK * BLOCK * 4, transcendentals=0
         ),
@@ -389,7 +389,9 @@
     return [jnp.sum(jnp.where(mine, value, 0.0), axis=0, keepdims=True) for value in found]
 
 
-def look_kernel(fluid_ref, cell_ref, seen_ref, table, rows_scratch, *, chunk):
+def look_kernel(fluid_ref, cell_ref, mask_ref, seen_ref, mask_out, table, rows_scratch, done, *, chunk):
+    copy = pltpu.make_async_copy(mask_ref, mask_out, done)
+    copy.start()
     fields, layers, rows, cols = fluid_ref.shape
     particles = cell_ref.shape[1]
     half = layers * rows // 2
@@ -417,28 +419,34 @@
         seen_ref[:, here] = jnp.concatenate(seen, axis=0)
         return 0
 
-    lax.fori_loop(0, particles // chunk, step, 0)
-
-
-def look_up(fluid, cells):
+    lax.fori_loop(0, particles // chunk, step, 0, unroll=2)
+    copy.wait()
+
+
+def look_up(fluid, cells, mask):
     fields, layers, rows, cols = fluid.shape
     particles = cells.shape[1]
     vmem = pl.BlockSpec(memory_space=VMEM)
+    anywhere = pl.BlockSpec(memory_space=pl.ANY)
     return pl.pallas_call(
         functools.partial(look_kernel, chunk=512),
-        out_shape=jax.ShapeDtypeStruct((fields, particles), F32),
-        in_specs=[vmem] * 2,
-        out_specs=vmem,
+        out_shape=(
+            jax.ShapeDtypeStruct((fields, particles), F32),
+            jax.ShapeDtypeStruct(mask.shape, mask.dtype),
+        ),
+        in_specs=[vmem, vmem, anywhere],
+        out_specs=(vmem, anywhere),
         scratch_shapes=[
             VMEM((fields * layers * rows // 2, 4 * cols), BF16),
             VMEM((layers * rows, cols), F32),
+            pltpu.SemaphoreType.DMA,
         ],
-        compiler_params=pltpu.CompilerParams(vmem_limit_bytes=40 << 20),
+        compiler_params=pltpu.CompilerParams(vmem_limit_bytes=32 << 20),
         cost_estimate=pl.CostEstimate(
             flops=8 * fields * layers * rows * cols * particles // 4, bytes_accessed=1 << 20, transcendentals=0
         ),
         name="look_up",
-    )(fluid, cells)
+    )(fluid, cells, mask)
 
 
 def deposit_kernel(
@@ -570,12 +578,11 @@
         cells = cell_ref[:, here]
         hot_low = hot_columns(wide, cells % wide)
         hot_high = hot(half, cells // wide)
-        parts = jnp.concatenate([hot_high * high, hot_high * low], axis=0)
-        added = lax.dot_general(parts, hot_low, NN, preferred_element_type=F32)
-        acc[...] += added[:half] + added[half:]
+        added = lax.dot_general(hot_high * high, hot_low, NN, preferred_element_type=F32)
+        acc[...] += added + lax.dot_general(hot_high * low, hot_low, NN, preferred_element_type=F32)
         return 0
 
-    lax.fori_loop(0, particles // chunk, step, 0)
+    lax.fori_loop(0, particles // chunk, step, 0, unroll=2)
     field = paired_rows(acc[...], 2 * half // rows, rows, rows_scratch)
     dep_ref[0] = field
     for edge, out in ((ey0_ref, dy0_ref), (ey1_ref, dy1_ref), (ex0_ref, dx0_ref), (ex1_ref, dx1_ref)):
@@ -746,9 +753,9 @@
         fluid[:, :, :, 0].reshape(-1, BLOCK),
         fluid[:, :, :, cols - 1].reshape(-1, BLOCK),
     )
-    seen = look_up(fluid, cells)
-    arrived, seen = lax.optimization_barrier((arrived, seen))
-    result = contact(arrived, contact_mask)
+    seen, mask = look_up(fluid, cells, contact_mask)
+    arrived, seen, mask = lax.optimization_barrier((arrived, seen, mask))
+    result = contact(arrived, mask)
 
     result, *fluid_halo = lax.optimization_barrier((result,) + tuple(fluid_halo))
     base, deposits, *edges = deposit(

time: 91.1 us -> 98 us (1.076)
  local copies, waits for them, and re-layouts: 1.73 us -> 10.9 us
  Pallas kernels: 48.7 us -> 45.3 us
  starting transfers between devices: 33.2 us -> 34.7 us
    unnamed x22 -> x26, local copies, waits for them, and re-layouts: 0.94 us -> 10.1 us
    pallas_call x1, Pallas kernels: 9.17 us -> 7.47 us  [contact(): pl.pallas_call(contact_kernel, grid=(devices // step,), out_shape=jax.Sha...]
    ppermute x8, starting transfers between devices: 21.6 us -> 22.8 us  [moved(): return lax.ppermute(value, axis, pairs)]
    pallas_call x1, Pallas kernels: 6.07 us -> 5.02 us  [heat_deposit(): pl.pallas_call(functools.partial(heat_kernel, chunk=1024, rows=rows), out...]
  transfers between devices with their start and end apart: 10 -> 10, of which waited for: 2 -> 1; matrix products, arithmetic and copies ran while one was open for 1% -> 1% of each run, Pallas kernels for 35% -> 30%
where the time goes in v9:
time: 98 us; the launch traced here: 96.5 us
  Pallas kernels  45.3 us (46%)
  starting transfers between devices  34.7 us (35%)
  local copies, waits for them, and re-layouts  10.9 us (11%)
  waiting for transfers between devices  4.76 us (5%)
    ppermute x8, starting transfers between devices, moved(): return lax.ppermute(value, axis, pairs)  22.8 us
    unnamed x26, local copies, waits for them, and re-layouts  10.1 us
    pallas_call x1, Pallas kernels, place(): pl.pallas_call(place_kernel, out_shape=(jax.ShapeDtypeStruct((devices, 12...  9.63 us
    pallas_call x1, Pallas kernels, deposit(): pl.pallas_call(functools.partial(deposit_kernel, chunk=1024), out_shape=(...  9.06 us
    pallas_call x1, Pallas kernels, contact(): pl.pallas_call(contact_kernel, grid=(devices // step,), out_shape=jax.Sha...  7.47 us
    pallas_call x1, Pallas kernels, look_up(): pl.pallas_call(functools.partial(look_kernel, chunk=512), out_shape=(jax....  7.23 us
    all_to_all x1, starting transfers between devices, shards(): lax.all_to_all(outgoing, ('gx', 'gy'), split_axis=0, concat_axis=0, tiled...  6.02 us
    all_to_all x1, starting transfers between devices, shards(): lax.all_to_all(result, ('gx', 'gy'), split_axis=0, concat_axis=0, tiled=T...  5.83 us
  transfers between devices with their start and end apart: 10, of which 1 were waited for; matrix products, arithmetic and copies ran while one was open for 1% of the time, Pallas kernels for 30%

profile of v9, /device:TPU:10, one launch (start us, length us, event | category | flops | bytes accessed | tf_op | source)
XLA Modules:
  0.0 96.5 jit_solution(3317492781208889750)
XLA Ops:
  0.7 9.6 %place_slots.1 = (f32[32,48,128]{2,1,0:T(8,128)}, s32[1,8192]{1,0:T(1,128)}, s32[1,8192]{1,0:T(1,128)}, s32[16,128]{1,0:T(8,128)}) custom-call(s32[32]{0:T(128)} %owner_ref.3, s32[1,8192]{1,0:T(1,128)} %bitcast.16, f32[3,8192]{1,0:T(4,128)} %pos_ref.1, f32[6,8192]{1,0:T(8,128)} %motion_ref.3, f32[1,8192]{1,0:T(1,128)} %bitcast.13, f32[1,8192]{1,0:T(1,128)} %bitcast.11), custom_call_target="tpu_custom_call" | custom-call | flops 3221225472 | bytes 1048576 | tf_op jit(solution)/shard_map/place_slots/pallas_call | solution.py:183
  10.3 6.0 %all-to-all-start = ((f32[32,48,128]{2,1,0:T(8,128)}), f32[32,48,128]{2,1,0:T(8,128)S(1)}, u32[]{:S(2)}, u32[]{:S(2)}) async-start(f32[32,48,128]{2,1,0:T(8,128)} %get-tuple-element.33), calls=%async_computation | async-start | bytes 1572864 | tf_op jit(solution)/shard_map/all_to_all | solution.py:747
  16.3 0.1 copy.14
  16.5 2.1 %collective-permute-start = (f32[4,32,128]{2,1,0:T(8,128)S(1)}, f32[4,32,128]{2,1,0:T(8,128)S(1)}, u32[]{:S(2)}, u32[]{:S(2)}) collective-permute-start(f32[4,32,128]{2,1,0:T(8,128)S(1)} %get-tuple-element.66), channel_id=1, source_target_pairs={{0,1},{1,2},{2,3},{3,4},{4,5},{5,6},{6,7},{8,9},{9,10},{10,11},{11... | collective-permute-start | bytes 196616 | tf_op jit(solution)/shard_map/ppermute | solution.py:721
  18.5 3.5 %collective-permute-start.1 = (f32[4,32,128]{2,1,0:T(8,128)S(1)}, f32[4,32,128]{2,1,0:T(8,128)S(1)}, u32[]{:S(2)}, u32[]{:S(2)}) collective-permute-start(f32[4,32,128]{2,1,0:T(8,128)S(1)} %get-tuple-element.65), channel_id=1, source_target_pairs={{1,0},{2,1},{3,2},{4,3},{5,4},{6,5},{7,6},{9,8},{10,9},{11,10},{12... | collective-permute-start | bytes 196616 | tf_op jit(solution)/shard_map/ppermute | solution.py:721
  22.0 0.5 slice_reduce_fusion
  22.5 0.1 reshape_squeeze.6
  22.6 3.4 %collective-permute-start.2 = (f32[8,128]{1,0:T(8,128)S(1)}, f32[8,128]{1,0:T(8,128)S(1)}, u32[]{:S(2)}, u32[]{:S(2)}) collective-permute-start(f32[8,128]{1,0:T(8,128)S(1)} %reshape_squeeze.6), channel_id=1, source_target_pairs={{0,8},{8,16},{16,24},{1,9},{9,17},{17,25},{2,10},{10,18},{18,26},{... | collective-permute-start | bytes 12296 | tf_op jit(solution)/shard_map/ppermute | solution.py:721
  26.0 0.1 reshape_squeeze.7
  26.1 2.5 %collective-permute-start.3 = (f32[8,128]{1,0:T(8,128)S(1)}, f32[8,128]{1,0:T(8,128)S(1)}, u32[]{:S(2)}, u32[]{:S(2)}) collective-permute-start(f32[8,128]{1,0:T(8,128)S(1)} %reshape_squeeze.7), channel_id=1, source_target_pairs={{8,0},{16,8},{24,16},{9,1},{17,9},{25,17},{10,2},{18,10},{26,18},{... | collective-permute-start | bytes 12296 | tf_op jit(solution)/shard_map/ppermute | solution.py:721
  28.6 0.0 copy-start.3
  28.6 3.4 %copy-done.3 = s32[128,128,128]{2,1,0:T(8,128)S(1)} copy-done((s32[128,128,128]{2,1,0:T(8,128)S(1)}, s32[128,128,128]{2,1,0:T(8,128)}, u32[]{:S(2)}) %copy-start.3) | copy-done | bytes 8388632
  32.0 7.2 %look_up.1 = (f32[4,8192]{1,0:T(4,128)S(1)}, s32[128,128,128]{2,1,0:T(8,128)S(1)}) custom-call(f32[4,32,8,128]{3,2,1,0:T(8,128)S(1)} %copy-done, s32[1,8192]{1,0:T(1,128)S(1)} %bitcast.8, s32[128,128,128]{2,1,0:T(8,128)S(1)} %copy-done.3), custom_call_target="tpu_custom_call" | custom-call | flops 2147483648 | bytes 1048576 | tf_op jit(solution)/shard_map/look_up/pallas_call | solution.py:431
  39.2 3.3 %copy-done.1 = s32[128,128,128]{2,1,0:T(8,128)} copy-done((s32[128,128,128]{2,1,0:T(8,128)}, s32[128,128,128]{2,1,0:T(8,128)S(1)}, u32[]{:S(2)}) %copy-start.1) | copy-done | bytes 8388632
  42.5 3.4 %copy-done.2 = s32[128,128,128]{2,1,0:T(8,128)S(1)} copy-done((s32[128,128,128]{2,1,0:T(8,128)S(1)}, s32[128,128,128]{2,1,0:T(8,128)}, u32[]{:S(2)}) %copy-start.2) | copy-done | bytes 8388632
  45.9 7.5 %contact_blocks.1 = f32[32,32,128]{2,1,0:T(8,128)} custom-call(f32[32,48,128]{2,1,0:T(8,128)S(1)} %all-to-all-done.slot_ref, s32[128,128,128]{2,1,0:T(8,128)S(1)} %copy-done.2), custom_call_target="tpu_custom_call" | custom-call | flops 134217728 | bytes 8388608 | tf_op jit(solution)/shard_map/contact_blocks/pallas_call | solution.py:309
  53.3 0.0 collective-permute-done.2.x0_ref
  53.3 0.0 collective-permute-done.3.x1_ref
  53.4 0.0 collective-permute-done.1.y1_ref
  53.4 5.8 %all-to-all-start.1 = ((f32[32,32,128]{2,1,0:T(8,128)}), f32[32,32,128]{2,1,0:T(8,128)S(1)}, u32[]{:S(2)}, u32[]{:S(2)}) async-start(f32[32,32,128]{2,1,0:T(8,128)} %contact_blocks.1), calls=%async_computation.1 | async-start | bytes 1048576 | tf_op jit(solution)/shard_map/all_to_all | solution.py:764
  59.2 0.0 copy-start.8
  59.2 0.0 copy-start.9
  59.3 0.0 copy-start.11
  59.3 9.1 %deposit_fields.1 = (f32[8,8192]{1,0:T(8,128)S(1)}, f32[4,32,8,128]{3,2,1,0:T(8,128)S(1)}, f32[4,32,128]{2,1,0:T(8,128)S(1)}, f32[4,32,128]{2,1,0:T(8,128)S(1)},...) custom-call(f32[4,32,128]{2,1,0:T(8,128)S(1)} %collective-permute-done.y0_ref, ...), custom_call_target="tpu_custom_call" | custom-call | flops 4294967296 | bytes 2097152 | tf_op jit(solution)/shard_map/deposit_fields/pallas_call | solution.py:530
  68.4 4.7 %all-to-all-done.1.back_ref = f32[32,32,128]{2,1,0:T(8,128)S(1)} async-done(((f32[32,32,128]{2,1,0:T(8,128)}), f32[32,32,128]{2,1,0:T(8,128)S(1)}, u32[]{:S(2)}, u32[]{:S(2)}) %all-to-all-start.1) | async-done | bytes 524320 | tf_op jit(solution)/shard_map/all_to_all | solution.py:764
  73.1 5.0 %heat_deposit.1 = (f32[1,8192]{1,0:T(1,128)S(1)}, f32[1,32,8,128]{3,2,1,0:T(8,128)S(1)}, f32[5,32,128]{2,1,0:T(8,128)S(1)}, f32[5,32,128]{2,1,0:T(8,128)S(1)}, f...) custom-call(f32[32,32,128]{2,1,0:T(8,128)S(1)} %all-to-all-done.1.back_ref, s32[1,8192]{1,0:T(1,128)S(1)} %copy-done.10, ...), custom_call_target="tpu_custom_call" | custom-call | flops 1073741824 | bytes 1048576 | tf_op jit(solution)/shard_map/heat_deposit/pallas_call | solution.py:600
  78.1 1.9 %collective-permute-start.4 = (f32[5,32,128]{2,1,0:T(8,128)S(1)}, f32[5,32,128]{2,1,0:T(8,128)S(1)}, u32[]{:S(2)}, u32[]{:S(2)}) collective-permute-start(f32[5,32,128]{2,1,0:T(8,128)S(1)} %get-tuple-element.54), channel_id=1, source_target_pairs={{0,1},{1,2},{2,3},{3,4},{4,5},{5,6},{6,7},{8,9},{9,10},{10,11},{11... | collective-permute-start | bytes 245768 | tf_op jit(solution)/shard_map/ppermute | solution.py:721
  80.0 3.6 %collective-permute-start.5 = (f32[5,32,128]{2,1,0:T(8,128)S(1)}, f32[5,32,128]{2,1,0:T(8,128)S(1)}, u32[]{:S(2)}, u32[]{:S(2)}) collective-permute-start(f32[5,32,128]{2,1,0:T(8,128)S(1)} %get-tuple-element.55), channel_id=1, source_target_pairs={{1,0},{2,1},{3,2},{4,3},{5,4},{6,5},{7,6},{9,8},{10,9},{11,10},{12... | collective-permute-start | bytes 245768 | tf_op jit(solution)/shard_map/ppermute | solution.py:721
  83.7 3.4 %collective-permute-start.6 = (f32[10,128]{1,0:T(8,128)S(1)}, f32[10,128]{1,0:T(8,128)S(1)}, u32[]{:S(2)}, u32[]{:S(2)}) collective-permute-start(f32[10,128]{1,0:T(8,128)S(1)} %get-tuple-element.56), channel_id=1, source_target_pairs={{0,8},{8,16},{16,24},{1,9},{9,17},{17,25},{2,10},{10,18},{18,26},{... | collective-permute-start | bytes 15368 | tf_op jit(solution)/shard_map/ppermute | solution.py:721
  87.1 2.5 %collective-permute-start.7 = (f32[10,128]{1,0:T(8,128)S(1)}, f32[10,128]{1,0:T(8,128)S(1)}, u32[]{:S(2)}, u32[]{:S(2)}) collective-permute-start(f32[10,128]{1,0:T(8,128)S(1)} %get-tuple-element.57), channel_id=1, source_target_pairs={{8,0},{16,8},{24,16},{9,1},{17,9},{25,17},{10,2},{18,10},{26,18},{... | collective-permute-start | bytes 15368 | tf_op jit(solution)/shard_map/ppermute | solution.py:721
  89.6 4.8 %fetch_slots.1 = f32[7,8192]{1,0:T(8,128)} custom-call(s32[32]{0:T(128)S(1)} %copy-done.9, s32[16,128]{1,0:T(8,128)S(1)} %copy-done.12, f32[32,32,128]{2,1,0:T(8,128)S(1)} %all-to-all-done.1.back_ref, s32[1,8192]{1,0:T(1,128)S(1)} %bitcast.17, s32[1,8192]{1,0:T(1,128)S(1)} %copy-done.11, f32[8,8192]{1,0:T(8,128)S(1)} %get-tuple-element.48.base_ref, ...), custom_call_target="tpu_custom_call" | custom-call | flops 2147483648 | bytes 1048576 | tf_op jit(solution)/shard_map/fetch_slots/pallas_call | solution.py:677
  94.5 2.0 %spread_fields.1 = (f32[4,32,8,128]{3,2,1,0:T(8,128)}, f32[32,8,128]{2,1,0:T(8,128)}) custom-call(f32[4,32,8,128]{3,2,1,0:T(8,128)S(1)} %get-tuple-element.45.dep_ref, f32[1,32,8,128]{3,2,1,0:T(8,128)S(1)} %get-tuple-element.53.heat_ref, f32[5,32,128]{2,1,0:T(8,128)S(1)} %collective-permute-done.4.y0_ref, f32[5,32,128]{2,1,0:T(8,128)S(1)} %collective-permute-done.5.y1_ref, ...), custom_call_target="tpu_custom_call" | custom-call | flops 2621440 | bytes 2097152 | tf_op jit(solution)/shard_map/spread_fields/pallas_call | solution.py:706
  (26 shorter events, 0.1 us)
Async XLA Ops:
  0.6 15.7 %copy-start = (f32[4,32,8,128]{3,2,1,0:T(8,128)S(1)}, f32[4,32,8,128]{3,2,1,0:T(8,128)}, u32[]{:S(2)}) copy-start(f32[4,32,8,128]{3,2,1,0:T(8,128)} %fluid_ref.2) | copy-start | bytes 1572868
  0.6 27.9 %copy-start.4 = (s32[8192]{0:T(1024)S(1)}, s32[8192]{0:T(1024)}, u32[]{:S(2)}) copy-start(s32[8192]{0:T(1024)} %param.14) | copy-start | bytes 98308
  10.3 32.2 %all-to-all-start = ((f32[32,48,128]{2,1,0:T(8,128)}), f32[32,48,128]{2,1,0:T(8,128)S(1)}, u32[]{:S(2)}, u32[]{:S(2)}) async-start(f32[32,48,128]{2,1,0:T(8,128)} %get-tuple-element.33), calls=%async_computation | async-start | bytes 1572864 | tf_op jit(solution)/shard_map/all_to_all | solution.py:747
  16.5 36.9 %collective-permute-start = (f32[4,32,128]{2,1,0:T(8,128)S(1)}, f32[4,32,128]{2,1,0:T(8,128)S(1)}, u32[]{:S(2)}, u32[]{:S(2)}) collective-permute-start(f32[4,32,128]{2,1,0:T(8,128)S(1)} %get-tuple-element.66), channel_id=1, source_target_pairs={{0,1},{1,2},{2,3},{3,4},{4,5},{5,6},{6,7},{8,9},{9,10},{10,11},{11... | collective-permute-start | bytes 196616 | tf_op jit(solution)/shard_map/ppermute | solution.py:721
  18.5 34.8 %collective-permute-start.1 = (f32[4,32,128]{2,1,0:T(8,128)S(1)}, f32[4,32,128]{2,1,0:T(8,128)S(1)}, u32[]{:S(2)}, u32[]{:S(2)}) collective-permute-start(f32[4,32,128]{2,1,0:T(8,128)S(1)} %get-tuple-element.65), channel_id=1, source_target_pairs={{1,0},{2,1},{3,2},{4,3},{5,4},{6,5},{7,6},{9,8},{10,9},{11,10},{12... | collective-permute-start | bytes 196616 | tf_op jit(solution)/shard_map/ppermute | solution.py:721
  22.6 30.7 %collective-permute-start.2 = (f32[8,128]{1,0:T(8,128)S(1)}, f32[8,128]{1,0:T(8,128)S(1)}, u32[]{:S(2)}, u32[]{:S(2)}) collective-permute-start(f32[8,128]{1,0:T(8,128)S(1)} %reshape_squeeze.6), channel_id=1, source_target_pairs={{0,8},{8,16},{16,24},{1,9},{9,17},{17,25},{2,10},{10,18},{18,26},{... | collective-permute-start | bytes 12296 | tf_op jit(solution)/shard_map/ppermute | solution.py:721
  26.1 27.2 %collective-permute-start.3 = (f32[8,128]{1,0:T(8,128)S(1)}, f32[8,128]{1,0:T(8,128)S(1)}, u32[]{:S(2)}, u32[]{:S(2)}) collective-permute-start(f32[8,128]{1,0:T(8,128)S(1)} %reshape_squeeze.7), channel_id=1, source_target_pairs={{8,0},{16,8},{24,16},{9,1},{17,9},{25,17},{10,2},{18,10},{26,18},{... | collective-permute-start | bytes 12296 | tf_op jit(solution)/shard_map/ppermute | solution.py:721
  28.6 3.4 %copy-start.3 = (s32[128,128,128]{2,1,0:T(8,128)S(1)}, s32[128,128,128]{2,1,0:T(8,128)}, u32[]{:S(2)}) copy-start(s32[128,128,128]{2,1,0:T(8,128)} %mask_ref.1) | copy-start | bytes 25165828
  32.0 27.2 %copy-start.5 = (f32[6,8192]{1,0:T(8,128)S(1)}, f32[6,8192]{1,0:T(8,128)}, u32[]{:S(2)}) copy-start(f32[6,8192]{1,0:T(8,128)} %motion_ref.3) | copy-start | bytes 589828
  32.0 27.2 %copy-start.6 = (f32[8192]{0:T(1024)S(1)}, f32[8192]{0:T(1024)}, u32[]{:S(2)}) copy-start(f32[8192]{0:T(1024)} %param.13) | copy-start | bytes 98308
  32.0 27.3 %copy-start.7 = (f32[8192]{0:T(1024)S(1)}, f32[8192]{0:T(1024)}, u32[]{:S(2)}) copy-start(f32[8192]{0:T(1024)} %param.12) | copy-start | bytes 98308
  39.2 3.3 %copy-start.1 = (s32[128,128,128]{2,1,0:T(8,128)}, s32[128,128,128]{2,1,0:T(8,128)S(1)}, u32[]{:S(2)}) copy-start(s32[128,128,128]{2,1,0:T(8,128)S(1)} %get-tuple-element.39.mask_ref) | copy-start | bytes 25165828
  42.5 3.4 %copy-start.2 = (s32[128,128,128]{2,1,0:T(8,128)S(1)}, s32[128,128,128]{2,1,0:T(8,128)}, u32[]{:S(2)}) copy-start(s32[128,128,128]{2,1,0:T(8,128)} %copy-done.1) | copy-start | bytes 25165828
  53.3 19.8 %copy-start.10 = (s32[1,8192]{1,0:T(1,128)S(1)}, s32[1,8192]{1,0:T(1,128)}, u32[]{:S(2)}) copy-start(s32[1,8192]{1,0:T(1,128)} %get-tuple-element.47.slot_ref) | copy-start | bytes 98308
  53.4 19.7 %all-to-all-start.1 = ((f32[32,32,128]{2,1,0:T(8,128)}), f32[32,32,128]{2,1,0:T(8,128)S(1)}, u32[]{:S(2)}, u32[]{:S(2)}) async-start(f32[32,32,128]{2,1,0:T(8,128)} %contact_blocks.1), calls=%async_computation.1 | async-start | bytes 1048576 | tf_op jit(solution)/shard_map/all_to_all | solution.py:764
  59.2 30.3 %copy-start.8 = (s32[8192,1]{0,1:T(1,128)S(1)}, s32[8192,1]{0,1:T(1,128)}, u32[]{:S(2)}) copy-start(s32[8192,1]{0,1:T(1,128)} %param.15) | copy-start | bytes 98308
  59.2 30.3 %copy-start.9 = (s32[32]{0:T(128)S(1)}, s32[32]{0:T(128)}, u32[]{:S(2)}) copy-start(s32[32]{0:T(128)} %owner_ref.3) | copy-start | bytes 388
  59.3 30.3 %copy-start.11 = (s32[1,8192]{1,0:T(1,128)S(1)}, s32[1,8192]{1,0:T(1,128)}, u32[]{:S(2)}) copy-start(s32[1,8192]{1,0:T(1,128)} %get-tuple-element.61.spot_ref) | copy-start | bytes 98308
  59.3 30.3 %copy-start.12 = (s32[16,128]{1,0:T(8,128)S(1)}, s32[16,128]{1,0:T(8,128)}, u32[]{:S(2)}) copy-start(s32[16,128]{1,0:T(8,128)} %get-tuple-element.60.tile_ref) | copy-start | bytes 24580
  78.1 16.3 %collective-permute-start.4 = (f32[5,32,128]{2,1,0:T(8,128)S(1)}, f32[5,32,128]{2,1,0:T(8,128)S(1)}, u32[]{:S(2)}, u32[]{:S(2)}) collective-permute-start(f32[5,32,128]{2,1,0:T(8,128)S(1)} %get-tuple-element.54), channel_id=1, source_target_pairs={{0,1},{1,2},{2,3},{3,4},{4,5},{5,6},{6,7},{8,9},{9,10},{10,11},{11... | collective-permute-start | bytes 245768 | tf_op jit(solution)/shard_map/ppermute | solution.py:721
  80.0 14.4 %collective-permute-start.5 = (f32[5,32,128]{2,1,0:T(8,128)S(1)}, f32[5,32,128]{2,1,0:T(8,128)S(1)}, u32[]{:S(2)}, u32[]{:S(2)}) collective-permute-start(f32[5,32,128]{2,1,0:T(8,128)S(1)} %get-tuple-element.55), channel_id=1, source_target_pairs={{1,0},{2,1},{3,2},{4,3},{5,4},{6,5},{7,6},{9,8},{10,9},{11,10},{12... | collective-permute-start | bytes 245768 | tf_op jit(solution)/shard_map/ppermute | solution.py:721
  83.7 10.7 %collective-permute-start.6 = (f32[10,128]{1,0:T(8,128)S(1)}, f32[10,128]{1,0:T(8,128)S(1)}, u32[]{:S(2)}, u32[]{:S(2)}) collective-permute-start(f32[10,128]{1,0:T(8,128)S(1)} %get-tuple-element.56), channel_id=1, source_target_pairs={{0,8},{8,16},{16,24},{1,9},{9,17},{17,25},{2,10},{10,18},{18,26},{... | collective-permute-start | bytes 15368 | tf_op jit(solution)/shard_map/ppermute | solution.py:721
  87.1 7.4 %collective-permute-start.7 = (f32[10,128]{1,0:T(8,128)S(1)}, f32[10,128]{1,0:T(8,128)S(1)}, u32[]{:S(2)}, u32[]{:S(2)}) collective-permute-start(f32[10,128]{1,0:T(8,128)S(1)} %get-tuple-element.57), channel_id=1, source_target_pairs={{8,0},{16,8},{24,16},{9,1},{17,9},{25,17},{10,2},{18,10},{26,18},{... | collective-permute-start | bytes 15368 | tf_op jit(solution)/shard_map/ppermute | solution.py:721

commit v10 on v7

--- a/solution.py
+++ b/solution.py
@@ -417,7 +417,7 @@
         seen_ref[:, here] = jnp.concatenate(seen, axis=0)
         return 0
 
-    lax.fori_loop(0, particles // chunk, step, 0)
+    lax.fori_loop(0, particles // chunk, step, 0, unroll=2)
 
 
 def look_up(fluid, cells):
@@ -570,12 +570,11 @@
         cells = cell_ref[:, here]
         hot_low = hot_columns(wide, cells % wide)
         hot_high = hot(half, cells // wide)
-        parts = jnp.concatenate([hot_high * high, hot_high * low], axis=0)
-        added = lax.dot_general(parts, hot_low, NN, preferred_element_type=F32)
-        acc[...] += added[:half] + added[half:]
+        added = lax.dot_general(hot_high * high, hot_low, NN, preferred_element_type=F32)
+        acc[...] += added + lax.dot_general(hot_high * low, hot_low, NN, preferred_element_type=F32)
         return 0
 
-    lax.fori_loop(0, particles // chunk, step, 0)
+    lax.fori_loop(0, particles // chunk, step, 0, unroll=2)
     field = paired_rows(acc[...], 2 * half // rows, rows, rows_scratch)
     dep_ref[0] = field
     for edge, out in ((ey0_ref, dy0_ref), (ey1_ref, dy1_ref), (ex0_ref, dx0_ref), (ex1_ref, dx1_ref)):

time: 91.1 us -> 89.8 us (0.986)
  Pallas kernels: 48.7 us -> 46.3 us
  waiting for transfers between devices: 5 us -> 6.4 us
    all_to_all x1, waiting for transfers between devices: 0.26 us -> 1.6 us  [shards(): lax.all_to_all(outgoing, ('gx', 'gy'), split_axis=0, concat_axis=0, tiled...]
    pallas_call x1, Pallas kernels: 7.98 us -> 6.65 us  [look_up(): pl.pallas_call(functools.partial(look_kernel, chunk=512), out_shape=jax.S...]
    pallas_call x1, Pallas kernels: 6.07 us -> 5.03 us  [heat_deposit(): pl.pallas_call(functools.partial(heat_kernel, chunk=1024, rows=rows), out...]
  transfers between devices with their start and end apart: 10 -> 10, of which waited for: 2 -> 2; matrix products, arithmetic and copies ran while one was open for 1% -> 1% of each run, Pallas kernels for 35% -> 34%
where the time goes in v10:
time: 89.8 us; the launch traced here: 88.2 us
  Pallas kernels  46.3 us (52%)
  starting transfers between devices  32.8 us (37%)
  waiting for transfers between devices  6.4 us (7%)
  local copies, waits for them, and re-layouts  1.73 us (2%)
  between operations  0.94 us (1%)
    ppermute x8, starting transfers between devices, moved(): return lax.ppermute(value, axis, pairs)  21.6 us
    pallas_call x1, Pallas kernels, place(): pl.pallas_call(place_kernel, out_shape=(jax.ShapeDtypeStruct((devices, 12...  9.53 us
    pallas_call x1, Pallas kernels, contact(): pl.pallas_call(contact_kernel, grid=(devices // step,), out_shape=jax.Sha...  9.17 us
    pallas_call x1, Pallas kernels, deposit(): pl.pallas_call(functools.partial(deposit_kernel, chunk=1024), out_shape=(...  9.08 us
    pallas_call x1, Pallas kernels, look_up(): pl.pallas_call(functools.partial(look_kernel, chunk=512), out_shape=jax.S...  6.65 us
    all_to_all x1, starting transfers between devices, shards(): lax.all_to_all(outgoing, ('gx', 'gy'), split_axis=0, concat_axis=0, tiled...  6.02 us
    all_to_all x1, starting transfers between devices, shards(): lax.all_to_all(result, ('gx', 'gy'), split_axis=0, concat_axis=0, tiled=T...  5.22 us
    pallas_call x1, Pallas kernels, heat_deposit(): pl.pallas_call(functools.partial(heat_kernel, chunk=1024, rows=rows), out...  5.03 us
  transfers between devices with their start and end apart: 10, of which 2 were waited for; matrix products, arithmetic and copies ran while one was open for 1% of the time, Pallas kernels for 34%

profile of v10, /device:TPU:10, one launch (start us, length us, event | category | flops | bytes accessed | tf_op | source)
XLA Modules:
  0.0 88.2 jit_solution(11983779676722884671)
XLA Ops:
  0.7 9.5 %place_slots.1 = (f32[32,48,128]{2,1,0:T(8,128)}, s32[1,8192]{1,0:T(1,128)}, s32[1,8192]{1,0:T(1,128)}, s32[16,128]{1,0:T(8,128)}) custom-call(s32[32]{0:T(128)} %owner_ref.3, s32[1,8192]{1,0:T(1,128)} %bitcast.16, f32[3,8192]{1,0:T(4,128)} %pos_ref.1, f32[6,8192]{1,0:T(8,128)} %motion_ref.3, f32[1,8192]{1,0:T(1,128)} %bitcast.13, f32[1,8192]{1,0:T(1,128)} %bitcast.8), custom_call_target="tpu_custom_call" | custom-call | flops 3221225472 | bytes 1048576 | tf_op jit(solution)/shard_map/place_slots/pallas_call | solution.py:183
  10.2 6.0 %all-to-all-start = ((f32[32,48,128]{2,1,0:T(8,128)}), f32[32,48,128]{2,1,0:T(8,128)S(1)}, u32[]{:S(2)}, u32[]{:S(2)}) async-start(f32[32,48,128]{2,1,0:T(8,128)} %get-tuple-element.30), calls=%async_computation | async-start | bytes 1572864 | tf_op jit(solution)/shard_map/all_to_all | solution.py:739
  16.2 0.5 slice_reduce_fusion
  16.7 0.1 reshape_squeeze.6
  16.8 3.4 %collective-permute-start.2 = (f32[8,128]{1,0:T(8,128)S(1)}, f32[8,128]{1,0:T(8,128)S(1)}, u32[]{:S(2)}, u32[]{:S(2)}) collective-permute-start(f32[8,128]{1,0:T(8,128)S(1)} %reshape_squeeze.6), channel_id=1, source_target_pairs={{0,8},{8,16},{16,24},{1,9},{9,17},{17,25},{2,10},{10,18},{18,26},{... | collective-permute-start | bytes 12296 | tf_op jit(solution)/shard_map/ppermute | solution.py:713
  20.2 0.1 reshape_squeeze.7
  20.3 2.5 %collective-permute-start.3 = (f32[8,128]{1,0:T(8,128)S(1)}, f32[8,128]{1,0:T(8,128)S(1)}, u32[]{:S(2)}, u32[]{:S(2)}) collective-permute-start(f32[8,128]{1,0:T(8,128)S(1)} %reshape_squeeze.7), channel_id=1, source_target_pairs={{8,0},{16,8},{24,16},{9,1},{17,9},{25,17},{10,2},{18,10},{26,18},{... | collective-permute-start | bytes 12296 | tf_op jit(solution)/shard_map/ppermute | solution.py:713
  22.8 0.1 copy.14
  22.9 1.9 %collective-permute-start.1 = (f32[4,32,128]{2,1,0:T(8,128)S(1)}, f32[4,32,128]{2,1,0:T(8,128)S(1)}, u32[]{:S(2)}, u32[]{:S(2)}) collective-permute-start(f32[4,32,128]{2,1,0:T(8,128)S(1)} %get-tuple-element.59), channel_id=1, source_target_pairs={{1,0},{2,1},{3,2},{4,3},{5,4},{6,5},{7,6},{9,8},{10,9},{11,10},{12... | collective-permute-start | bytes 196616 | tf_op jit(solution)/shard_map/ppermute | solution.py:713
  24.8 2.4 %collective-permute-start = (f32[4,32,128]{2,1,0:T(8,128)S(1)}, f32[4,32,128]{2,1,0:T(8,128)S(1)}, u32[]{:S(2)}, u32[]{:S(2)}) collective-permute-start(f32[4,32,128]{2,1,0:T(8,128)S(1)} %get-tuple-element.60), channel_id=1, source_target_pairs={{0,1},{1,2},{2,3},{3,4},{4,5},{5,6},{6,7},{8,9},{9,10},{10,11},{11... | collective-permute-start | bytes 196616 | tf_op jit(solution)/shard_map/ppermute | solution.py:713
  27.2 0.0 copy-start.1
  27.3 0.0 copy-start.2
  27.3 0.0 copy-start.4
  27.3 6.6 %look_up.1.seen_ref = f32[4,8192]{1,0:T(4,128)S(1)} custom-call(f32[4,32,8,128]{3,2,1,0:T(8,128)S(1)} %copy-done, s32[1,8192]{1,0:T(1,128)S(1)} %bitcast.10), custom_call_target="tpu_custom_call" | custom-call | flops 2147483648 | bytes 1048576 | tf_op jit(solution)/shard_map/look_up/pallas_call | solution.py:427
  33.9 1.6 %all-to-all-done.slot_ref = f32[32,48,128]{2,1,0:T(8,128)S(1)} async-done(((f32[32,48,128]{2,1,0:T(8,128)}), f32[32,48,128]{2,1,0:T(8,128)S(1)}, u32[]{:S(2)}, u32[]{:S(2)}) %all-to-all-start) | async-done | bytes 786464 | tf_op jit(solution)/shard_map/all_to_all | solution.py:739
  35.5 0.9 %copy-done.10 = f32[32,48,128]{2,1,0:T(8,128)} copy-done((f32[32,48,128]{2,1,0:T(8,128)}, f32[32,48,128]{2,1,0:T(8,128)S(1)}, u32[]{:S(2)}) %copy-start.10) | copy-done | bytes 786456
  36.4 9.2 %contact_blocks.1 = f32[32,32,128]{2,1,0:T(8,128)} custom-call(f32[32,48,128]{2,1,0:T(8,128)} %copy-done.10, s32[128,128,128]{2,1,0:T(8,128)} %mask_ref.1), custom_call_target="tpu_custom_call" | custom-call | flops 134217728 | bytes 8388608 | tf_op jit(solution)/shard_map/contact_blocks/pallas_call | solution.py:309
  45.6 0.0 collective-permute-done.3.x1_ref
  45.6 0.0 collective-permute-done.1.y1_ref
  45.6 5.2 %all-to-all-start.1 = ((f32[32,32,128]{2,1,0:T(8,128)}), f32[32,32,128]{2,1,0:T(8,128)S(1)}, u32[]{:S(2)}, u32[]{:S(2)}) async-start(f32[32,32,128]{2,1,0:T(8,128)} %contact_blocks.1), calls=%async_computation.1 | async-start | bytes 1048576 | tf_op jit(solution)/shard_map/all_to_all | solution.py:756
  50.9 0.0 copy-start.5
  50.9 0.0 copy-start.6
  50.9 0.0 copy-start.8
  50.9 9.1 %deposit_fields.1 = (f32[8,8192]{1,0:T(8,128)S(1)}, f32[4,32,8,128]{3,2,1,0:T(8,128)S(1)}, f32[4,32,128]{2,1,0:T(8,128)S(1)}, f32[4,32,128]{2,1,0:T(8,128)S(1)},...) custom-call(f32[4,32,128]{2,1,0:T(8,128)S(1)} %collective-permute-done.y0_ref, ...), custom_call_target="tpu_custom_call" | custom-call | flops 4294967296 | bytes 2097152 | tf_op jit(solution)/shard_map/deposit_fields/pallas_call | solution.py:522
  60.0 4.8 %all-to-all-done.1.back_ref = f32[32,32,128]{2,1,0:T(8,128)S(1)} async-done(((f32[32,32,128]{2,1,0:T(8,128)}), f32[32,32,128]{2,1,0:T(8,128)S(1)}, u32[]{:S(2)}, u32[]{:S(2)}) %all-to-all-start.1) | async-done | bytes 524320 | tf_op jit(solution)/shard_map/all_to_all | solution.py:756
  64.8 5.0 %heat_deposit.1 = (f32[1,8192]{1,0:T(1,128)S(1)}, f32[1,32,8,128]{3,2,1,0:T(8,128)S(1)}, f32[5,32,128]{2,1,0:T(8,128)S(1)}, f32[5,32,128]{2,1,0:T(8,128)S(1)}, f...) custom-call(f32[32,32,128]{2,1,0:T(8,128)S(1)} %all-to-all-done.1.back_ref, s32[1,8192]{1,0:T(1,128)S(1)} %copy-done.7, ...), custom_call_target="tpu_custom_call" | custom-call | flops 1073741824 | bytes 1048576 | tf_op jit(solution)/shard_map/heat_deposit/pallas_call | solution.py:592
  69.8 3.4 %collective-permute-start.6 = (f32[10,128]{1,0:T(8,128)S(1)}, f32[10,128]{1,0:T(8,128)S(1)}, u32[]{:S(2)}, u32[]{:S(2)}) collective-permute-start(f32[10,128]{1,0:T(8,128)S(1)} %get-tuple-element.50), channel_id=1, source_target_pairs={{0,8},{8,16},{16,24},{1,9},{9,17},{17,25},{2,10},{10,18},{18,26},{... | collective-permute-start | bytes 15368 | tf_op jit(solution)/shard_map/ppermute | solution.py:713
  73.2 2.5 %collective-permute-start.7 = (f32[10,128]{1,0:T(8,128)S(1)}, f32[10,128]{1,0:T(8,128)S(1)}, u32[]{:S(2)}, u32[]{:S(2)}) collective-permute-start(f32[10,128]{1,0:T(8,128)S(1)} %get-tuple-element.51), channel_id=1, source_target_pairs={{8,0},{16,8},{24,16},{9,1},{17,9},{25,17},{10,2},{18,10},{26,18},{... | collective-permute-start | bytes 15368 | tf_op jit(solution)/shard_map/ppermute | solution.py:713
  75.7 1.9 %collective-permute-start.4 = (f32[5,32,128]{2,1,0:T(8,128)S(1)}, f32[5,32,128]{2,1,0:T(8,128)S(1)}, u32[]{:S(2)}, u32[]{:S(2)}) collective-permute-start(f32[5,32,128]{2,1,0:T(8,128)S(1)} %get-tuple-element.48), channel_id=1, source_target_pairs={{0,1},{1,2},{2,3},{3,4},{4,5},{5,6},{6,7},{8,9},{9,10},{10,11},{11... | collective-permute-start | bytes 245768 | tf_op jit(solution)/shard_map/ppermute | solution.py:713
  77.6 3.6 %collective-permute-start.5 = (f32[5,32,128]{2,1,0:T(8,128)S(1)}, f32[5,32,128]{2,1,0:T(8,128)S(1)}, u32[]{:S(2)}, u32[]{:S(2)}) collective-permute-start(f32[5,32,128]{2,1,0:T(8,128)S(1)} %get-tuple-element.49), channel_id=1, source_target_pairs={{1,0},{2,1},{3,2},{4,3},{5,4},{6,5},{7,6},{9,8},{10,9},{11,10},{12... | collective-permute-start | bytes 245768 | tf_op jit(solution)/shard_map/ppermute | solution.py:713
  81.3 4.8 %fetch_slots.1 = f32[7,8192]{1,0:T(8,128)} custom-call(s32[32]{0:T(128)S(1)} %copy-done.6, s32[16,128]{1,0:T(8,128)S(1)} %copy-done.9, f32[32,32,128]{2,1,0:T(8,128)S(1)} %all-to-all-done.1.back_ref, s32[1,8192]{1,0:T(1,128)S(1)} %bitcast.17, s32[1,8192]{1,0:T(1,128)S(1)} %copy-done.8, f32[8,8192]{1,0:T(8,128)S(1)} %get-tuple-element.42.base_ref, ...), custom_call_target="tpu_custom_call" | custom-call | flops 2147483648 | bytes 1048576 | tf_op jit(solution)/shard_map/fetch_slots/pallas_call | solution.py:669
  86.2 2.0 %spread_fields.1 = (f32[4,32,8,128]{3,2,1,0:T(8,128)}, f32[32,8,128]{2,1,0:T(8,128)}) custom-call(f32[4,32,8,128]{3,2,1,0:T(8,128)S(1)} %get-tuple-element.39.dep_ref, f32[1,32,8,128]{3,2,1,0:T(8,128)S(1)} %get-tuple-element.47.heat_ref, f32[5,32,128]{2,1,0:T(8,128)S(1)} %collective-permute-done.4.y0_ref, f32[5,32,128]{2,1,0:T(8,128)S(1)} %collective-permute-done.5.y1_ref, ...), custom_call_target="tpu_custom_call" | custom-call | flops 2621440 | bytes 2097152 | tf_op jit(solution)/shard_map/spread_fields/pallas_call | solution.py:698
  (22 shorter events, 0.1 us)
Async XLA Ops:
  0.6 15.6 %copy-start = (f32[4,32,8,128]{3,2,1,0:T(8,128)S(1)}, f32[4,32,8,128]{3,2,1,0:T(8,128)}, u32[]{:S(2)}) copy-start(f32[4,32,8,128]{3,2,1,0:T(8,128)} %fluid_ref.2) | copy-start | bytes 1572868
  0.6 26.6 %copy-start.3 = (s32[8192]{0:T(1024)S(1)}, s32[8192]{0:T(1024)}, u32[]{:S(2)}) copy-start(s32[8192]{0:T(1024)} %param.14) | copy-start | bytes 98308
  10.2 25.4 %all-to-all-start = ((f32[32,48,128]{2,1,0:T(8,128)}), f32[32,48,128]{2,1,0:T(8,128)S(1)}, u32[]{:S(2)}, u32[]{:S(2)}) async-start(f32[32,48,128]{2,1,0:T(8,128)} %get-tuple-element.30), calls=%async_computation | async-start | bytes 1572864 | tf_op jit(solution)/shard_map/all_to_all | solution.py:739
  16.8 28.8 %collective-permute-start.2 = (f32[8,128]{1,0:T(8,128)S(1)}, f32[8,128]{1,0:T(8,128)S(1)}, u32[]{:S(2)}, u32[]{:S(2)}) collective-permute-start(f32[8,128]{1,0:T(8,128)S(1)} %reshape_squeeze.6), channel_id=1, source_target_pairs={{0,8},{8,16},{16,24},{1,9},{9,17},{17,25},{2,10},{10,18},{18,26},{... | collective-permute-start | bytes 12296 | tf_op jit(solution)/shard_map/ppermute | solution.py:713
  20.3 25.3 %collective-permute-start.3 = (f32[8,128]{1,0:T(8,128)S(1)}, f32[8,128]{1,0:T(8,128)S(1)}, u32[]{:S(2)}, u32[]{:S(2)}) collective-permute-start(f32[8,128]{1,0:T(8,128)S(1)} %reshape_squeeze.7), channel_id=1, source_target_pairs={{8,0},{16,8},{24,16},{9,1},{17,9},{25,17},{10,2},{18,10},{26,18},{... | collective-permute-start | bytes 12296 | tf_op jit(solution)/shard_map/ppermute | solution.py:713
  22.9 22.7 %collective-permute-start.1 = (f32[4,32,128]{2,1,0:T(8,128)S(1)}, f32[4,32,128]{2,1,0:T(8,128)S(1)}, u32[]{:S(2)}, u32[]{:S(2)}) collective-permute-start(f32[4,32,128]{2,1,0:T(8,128)S(1)} %get-tuple-element.59), channel_id=1, source_target_pairs={{1,0},{2,1},{3,2},{4,3},{5,4},{6,5},{7,6},{9,8},{10,9},{11,10},{12... | collective-permute-start | bytes 196616 | tf_op jit(solution)/shard_map/ppermute | solution.py:713
  24.8 20.8 %collective-permute-start = (f32[4,32,128]{2,1,0:T(8,128)S(1)}, f32[4,32,128]{2,1,0:T(8,128)S(1)}, u32[]{:S(2)}, u32[]{:S(2)}) collective-permute-start(f32[4,32,128]{2,1,0:T(8,128)S(1)} %get-tuple-element.60), channel_id=1, source_target_pairs={{0,1},{1,2},{2,3},{3,4},{4,5},{5,6},{6,7},{8,9},{9,10},{10,11},{11... | collective-permute-start | bytes 196616 | tf_op jit(solution)/shard_map/ppermute | solution.py:713
  27.2 23.6 %copy-start.1 = (f32[6,8192]{1,0:T(8,128)S(1)}, f32[6,8192]{1,0:T(8,128)}, u32[]{:S(2)}) copy-start(f32[6,8192]{1,0:T(8,128)} %motion_ref.3) | copy-start | bytes 589828
  27.3 23.6 %copy-start.2 = (f32[8192]{0:T(1024)S(1)}, f32[8192]{0:T(1024)}, u32[]{:S(2)}) copy-start(f32[8192]{0:T(1024)} %param.13) | copy-start | bytes 98308
  27.3 23.6 %copy-start.4 = (f32[8192]{0:T(1024)S(1)}, f32[8192]{0:T(1024)}, u32[]{:S(2)}) copy-start(f32[8192]{0:T(1024)} %param.12) | copy-start | bytes 98308
  35.5 0.9 %copy-start.10 = (f32[32,48,128]{2,1,0:T(8,128)}, f32[32,48,128]{2,1,0:T(8,128)S(1)}, u32[]{:S(2)}) copy-start(f32[32,48,128]{2,1,0:T(8,128)S(1)} %all-to-all-done.slot_ref) | copy-start | bytes 2359300
  45.6 19.2 %copy-start.7 = (s32[1,8192]{1,0:T(1,128)S(1)}, s32[1,8192]{1,0:T(1,128)}, u32[]{:S(2)}) copy-start(s32[1,8192]{1,0:T(1,128)} %get-tuple-element.41.slot_ref) | copy-start | bytes 98308
  45.6 19.2 %all-to-all-start.1 = ((f32[32,32,128]{2,1,0:T(8,128)}), f32[32,32,128]{2,1,0:T(8,128)S(1)}, u32[]{:S(2)}, u32[]{:S(2)}) async-start(f32[32,32,128]{2,1,0:T(8,128)} %contact_blocks.1), calls=%async_computation.1 | async-start | bytes 1048576 | tf_op jit(solution)/shard_map/all_to_all | solution.py:756
  50.9 30.4 %copy-start.5 = (s32[8192,1]{0,1:T(1,128)S(1)}, s32[8192,1]{0,1:T(1,128)}, u32[]{:S(2)}) copy-start(s32[8192,1]{0,1:T(1,128)} %param.15) | copy-start | bytes 98308
  50.9 30.4 %copy-start.6 = (s32[32]{0:T(128)S(1)}, s32[32]{0:T(128)}, u32[]{:S(2)}) copy-start(s32[32]{0:T(128)} %owner_ref.3) | copy-start | bytes 388
  50.9 30.4 %copy-start.8 = (s32[1,8192]{1,0:T(1,128)S(1)}, s32[1,8192]{1,0:T(1,128)}, u32[]{:S(2)}) copy-start(s32[1,8192]{1,0:T(1,128)} %get-tuple-element.55.spot_ref) | copy-start | bytes 98308
  50.9 30.4 %copy-start.9 = (s32[16,128]{1,0:T(8,128)S(1)}, s32[16,128]{1,0:T(8,128)}, u32[]{:S(2)}) copy-start(s32[16,128]{1,0:T(8,128)} %get-tuple-element.54.tile_ref) | copy-start | bytes 24580
  69.8 16.3 %collective-permute-start.6 = (f32[10,128]{1,0:T(8,128)S(1)}, f32[10,128]{1,0:T(8,128)S(1)}, u32[]{:S(2)}, u32[]{:S(2)}) collective-permute-start(f32[10,128]{1,0:T(8,128)S(1)} %get-tuple-element.50), channel_id=1, source_target_pairs={{0,8},{8,16},{16,24},{1,9},{9,17},{17,25},{2,10},{10,18},{18,26},{... | collective-permute-start | bytes 15368 | tf_op jit(solution)/shard_map/ppermute | solution.py:713
  73.2 12.9 %collective-permute-start.7 = (f32[10,128]{1,0:T(8,128)S(1)}, f32[10,128]{1,0:T(8,128)S(1)}, u32[]{:S(2)}, u32[]{:S(2)}) collective-permute-start(f32[10,128]{1,0:T(8,128)S(1)} %get-tuple-element.51), channel_id=1, source_target_pairs={{8,0},{16,8},{24,16},{9,1},{17,9},{25,17},{10,2},{18,10},{26,18},{... | collective-permute-start | bytes 15368 | tf_op jit(solution)/shard_map/ppermute | solution.py:713
  75.7 10.5 %collective-permute-start.4 = (f32[5,32,128]{2,1,0:T(8,128)S(1)}, f32[5,32,128]{2,1,0:T(8,128)S(1)}, u32[]{:S(2)}, u32[]{:S(2)}) collective-permute-start(f32[5,32,128]{2,1,0:T(8,128)S(1)} %get-tuple-element.48), channel_id=1, source_target_pairs={{0,1},{1,2},{2,3},{3,4},{4,5},{5,6},{6,7},{8,9},{9,10},{10,11},{11... | collective-permute-start | bytes 245768 | tf_op jit(solution)/shard_map/ppermute | solution.py:713
  77.6 8.5 %collective-permute-start.5 = (f32[5,32,128]{2,1,0:T(8,128)S(1)}, f32[5,32,128]{2,1,0:T(8,128)S(1)}, u32[]{:S(2)}, u32[]{:S(2)}) collective-permute-start(f32[5,32,128]{2,1,0:T(8,128)S(1)} %get-tuple-element.49), channel_id=1, source_target_pairs={{1,0},{2,1},{3,2},{4,3},{5,4},{6,5},{7,6},{9,8},{10,9},{11,10},{12... | collective-permute-start | bytes 245768 | tf_op jit(solution)/shard_map/ppermute | solution.py:713

commit v11 on v10

--- a/solution.py
+++ b/solution.py
@@ -231,13 +231,23 @@
     return left, right.astype(BF16)
 
 
-def contact_kernel(slot_ref, mask_ref, out_ref):
+def contact_kernel(slot_ref, mask_hbm, out_ref, mask_ref, arrived):
     homes, rows, _ = slot_ref.shape
     layers = rows // 12
     blocks = [(s, q) for s in range(homes) for q in range(layers)]
     row = lax.broadcasted_iota(jnp.int32, (8, 1), 0)
     sign = jnp.where((row >= 3) & (row < 6), 1.0, -1.0)
     lane = lax.broadcasted_iota(jnp.int32, (BLOCK, BLOCK), 1) // 16
+    at_step = pl.program_id(0)
+
+    def mask_copy(number):
+        part = pl.ds(8 * number, 8)
+        return pltpu.make_async_copy(mask_hbm.at[part], mask_ref.at[part], arrived.at[number])
+
+    @pl.when(at_step == 0)
+    def _():
+        for number in range(mask_hbm.shape[0] // 8):
+            mask_copy(number).start()
 
     def pairs_of(group):
         pairs = []
@@ -272,7 +282,7 @@
             reach = pair[:, at + BLOCK : at + 2 * BLOCK]
             inverse = pl.reciprocal(reach, approx=True)
             inverse = inverse * (2.0 - reach * inverse)
-            weight = mask_ref[8 * number + b].astype(F32) * jnp.exp(pair[:, at : at + BLOCK] * inverse)
+            weight = mask_ref[at_step * len(blocks) + 8 * number + b].astype(F32) * jnp.exp(pair[:, at : at + BLOCK] * inverse)
             high, low = split(weight)
             highs.append(high)
             lows.append(low)
@@ -293,6 +303,7 @@
     before = None
     for number, group in enumerate(groups):
         later = pairs_of(groups[number + 1]) if number + 1 < len(groups) else None
+        mask_copy(at_step * len(groups) + number).wait()
         sums = sums_of(number, group, pairs)
         if before is not None:
             finish(*before)
@@ -312,10 +323,11 @@
         out_shape=jax.ShapeDtypeStruct((devices, 8 * layers, BLOCK), F32),
         in_specs=[
             pl.BlockSpec((step, rows, BLOCK), lambda h: (h, 0, 0)),
-            pl.BlockSpec((step * layers, BLOCK, BLOCK), lambda h: (h, 0, 0)),
+            pl.BlockSpec(memory_space=pltpu.HBM),
         ],
         out_specs=pl.BlockSpec((step, 8 * layers, BLOCK), lambda h: (h, 0, 0)),
-        compiler_params=pltpu.CompilerParams(vmem_limit_bytes=54 << 20),
+        scratch_shapes=[VMEM(mask.shape, mask.dtype), pltpu.SemaphoreType.DMA((blocks // 8,))],
+        compiler_params=pltpu.CompilerParams(vmem_limit_bytes=60 << 20),
         cost_estimate=pl.CostEstimate(
             flops=64 * blocks * BLOCK * BLOCK, bytes_accessed=blocks * BLOCK * BLOCK * 4, transcendentals=0
         ),

time: 89.8 us -> 93.1 us (1.037)
  Pallas kernels: 46.3 us -> 49.7 us
    pallas_call x1, Pallas kernels: 9.17 us -> 12.6 us  [contact(): pl.pallas_call(contact_kernel, grid=(devices // step,), out_shape=jax.Sha...]
  transfers between devices with their start and end apart: 10 -> 10, of which waited for: 2 -> 2; matrix products, arithmetic and copies ran while one was open for 1% -> 1% of each run, Pallas kernels for 34% -> 36%
where the time goes in v11:
time: 93.1 us; the launch traced here: 91.6 us
  Pallas kernels  49.7 us (53%)
  starting transfers between devices  32.8 us (35%)
  waiting for transfers between devices  6.4 us (7%)
  local copies, waits for them, and re-layouts  1.73 us (2%)
  between operations  0.97 us (1%)
    ppermute x8, starting transfers between devices, moved(): return lax.ppermute(value, axis, pairs)  21.6 us
    pallas_call x1, Pallas kernels, contact(): pl.pallas_call(contact_kernel, grid=(devices // step,), out_shape=jax.Sha...  12.6 us
    pallas_call x1, Pallas kernels, place(): pl.pallas_call(place_kernel, out_shape=(jax.ShapeDtypeStruct((devices, 12...  9.53 us
    pallas_call x1, Pallas kernels, deposit(): pl.pallas_call(functools.partial(deposit_kernel, chunk=1024), out_shape=(...  9.08 us
    pallas_call x1, Pallas kernels, look_up(): pl.pallas_call(functools.partial(look_kernel, chunk=512), out_shape=jax.S...  6.65 us
    all_to_all x1, starting transfers between devices, shards(): lax.all_to_all(outgoing, ('gx', 'gy'), split_axis=0, concat_axis=0, tiled...  6.02 us
    all_to_all x1, starting transfers between devices, shards(): lax.all_to_all(result, ('gx', 'gy'), split_axis=0, concat_axis=0, tiled=T...  5.21 us
    pallas_call x1, Pallas kernels, heat_deposit(): pl.pallas_call(functools.partial(heat_kernel, chunk=1024, rows=rows), out...  5.03 us
  transfers between devices with their start and end apart: 10, of which 2 were waited for; matrix products, arithmetic and copies ran while one was open for 1% of the time, Pallas kernels for 36%

profile of v11, /device:TPU:10, one launch (start us, length us, event | category | flops | bytes accessed | tf_op | source)
XLA Modules:
  0.0 91.6 jit_solution(8334106124168971528)
XLA Ops:
  0.7 9.5 %place_slots.1 = (f32[32,48,128]{2,1,0:T(8,128)}, s32[1,8192]{1,0:T(1,128)}, s32[1,8192]{1,0:T(1,128)}, s32[16,128]{1,0:T(8,128)}) custom-call(s32[32]{0:T(128)} %owner_ref.3, s32[1,8192]{1,0:T(1,128)} %bitcast.16, f32[3,8192]{1,0:T(4,128)} %pos_ref.1, f32[6,8192]{1,0:T(8,128)} %motion_ref.3, f32[1,8192]{1,0:T(1,128)} %bitcast.13, f32[1,8192]{1,0:T(1,128)} %bitcast.8), custom_call_target="tpu_custom_call" | custom-call | flops 3221225472 | bytes 1048576 | tf_op jit(solution)/shard_map/place_slots/pallas_call | solution.py:183
  10.2 6.0 %all-to-all-start = ((f32[32,48,128]{2,1,0:T(8,128)}), f32[32,48,128]{2,1,0:T(8,128)S(1)}, u32[]{:S(2)}, u32[]{:S(2)}) async-start(f32[32,48,128]{2,1,0:T(8,128)} %get-tuple-element.30), calls=%async_computation | async-start | bytes 1572864 | tf_op jit(solution)/shard_map/all_to_all | solution.py:751
  16.2 0.5 slice_reduce_fusion
  16.7 0.1 reshape_squeeze.6
  16.8 3.4 %collective-permute-start.2 = (f32[8,128]{1,0:T(8,128)S(1)}, f32[8,128]{1,0:T(8,128)S(1)}, u32[]{:S(2)}, u32[]{:S(2)}) collective-permute-start(f32[8,128]{1,0:T(8,128)S(1)} %reshape_squeeze.6), channel_id=1, source_target_pairs={{0,8},{8,16},{16,24},{1,9},{9,17},{17,25},{2,10},{10,18},{18,26},{... | collective-permute-start | bytes 12296 | tf_op jit(solution)/shard_map/ppermute | solution.py:725
  20.2 0.1 reshape_squeeze.7
  20.3 2.5 %collective-permute-start.3 = (f32[8,128]{1,0:T(8,128)S(1)}, f32[8,128]{1,0:T(8,128)S(1)}, u32[]{:S(2)}, u32[]{:S(2)}) collective-permute-start(f32[8,128]{1,0:T(8,128)S(1)} %reshape_squeeze.7), channel_id=1, source_target_pairs={{8,0},{16,8},{24,16},{9,1},{17,9},{25,17},{10,2},{18,10},{26,18},{... | collective-permute-start | bytes 12296 | tf_op jit(solution)/shard_map/ppermute | solution.py:725
  22.8 0.1 copy.14
  22.9 1.9 %collective-permute-start.1 = (f32[4,32,128]{2,1,0:T(8,128)S(1)}, f32[4,32,128]{2,1,0:T(8,128)S(1)}, u32[]{:S(2)}, u32[]{:S(2)}) collective-permute-start(f32[4,32,128]{2,1,0:T(8,128)S(1)} %get-tuple-element.59), channel_id=1, source_target_pairs={{1,0},{2,1},{3,2},{4,3},{5,4},{6,5},{7,6},{9,8},{10,9},{11,10},{12... | collective-permute-start | bytes 196616 | tf_op jit(solution)/shard_map/ppermute | solution.py:725
  24.8 2.4 %collective-permute-start = (f32[4,32,128]{2,1,0:T(8,128)S(1)}, f32[4,32,128]{2,1,0:T(8,128)S(1)}, u32[]{:S(2)}, u32[]{:S(2)}) collective-permute-start(f32[4,32,128]{2,1,0:T(8,128)S(1)} %get-tuple-element.60), channel_id=1, source_target_pairs={{0,1},{1,2},{2,3},{3,4},{4,5},{5,6},{6,7},{8,9},{9,10},{10,11},{11... | collective-permute-start | bytes 196616 | tf_op jit(solution)/shard_map/ppermute | solution.py:725
  27.2 0.0 copy-start.1
  27.3 0.0 copy-start.2
  27.3 0.0 copy-start.4
  27.3 6.6 %look_up.1.seen_ref = f32[4,8192]{1,0:T(4,128)S(1)} custom-call(f32[4,32,8,128]{3,2,1,0:T(8,128)S(1)} %copy-done, s32[1,8192]{1,0:T(1,128)S(1)} %bitcast.10), custom_call_target="tpu_custom_call" | custom-call | flops 2147483648 | bytes 1048576 | tf_op jit(solution)/shard_map/look_up/pallas_call | solution.py:439
  33.9 1.6 %all-to-all-done.slot_ref = f32[32,48,128]{2,1,0:T(8,128)S(1)} async-done(((f32[32,48,128]{2,1,0:T(8,128)}), f32[32,48,128]{2,1,0:T(8,128)S(1)}, u32[]{:S(2)}, u32[]{:S(2)}) %all-to-all-start) | async-done | bytes 786464 | tf_op jit(solution)/shard_map/all_to_all | solution.py:751
  35.5 0.9 copy-done.10
  36.4 12.6 %contact_blocks.1 = f32[32,32,128]{2,1,0:T(8,128)} custom-call(f32[32,48,128]{2,1,0:T(8,128)} %copy-done.10, s32[128,128,128]{2,1,0:T(8,128)} %mask_hbm.1), custom_call_target="tpu_custom_call" | custom-call | flops 134217728 | bytes 8388608 | tf_op jit(solution)/shard_map/contact_blocks/pallas_call | solution.py:320
  49.0 0.0 copy-start.7
  49.0 0.0 collective-permute-done.2.x0_ref
  49.0 5.2 %all-to-all-start.1 = ((f32[32,32,128]{2,1,0:T(8,128)}), f32[32,32,128]{2,1,0:T(8,128)S(1)}, u32[]{:S(2)}, u32[]{:S(2)}) async-start(f32[32,32,128]{2,1,0:T(8,128)} %contact_blocks.1), calls=%async_computation.1 | async-start | bytes 1048576 | tf_op jit(solution)/shard_map/all_to_all | solution.py:768
  54.3 0.0 copy-start.5
  54.3 0.0 copy-start.6
  54.3 0.0 copy-start.8
  54.3 9.1 %deposit_fields.1 = (f32[8,8192]{1,0:T(8,128)S(1)}, f32[4,32,8,128]{3,2,1,0:T(8,128)S(1)}, f32[4,32,128]{2,1,0:T(8,128)S(1)}, f32[4,32,128]{2,1,0:T(8,128)S(1)},...) custom-call(f32[4,32,128]{2,1,0:T(8,128)S(1)} %collective-permute-done.y0_ref, ...), custom_call_target="tpu_custom_call" | custom-call | flops 4294967296 | bytes 2097152 | tf_op jit(solution)/shard_map/deposit_fields/pallas_call | solution.py:534
  63.4 4.8 %all-to-all-done.1.back_ref = f32[32,32,128]{2,1,0:T(8,128)S(1)} async-done(((f32[32,32,128]{2,1,0:T(8,128)}), f32[32,32,128]{2,1,0:T(8,128)S(1)}, u32[]{:S(2)}, u32[]{:S(2)}) %all-to-all-start.1) | async-done | bytes 524320 | tf_op jit(solution)/shard_map/all_to_all | solution.py:768
  68.2 5.0 %heat_deposit.1 = (f32[1,8192]{1,0:T(1,128)S(1)}, f32[1,32,8,128]{3,2,1,0:T(8,128)S(1)}, f32[5,32,128]{2,1,0:T(8,128)S(1)}, f32[5,32,128]{2,1,0:T(8,128)S(1)}, f...) custom-call(f32[32,32,128]{2,1,0:T(8,128)S(1)} %all-to-all-done.1.back_ref, s32[1,8192]{1,0:T(1,128)S(1)} %copy-done.7, ...), custom_call_target="tpu_custom_call" | custom-call | flops 1073741824 | bytes 1048576 | tf_op jit(solution)/shard_map/heat_deposit/pallas_call | solution.py:604
  73.2 3.4 %collective-permute-start.6 = (f32[10,128]{1,0:T(8,128)S(1)}, f32[10,128]{1,0:T(8,128)S(1)}, u32[]{:S(2)}, u32[]{:S(2)}) collective-permute-start(f32[10,128]{1,0:T(8,128)S(1)} %get-tuple-element.50), channel_id=1, source_target_pairs={{0,8},{8,16},{16,24},{1,9},{9,17},{17,25},{2,10},{10,18},{18,26},{... | collective-permute-start | bytes 15368 | tf_op jit(solution)/shard_map/ppermute | solution.py:725
  76.6 2.5 %collective-permute-start.7 = (f32[10,128]{1,0:T(8,128)S(1)}, f32[10,128]{1,0:T(8,128)S(1)}, u32[]{:S(2)}, u32[]{:S(2)}) collective-permute-start(f32[10,128]{1,0:T(8,128)S(1)} %get-tuple-element.51), channel_id=1, source_target_pairs={{8,0},{16,8},{24,16},{9,1},{17,9},{25,17},{10,2},{18,10},{26,18},{... | collective-permute-start | bytes 15368 | tf_op jit(solution)/shard_map/ppermute | solution.py:725
  79.1 1.9 %collective-permute-start.4 = (f32[5,32,128]{2,1,0:T(8,128)S(1)}, f32[5,32,128]{2,1,0:T(8,128)S(1)}, u32[]{:S(2)}, u32[]{:S(2)}) collective-permute-start(f32[5,32,128]{2,1,0:T(8,128)S(1)} %get-tuple-element.48), channel_id=1, source_target_pairs={{0,1},{1,2},{2,3},{3,4},{4,5},{5,6},{6,7},{8,9},{9,10},{10,11},{11... | collective-permute-start | bytes 245768 | tf_op jit(solution)/shard_map/ppermute | solution.py:725
  81.0 3.6 %collective-permute-start.5 = (f32[5,32,128]{2,1,0:T(8,128)S(1)}, f32[5,32,128]{2,1,0:T(8,128)S(1)}, u32[]{:S(2)}, u32[]{:S(2)}) collective-permute-start(f32[5,32,128]{2,1,0:T(8,128)S(1)} %get-tuple-element.49), channel_id=1, source_target_pairs={{1,0},{2,1},{3,2},{4,3},{5,4},{6,5},{7,6},{9,8},{10,9},{11,10},{12... | collective-permute-start | bytes 245768 | tf_op jit(solution)/shard_map/ppermute | solution.py:725
  84.7 4.8 %fetch_slots.1 = f32[7,8192]{1,0:T(8,128)} custom-call(s32[32]{0:T(128)S(1)} %copy-done.6, s32[16,128]{1,0:T(8,128)S(1)} %copy-done.9, f32[32,32,128]{2,1,0:T(8,128)S(1)} %all-to-all-done.1.back_ref, s32[1,8192]{1,0:T(1,128)S(1)} %bitcast.17, s32[1,8192]{1,0:T(1,128)S(1)} %copy-done.8, f32[8,8192]{1,0:T(8,128)S(1)} %get-tuple-element.42.base_ref, ...), custom_call_target="tpu_custom_call" | custom-call | flops 2147483648 | bytes 1048576 | tf_op jit(solution)/shard_map/fetch_slots/pallas_call | solution.py:681
  89.6 2.0 %spread_fields.1 = (f32[4,32,8,128]{3,2,1,0:T(8,128)}, f32[32,8,128]{2,1,0:T(8,128)}) custom-call(f32[4,32,8,128]{3,2,1,0:T(8,128)S(1)} %get-tuple-element.39.dep_ref, f32[1,32,8,128]{3,2,1,0:T(8,128)S(1)} %get-tuple-element.47.heat_ref, f32[5,32,128]{2,1,0:T(8,128)S(1)} %collective-permute-done.4.y0_ref, f32[5,32,128]{2,1,0:T(8,128)S(1)} %collective-permute-done.5.y1_ref, ...), custom_call_target="tpu_custom_call" | custom-call | flops 2621440 | bytes 2097152 | tf_op jit(solution)/shard_map/spread_fields/pallas_call | solution.py:710
  (22 shorter events, 0.1 us)
Async XLA Ops:
  0.6 15.6 %copy-start = (f32[4,32,8,128]{3,2,1,0:T(8,128)S(1)}, f32[4,32,8,128]{3,2,1,0:T(8,128)}, u32[]{:S(2)}) copy-start(f32[4,32,8,128]{3,2,1,0:T(8,128)} %fluid_ref.2) | copy-start | bytes 1572868
  0.6 26.6 %copy-start.3 = (s32[8192]{0:T(1024)S(1)}, s32[8192]{0:T(1024)}, u32[]{:S(2)}) copy-start(s32[8192]{0:T(1024)} %param.14) | copy-start | bytes 98308
  10.2 25.4 %all-to-all-start = ((f32[32,48,128]{2,1,0:T(8,128)}), f32[32,48,128]{2,1,0:T(8,128)S(1)}, u32[]{:S(2)}, u32[]{:S(2)}) async-start(f32[32,48,128]{2,1,0:T(8,128)} %get-tuple-element.30), calls=%async_computation | async-start | bytes 1572864 | tf_op jit(solution)/shard_map/all_to_all | solution.py:751
  16.8 32.2 %collective-permute-start.2 = (f32[8,128]{1,0:T(8,128)S(1)}, f32[8,128]{1,0:T(8,128)S(1)}, u32[]{:S(2)}, u32[]{:S(2)}) collective-permute-start(f32[8,128]{1,0:T(8,128)S(1)} %reshape_squeeze.6), channel_id=1, source_target_pairs={{0,8},{8,16},{16,24},{1,9},{9,17},{17,25},{2,10},{10,18},{18,26},{... | collective-permute-start | bytes 12296 | tf_op jit(solution)/shard_map/ppermute | solution.py:725
  20.3 28.7 %collective-permute-start.3 = (f32[8,128]{1,0:T(8,128)S(1)}, f32[8,128]{1,0:T(8,128)S(1)}, u32[]{:S(2)}, u32[]{:S(2)}) collective-permute-start(f32[8,128]{1,0:T(8,128)S(1)} %reshape_squeeze.7), channel_id=1, source_target_pairs={{8,0},{16,8},{24,16},{9,1},{17,9},{25,17},{10,2},{18,10},{26,18},{... | collective-permute-start | bytes 12296 | tf_op jit(solution)/shard_map/ppermute | solution.py:725
  22.9 26.1 %collective-permute-start.1 = (f32[4,32,128]{2,1,0:T(8,128)S(1)}, f32[4,32,128]{2,1,0:T(8,128)S(1)}, u32[]{:S(2)}, u32[]{:S(2)}) collective-permute-start(f32[4,32,128]{2,1,0:T(8,128)S(1)} %get-tuple-element.59), channel_id=1, source_target_pairs={{1,0},{2,1},{3,2},{4,3},{5,4},{6,5},{7,6},{9,8},{10,9},{11,10},{12... | collective-permute-start | bytes 196616 | tf_op jit(solution)/shard_map/ppermute | solution.py:725
  24.8 24.2 %collective-permute-start = (f32[4,32,128]{2,1,0:T(8,128)S(1)}, f32[4,32,128]{2,1,0:T(8,128)S(1)}, u32[]{:S(2)}, u32[]{:S(2)}) collective-permute-start(f32[4,32,128]{2,1,0:T(8,128)S(1)} %get-tuple-element.60), channel_id=1, source_target_pairs={{0,1},{1,2},{2,3},{3,4},{4,5},{5,6},{6,7},{8,9},{9,10},{10,11},{11... | collective-permute-start | bytes 196616 | tf_op jit(solution)/shard_map/ppermute | solution.py:725
  27.2 27.0 %copy-start.1 = (f32[6,8192]{1,0:T(8,128)S(1)}, f32[6,8192]{1,0:T(8,128)}, u32[]{:S(2)}) copy-start(f32[6,8192]{1,0:T(8,128)} %motion_ref.3) | copy-start | bytes 589828
  27.3 27.0 %copy-start.2 = (f32[8192]{0:T(1024)S(1)}, f32[8192]{0:T(1024)}, u32[]{:S(2)}) copy-start(f32[8192]{0:T(1024)} %param.13) | copy-start | bytes 98308
  27.3 27.0 %copy-start.4 = (f32[8192]{0:T(1024)S(1)}, f32[8192]{0:T(1024)}, u32[]{:S(2)}) copy-start(f32[8192]{0:T(1024)} %param.12) | copy-start | bytes 98308
  35.5 0.9 copy-start.10
  49.0 19.2 %copy-start.7 = (s32[1,8192]{1,0:T(1,128)S(1)}, s32[1,8192]{1,0:T(1,128)}, u32[]{:S(2)}) copy-start(s32[1,8192]{1,0:T(1,128)} %get-tuple-element.41.slot_ref) | copy-start | bytes 98308
  49.0 19.2 %all-to-all-start.1 = ((f32[32,32,128]{2,1,0:T(8,128)}), f32[32,32,128]{2,1,0:T(8,128)S(1)}, u32[]{:S(2)}, u32[]{:S(2)}) async-start(f32[32,32,128]{2,1,0:T(8,128)} %contact_blocks.1), calls=%async_computation.1 | async-start | bytes 1048576 | tf_op jit(solution)/shard_map/all_to_all | solution.py:768
  54.3 30.4 %copy-start.5 = (s32[8192,1]{0,1:T(1,128)S(1)}, s32[8192,1]{0,1:T(1,128)}, u32[]{:S(2)}) copy-start(s32[8192,1]{0,1:T(1,128)} %param.15) | copy-start | bytes 98308
  54.3 30.4 %copy-start.6 = (s32[32]{0:T(128)S(1)}, s32[32]{0:T(128)}, u32[]{:S(2)}) copy-start(s32[32]{0:T(128)} %owner_ref.3) | copy-start | bytes 388
  54.3 30.4 %copy-start.8 = (s32[1,8192]{1,0:T(1,128)S(1)}, s32[1,8192]{1,0:T(1,128)}, u32[]{:S(2)}) copy-start(s32[1,8192]{1,0:T(1,128)} %get-tuple-element.55.spot_ref) | copy-start | bytes 98308
  54.3 30.4 %copy-start.9 = (s32[16,128]{1,0:T(8,128)S(1)}, s32[16,128]{1,0:T(8,128)}, u32[]{:S(2)}) copy-start(s32[16,128]{1,0:T(8,128)} %get-tuple-element.54.tile_ref) | copy-start | bytes 24580
  73.2 16.3 %collective-permute-start.6 = (f32[10,128]{1,0:T(8,128)S(1)}, f32[10,128]{1,0:T(8,128)S(1)}, u32[]{:S(2)}, u32[]{:S(2)}) collective-permute-start(f32[10,128]{1,0:T(8,128)S(1)} %get-tuple-element.50), channel_id=1, source_target_pairs={{0,8},{8,16},{16,24},{1,9},{9,17},{17,25},{2,10},{10,18},{18,26},{... | collective-permute-start | bytes 15368 | tf_op jit(solution)/shard_map/ppermute | solution.py:725
  76.6 12.9 %collective-permute-start.7 = (f32[10,128]{1,0:T(8,128)S(1)}, f32[10,128]{1,0:T(8,128)S(1)}, u32[]{:S(2)}, u32[]{:S(2)}) collective-permute-start(f32[10,128]{1,0:T(8,128)S(1)} %get-tuple-element.51), channel_id=1, source_target_pairs={{8,0},{16,8},{24,16},{9,1},{17,9},{25,17},{10,2},{18,10},{26,18},{... | collective-permute-start | bytes 15368 | tf_op jit(solution)/shard_map/ppermute | solution.py:725
  79.1 10.5 %collective-permute-start.4 = (f32[5,32,128]{2,1,0:T(8,128)S(1)}, f32[5,32,128]{2,1,0:T(8,128)S(1)}, u32[]{:S(2)}, u32[]{:S(2)}) collective-permute-start(f32[5,32,128]{2,1,0:T(8,128)S(1)} %get-tuple-element.48), channel_id=1, source_target_pairs={{0,1},{1,2},{2,3},{3,4},{4,5},{5,6},{6,7},{8,9},{9,10},{10,11},{11... | collective-permute-start | bytes 245768 | tf_op jit(solution)/shard_map/ppermute | solution.py:725
  81.0 8.6 %collective-permute-start.5 = (f32[5,32,128]{2,1,0:T(8,128)S(1)}, f32[5,32,128]{2,1,0:T(8,128)S(1)}, u32[]{:S(2)}, u32[]{:S(2)}) collective-permute-start(f32[5,32,128]{2,1,0:T(8,128)S(1)} %get-tuple-element.49), channel_id=1, source_target_pairs={{1,0},{2,1},{3,2},{4,3},{5,4},{6,5},{7,6},{9,8},{10,9},{11,10},{12... | collective-permute-start | bytes 245768 | tf_op jit(solution)/shard_map/ppermute | solution.py:725

commit v12 on v10

--- a/solution.py
+++ b/solution.py
@@ -157,7 +157,7 @@
         return 0
 
     chunks = particles // CHUNK
-    lax.fori_loop(0, chunks, functools.partial(step, 0), 0, unroll=2)
+    lax.fori_loop(0, chunks, functools.partial(step, 0), 0, unroll=4)
 
     def later(w, _):
         return lax.fori_loop(0, chunks, functools.partial(step, w), 0)
@@ -574,7 +574,7 @@
         acc[...] += added + lax.dot_general(hot_high * low, hot_low, NN, preferred_element_type=F32)
         return 0
 
-    lax.fori_loop(0, particles // chunk, step, 0, unroll=2)
+    lax.fori_loop(0, particles // chunk, step, 0, unroll=4)
     field = paired_rows(acc[...], 2 * half // rows, rows, rows_scratch)
     dep_ref[0] = field
     for edge, out in ((ey0_ref, dy0_ref), (ey1_ref, dy1_ref), (ex0_ref, dx0_ref), (ex1_ref, dx1_ref)):
@@ -647,7 +647,7 @@
         return 0
 
     chunks = particles // CHUNK
-    lax.fori_loop(0, chunks, step, 0, unroll=2)
+    lax.fori_loop(0, chunks, step, 0, unroll=4)
 
     def later(w, _):
         def again(c, _):

time: 89.8 us -> 87.8 us (0.978)
  Pallas kernels: 46.3 us -> 44.2 us
    pallas_call x1, Pallas kernels: 5.03 us -> 4 us  [heat_deposit(): pl.pallas_call(functools.partial(heat_kernel, chunk=1024, rows=rows), out...]
where the time goes in v12:
time: 87.8 us; the launch traced here: 86.2 us
  Pallas kernels  44.2 us (50%)
  starting transfers between devices  33 us (38%)
  waiting for transfers between devices  6.4 us (7%)
  local copies, waits for them, and re-layouts  1.73 us (2%)
  between operations  0.94 us (1%)
    ppermute x8, starting transfers between devices, moved(): return lax.ppermute(value, axis, pairs)  21.7 us
    pallas_call x1, Pallas kernels, contact(): pl.pallas_call(contact_kernel, grid=(devices // step,), out_shape=jax.Sha...  9.18 us
    pallas_call x1, Pallas kernels, deposit(): pl.pallas_call(functools.partial(deposit_kernel, chunk=1024), out_shape=(...  9.08 us
    pallas_call x1, Pallas kernels, place(): pl.pallas_call(place_kernel, out_shape=(jax.ShapeDtypeStruct((devices, 12...  8.65 us
    pallas_call x1, Pallas kernels, look_up(): pl.pallas_call(functools.partial(look_kernel, chunk=512), out_shape=jax.S...  6.65 us
    all_to_all x1, starting transfers between devices, shards(): lax.all_to_all(outgoing, ('gx', 'gy'), split_axis=0, concat_axis=0, tiled...  6.03 us
    all_to_all x1, starting transfers between devices, shards(): lax.all_to_all(result, ('gx', 'gy'), split_axis=0, concat_axis=0, tiled=T...  5.22 us
    all_to_all x1, waiting for transfers between devices, shards(): lax.all_to_all(result, ('gx', 'gy'), split_axis=0, concat_axis=0, tiled=T...  4.78 us
  transfers between devices with their start and end apart: 10, of which 2 were waited for; matrix products, arithmetic and copies ran while one was open for 1% of the time, Pallas kernels for 34%

profile of v12, /device:TPU:10, one launch (start us, length us, event | category | flops | bytes accessed | tf_op | source)
XLA Modules:
  0.0 86.2 jit_solution(2751657074761077335)
XLA Ops:
  0.7 8.7 %place_slots.1 = (f32[32,48,128]{2,1,0:T(8,128)}, s32[1,8192]{1,0:T(1,128)}, s32[1,8192]{1,0:T(1,128)}, s32[16,128]{1,0:T(8,128)}) custom-call(s32[32]{0:T(128)} %owner_ref.3, s32[1,8192]{1,0:T(1,128)} %bitcast.16, f32[3,8192]{1,0:T(4,128)} %pos_ref.1, f32[6,8192]{1,0:T(8,128)} %motion_ref.3, f32[1,8192]{1,0:T(1,128)} %bitcast.13, f32[1,8192]{1,0:T(1,128)} %bitcast.8), custom_call_target="tpu_custom_call" | custom-call | flops 3221225472 | bytes 1048576 | tf_op jit(solution)/shard_map/place_slots/pallas_call | solution.py:183
  9.3 6.0 %all-to-all-start = ((f32[32,48,128]{2,1,0:T(8,128)}), f32[32,48,128]{2,1,0:T(8,128)S(1)}, u32[]{:S(2)}, u32[]{:S(2)}) async-start(f32[32,48,128]{2,1,0:T(8,128)} %get-tuple-element.30), calls=%async_computation | async-start | bytes 1572864 | tf_op jit(solution)/shard_map/all_to_all | solution.py:739
  15.4 0.5 slice_reduce_fusion
  15.9 0.1 reshape_squeeze.6
  16.0 3.4 %collective-permute-start.2 = (f32[8,128]{1,0:T(8,128)S(1)}, f32[8,128]{1,0:T(8,128)S(1)}, u32[]{:S(2)}, u32[]{:S(2)}) collective-permute-start(f32[8,128]{1,0:T(8,128)S(1)} %reshape_squeeze.6), channel_id=1, source_target_pairs={{0,8},{8,16},{16,24},{1,9},{9,17},{17,25},{2,10},{10,18},{18,26},{... | collective-permute-start | bytes 12296 | tf_op jit(solution)/shard_map/ppermute | solution.py:713
  19.3 0.1 reshape_squeeze.7
  19.4 2.5 %collective-permute-start.3 = (f32[8,128]{1,0:T(8,128)S(1)}, f32[8,128]{1,0:T(8,128)S(1)}, u32[]{:S(2)}, u32[]{:S(2)}) collective-permute-start(f32[8,128]{1,0:T(8,128)S(1)} %reshape_squeeze.7), channel_id=1, source_target_pairs={{8,0},{16,8},{24,16},{9,1},{17,9},{25,17},{10,2},{18,10},{26,18},{... | collective-permute-start | bytes 12296 | tf_op jit(solution)/shard_map/ppermute | solution.py:713
  21.9 0.1 copy.14
  22.0 1.9 %collective-permute-start.1 = (f32[4,32,128]{2,1,0:T(8,128)S(1)}, f32[4,32,128]{2,1,0:T(8,128)S(1)}, u32[]{:S(2)}, u32[]{:S(2)}) collective-permute-start(f32[4,32,128]{2,1,0:T(8,128)S(1)} %get-tuple-element.59), channel_id=1, source_target_pairs={{1,0},{2,1},{3,2},{4,3},{5,4},{6,5},{7,6},{9,8},{10,9},{11,10},{12... | collective-permute-start | bytes 196616 | tf_op jit(solution)/shard_map/ppermute | solution.py:713
  24.0 2.4 %collective-permute-start = (f32[4,32,128]{2,1,0:T(8,128)S(1)}, f32[4,32,128]{2,1,0:T(8,128)S(1)}, u32[]{:S(2)}, u32[]{:S(2)}) collective-permute-start(f32[4,32,128]{2,1,0:T(8,128)S(1)} %get-tuple-element.60), channel_id=1, source_target_pairs={{0,1},{1,2},{2,3},{3,4},{4,5},{5,6},{6,7},{8,9},{9,10},{10,11},{11... | collective-permute-start | bytes 196616 | tf_op jit(solution)/shard_map/ppermute | solution.py:713
  26.4 0.0 copy-start.1
  26.4 0.0 copy-start.2
  26.4 0.0 copy-start.4
  26.4 6.6 %look_up.1.seen_ref = f32[4,8192]{1,0:T(4,128)S(1)} custom-call(f32[4,32,8,128]{3,2,1,0:T(8,128)S(1)} %copy-done, s32[1,8192]{1,0:T(1,128)S(1)} %bitcast.10), custom_call_target="tpu_custom_call" | custom-call | flops 2147483648 | bytes 1048576 | tf_op jit(solution)/shard_map/look_up/pallas_call | solution.py:427
  33.1 1.6 %all-to-all-done.slot_ref = f32[32,48,128]{2,1,0:T(8,128)S(1)} async-done(((f32[32,48,128]{2,1,0:T(8,128)}), f32[32,48,128]{2,1,0:T(8,128)S(1)}, u32[]{:S(2)}, u32[]{:S(2)}) %all-to-all-start) | async-done | bytes 786464 | tf_op jit(solution)/shard_map/all_to_all | solution.py:739
  34.7 0.9 %copy-done.10 = f32[32,48,128]{2,1,0:T(8,128)} copy-done((f32[32,48,128]{2,1,0:T(8,128)}, f32[32,48,128]{2,1,0:T(8,128)S(1)}, u32[]{:S(2)}) %copy-start.10) | copy-done | bytes 786456
  35.6 9.2 %contact_blocks.1 = f32[32,32,128]{2,1,0:T(8,128)} custom-call(f32[32,48,128]{2,1,0:T(8,128)} %copy-done.10, s32[128,128,128]{2,1,0:T(8,128)} %mask_ref.1), custom_call_target="tpu_custom_call" | custom-call | flops 134217728 | bytes 8388608 | tf_op jit(solution)/shard_map/contact_blocks/pallas_call | solution.py:309
  44.7 0.0 collective-permute-done.2.x0_ref
  44.7 0.0 collective-permute-done.3.x1_ref
  44.8 5.2 %all-to-all-start.1 = ((f32[32,32,128]{2,1,0:T(8,128)}), f32[32,32,128]{2,1,0:T(8,128)S(1)}, u32[]{:S(2)}, u32[]{:S(2)}) async-start(f32[32,32,128]{2,1,0:T(8,128)} %contact_blocks.1), calls=%async_computation.1 | async-start | bytes 1048576 | tf_op jit(solution)/shard_map/all_to_all | solution.py:756
  50.0 0.0 copy-start.5
  50.0 0.0 copy-start.6
  50.0 0.0 copy-start.8
  50.1 9.1 %deposit_fields.1 = (f32[8,8192]{1,0:T(8,128)S(1)}, f32[4,32,8,128]{3,2,1,0:T(8,128)S(1)}, f32[4,32,128]{2,1,0:T(8,128)S(1)}, f32[4,32,128]{2,1,0:T(8,128)S(1)},...) custom-call(f32[4,32,128]{2,1,0:T(8,128)S(1)} %collective-permute-done.y0_ref, ...), custom_call_target="tpu_custom_call" | custom-call | flops 4294967296 | bytes 2097152 | tf_op jit(solution)/shard_map/deposit_fields/pallas_call | solution.py:522
  59.1 4.8 %all-to-all-done.1.back_ref = f32[32,32,128]{2,1,0:T(8,128)S(1)} async-done(((f32[32,32,128]{2,1,0:T(8,128)}), f32[32,32,128]{2,1,0:T(8,128)S(1)}, u32[]{:S(2)}, u32[]{:S(2)}) %all-to-all-start.1) | async-done | bytes 524320 | tf_op jit(solution)/shard_map/all_to_all | solution.py:756
  63.9 4.0 %heat_deposit.1 = (f32[1,8192]{1,0:T(1,128)S(1)}, f32[1,32,8,128]{3,2,1,0:T(8,128)S(1)}, f32[5,32,128]{2,1,0:T(8,128)S(1)}, f32[5,32,128]{2,1,0:T(8,128)S(1)}, f...) custom-call(f32[32,32,128]{2,1,0:T(8,128)S(1)} %all-to-all-done.1.back_ref, s32[1,8192]{1,0:T(1,128)S(1)} %copy-done.7, ...), custom_call_target="tpu_custom_call" | custom-call | flops 1073741824 | bytes 1048576 | tf_op jit(solution)/shard_map/heat_deposit/pallas_call | solution.py:592
  67.9 3.4 %collective-permute-start.6 = (f32[10,128]{1,0:T(8,128)S(1)}, f32[10,128]{1,0:T(8,128)S(1)}, u32[]{:S(2)}, u32[]{:S(2)}) collective-permute-start(f32[10,128]{1,0:T(8,128)S(1)} %get-tuple-element.50), channel_id=1, source_target_pairs={{0,8},{8,16},{16,24},{1,9},{9,17},{17,25},{2,10},{10,18},{18,26},{... | collective-permute-start | bytes 15368 | tf_op jit(solution)/shard_map/ppermute | solution.py:713
  71.3 2.4 %collective-permute-start.7 = (f32[10,128]{1,0:T(8,128)S(1)}, f32[10,128]{1,0:T(8,128)S(1)}, u32[]{:S(2)}, u32[]{:S(2)}) collective-permute-start(f32[10,128]{1,0:T(8,128)S(1)} %get-tuple-element.51), channel_id=1, source_target_pairs={{8,0},{16,8},{24,16},{9,1},{17,9},{25,17},{10,2},{18,10},{26,18},{... | collective-permute-start | bytes 15368 | tf_op jit(solution)/shard_map/ppermute | solution.py:713
  73.8 1.9 %collective-permute-start.4 = (f32[5,32,128]{2,1,0:T(8,128)S(1)}, f32[5,32,128]{2,1,0:T(8,128)S(1)}, u32[]{:S(2)}, u32[]{:S(2)}) collective-permute-start(f32[5,32,128]{2,1,0:T(8,128)S(1)} %get-tuple-element.48), channel_id=1, source_target_pairs={{0,1},{1,2},{2,3},{3,4},{4,5},{5,6},{6,7},{8,9},{9,10},{10,11},{11... | collective-permute-start | bytes 245768 | tf_op jit(solution)/shard_map/ppermute | solution.py:713
  75.7 3.8 %collective-permute-start.5 = (f32[5,32,128]{2,1,0:T(8,128)S(1)}, f32[5,32,128]{2,1,0:T(8,128)S(1)}, u32[]{:S(2)}, u32[]{:S(2)}) collective-permute-start(f32[5,32,128]{2,1,0:T(8,128)S(1)} %get-tuple-element.49), channel_id=1, source_target_pairs={{1,0},{2,1},{3,2},{4,3},{5,4},{6,5},{7,6},{9,8},{10,9},{11,10},{12... | collective-permute-start | bytes 245768 | tf_op jit(solution)/shard_map/ppermute | solution.py:713
  79.6 4.6 %fetch_slots.1 = f32[7,8192]{1,0:T(8,128)} custom-call(s32[32]{0:T(128)S(1)} %copy-done.6, s32[16,128]{1,0:T(8,128)S(1)} %copy-done.9, f32[32,32,128]{2,1,0:T(8,128)S(1)} %all-to-all-done.1.back_ref, s32[1,8192]{1,0:T(1,128)S(1)} %bitcast.17, s32[1,8192]{1,0:T(1,128)S(1)} %copy-done.8, f32[8,8192]{1,0:T(8,128)S(1)} %get-tuple-element.42.base_ref, ...), custom_call_target="tpu_custom_call" | custom-call | flops 2147483648 | bytes 1048576 | tf_op jit(solution)/shard_map/fetch_slots/pallas_call | solution.py:669
  84.2 2.0 %spread_fields.1 = (f32[4,32,8,128]{3,2,1,0:T(8,128)}, f32[32,8,128]{2,1,0:T(8,128)}) custom-call(f32[4,32,8,128]{3,2,1,0:T(8,128)S(1)} %get-tuple-element.39.dep_ref, f32[1,32,8,128]{3,2,1,0:T(8,128)S(1)} %get-tuple-element.47.heat_ref, f32[5,32,128]{2,1,0:T(8,128)S(1)} %collective-permute-done.4.y0_ref, f32[5,32,128]{2,1,0:T(8,128)S(1)} %collective-permute-done.5.y1_ref, ...), custom_call_target="tpu_custom_call" | custom-call | flops 2621440 | bytes 2097152 | tf_op jit(solution)/shard_map/spread_fields/pallas_call | solution.py:698
  (22 shorter events, 0.1 us)
Async XLA Ops:
  0.6 14.7 %copy-start = (f32[4,32,8,128]{3,2,1,0:T(8,128)S(1)}, f32[4,32,8,128]{3,2,1,0:T(8,128)}, u32[]{:S(2)}) copy-start(f32[4,32,8,128]{3,2,1,0:T(8,128)} %fluid_ref.2) | copy-start | bytes 1572868
  0.6 25.7 %copy-start.3 = (s32[8192]{0:T(1024)S(1)}, s32[8192]{0:T(1024)}, u32[]{:S(2)}) copy-start(s32[8192]{0:T(1024)} %param.14) | copy-start | bytes 98308
  9.3 25.4 %all-to-all-start = ((f32[32,48,128]{2,1,0:T(8,128)}), f32[32,48,128]{2,1,0:T(8,128)S(1)}, u32[]{:S(2)}, u32[]{:S(2)}) async-start(f32[32,48,128]{2,1,0:T(8,128)} %get-tuple-element.30), calls=%async_computation | async-start | bytes 1572864 | tf_op jit(solution)/shard_map/all_to_all | solution.py:739
  16.0 28.8 %collective-permute-start.2 = (f32[8,128]{1,0:T(8,128)S(1)}, f32[8,128]{1,0:T(8,128)S(1)}, u32[]{:S(2)}, u32[]{:S(2)}) collective-permute-start(f32[8,128]{1,0:T(8,128)S(1)} %reshape_squeeze.6), channel_id=1, source_target_pairs={{0,8},{8,16},{16,24},{1,9},{9,17},{17,25},{2,10},{10,18},{18,26},{... | collective-permute-start | bytes 12296 | tf_op jit(solution)/shard_map/ppermute | solution.py:713
  19.4 25.3 %collective-permute-start.3 = (f32[8,128]{1,0:T(8,128)S(1)}, f32[8,128]{1,0:T(8,128)S(1)}, u32[]{:S(2)}, u32[]{:S(2)}) collective-permute-start(f32[8,128]{1,0:T(8,128)S(1)} %reshape_squeeze.7), channel_id=1, source_target_pairs={{8,0},{16,8},{24,16},{9,1},{17,9},{25,17},{10,2},{18,10},{26,18},{... | collective-permute-start | bytes 12296 | tf_op jit(solution)/shard_map/ppermute | solution.py:713
  22.0 22.7 %collective-permute-start.1 = (f32[4,32,128]{2,1,0:T(8,128)S(1)}, f32[4,32,128]{2,1,0:T(8,128)S(1)}, u32[]{:S(2)}, u32[]{:S(2)}) collective-permute-start(f32[4,32,128]{2,1,0:T(8,128)S(1)} %get-tuple-element.59), channel_id=1, source_target_pairs={{1,0},{2,1},{3,2},{4,3},{5,4},{6,5},{7,6},{9,8},{10,9},{11,10},{12... | collective-permute-start | bytes 196616 | tf_op jit(solution)/shard_map/ppermute | solution.py:713
  24.0 20.8 %collective-permute-start = (f32[4,32,128]{2,1,0:T(8,128)S(1)}, f32[4,32,128]{2,1,0:T(8,128)S(1)}, u32[]{:S(2)}, u32[]{:S(2)}) collective-permute-start(f32[4,32,128]{2,1,0:T(8,128)S(1)} %get-tuple-element.60), channel_id=1, source_target_pairs={{0,1},{1,2},{2,3},{3,4},{4,5},{5,6},{6,7},{8,9},{9,10},{10,11},{11... | collective-permute-start | bytes 196616 | tf_op jit(solution)/shard_map/ppermute | solution.py:713
  26.4 23.6 %copy-start.1 = (f32[6,8192]{1,0:T(8,128)S(1)}, f32[6,8192]{1,0:T(8,128)}, u32[]{:S(2)}) copy-start(f32[6,8192]{1,0:T(8,128)} %motion_ref.3) | copy-start | bytes 589828
  26.4 23.6 %copy-start.2 = (f32[8192]{0:T(1024)S(1)}, f32[8192]{0:T(1024)}, u32[]{:S(2)}) copy-start(f32[8192]{0:T(1024)} %param.13) | copy-start | bytes 98308
  26.4 23.6 %copy-start.4 = (f32[8192]{0:T(1024)S(1)}, f32[8192]{0:T(1024)}, u32[]{:S(2)}) copy-start(f32[8192]{0:T(1024)} %param.12) | copy-start | bytes 98308
  34.7 0.9 %copy-start.10 = (f32[32,48,128]{2,1,0:T(8,128)}, f32[32,48,128]{2,1,0:T(8,128)S(1)}, u32[]{:S(2)}) copy-start(f32[32,48,128]{2,1,0:T(8,128)S(1)} %all-to-all-done.slot_ref) | copy-start | bytes 2359300
  44.7 19.2 %copy-start.7 = (s32[1,8192]{1,0:T(1,128)S(1)}, s32[1,8192]{1,0:T(1,128)}, u32[]{:S(2)}) copy-start(s32[1,8192]{1,0:T(1,128)} %get-tuple-element.41.slot_ref) | copy-start | bytes 98308
  44.8 19.2 %all-to-all-start.1 = ((f32[32,32,128]{2,1,0:T(8,128)}), f32[32,32,128]{2,1,0:T(8,128)S(1)}, u32[]{:S(2)}, u32[]{:S(2)}) async-start(f32[32,32,128]{2,1,0:T(8,128)} %contact_blocks.1), calls=%async_computation.1 | async-start | bytes 1048576 | tf_op jit(solution)/shard_map/all_to_all | solution.py:756
  50.0 29.5 %copy-start.5 = (s32[8192,1]{0,1:T(1,128)S(1)}, s32[8192,1]{0,1:T(1,128)}, u32[]{:S(2)}) copy-start(s32[8192,1]{0,1:T(1,128)} %param.15) | copy-start | bytes 98308
  50.0 29.5 %copy-start.6 = (s32[32]{0:T(128)S(1)}, s32[32]{0:T(128)}, u32[]{:S(2)}) copy-start(s32[32]{0:T(128)} %owner_ref.3) | copy-start | bytes 388
  50.0 29.5 %copy-start.8 = (s32[1,8192]{1,0:T(1,128)S(1)}, s32[1,8192]{1,0:T(1,128)}, u32[]{:S(2)}) copy-start(s32[1,8192]{1,0:T(1,128)} %get-tuple-element.55.spot_ref) | copy-start | bytes 98308
  50.1 29.5 %copy-start.9 = (s32[16,128]{1,0:T(8,128)S(1)}, s32[16,128]{1,0:T(8,128)}, u32[]{:S(2)}) copy-start(s32[16,128]{1,0:T(8,128)} %get-tuple-element.54.tile_ref) | copy-start | bytes 24580
  67.9 16.3 %collective-permute-start.6 = (f32[10,128]{1,0:T(8,128)S(1)}, f32[10,128]{1,0:T(8,128)S(1)}, u32[]{:S(2)}, u32[]{:S(2)}) collective-permute-start(f32[10,128]{1,0:T(8,128)S(1)} %get-tuple-element.50), channel_id=1, source_target_pairs={{0,8},{8,16},{16,24},{1,9},{9,17},{17,25},{2,10},{10,18},{18,26},{... | collective-permute-start | bytes 15368 | tf_op jit(solution)/shard_map/ppermute | solution.py:713
  71.3 12.9 %collective-permute-start.7 = (f32[10,128]{1,0:T(8,128)S(1)}, f32[10,128]{1,0:T(8,128)S(1)}, u32[]{:S(2)}, u32[]{:S(2)}) collective-permute-start(f32[10,128]{1,0:T(8,128)S(1)} %get-tuple-element.51), channel_id=1, source_target_pairs={{8,0},{16,8},{24,16},{9,1},{17,9},{25,17},{10,2},{18,10},{26,18},{... | collective-permute-start | bytes 15368 | tf_op jit(solution)/shard_map/ppermute | solution.py:713
  73.8 10.4 %collective-permute-start.4 = (f32[5,32,128]{2,1,0:T(8,128)S(1)}, f32[5,32,128]{2,1,0:T(8,128)S(1)}, u32[]{:S(2)}, u32[]{:S(2)}) collective-permute-start(f32[5,32,128]{2,1,0:T(8,128)S(1)} %get-tuple-element.48), channel_id=1, source_target_pairs={{0,1},{1,2},{2,3},{3,4},{4,5},{5,6},{6,7},{8,9},{9,10},{10,11},{11... | collective-permute-start | bytes 245768 | tf_op jit(solution)/shard_map/ppermute | solution.py:713
  75.7 8.5 %collective-permute-start.5 = (f32[5,32,128]{2,1,0:T(8,128)S(1)}, f32[5,32,128]{2,1,0:T(8,128)S(1)}, u32[]{:S(2)}, u32[]{:S(2)}) collective-permute-start(f32[5,32,128]{2,1,0:T(8,128)S(1)} %get-tuple-element.49), channel_id=1, source_target_pairs={{1,0},{2,1},{3,2},{4,3},{5,4},{6,5},{7,6},{9,8},{10,9},{11,10},{12... | collective-permute-start | bytes 245768 | tf_op jit(solution)/shard_map/ppermute | solution.py:713
